TPU v7x, 32 devices: a whole 2x2x4 slice. The times are simulated.
32 devices in a mesh: tm: 8 (over y, x, core), feat: 4 (over z).
Axes of the slice: x: 2, y: 2, z: 4, core: 2. Of those that a mesh axis runs over, the one named last changes fastest.
Arguments:
- coords: int32 [4096, 3, 1500], P('tm'), may hold values from -29696 to 29696
- frame_scale: float32 [4096], P('tm'), may hold values from 1e-05 to 4e-05, as said below
- pairs: int32 [2, 8192], P(None, 'feat'), may hold values from 0 to 1499, as said below
- walker_lengths: int32 [8], replicated, may hold values from 1 to 1024, 4096 in all
Outputs:
- cov_zero: float32 [8192, 8192], P('tm', 'feat')
- cov_lag: float32 [8192, 8192], P('tm', 'feat')
Inputs may be any that keep to these rules, and one draw needn't show every extreme that they name: `frame_scale`: varies smoothly over frames with frame-to-frame noise. `pairs`: the two residues of a feature differ.
All inputs are finite; a program needn't handle non-finite values.
Results may differ from a plain program's by a relative error of at most 0.0016.
Values may be sent and summed in bfloat16 or wider, within the bound.
No kernel may reach another device: no remote copies, remote signals or barrier semaphores. Data moves between devices by JAX's collectives and lax.ppermute only.
A program may use at most 192 MiB of HBM per device.

v0:
```python
import jax
import jax.numpy as jnp
from jax import lax
from jax.sharding import PartitionSpec as P

LAG = 384


def contact_values(coords, frame_scale, pairs):
    frames_dev = coords.shape[0]
    residues = coords.shape[2]
    flat = coords.astype(jnp.float32).reshape(frames_dev * 3, residues)
    rows_iota = jnp.arange(residues, dtype=jnp.int32)[:, None]
    selector = (rows_iota == pairs[0][None, :]).astype(jnp.float32) - (
        rows_iota == pairs[1][None, :]
    ).astype(jnp.float32)
    diff = jnp.dot(
        flat, selector, precision=lax.Precision.HIGHEST, preferred_element_type=jnp.float32
    )
    diff = diff.reshape(frames_dev, 3, pairs.shape[1])
    squares = diff[:, 0] * diff[:, 0] + diff[:, 1] * diff[:, 1] + diff[:, 2] * diff[:, 2]
    dist_sq = (frame_scale * frame_scale)[:, None] * squares
    return 1.0 / (1.0 + dist_sq * dist_sq * dist_sq)


def walker_mask(walker_lengths, count, frames_all):
    ends = jnp.cumsum(walker_lengths)
    times = jnp.arange(count, dtype=jnp.int32)
    later = times + LAG
    own = jnp.sum((times[:, None] >= ends[None, :]).astype(jnp.int32), axis=1)
    ahead = jnp.sum((later[:, None] >= ends[None, :]).astype(jnp.int32), axis=1)
    return (own == ahead) & (later < frames_all)


def contract(left, right):
    return lax.dot_general(
        left, right, (((0,), (0,)), ((), ())), preferred_element_type=jnp.float32
    )


def shards(coords, frame_scale, pairs, walker_lengths):
    tm_count = lax.axis_size("tm")
    frames_dev = coords.shape[0]
    local_feats = pairs.shape[1]
    frames_all = frames_dev * tm_count
    contact = contact_values(coords, frame_scale, pairs)
    totals = lax.psum(jnp.sum(contact, axis=0), "tm")
    centered = (contact - totals / jnp.float32(frames_all)).astype(jnp.bfloat16)
    npairs = jnp.sum(jnp.maximum(walker_lengths - LAG, 0)).astype(jnp.float32)
    column_series = lax.all_gather(centered, "tm", axis=0, tiled=True)
    wide = lax.all_gather(centered, "feat", axis=1, tiled=True)
    row_series = lax.all_to_all(wide, "tm", split_axis=1, concat_axis=0, tiled=True)
    valid = walker_mask(walker_lengths, frames_all, frames_all)
    later = jnp.concatenate(
        [column_series[LAG:], jnp.zeros((LAG, local_feats), jnp.bfloat16)], axis=0
    )
    lagged = jnp.where(valid[:, None], later, jnp.zeros_like(later))
    same = contract(row_series, column_series)
    cross = contract(row_series, lagged)
    return (same / jnp.float32(frames_all), cross / npairs)


def solution(mesh):
    return jax.shard_map(
        shards,
        mesh=mesh,
        in_specs=(P("tm", None, None), P("tm"), P(None, "feat"), P()),
        out_specs=(P("tm", "feat"), P("tm", "feat")),
        check_vma=False,
    )
```

profile of v0, /device:TPU:0, one launch (start us, length us, event | category | flops | bytes accessed | tf_op | source)
XLA Modules:
  0.0 589.2 jit_solution(8876588444259159393)
XLA Ops:
  7.2 0.0 all-gather.3.cloned.1.call-start
  7.2 8.6 %convert_element_type.23 = f32[512,3,1500]{0,2,1:T(8,128)} convert(s32[512,3,1500]{0,2,1:T(8,128)} %param.4) | non-fusion elementwise | flops 2304000 | bytes 18432000 | tf_op jit(solution)/shard_map/convert_element_type | solution.py:12
  15.8 13.9 %copy.8 = f32[512,3,1500]{2,1,0:T(4,128)} copy(f32[512,3,1500]{0,2,1:T(8,128)} %convert_element_type.23) | data formatting | bytes 18432000 | tf_op jit(solution)/shard_map/convert_element_type | solution.py:12
  29.7 15.0 %reshape.57 = f32[1536,1500]{1,0:T(8,128)} reshape(f32[512,3,1500]{2,1,0:T(4,128)} %copy.8) | data formatting | bytes 18432000 | tf_op jit(solution)/shard_map/reshape | solution.py:12
  44.7 3.3 fusion.30
  48.0 79.1 %fusion.8 = f32[1536,2048]{1,0:T(8,128)} fusion(f32[1536,1500]{1,0:T(8,128)} %reshape.57, f32[1500,2048]{1,0:T(8,128)S(1)} %fusion.30), kind=kOutput, calls=%fused_computation.10 | convolution fusion | flops 56623104000 | bytes 34086912 | tf_op jit(solution)/shard_map/dot_general | solution.py:17
  127.1 19.3 %reshape.58 = f32[512,3,2048]{2,1,0:T(4,128)} reshape(f32[1536,2048]{1,0:T(8,128)} %fusion.8) | data formatting | bytes 25165824 | tf_op jit(solution)/shard_map/reshape | solution.py:20
  146.3 26.5 %fusion.16 = f32[512,1,2048]{2,1,0:T(1,128)S(1)} fusion(f32[512,3,2048]{2,1,0:T(4,128)} %reshape.58), kind=kLoop, calls=%fused_computation.20 | loop fusion | flops 5242880 | bytes 16777216 | tf_op jit(solution)/shard_map/add | solution.py:21
  172.9 2.0 copy-done
  174.9 2.2 fusion.21
  177.1 15.5 %psum.7 = f32[2048]{0:T(1024)S(1)} all-reduce(f32[2048]{0:T(1024)S(1)} %fusion.21), channel_id=1, replica_groups=mesh['tm'=8,'feat'=4] {'tm'}, use_global_device_ids=true, to_apply=%region_1.0 | all-reduce | flops 2048 | bytes 16384 | tf_op jit(solution)/shard_map/psum | solution.py:47
  192.6 5.9 subtract_convert_fusion
  198.5 0.0 all-gather.5.cloned.1.call-start
  198.6 0.7 all-gather.5.cloned.1.call-update
  199.3 148.4 %all-gather.3.cloned.1.call-done = bf16[512,8192]{1,0:T(8,128)(2,1)} async-done(((bf16[512,2048]{1,0:T(8,128)(2,1)}), bf16[512,8192]{1,0:T(8,128)(2,1)}) %all-gather.3.cloned.1.call-update) | async-done | bytes 8388624 | tf_op jit(solution)/shard_map/all_gather | solution.py:51
  347.7 8.5 %copy.18 = bf16[64,8,8,1024]{3,2,0,1:T(8,128)(2,1)} copy(bf16[64,8,8,1024]{3,2,1,0:T(8,128)(2,1)} %bitcast.29) | data formatting | bytes 16777216 | tf_op jit(solution)/shard_map/all_to_all | solution.py:52
  356.1 5.4 all-to-all-start
  361.6 0.6 maximum_reduce_fusion
  362.7 0.2 reduce-window.8
  362.9 0.1 convert_reduce_fusion
  363.1 157.8 %all-gather.5.cloned.1.call-done = bf16[4096,2048]{1,0:T(8,128)(2,1)} async-done(((bf16[512,2048]{1,0:T(8,128)(2,1)}), bf16[4096,2048]{1,0:T(8,128)(2,1)}) %all-gather.5.cloned.1.call-update) | async-done | bytes 16777232 | tf_op jit(solution)/shard_map/all_gather | solution.py:50
  520.9 11.2 %slice.30 = bf16[3712,2048]{1,0:T(8,128)(2,1)} slice(bf16[4096,2048]{1,0:T(8,128)(2,1)} %all-gather.5.cloned.1.call-done), slice={[384:4096], [0:2048]} | slice | bytes 30408704 | tf_op jit(solution)/shard_map/slice | solution.py:55
  532.1 25.6 %broadcast_divide_fusion = f32[1024,2048]{1,0:T(8,128)} fusion(f32[]{:T(128)S(6)} %convert_element_type.27, bf16[4096,1024]{1,0:T(8,128)(2,1)} %bitcast.4, bf16[3712,2048]{1,0:T(8,128)(2,1)} %slice.30, pred[4096]{0:T(1024)(128)(4,1)S(1)} %compare_and_fusion), kind=kOutput, calls=%fused_computation.25 | convolution fusion | flops 17190354944 | bytes 31985668 | tf_op jit(solution)/shard_map/dot_general | solution.py:36
  557.8 24.3 %convolution_multiply_fusion = f32[1024,2048]{1,0:T(8,128)} fusion(bf16[4096,1024]{1,0:T(8,128)(2,1)} %bitcast.4, bf16[4096,2048]{1,0:T(8,128)(2,1)} %all-gather.5.cloned.1.call-done), kind=kOutput, calls=%fused_computation.16 | convolution fusion | flops 17181966336 | bytes 33554432 | tf_op jit(solution)/shard_map/dot_general | solution.py:36
  (14 shorter events, 0.1 us)
Async XLA Ops:
  7.2 340.5 %all-gather.3.cloned.1.call-start = ((), (), s32[]{:S(2)}) async-start(), calls=%async_computation.1 | async-start | bytes 10485760 | tf_op jit(solution)/shard_map/all_gather | solution.py:51
  29.7 15.0 %copy-start.1 = (s32[2,2048]{1,0:T(2,128)S(1)}, s32[2,2048]{1,0:T(2,128)}, u32[]{:S(2)}) copy-start(s32[2,2048]{1,0:T(2,128)} %param.6) | copy-start | bytes 49156
  146.3 26.5 %copy-start.2 = (f32[512]{0:T(512)S(1)}, f32[512]{0:T(512)}, u32[]{:S(2)}) copy-start(f32[512]{0:T(512)} %param.5) | copy-start | bytes 6148
  172.9 2.0 copy-start
  198.5 322.4 %all-gather.5.cloned.1.call-start = ((), (), s32[]{:S(2)}) async-start(), calls=%async_computation.2 | async-start | bytes 18874368 | tf_op jit(solution)/shard_map/all_gather | solution.py:50
  356.1 5.4 copy-start.3
  356.1 176.0 %all-to-all-start = ((bf16[512,8,1024]{2,0,1:T(8,128)(2,1)}), bf16[512,8,1024]{2,0,1:T(8,128)(2,1)}, u32[]{:S(2)}, u32[]{:S(2)}) async-start(bf16[512,8,1024]{2,0,1:T(8,128)(2,1)} %bitcast.28), calls=%async_computation | async-start | bytes 16777216 | tf_op jit(solution)/shard_map/all_to_all | solution.py:52
Sparse Core Ops, SparseCore 0:
  198.6 148.9 all-gather.2
  350.1 170.7 all-gather.4
where the time goes:
time: 595 us; the launch traced here: 589 us
  waiting for transfers between devices  307 us (52%)
  matrix products  129 us (22%)
  local copies, waits for them, and re-layouts  69.8 us (12%)
  other arithmetic  47.5 us (8%)
  blocking collectives  15.5 us (3%)
  between operations  14.9 us (3%)
    all_gather x1, waiting for transfers between devices, shards(): column_series = lax.all_gather(centered, 'tm', axis=0, tiled=True)  158 us
    all_gather x1, waiting for transfers between devices, shards(): wide = lax.all_gather(centered, 'feat', axis=1, tiled=True)  148 us
    dot_general x1, matrix products, contact_values(): jnp.dot(flat, selector, precision=lax.Precision.HIGHEST, preferred_elemen...  79.1 us
    dot_general x2, matrix products, contract(): lax.dot_general(left, right, (((0,), (0,)), ((), ())), preferred_element_...  50 us
    add x1, other arithmetic, contact_values(): diff[:, 0] * diff[:, 0] + diff[:, 1] * diff[:, 1] + diff[:, 2] * diff[:, 2]  26.5 us
    reshape x1, local copies, waits for them, and re-layouts, contact_values(): diff = diff.reshape(frames_dev, 3, pairs.shape[1])  19.3 us
    psum x1, blocking collectives, shards(): totals = lax.psum(jnp.sum(contact, axis=0), 'tm')  15.5 us
    reshape x1, local copies, waits for them, and re-layouts, contact_values(): flat = coords.astype(jnp.float32).reshape(frames_dev * 3, residues)  15 us
  transfers between devices with their start and end apart: 3, of which 2 were waited for; matrix products, arithmetic and copies ran while one was open for 4% of the time, Pallas kernels for 0%

commit v1 on v0

--- a/solution.py
+++ b/solution.py
@@ -1,9 +1,15 @@
+import functools
+
 import jax
 import jax.numpy as jnp
 from jax import lax
+from jax.experimental import pallas as pl
+from jax.experimental.pallas import tpu as pltpu
 from jax.sharding import PartitionSpec as P
 
 LAG = 384
+CHUNK = 128
+VMEM_LIMIT = 56 * 1024 * 1024
 
 
 def contact_values(coords, frame_scale, pairs):
@@ -38,7 +44,7 @@
     )
 
 
-def shards(coords, frame_scale, pairs, walker_lengths):
+def plain_shards(coords, frame_scale, pairs, walker_lengths):
     tm_count = lax.axis_size("tm")
     frames_dev = coords.shape[0]
     local_feats = pairs.shape[1]
@@ -60,11 +66,270 @@
     return (same / jnp.float32(frames_all), cross / npairs)
 
 
+def split_coords(x):
+    high = ((x + 128) >> 8) << 8
+    low = x - high
+    return (
+        high.astype(jnp.float32).astype(jnp.bfloat16),
+        low.astype(jnp.float32).astype(jnp.bfloat16),
+    )
+
+
+def selector_rows(pairs_block, depth):
+    feats = pairs_block.shape[0]
+    lanes = lax.broadcasted_iota(jnp.int32, (feats, depth), 1)
+    first = pairs_block[:, 0:1]
+    second = pairs_block[:, 1:2]
+    one = jnp.float32(1.0)
+    zero = jnp.float32(0.0)
+    value = jnp.where(lanes == first, one, jnp.where(lanes == second, -one, zero))
+    return value.astype(jnp.bfloat16)
+
+
+def switch(squares, scale):
+    dist_sq = (scale * scale) * squares
+    return 1.0 / (1.0 + dist_sq * dist_sq * dist_sq)
+
+
+def contact_kernel(with_sums, slot_ref, coords_ref, scale_ref, pairs_ref, out_ref, *rest):
+    if with_sums:
+        sums_ref, padded, parts = rest
+    else:
+        padded, parts = rest
+    residues, frames = coords_ref.shape[1:]
+    depth = padded.shape[0]
+
+    @pl.when(pl.program_id(0) == 0)
+    def _():
+        padded[...] = jnp.zeros_like(padded)
+        for k in range(3):
+            padded[0:residues, :] = coords_ref[k]
+            high, low = split_coords(padded[...])
+            parts[0:depth, k * frames : (k + 1) * frames] = high
+            parts[depth : 2 * depth, k * frames : (k + 1) * frames] = low
+
+    selector = selector_rows(pairs_ref[...], depth)
+    both = jnp.concatenate([selector, selector], axis=1)
+    diff = jnp.dot(both, parts[...], preferred_element_type=jnp.float32)
+    d0 = diff[:, 0:frames]
+    d1 = diff[:, frames : 2 * frames]
+    d2 = diff[:, 2 * frames : 3 * frames]
+    contact = switch(d0 * d0 + d1 * d1 + d2 * d2, scale_ref[...])
+    out_ref[...] = contact
+    if with_sums:
+        part = contact[:, 0:CHUNK]
+        for c in range(1, frames // CHUNK):
+            part = part + contact[:, c * CHUNK : (c + 1) * CHUNK]
+        sums_ref[...] = jnp.sum(part.T, axis=0, keepdims=True)
+
+
+def contacts(slot, coords_t, scale_row, pairs_t, frames, block, with_sums):
+    residues = coords_t.shape[1]
+    feats = pairs_t.shape[0]
+    depth = -(-residues // 256) * 256
+    out_shape = [jax.ShapeDtypeStruct((feats, frames), jnp.float32)]
+    out_specs = [pl.BlockSpec((block, frames), lambda n, s: (n, 0))]
+    if with_sums:
+        out_shape.append(jax.ShapeDtypeStruct((1, feats), jnp.float32))
+        out_specs.append(pl.BlockSpec((1, block), lambda n, s: (0, n)))
+    flops = 2 * feats * 2 * depth * 3 * frames
+    return pl.pallas_call(
+        functools.partial(contact_kernel, with_sums),
+        out_shape=out_shape,
+        grid_spec=pltpu.PrefetchScalarGridSpec(
+            num_scalar_prefetch=1,
+            grid=(feats // block,),
+            in_specs=[
+                pl.BlockSpec((3, residues, frames), lambda n, s: (0, 0, s[0])),
+                pl.BlockSpec((1, frames), lambda n, s: (0, s[0])),
+                pl.BlockSpec((block, 2), lambda n, s: (n, 0)),
+            ],
+            out_specs=out_specs,
+            scratch_shapes=[
+                pltpu.VMEM((depth, frames), jnp.int32),
+                pltpu.VMEM((2 * depth, 3 * frames), jnp.bfloat16),
+            ],
+        ),
+        compiler_params=pltpu.CompilerParams(vmem_limit_bytes=VMEM_LIMIT),
+        cost_estimate=pl.CostEstimate(
+            flops=flops, bytes_accessed=12 * residues * frames + 4 * feats * frames, transcendentals=0
+        ),
+    )(slot, coords_t, scale_row, pairs_t)
+
+
+def as_column(row):
+    return jnp.broadcast_to(row, (CHUNK, row.shape[1])).T
+
+
+def center_kernel(slot_ref, cols_ref, cols_mean_ref, rows_ref, rows_mean_ref, cols_out, rows_out):
+    col = as_column(cols_mean_ref[...])
+    for c in range(cols_ref.shape[1] // CHUNK):
+        lanes = slice(c * CHUNK, (c + 1) * CHUNK)
+        cols_out[:, lanes] = (cols_ref[:, lanes] - col).astype(jnp.bfloat16)
+    rows_out[...] = (rows_ref[...] - as_column(rows_mean_ref[...])).astype(jnp.bfloat16)
+
+
+def center(slot, cols, rows, mean, steps=4):
+    feats, frames = cols.shape
+    all_feats, chunk = rows.shape
+    cols_block = feats // steps
+    rows_block = all_feats // steps
+    return pl.pallas_call(
+        center_kernel,
+        out_shape=[
+            jax.ShapeDtypeStruct(cols.shape, jnp.bfloat16),
+            jax.ShapeDtypeStruct(rows.shape, jnp.bfloat16),
+        ],
+        grid_spec=pltpu.PrefetchScalarGridSpec(
+            num_scalar_prefetch=1,
+            grid=(steps,),
+            in_specs=[
+                pl.BlockSpec((cols_block, frames), lambda n, s: (n, 0)),
+                pl.BlockSpec((1, cols_block), lambda n, s: (0, s[0] * steps + n)),
+                pl.BlockSpec((rows_block, chunk), lambda n, s: (n, 0)),
+                pl.BlockSpec((1, rows_block), lambda n, s: (0, n)),
+            ],
+            out_specs=[
+                pl.BlockSpec((cols_block, frames), lambda n, s: (n, 0)),
+                pl.BlockSpec((rows_block, chunk), lambda n, s: (n, 0)),
+            ],
+        ),
+        compiler_params=pltpu.CompilerParams(vmem_limit_bytes=VMEM_LIMIT),
+        cost_estimate=pl.CostEstimate(
+            flops=2 * (cols.size + rows.size), bytes_accessed=6 * (cols.size + rows.size), transcendentals=0
+        ),
+    )(slot, cols, mean, rows, mean)
+
+
+def product_kernel(
+    count, parts, me_ref, rows_ref, mask_ref, factors_ref, *rest
+):
+    cols_refs = rest[:count]
+    same_ref, cross_ref, left = rest[count:]
+    frames = parts * CHUNK
+    behind = LAG // CHUNK
+
+    @pl.when(pl.program_id(0) == 0)
+    def _():
+        for d in range(count):
+            j = me_ref[0] ^ d
+            before = jnp.maximum(j - 1, 0)
+            mask = mask_ref[j]
+            for z in range(parts):
+                lanes = slice(d * frames + z * CHUNK, d * frames + (z + 1) * CHUNK)
+                left[0, :, lanes] = rows_ref[z, j]
+                if z >= behind:
+                    shifted = rows_ref[z - behind, j]
+                else:
+                    shifted = rows_ref[z - behind + parts, before]
+                left[1, :, lanes] = shifted * mask[:, z * CHUNK : (z + 1) * CHUNK].astype(jnp.bfloat16)
+
+    right = jnp.concatenate([ref[...] for ref in cols_refs], axis=1)
+    dims = (((1,), (1,)), ((), ()))
+    same = lax.dot_general(left[0], right, dims, preferred_element_type=jnp.float32)
+    same_ref[...] = same * factors_ref[0]
+    cross = lax.dot_general(left[1], right, dims, preferred_element_type=jnp.float32)
+    cross_ref[...] = cross / factors_ref[1]
+
+
+def products(me, rows, mask, factors, cols, block=512):
+    parts, count, row_feats, _ = rows.shape
+    feats, frames = cols[0].shape
+    out = jax.ShapeDtypeStruct((row_feats, feats), jnp.float32)
+    whole = lambda shape: pl.BlockSpec(shape, lambda n, s: (0,) * len(shape))
+    return pl.pallas_call(
+        functools.partial(product_kernel, count, parts),
+        out_shape=[out, out],
+        grid_spec=pltpu.PrefetchScalarGridSpec(
+            num_scalar_prefetch=1,
+            grid=(feats // block,),
+            in_specs=[
+                pl.BlockSpec(rows.shape, lambda n, s: (0, 0, 0, 0), pipeline_mode=pl.Buffered(1)),
+                whole(mask.shape),
+                pl.BlockSpec(memory_space=pltpu.SMEM),
+            ]
+            + [pl.BlockSpec((block, frames), lambda n, s: (n, 0))] * count,
+            out_specs=[pl.BlockSpec((row_feats, block), lambda n, s: (0, n))] * 2,
+            scratch_shapes=[pltpu.VMEM((2, row_feats, count * frames), jnp.bfloat16)],
+        ),
+        compiler_params=pltpu.CompilerParams(vmem_limit_bytes=VMEM_LIMIT),
+        cost_estimate=pl.CostEstimate(
+            flops=4 * row_feats * feats * count * frames,
+            bytes_accessed=2 * rows.size + 2 * count * feats * frames + 8 * row_feats * feats,
+            transcendentals=0,
+        ),
+    )(me, rows, mask, factors, *cols)
+
+
+def swap(x, bit, count):
+    return lax.ppermute(x, "tm", [(i, i ^ bit) for i in range(count)])
+
+
+def square_gather(x):
+    half = x.shape[0] // 2
+    core = swap(x, 1, 8)
+    along_x = swap(x, 2, 8)
+    along_y = swap(x, 4, 8)
+    corner_low = swap(along_x[:half], 4, 8)
+    corner_high = swap(along_y[half:], 2, 8)
+    corner = jnp.concatenate([corner_low, corner_high], axis=0)
+    return [
+        x,
+        core,
+        along_x,
+        swap(along_x, 1, 8),
+        along_y,
+        swap(along_y, 1, 8),
+        corner,
+        swap(corner, 1, 8),
+    ]
+
+
+def shards(coords, frame_scale, pairs, walker_lengths):
+    tm_count = lax.axis_size("tm")
+    feat_count = lax.axis_size("feat")
+    frames_dev = coords.shape[0]
+    feats = pairs.shape[1]
+    all_feats = feats * feat_count
+    frames_all = frames_dev * tm_count
+    me = lax.axis_index("tm").astype(jnp.int32).reshape(1)
+    slot = lax.axis_index("feat").astype(jnp.int32).reshape(1)
+    start = jnp.zeros((1,), jnp.int32)
+
+    coords_t = jnp.transpose(coords, (1, 2, 0))
+    scale_row = frame_scale.reshape(1, frames_dev)
+    all_pairs = lax.all_gather(pairs, "feat", axis=1, tiled=True)
+
+    raw_cols, sums = contacts(start, coords_t, scale_row, pairs.T, frames_dev, 512, True)
+    every = lax.all_gather(sums, ("tm", "feat"), axis=0, tiled=True)
+    (raw_rows,) = contacts(slot, coords_t, scale_row, all_pairs.T, CHUNK, 1024, False)
+    totals = jnp.sum(every.reshape(tm_count, feat_count * feats), axis=0)
+    mean = (totals / jnp.float32(frames_all)).reshape(1, all_feats)
+
+    cols, rows = center(slot, raw_cols, raw_rows, mean)
+    rows = rows.reshape(tm_count, all_feats // tm_count, CHUNK)
+    rows = lax.all_to_all(rows, "tm", split_axis=0, concat_axis=0, tiled=True)
+    rows = lax.all_gather(rows, "feat", axis=0, tiled=False)
+    cols = square_gather(cols)
+
+    valid = walker_mask(walker_lengths, frames_all, frames_all)
+    mask = jnp.concatenate([jnp.zeros((LAG,), jnp.float32), valid[:-LAG].astype(jnp.float32)])
+    npairs = jnp.sum(jnp.maximum(walker_lengths - LAG, 0)).astype(jnp.float32)
+    factors = jnp.stack([jnp.float32(1.0 / frames_all), npairs])
+    return products(me, rows, mask.reshape(tm_count, 1, frames_dev), factors, cols)
+
+
 def solution(mesh):
-    return jax.shard_map(
-        shards,
-        mesh=mesh,
-        in_specs=(P("tm", None, None), P("tm"), P(None, "feat"), P()),
-        out_specs=(P("tm", "feat"), P("tm", "feat")),
-        check_vma=False,
-    )
+    def run(coords, frame_scale, pairs, walker_lengths):
+        tm_count, feat_count = mesh.shape["tm"], mesh.shape["feat"]
+        frames_dev = coords.shape[0] // tm_count
+        fits = tm_count == 8 and frames_dev == feat_count * CHUNK and frames_dev > LAG
+        return jax.shard_map(
+            shards if fits else plain_shards,
+            mesh=mesh,
+            in_specs=(P("tm", None, None), P("tm"), P(None, "feat"), P()),
+            out_specs=(P("tm", "feat"), P("tm", "feat")),
+            check_vma=False,
+        )(coords, frame_scale, pairs, walker_lengths)
+
+    return run

time: 595 us -> 454 us (0.76)
  waiting for transfers between devices: 307 us -> 136 us
  blocking collectives: 15.5 us -> 175 us
  matrix products: 129 us -> 0 us
  Pallas kernels: 0 us -> 116 us
  local copies, waits for them, and re-layouts: 69.8 us -> 4.75 us
  other arithmetic: 47.5 us -> 3.48 us
    all_gather x2 -> x1, waiting for transfers between devices: 306 us -> 67.3 us  [shards(): rows = lax.all_gather(rows, 'feat', axis=0, tiled=False)]
    all_gather x0 -> x2, blocking collectives: none -> 144 us  [the longest x1 73.2 us: shards(): all_pairs = lax.all_gather(pairs, 'feat', axis=1, tiled=True)]
    dot_general x3 -> x0, matrix products: 129 us -> none  [the longest x1 79.1 us: contact_values(): jnp.dot(flat, selector, precision=lax.Precision.HIGHEST, preferred_elemen...]
    pallas_call x0 -> x4, Pallas kernels: none -> 116 us  [the longest x2 62.8 us: contacts(): pl.pallas_call(functools.partial(contact_kernel, with_sums), out_shape=ou...]
    ppermute x0 -> x8, waiting for transfers between devices: none -> 69.1 us  [swap(): return lax.ppermute(x, 'tm', [(i, i ^ bit) for i in range(count)])]
    reshape x2 -> x1, local copies, waits for them, and re-layouts: 34.2 us -> 0.12 us  [shards(): totals = jnp.sum(every.reshape(tm_count, feat_count * feats), axis=0)]
    all_to_all x0 -> x1, blocking collectives: none -> 30.9 us  [shards(): rows = lax.all_to_all(rows, 'tm', split_axis=0, concat_axis=0, tiled=True)]
    add x1 -> x0, other arithmetic: 26.5 us -> none  [contact_values(): diff[:, 0] * diff[:, 0] + diff[:, 1] * diff[:, 1] + diff[:, 2] * diff[:, 2]]
  transfers between devices with their start and end apart: 3 -> 9, of which waited for: 2 -> 6; matrix products, arithmetic and copies ran while one was open for 4% -> 1% of each run, Pallas kernels for 0% -> 0%
where the time goes in v1:
time: 454 us
  blocking collectives  175 us (39%)
  waiting for transfers between devices  136 us (30%)
  Pallas kernels  116 us (26%)
  between operations  14.8 us (3%)
  local copies, waits for them, and re-layouts  4.75 us (1%)
    all_gather x1, blocking collectives, shards(): all_pairs = lax.all_gather(pairs, 'feat', axis=1, tiled=True)  73.2 us
    all_gather x1, blocking collectives, shards(): every = lax.all_gather(sums, ('tm', 'feat'), axis=0, tiled=True)  70.6 us
    ppermute x8, waiting for transfers between devices, swap(): return lax.ppermute(x, 'tm', [(i, i ^ bit) for i in range(count)])  69.1 us
    all_gather x1, waiting for transfers between devices, shards(): rows = lax.all_gather(rows, 'feat', axis=0, tiled=False)  67.3 us
    pallas_call x2, Pallas kernels, contacts(): pl.pallas_call(functools.partial(contact_kernel, with_sums), out_shape=ou...  62.8 us
    pallas_call x1, Pallas kernels, products(): pl.pallas_call(functools.partial(product_kernel, count, parts), out_shape...  47 us
    all_to_all x1, blocking collectives, shards(): rows = lax.all_to_all(rows, 'tm', split_axis=0, concat_axis=0, tiled=True)  30.9 us
  transfers between devices with their start and end apart: 9, of which 6 were waited for; matrix products, arithmetic and copies ran while one was open for 1% of the time, Pallas kernels for 0%

profile of v1, /device:TPU:0, one launch (start us, length us, event | category | flops | bytes accessed | tf_op | source)
XLA Modules:
  0.0 453.6 jit_solution(13948763993417740099)
XLA Ops:
  7.2 1.1 copy.10
  8.3 73.2 %all_gather.13 = s32[2,8192]{0,1:T(8,128)} all-gather(s32[2,2048]{0,1:T(8,128)S(1)} %copy.10), channel_id=1, replica_groups=mesh['tm'=8,'feat'=4] {'feat'}, dimensions={1}, use_global_device_ids=true | all-gather | bytes 81920 | tf_op jit(solution)/shard_map/all_gather | solution.py:301
  81.5 30.2 %shard_map.59 = (f32[2048,512]{1,0:T(8,128)}, f32[1,2048]{1,0:T(1,128)}) custom-call(s32[1]{0:T(128)} %constant.9.clone.1.slot_ref, s32[3,1500,512]{2,1,0:T(8,128)} %bitcast.22, f32[1,512]{1,0:T(1,128)} %bitcast.25, s32[2048,2]{1,0:T(8,128)} %bitcast.15), custom_call_target="tpu_custom_call" | custom-call | flops 19327352832 | bytes 13410304 | tf_op jit(solution)/shard_map/pallas_call | solution.py:136
  111.7 70.6 %all-gather.1 = f32[32,1,2048]{2,1,0:T(1,128)S(1)} all-gather(f32[1,1,2048]{2,1,0:T(1,128)} %bitcast.20), channel_id=1, replica_groups=mesh['tm'=8,'feat'=4] {'tm','feat'}, dimensions={0}, use_global_device_ids=true | all-gather | bytes 270336 | tf_op jit(solution)/shard_map/all_gather | solution.py:304
  182.3 0.6 reduce
  183.1 0.6 broadcast_multiply_fusion
  183.7 32.6 %shard_map.60.rows_ref = f32[8192,128]{1,0:T(8,128)} custom-call(s32[1]{0:T(128)} %bitcast.1.slot_ref, s32[3,1500,512]{2,1,0:T(8,128)} %bitcast.23, f32[1,512]{1,0:T(1,128)} %bitcast.26, s32[8192,2]{1,0:T(8,128)} %bitcast.14), custom_call_target="tpu_custom_call" | custom-call | flops 19327352832 | bytes 6498304 | tf_op jit(solution)/shard_map/pallas_call | solution.py:136
  216.3 6.4 %shard_map.61 = (bf16[2048,512]{1,0:T(8,128)(2,1)}, bf16[8192,128]{1,0:T(8,128)(2,1)}) custom-call(s32[1]{0:T(128)} %bitcast.1.slot_ref, f32[2048,512]{1,0:T(8,128)} %get-tuple-element.6.cols_ref, f32[1,8192]{1,0:T(1,128)} %bitcast.17, f32[8192,128]{1,0:T(8,128)} %shard_map.60.rows_ref, f32[1,8192]{1,0:T(1,128)} %bitcast.18), custom_call_target="tpu_custom_call" | custom-call | flops 4194304 | bytes 12582912 | tf_op jit(solution)/shard_map/pallas_call | solution.py:177
  222.7 30.9 %all_to_all.5 = bf16[8,1024,128]{2,1,0:T(8,128)(2,1)} all-to-all(bf16[8,1024,128]{2,1,0:T(8,128)(2,1)} %bitcast.16), channel_id=1, replica_groups=mesh['tm'=8,'feat'=4] {'tm'}, dimensions={0} | all-to-all | bytes 4194304 | tf_op jit(solution)/shard_map/all_to_all | solution.py:311
  253.7 0.6 collective-permute-start.1
  254.8 45.8 %collective-permute-done.1.rest_2_ = bf16[2048,512]{1,0:T(8,128)(2,1)S(1)} collective-permute-done((bf16[2048,512]{1,0:T(8,128)(2,1)}, bf16[2048,512]{1,0:T(8,128)(2,1)S(1)}, u32[]{:S(2)}, u32[]{:S(2)}) %collective-permute-start.1) | collective-permute-done | bytes 2097184 | tf_op jit(solution)/shard_map/ppermute | solution.py:265
  300.7 0.6 collective-permute-start.5
  301.8 1.3 slice.16
  303.1 1.0 collective-permute-start.6
  304.6 19.6 %collective-permute-done.5 = bf16[1024,512]{1,0:T(8,128)(2,1)S(1)} collective-permute-done((bf16[1024,512]{1,0:T(8,128)(2,1)S(1)}, bf16[1024,512]{1,0:T(8,128)(2,1)S(1)}, u32[]{:S(2)}, u32[]{:S(2)}) %collective-permute-start.5) | collective-permute-done | bytes 1048608 | tf_op jit(solution)/shard_map/ppermute | solution.py:265
  324.2 1.1 constant_dynamic-update-slice_fusion.1
  325.4 1.6 collective-permute-done.6
  327.0 1.0 constant_dynamic-update-slice_fusion.rest_6_
  328.0 0.6 maximum_reduce_fusion
  329.5 0.6 pad_maximum_fusion.factors_ref
  330.3 0.6 pad_convert_fusion
  330.9 1.6 collective-permute-done.7.rest_7_
  332.5 67.3 %all-gather.4.cloned.1.call-done = bf16[32,1024,128]{2,1,0:T(8,128)(2,1)} async-done(((bf16[8,1024,128]{2,1,0:T(8,128)(2,1)}), bf16[32,1024,128]{2,1,0:T(8,128)(2,1)}) %all-gather.4.cloned.1.call-update) | async-done | bytes 8388624 | tf_op jit(solution)/shard_map/all_gather | solution.py:312
  399.8 47.0 %shard_map.62 = (f32[1024,2048]{1,0:T(8,128)}, f32[1024,2048]{1,0:T(8,128)}) custom-call(s32[1]{0:T(128)} %bitcast.me_ref, bf16[4,8,1024,128]{3,2,1,0:T(8,128)(2,1)} %bitcast.24, f32[8,1,512]{2,1,0:T(1,128)} %bitcast.19, f32[2]{0:T(128)} %pad_maximum_fusion.factors_ref, bf16[2048,512]{1,0:T(8,128)(2,1)} %get-tuple-element.9.rest_0_, ...), custom_call_target="tpu_custom_call" | custom-call | flops 34359738368 | bytes 41943040 | tf_op jit(solution)/shard_map/pallas_call | solution.py:240
  (24 shorter events, 2.2 us)
Async XLA Ops:
  7.2 392.6 %all-gather.4.cloned.1.call-start = ((), (), s32[]{:S(2)}) async-start(), calls=%async_computation.1 | async-start | bytes 10485760 | tf_op jit(solution)/shard_map/all_gather | solution.py:312
  8.3 73.2 %copy-start = (s32[2,2048]{0,1:T(8,128)}, s32[2,2048]{0,1:T(8,128)S(1)}, u32[]{:S(2)}) copy-start(s32[2,2048]{0,1:T(8,128)S(1)} %copy.10) | copy-start | bytes 49156
  253.7 47.0 %collective-permute-start.1 = (bf16[2048,512]{1,0:T(8,128)(2,1)}, bf16[2048,512]{1,0:T(8,128)(2,1)S(1)}, u32[]{:S(2)}, u32[]{:S(2)}) collective-permute-start(bf16[2048,512]{1,0:T(8,128)(2,1)} %get-tuple-element.9.rest_0_), channel_id=1, source_target_pairs={{0,8},{4,12},{8,0},{12,4},{16,24},{20,28},{24,16},{28,20},{1,9},{5... | collective-permute-start | bytes 6291464 | tf_op jit(solution)/shard_map/ppermute | solution.py:265
  254.3 47.5 %collective-permute-start.3 = (bf16[2048,512]{1,0:T(8,128)(2,1)}, bf16[2048,512]{1,0:T(8,128)(2,1)}, u32[]{:S(2)}, u32[]{:S(2)}) collective-permute-start(bf16[2048,512]{1,0:T(8,128)(2,1)} %get-tuple-element.9.rest_0_), channel_id=1, source_target_pairs={{0,16},{4,20},{8,24},{12,28},{16,0},{20,4},{24,8},{28,12},{1,17},{... | collective-permute-start | bytes 6291464 | tf_op jit(solution)/shard_map/ppermute | solution.py:265
  300.6 3.9 copy-start.1
  300.7 23.5 %collective-permute-start.5 = (bf16[1024,512]{1,0:T(8,128)(2,1)S(1)}, bf16[1024,512]{1,0:T(8,128)(2,1)S(1)}, u32[]{:S(2)}, u32[]{:S(2)}) collective-permute-start(bf16[1024,512]{1,0:T(8,128)(2,1)S(1)} %slice.15), channel_id=1, source_target_pairs={{0,16},{4,20},{8,24},{12,28},{16,0},{20,4},{24,8},{28,12},{1,17},{... | collective-permute-start | bytes 3145736 | tf_op jit(solution)/shard_map/ppermute | solution.py:265
  303.1 24.9 %copy-start.2 = (s32[8]{0:T(128)S(1)}, s32[8]{0:T(128)}, u32[]{:S(2)}) copy-start(s32[8]{0:T(128)} %param.7) | copy-start | bytes 100
  303.1 23.9 %collective-permute-start.6 = (bf16[1024,512]{1,0:T(8,128)(2,1)S(1)}, bf16[1024,512]{1,0:T(8,128)(2,1)S(1)}, u32[]{:S(2)}, u32[]{:S(2)}) collective-permute-start(bf16[1024,512]{1,0:T(8,128)(2,1)S(1)} %slice.16), channel_id=1, source_target_pairs={{0,8},{4,12},{8,0},{12,4},{16,24},{20,28},{24,16},{28,20},{1,9},{5... | collective-permute-start | bytes 3145736 | tf_op jit(solution)/shard_map/ppermute | solution.py:265
  304.1 26.8 %collective-permute-start = (bf16[2048,512]{1,0:T(8,128)(2,1)}, bf16[2048,512]{1,0:T(8,128)(2,1)}, u32[]{:S(2)}, u32[]{:S(2)}) collective-permute-start(bf16[2048,512]{1,0:T(8,128)(2,1)} %get-tuple-element.9.rest_0_), channel_id=1, source_target_pairs={{0,4},{4,0},{8,12},{12,8},{16,20},{20,16},{24,28},{28,24},{1,5},{5... | collective-permute-start | bytes 6291464 | tf_op jit(solution)/shard_map/ppermute | solution.py:265
  304.1 26.8 %collective-permute-start.4 = (bf16[2048,512]{1,0:T(8,128)(2,1)}, bf16[2048,512]{1,0:T(8,128)(2,1)}, u32[]{:S(2)}, u32[]{:S(2)}) collective-permute-start(bf16[2048,512]{1,0:T(8,128)(2,1)} %collective-permute-done.3.rest_4_), channel_id=1, source_target_pairs={{0,4},{4,0},{8,12},{12,8},{16,20},{20,16},{24,28},{28,24},{1,5},{5... | collective-permute-start | bytes 6291464 | tf_op jit(solution)/shard_map/ppermute | solution.py:265
  304.6 26.3 %collective-permute-start.2 = (bf16[2048,512]{1,0:T(8,128)(2,1)S(1)}, bf16[2048,512]{1,0:T(8,128)(2,1)}, u32[]{:S(2)}, u32[]{:S(2)}) collective-permute-start(bf16[2048,512]{1,0:T(8,128)(2,1)S(1)} %collective-permute-done.1.rest_2_), channel_id=1, source_target_pairs={{0,4},{4,0},{8,12},{12,8},{16,20},{20,16},{24,28},{28,24},{1,5},{5... | collective-permute-start | bytes 6291464 | tf_op jit(solution)/shard_map/ppermute | solution.py:265
  328.0 4.5 collective-permute-start.7
Sparse Core Ops, SparseCore 0:
  253.8 145.9 all-gather.3

commit v2 on v0

--- a/solution.py
+++ b/solution.py
@@ -1,9 +1,15 @@
+import functools
+
 import jax
 import jax.numpy as jnp
 from jax import lax
+from jax.experimental import pallas as pl
+from jax.experimental.pallas import tpu as pltpu
 from jax.sharding import PartitionSpec as P
 
 LAG = 384
+CHUNK = 128
+VMEM_LIMIT = 56 * 1024 * 1024
 
 
 def contact_values(coords, frame_scale, pairs):
@@ -38,7 +44,7 @@
     )
 
 
-def shards(coords, frame_scale, pairs, walker_lengths):
+def plain_shards(coords, frame_scale, pairs, walker_lengths):
     tm_count = lax.axis_size("tm")
     frames_dev = coords.shape[0]
     local_feats = pairs.shape[1]
@@ -60,11 +66,379 @@
     return (same / jnp.float32(frames_all), cross / npairs)
 
 
+def switch(squares, scale):
+    dist_sq = (scale * scale) * squares
+    return 1.0 / (1.0 + dist_sq * dist_sq * dist_sq)
+
+
+def as_column(row):
+    return jnp.broadcast_to(row, (CHUNK, row.shape[1])).T
+
+
+def square_rows(pairs_ref, base, feats, table, stride, squares):
+    for f in range(feats):
+        first = pl.multiple_of(pairs_ref[0, base + f] * stride, 8)
+        second = pl.multiple_of(pairs_ref[1, base + f] * stride, 8)
+        diff = table[pl.ds(first, stride), :] - table[pl.ds(second, stride), :]
+        diff = diff.astype(jnp.float32)
+        squares[pl.ds(f * stride, stride), :] = diff * diff
+
+
+def add_axes(squares, start, feats, stride, step):
+    at = lambda k: squares[pl.ds(start + k * step, feats, stride=stride), :]
+    return at(0) + at(1) + at(2)
+
+
+def own_kernel(centered, pairs_ref, coords_ref, scale_ref, *rest):
+    if centered:
+        mean_ref, out_ref, table, squares, part = rest
+    else:
+        out_ref, sums_ref, table, squares, part = rest
+    residues, frames = coords_ref.shape[1:]
+    chunks = frames // CHUNK
+    stride = -(-3 * chunks // 8) * 8
+    block = out_ref.shape[0]
+    group = squares.shape[0] // stride
+    step = pl.program_id(0)
+
+    @pl.when(step == 0)
+    def _():
+        for k in range(3):
+            for c in range(chunks):
+                table[pl.ds(k * chunks + c, residues, stride=stride), :] = coords_ref[
+                    k, :, c * CHUNK : (c + 1) * CHUNK
+                ]
+
+    if centered:
+        part[...] = as_column(mean_ref[...])
+
+    @pl.loop(0, block // group)
+    def _(g):
+        at = pl.multiple_of(g * group, group)
+        square_rows(pairs_ref, step * block + at, group, table, stride, squares)
+        for h in range(group // 16):
+            here = pl.ds(pl.multiple_of(at + h * 16, 16), 16)
+            total = jnp.zeros((16, CHUNK), jnp.float32)
+            for c in range(chunks):
+                lanes = slice(c * CHUNK, (c + 1) * CHUNK)
+                added = add_axes(squares, h * 16 * stride + c, 16, stride, chunks)
+                contact = switch(added, scale_ref[:, lanes])
+                if centered:
+                    out_ref[here, lanes] = (contact - part[here, :]).astype(jnp.bfloat16)
+                else:
+                    out_ref[here, lanes] = contact
+                    total = total + contact
+            if not centered:
+                part[here, :] = total
+
+    if not centered:
+        sums_ref[...] = jnp.sum(part[...].T, axis=0, keepdims=True)
+
+
+def own_contacts(pairs, coords_t, scale_row, mean=None, block=256, group=32):
+    residues, frames = coords_t.shape[1:]
+    feats = pairs.shape[1]
+    stride = -(-3 * (frames // CHUNK) // 8) * 8
+    centered = mean is not None
+    in_specs = [
+        pl.BlockSpec(memory_space=pltpu.SMEM),
+        pl.BlockSpec(coords_t.shape, lambda n: (0, 0, 0), pipeline_mode=pl.Buffered(1)),
+        pl.BlockSpec((1, frames), lambda n: (0, 0)),
+    ]
+    out_spec = pl.BlockSpec((block, frames), lambda n: (n, 0))
+    row_spec = pl.BlockSpec((1, block), lambda n: (0, n))
+    args = [pairs, coords_t, scale_row]
+    if centered:
+        in_specs.append(row_spec)
+        args.append(mean)
+        out_shape = jax.ShapeDtypeStruct((feats, frames), jnp.bfloat16)
+        out_specs = out_spec
+    else:
+        out_shape = [
+            jax.ShapeDtypeStruct((feats, frames), jnp.float32),
+            jax.ShapeDtypeStruct((1, feats), jnp.float32),
+        ]
+        out_specs = [out_spec, row_spec]
+    return pl.pallas_call(
+        functools.partial(own_kernel, centered),
+        out_shape=out_shape,
+        grid=(feats // block,),
+        in_specs=in_specs,
+        out_specs=out_specs,
+        scratch_shapes=[
+            pltpu.VMEM((residues * stride, CHUNK), jnp.int32),
+            pltpu.VMEM((group * stride, CHUNK), jnp.float32),
+            pltpu.VMEM((block, CHUNK), jnp.float32),
+        ],
+        compiler_params=pltpu.CompilerParams(vmem_limit_bytes=VMEM_LIMIT),
+        cost_estimate=pl.CostEstimate(
+            flops=40 * feats * frames, bytes_accessed=4 * coords_t.size + 4 * feats * frames, transcendentals=0
+        ),
+    )(*args)
+
+
+def sent_kernel(pairs_ref, first_ref, second_ref, scale_ref, mean_ref, out_ref, table, squares, column):
+    residues = first_ref.shape[1]
+    block = out_ref.shape[1]
+    group = squares.shape[0] // 8
+    step = pl.program_id(0)
+
+    @pl.when(step == 0)
+    def _():
+        for s, ref in enumerate((first_ref, second_ref)):
+            for k in range(3):
+                table[pl.ds(2 * k + s, residues, stride=8), :] = ref[k].astype(jnp.int32)
+
+    column[...] = as_column(mean_ref[...])
+
+    @pl.loop(0, block // group)
+    def _(g):
+        at = pl.multiple_of(g * group, group)
+        square_rows(pairs_ref, step * block + at, group, table, 8, squares)
+        for h in range(group // 16):
+            here = pl.ds(pl.multiple_of(at + h * 16, 16), 16)
+            for s in range(2):
+                added = add_axes(squares, h * 128 + s, 16, 8, 2)
+                contact = switch(added, scale_ref[s : s + 1, :])
+                out_ref[s, here, :] = (contact - column[here, :]).astype(jnp.bfloat16)
+
+
+def sent_contacts(pairs, first, second, scales, mean, block=512, group=64):
+    residues = first.shape[1]
+    feats = pairs.shape[1]
+    whole = pl.BlockSpec(first.shape, lambda n: (0, 0, 0), pipeline_mode=pl.Buffered(1))
+    return pl.pallas_call(
+        sent_kernel,
+        out_shape=jax.ShapeDtypeStruct((2, feats, CHUNK), jnp.bfloat16),
+        grid=(feats // block,),
+        in_specs=[
+            pl.BlockSpec(memory_space=pltpu.SMEM),
+            whole,
+            whole,
+            pl.BlockSpec((2, CHUNK), lambda n: (0, 0)),
+            pl.BlockSpec((1, block), lambda n: (0, n)),
+        ],
+        out_specs=pl.BlockSpec((2, block, CHUNK), lambda n: (0, n, 0)),
+        scratch_shapes=[
+            pltpu.VMEM((residues * 8, CHUNK), jnp.int32),
+            pltpu.VMEM((group * 8, CHUNK), jnp.float32),
+            pltpu.VMEM((block, CHUNK), jnp.float32),
+        ],
+        compiler_params=pltpu.CompilerParams(vmem_limit_bytes=VMEM_LIMIT),
+        cost_estimate=pl.CostEstimate(
+            flops=80 * feats * CHUNK, bytes_accessed=4 * first.size + 4 * feats * CHUNK, transcendentals=0
+        ),
+    )(pairs, first, second, scales, mean)
+
+
+def center_kernel(raw_ref, mean_ref, out_ref):
+    col = as_column(mean_ref[...])
+    for c in range(raw_ref.shape[1] // CHUNK):
+        lanes = slice(c * CHUNK, (c + 1) * CHUNK)
+        out_ref[:, lanes] = (raw_ref[:, lanes] - col).astype(jnp.bfloat16)
+
+
+def center(raw, mean, block=512):
+    feats, frames = raw.shape
+    return pl.pallas_call(
+        center_kernel,
+        out_shape=jax.ShapeDtypeStruct(raw.shape, jnp.bfloat16),
+        grid=(feats // block,),
+        in_specs=[
+            pl.BlockSpec((block, frames), lambda n: (n, 0)),
+            pl.BlockSpec((1, block), lambda n: (0, n)),
+        ],
+        out_specs=pl.BlockSpec((block, frames), lambda n: (n, 0)),
+        compiler_params=pltpu.CompilerParams(vmem_limit_bytes=VMEM_LIMIT),
+        cost_estimate=pl.CostEstimate(flops=2 * raw.size, bytes_accessed=6 * raw.size, transcendentals=0),
+    )(raw, mean)
+
+
+def product_kernel(first, plan, last, has_sum, me_ref, mask_ref, factors_ref, *rest):
+    rows_refs = rest[: len(plan)]
+    rest = rest[len(plan) :]
+    cols_refs, rest = rest[:8], rest[8:]
+    if has_sum:
+        same_in, cross_in, same_ref, cross_ref, left, right, ahead = rest
+    else:
+        same_ref, cross_ref, left, right, ahead = rest
+    frames = cols_refs[0].shape[1]
+    me = me_ref[0]
+    count = left.shape[2] // frames
+
+    @pl.when(pl.program_id(0) == 0)
+    def _():
+        ahead[...] = jnp.zeros_like(ahead)
+        slot = 0
+        for form, ref in zip(plan, rows_refs):
+            for b in range(1 if form is None else form[1]):
+                mask = mask_ref[me ^ (first + slot)]
+                for c in range(frames // CHUNK):
+                    lanes = slice(slot * frames + c * CHUNK, slot * frames + (c + 1) * CHUNK)
+                    inner = slice(c * CHUNK, (c + 1) * CHUNK)
+                    value = ref[:, inner] if form is None else ref[c, b]
+                    left[0, :, lanes] = value
+                    left[1, :, lanes] = value * mask[:, inner].astype(jnp.bfloat16)
+                slot += 1
+
+    kept = frames - LAG
+    for d in range(8):
+        j = me ^ d
+        if first <= d < first + count:
+            at = (d - first) * frames
+            right[:, at : at + frames] = cols_refs[d][...]
+            ahead[:, at : at + kept] = cols_refs[d][:, LAG:]
+        slot = (me ^ (j - 1)) - first
+
+        @pl.when((j > 0) & (slot >= 0) & (slot < count))
+        def _():
+            ahead[:, pl.ds(pl.multiple_of(slot * frames + kept, CHUNK), LAG)] = cols_refs[d][:, :LAG]
+
+    dims = (((1,), (1,)), ((), ()))
+    same = lax.dot_general(left[0], right[...], dims, preferred_element_type=jnp.float32)
+    if has_sum:
+        same = same + same_in[...]
+    same_ref[...] = same * factors_ref[0] if last else same
+    cross = lax.dot_general(left[1], ahead[...], dims, preferred_element_type=jnp.float32)
+    if has_sum:
+        cross = cross + cross_in[...]
+    cross_ref[...] = cross / factors_ref[1] if last else cross
+
+
+def products(me, mask, factors, first, rows, cols, sums=None, last=False, block=512):
+    plan = tuple(None if r.ndim == 2 else (r.shape[0], r.shape[1]) for r in rows)
+    count = sum(1 if form is None else form[1] for form in plan)
+    feats, frames = cols[0].shape
+    row_feats = rows[0].shape[-2]
+    out = jax.ShapeDtypeStruct((row_feats, feats), jnp.float32)
+    whole = lambda x: pl.BlockSpec(x.shape, lambda n, s: (0,) * x.ndim, pipeline_mode=pl.Buffered(1))
+    tile = pl.BlockSpec((row_feats, block), lambda n, s: (0, n))
+    sums = () if sums is None else tuple(sums)
+    inputs = [mask, factors, *rows, *cols, *sums]
+    aliases = {1 + len(inputs) - 2 + i: i for i in range(2)} if sums else {}
+    return pl.pallas_call(
+        functools.partial(product_kernel, first, plan, last, bool(sums)),
+        out_shape=[out, out],
+        grid_spec=pltpu.PrefetchScalarGridSpec(
+            num_scalar_prefetch=1,
+            grid=(feats // block,),
+            in_specs=[whole(mask), pl.BlockSpec(memory_space=pltpu.SMEM)]
+            + [whole(r) for r in rows]
+            + [pl.BlockSpec((block, frames), lambda n, s: (n, 0))] * 8
+            + [tile] * len(sums),
+            out_specs=[tile] * 2,
+            scratch_shapes=[
+                pltpu.VMEM((2, row_feats, count * frames), jnp.bfloat16),
+                pltpu.VMEM((block, count * frames), jnp.bfloat16),
+                pltpu.VMEM((block, count * frames), jnp.bfloat16),
+            ],
+        ),
+        input_output_aliases=aliases,
+        compiler_params=pltpu.CompilerParams(vmem_limit_bytes=VMEM_LIMIT),
+        cost_estimate=pl.CostEstimate(
+            flops=4 * row_feats * feats * count * frames,
+            bytes_accessed=2 * count * frames * row_feats
+            + 16 * feats * frames
+            + (16 if sums else 8) * row_feats * feats,
+            transcendentals=0,
+        ),
+    )(me, *inputs)
+
+
+def swap(x, bits):
+    return lax.ppermute(x, "tm", [(i, i ^ bits) for i in range(8)])
+
+
+def square_gather(x, axis, half):
+    core = swap(x, 1)
+    along_x = swap(x, 2)
+    along_y = swap(x, 4)
+    low = swap(lax.slice_in_dim(along_x, 0, half, axis=axis), 4)
+    high = swap(lax.slice_in_dim(along_y, half, x.shape[axis], axis=axis), 2)
+    corner = jnp.concatenate([low, high], axis=axis)
+    return [x, core, along_x, swap(along_x, 1), along_y, swap(along_y, 1), corner, swap(corner, 1)]
+
+
+def from_owner(x, feat_count):
+    owner = lambda i: i * feat_count // 8
+    total = jnp.where(lax.axis_index("feat") == owner(lax.axis_index("tm")), x, jnp.zeros_like(x))
+    for s in range(1, feat_count):
+        perm = [
+            (i * feat_count + owner(i), i * feat_count + (owner(i) + s) % feat_count)
+            for i in range(8)
+        ]
+        total = total + lax.ppermute(x, ("tm", "feat"), perm)
+    return total
+
+
+def shards(coords, frame_scale, pairs, walker_lengths):
+    tm_count = lax.axis_size("tm")
+    feat_count = lax.axis_size("feat")
+    frames_dev = coords.shape[0]
+    feats = pairs.shape[1]
+    frames_all = frames_dev * tm_count
+    row_feats = feats * feat_count // tm_count
+    tm = lax.axis_index("tm").astype(jnp.int32)
+    z = lax.axis_index("feat").astype(jnp.int32)
+    me = tm.reshape(1)
+    own_half = (tm % (feats // row_feats)) * row_feats
+
+    coords_t = jnp.transpose(coords, (1, 2, 0))
+    scale_row = frame_scale.reshape(1, frames_dev)
+    quarter = lax.dynamic_slice_in_dim(coords_t, z * CHUNK, CHUNK, axis=2).astype(jnp.int16)
+    quarters = square_gather(quarter, 1, (coords_t.shape[1] // 32) * 16)
+    chip_pairs = from_owner(pairs, feat_count)
+
+    raw, sums = own_contacts(pairs, coords_t, scale_row)
+    note = jnp.concatenate([sums, scale_row], axis=1)
+    notes = [note] + [swap(note, d) for d in range(1, 8)]
+    totals = notes[0][:, :feats]
+    for other in notes[1:]:
+        totals = totals + other[:, :feats]
+    mean = totals / jnp.float32(frames_all)
+    chip_mean = from_owner(mean, feat_count)
+    scales = [lax.dynamic_slice_in_dim(n, feats + z * CHUNK, CHUNK, axis=1) for n in notes]
+
+    cols = square_gather(center(raw, mean), 0, feats // 2)
+
+    row_pairs = lax.dynamic_slice_in_dim(chip_pairs, own_half, row_feats, axis=1)
+    row_mean = lax.dynamic_slice_in_dim(chip_mean, own_half, row_feats, axis=1)
+    pieces = []
+    for d in (2, 4, 6):
+        piece = sent_contacts(
+            row_pairs,
+            quarters[d],
+            quarters[d + 1],
+            jnp.concatenate([scales[d], scales[d + 1]], axis=0),
+            row_mean,
+        )
+        pieces.append(lax.all_gather(piece, "feat", axis=0, tiled=False))
+
+    chip = own_contacts(chip_pairs, coords_t, scale_row, chip_mean)
+    mine = lax.dynamic_slice_in_dim(chip, own_half, row_feats, axis=0)
+    others = lax.dynamic_slice_in_dim(chip, row_feats - own_half, row_feats, axis=0)
+    partner = swap(others, 1)
+
+    valid = walker_mask(walker_lengths, frames_all, frames_all)
+    mask = valid.astype(jnp.float32).reshape(tm_count, 1, frames_dev)
+    npairs = jnp.sum(jnp.maximum(walker_lengths - LAG, 0)).astype(jnp.float32)
+    factors = jnp.stack([jnp.float32(1.0 / frames_all), npairs])
+    partial = products(me, mask, factors, 0, [mine, partner, pieces[0], pieces[1]], cols)
+    return products(me, mask, factors, 6, [pieces[2]], cols, sums=partial, last=True)
+
+
 def solution(mesh):
-    return jax.shard_map(
-        shards,
-        mesh=mesh,
-        in_specs=(P("tm", None, None), P("tm"), P(None, "feat"), P()),
-        out_specs=(P("tm", "feat"), P("tm", "feat")),
-        check_vma=False,
-    )
+    def run(coords, frame_scale, pairs, walker_lengths):
+        tm_count, feat_count = mesh.shape["tm"], mesh.shape["feat"]
+        frames_dev = coords.shape[0] // tm_count
+        square = tm_count == 8 and feat_count == 4
+        fits = square and frames_dev == feat_count * CHUNK and pairs.shape[1] % (tm_count * 512) == 0
+        return jax.shard_map(
+            shards if fits else plain_shards,
+            mesh=mesh,
+            in_specs=(P("tm", None, None), P("tm"), P(None, "feat"), P()),
+            out_specs=(P("tm", "feat"), P("tm", "feat")),
+            check_vma=False,
+        )(coords, frame_scale, pairs, walker_lengths)
+
+    return run

time: 595 us -> 282 us (0.47)
  waiting for transfers between devices: 307 us -> 86.1 us
  matrix products: 129 us -> 0 us
  Pallas kernels: 0 us -> 129 us
  local copies, waits for them, and re-layouts: 69.8 us -> 13.4 us
  other arithmetic: 47.5 us -> 7.35 us
  starting transfers between devices: 5.48 us -> 30.7 us
  blocking collectives: 15.5 us -> 0 us
    all_gather x2 -> x3, waiting for transfers between devices: 306 us -> 1.27 us  [shards(): pieces.append(lax.all_gather(piece, 'feat', axis=0, tiled=False))]
    dot_general x3 -> x0, matrix products: 129 us -> none  [the longest x1 79.1 us: contact_values(): jnp.dot(flat, selector, precision=lax.Precision.HIGHEST, preferred_elemen...]
    pallas_call x0 -> x8, Pallas kernels: none -> 129 us  [the longest x2 60.2 us: products(): pl.pallas_call(functools.partial(product_kernel, first, plan, last, bool(...]
    ppermute x0 -> x29, waiting for transfers between devices: none -> 84.7 us  [the longest x23 84 us: swap(): return lax.ppermute(x, 'tm', [(i, i ^ bits) for i in range(8)])]
    reshape x2 -> x0, local copies, waits for them, and re-layouts: 34.2 us -> none  [the longest x1 19.3 us: contact_values(): diff = diff.reshape(frames_dev, 3, pairs.shape[1])]
    ppermute x0 -> x29, starting transfers between devices: none -> 30.4 us  [the longest x23 19.5 us: swap(): return lax.ppermute(x, 'tm', [(i, i ^ bits) for i in range(8)])]
    add x1 -> x2, other arithmetic: 26.5 us -> 0.04 us  [from_owner(): total = total + lax.ppermute(x, ('tm', 'feat'), perm)]
    psum x1 -> x0, blocking collectives: 15.5 us -> none  [shards(): totals = lax.psum(jnp.sum(contact, axis=0), 'tm')]
  transfers between devices with their start and end apart: 3 -> 32, of which waited for: 2 -> 9; matrix products, arithmetic and copies ran while one was open for 4% -> 6% of each run, Pallas kernels for 0% -> 36%
where the time goes in v2:
time: 282 us; the launch traced here: 281 us
  Pallas kernels  129 us (46%)
  waiting for transfers between devices  86.1 us (31%)
  starting transfers between devices  30.7 us (11%)
  between operations  14.8 us (5%)
  local copies, waits for them, and re-layouts  13.4 us (5%)
  other arithmetic  7.35 us (3%)
    ppermute x23, waiting for transfers between devices, swap(): return lax.ppermute(x, 'tm', [(i, i ^ bits) for i in range(8)])  84 us
    pallas_call x2, Pallas kernels, products(): pl.pallas_call(functools.partial(product_kernel, first, plan, last, bool(...  60.2 us
    pallas_call x2, Pallas kernels, own_contacts(): pl.pallas_call(functools.partial(own_kernel, centered), out_shape=out_sha...  40.9 us
    pallas_call x3, Pallas kernels, sent_contacts(): pl.pallas_call(sent_kernel, out_shape=jax.ShapeDtypeStruct((2, feats, CHU...  23.4 us
    ppermute x23, starting transfers between devices, swap(): return lax.ppermute(x, 'tm', [(i, i ^ bits) for i in range(8)])  19.5 us
    ppermute x6, starting transfers between devices, from_owner(): total = total + lax.ppermute(x, ('tm', 'feat'), perm)  10.9 us
  transfers between devices with their start and end apart: 32, of which 9 were waited for; matrix products, arithmetic and copies ran while one was open for 6% of the time, Pallas kernels for 36%

profile of v2, /device:TPU:0, one launch (start us, length us, event | category | flops | bytes accessed | tf_op | source)
XLA Modules:
  0.0 281.3 jit_solution(17733913549181842332)
XLA Ops:
  7.2 1.8 fusion
  9.0 3.0 %collective-permute-start.3 = (s16[3,1500,128]{2,1,0:T(8,128)(2,1)S(1)}, s16[3,1500,128]{2,1,0:T(8,128)(2,1)S(1)}, u32[]{:S(2)}, u32[]{:S(2)}) collective-permute-start(s16[3,1500,128]{2,1,0:T(8,128)(2,1)S(1)} %fusion), channel_id=1, source_target_pairs={{0,8},{4,12},{8,0},{12,4},{16,24},{20,28},{24,16},{28,20},{1,9},{5... | collective-permute-start | bytes 3456008 | tf_op jit(solution)/shard_map/ppermute | solution.py:349
  12.0 20.4 %shard_map.59 = (f32[2048,512]{1,0:T(8,128)}, f32[1,2048]{1,0:T(1,128)}) custom-call(s32[2,2048]{1,0:T(2,128)} %pairs_ref.1, s32[3,1500,512]{2,1,0:T(8,128)} %bitcast.11, f32[1,512]{1,0:T(1,128)} %bitcast.14), custom_call_target="tpu_custom_call" | custom-call | flops 41943040 | bytes 13410304 | tf_op jit(solution)/shard_map/pallas_call | solution.py:162
  35.0 1.7 collective-permute-start.11
  38.3 2.0 collective-permute-start.8
  40.3 4.5 %collective-permute-start.1 = (s32[2,2048]{1,0:T(2,128)S(1)}, s32[2,2048]{1,0:T(2,128)S(1)}, u32[]{:S(2)}, u32[]{:S(2)}) collective-permute-start(s32[2,2048]{1,0:T(2,128)S(1)} %copy-done.9), channel_id=1, source_target_pairs={{0,2},{4,6},{9,11},{13,15},{18,16},{22,20},{27,25},{31,29}} | collective-permute-start | bytes 49160 | tf_op jit(solution)/shard_map/ppermute | solution.py:370
  55.9 7.8 %shard_map.63 = bf16[2,1024,128]{2,1,0:T(8,128)(2,1)} custom-call(s32[2,1024]{1,0:T(2,128)} %constant_dynamic-slice_fusion.9.pairs_ref, s16[3,1500,128]{2,1,0:T(8,128)(2,1)} %copy-done.3, s16[3,1500,128]{2,1,0:T(8,128)(2,1)} %copy-done.5, f32[2,128]{1,0:T(2,128)} %pad_maximum_fusion.2.scale_ref, f32[1,1024]{1,0:T(1,128)} %constant_dynamic-slice_fusion.6.mean_ref), custom_call_target="tpu_custom_call" | custom-call | flops 10485760 | bytes 2828288 | tf_op jit(solution)/shard_map/pallas_call | solution.py:210
  64.7 4.4 %shard_map.61.rest_4_.rest_1_ = bf16[2048,512]{1,0:T(8,128)(2,1)} custom-call(f32[2048,512]{1,0:T(8,128)} %get-tuple-element.7.raw_ref, f32[1,2048]{1,0:T(1,128)} %copy-done.8), custom_call_target="tpu_custom_call" | custom-call | flops 2097152 | bytes 6291456 | tf_op jit(solution)/shard_map/pallas_call | solution.py:243
  69.2 3.0 %collective-permute-start.19 = (bf16[2048,512]{1,0:T(8,128)(2,1)}, bf16[2048,512]{1,0:T(8,128)(2,1)}, u32[]{:S(2)}, u32[]{:S(2)}) collective-permute-start(bf16[2048,512]{1,0:T(8,128)(2,1)} %shard_map.61.rest_4_.rest_1_), channel_id=1, source_target_pairs={{0,8},{4,12},{8,0},{12,4},{16,24},{20,28},{24,16},{28,20},{1,9},{5... | collective-permute-start | bytes 6291464 | tf_op jit(solution)/shard_map/ppermute | solution.py:349
  72.2 19.9 %collective-permute-done.5.first_ref = s16[3,1500,128]{2,1,0:T(8,128)(2,1)S(1)} collective-permute-done((s16[3,1500,128]{2,1,0:T(8,128)(2,1)S(1)}, s16[3,1500,128]{2,1,0:T(8,128)(2,1)S(1)}, u32[]{:S(2)}, u32[]{:S(2)}) %collective-permute-start.5) | collective-permute-done | bytes 1152032 | tf_op jit(solution)/shard_map/ppermute | solution.py:349
  92.8 2.2 collective-permute-done.28.second_ref
  96.0 7.8 %shard_map.64 = bf16[2,1024,128]{2,1,0:T(8,128)(2,1)} custom-call(s32[2,1024]{1,0:T(2,128)} %constant_dynamic-slice_fusion.9.pairs_ref, s16[3,1500,128]{2,1,0:T(8,128)(2,1)} %copy-done.1, s16[3,1500,128]{2,1,0:T(8,128)(2,1)} %copy-done.6, f32[2,128]{1,0:T(2,128)} %pad_maximum_fusion.3.scale_ref, f32[1,1024]{1,0:T(1,128)} %constant_dynamic-slice_fusion.6.mean_ref), custom_call_target="tpu_custom_call" | custom-call | flops 10485760 | bytes 2828288 | tf_op jit(solution)/shard_map/pallas_call | solution.py:210
  104.1 12.8 %collective-permute-done.19.rest_6_.rest_3_ = bf16[2048,512]{1,0:T(8,128)(2,1)} collective-permute-done((bf16[2048,512]{1,0:T(8,128)(2,1)}, bf16[2048,512]{1,0:T(8,128)(2,1)}, u32[]{:S(2)}, u32[]{:S(2)}) %collective-permute-start.19) | collective-permute-done | bytes 2097184 | tf_op jit(solution)/shard_map/ppermute | solution.py:349
  116.9 1.5 slice.53
  119.3 17.9 %collective-permute-done.21.rest_8_.rest_5_ = bf16[2048,512]{1,0:T(8,128)(2,1)} collective-permute-done((bf16[2048,512]{1,0:T(8,128)(2,1)}, bf16[2048,512]{1,0:T(8,128)(2,1)}, u32[]{:S(2)}, u32[]{:S(2)}) %collective-permute-start.21) | collective-permute-done | bytes 2097184 | tf_op jit(solution)/shard_map/ppermute | solution.py:349
  138.5 1.9 collective-permute-start.24
  141.5 2.1 collective-permute-start.4
  143.8 26.7 %collective-permute-done.4 = s16[3,736,128]{2,1,0:T(8,128)(2,1)S(1)} collective-permute-done((s16[3,736,128]{2,1,0:T(8,128)(2,1)S(1)}, s16[3,736,128]{2,1,0:T(8,128)(2,1)S(1)}, u32[]{:S(2)}, u32[]{:S(2)}) %collective-permute-start.4) | collective-permute-done | bytes 565280 | tf_op jit(solution)/shard_map/ppermute | solution.py:349
  170.6 3.5 %collective-permute-done.6 = s16[3,764,128]{2,1,0:T(8,128)(2,1)S(1)} collective-permute-done((s16[3,764,128]{2,1,0:T(8,128)(2,1)S(1)}, s16[3,764,128]{2,1,0:T(8,128)(2,1)S(1)}, u32[]{:S(2)}, u32[]{:S(2)}) %collective-permute-start.6) | collective-permute-done | bytes 586784 | tf_op jit(solution)/shard_map/ppermute | solution.py:349
  177.4 20.5 %shard_map.62 = bf16[2048,512]{1,0:T(8,128)(2,1)} custom-call(s32[2,2048]{1,0:T(2,128)} %copy-done.7, s32[3,1500,512]{2,1,0:T(8,128)} %bitcast.12, f32[1,512]{1,0:T(1,128)} %bitcast.15, f32[1,2048]{1,0:T(1,128)} %copy-done.10), custom_call_target="tpu_custom_call" | custom-call | flops 41943040 | bytes 13410304 | tf_op jit(solution)/shard_map/pallas_call | solution.py:162
  197.9 3.0 %constant_dynamic-slice_fusion.4 = (bf16[1024,512]{1,0:T(8,128)(2,1)}, bf16[1024,512]{1,0:T(8,128)(2,1)}) fusion(bf16[2048,512]{1,0:T(8,128)(2,1)} %shard_map.62, s32[]{:T(128)S(6)} %select_n.56, s32[]{:T(128)S(6)} %select_n.51), kind=kLoop, calls=%fused_computation.29 | loop fusion | bytes 4194312 | tf_op jit(solution)/shard_map/dynamic_slice | solution.py:419
  201.5 7.8 %shard_map.60 = bf16[2,1024,128]{2,1,0:T(8,128)(2,1)} custom-call(s32[2,1024]{1,0:T(2,128)} %constant_dynamic-slice_fusion.9.pairs_ref, s16[3,1500,128]{2,1,0:T(8,128)(2,1)} %copy-done.4, s16[3,1500,128]{2,1,0:T(8,128)(2,1)} %collective-permute-done.7.second_ref, f32[2,128]{1,0:T(2,128)} %pad_maximum_fusion.1.scale_ref, ...), custom_call_target="tpu_custom_call" | custom-call | flops 10485760 | bytes 2828288 | tf_op jit(solution)/shard_map/pallas_call | solution.py:210
  213.3 39.5 %shard_map.65 = (f32[1024,2048]{1,0:T(8,128)}, f32[1024,2048]{1,0:T(8,128)}) custom-call(s32[1]{0:T(128)} %bitcast.me_ref, f32[8,1,512]{2,1,0:T(1,128)} %and_convert_fusion.mask_ref, f32[2]{0:T(128)} %pad_maximum_fusion.4.factors_ref, bf16[1024,512]{1,0:T(8,128)(2,1)} %get-tuple-element.13.rest_0_, bf16[1024,512]{1,0:T(8,128)(2,1)} %copy-done.12, ...), custom_call_target="tpu_custom_call" | custom-call | flops 25769803776 | bytes 39845888 | tf_op jit(solution)/shard_map/pallas_call | solution.py:319
  254.0 20.8 %shard_map.66 = (f32[1024,2048]{1,0:T(8,128)}, f32[1024,2048]{1,0:T(8,128)}) custom-call(s32[1]{0:T(128)} %bitcast.me_ref, f32[8,1,512]{2,1,0:T(1,128)} %and_convert_fusion.mask_ref, f32[2]{0:T(128)} %pad_maximum_fusion.4.factors_ref, bf16[4,2,1024,128]{3,2,1,0:T(8,128)(2,1)} %bitcast.13, ...), custom_call_target="tpu_custom_call", output_to_operand_aliasing={{0}: (12, {}), {1}: (13, {})} | custom-call | flops 8589934592 | bytes 52428800 | tf_op jit(solution)/shard_map/pallas_call | solution.py:319
  (112 shorter events, 30.0 us)
Async XLA Ops:
  7.2 205.1 %all-gather.9.cloned.1.call-start = ((), (), s32[]{:S(2)}) async-start(), calls=%async_computation.1 | async-start | bytes 2621440 | tf_op jit(solution)/shard_map/all_gather | solution.py:415
  9.0 40.5 %collective-permute-start.3 = (s16[3,1500,128]{2,1,0:T(8,128)(2,1)S(1)}, s16[3,1500,128]{2,1,0:T(8,128)(2,1)S(1)}, u32[]{:S(2)}, u32[]{:S(2)}) collective-permute-start(s16[3,1500,128]{2,1,0:T(8,128)(2,1)S(1)} %fusion), channel_id=1, source_target_pairs={{0,8},{4,12},{8,0},{12,4},{16,24},{20,28},{24,16},{28,20},{1,9},{5... | collective-permute-start | bytes 3456008 | tf_op jit(solution)/shard_map/ppermute | solution.py:349
  36.7 8.1 %collective-permute-start.10 = (f32[1,2560]{1,0:T(1,128)S(1)}, f32[1,2560]{1,0:T(1,128)S(1)}, u32[]{:S(2)}, u32[]{:S(2)}) collective-permute-start(f32[1,2560]{1,0:T(1,128)S(1)} %pad_maximum_fusion), channel_id=1, source_target_pairs={{0,4},{4,0},{8,12},{12,8},{16,20},{20,16},{24,28},{28,24},{1,5},{5... | collective-permute-start | bytes 30728 | tf_op jit(solution)/shard_map/ppermute | solution.py:349
  37.6 8.4 %collective-permute-start.9 = (f32[1,2560]{1,0:T(1,128)S(1)}, f32[1,2560]{1,0:T(1,128)S(1)}, u32[]{:S(2)}, u32[]{:S(2)}) collective-permute-start(f32[1,2560]{1,0:T(1,128)S(1)} %pad_maximum_fusion), channel_id=1, source_target_pairs={{0,28},{4,24},{8,20},{12,16},{16,12},{20,8},{24,4},{28,0},{1,29},{... | collective-permute-start | bytes 30728 | tf_op jit(solution)/shard_map/ppermute | solution.py:349
  38.3 9.1 %collective-permute-start.8 = (f32[1,2560]{1,0:T(1,128)S(1)}, f32[1,2560]{1,0:T(1,128)S(1)}, u32[]{:S(2)}, u32[]{:S(2)}) collective-permute-start(f32[1,2560]{1,0:T(1,128)S(1)} %pad_maximum_fusion), channel_id=1, source_target_pairs={{0,24},{4,28},{8,16},{12,20},{16,8},{20,12},{24,0},{28,4},{1,25},{... | collective-permute-start | bytes 30728 | tf_op jit(solution)/shard_map/ppermute | solution.py:349
  40.3 10.0 %collective-permute-start.1 = (s32[2,2048]{1,0:T(2,128)S(1)}, s32[2,2048]{1,0:T(2,128)S(1)}, u32[]{:S(2)}, u32[]{:S(2)}) collective-permute-start(s32[2,2048]{1,0:T(2,128)S(1)} %copy-done.9), channel_id=1, source_target_pairs={{0,2},{4,6},{9,11},{13,15},{18,16},{22,20},{27,25},{31,29}} | collective-permute-start | bytes 49160 | tf_op jit(solution)/shard_map/ppermute | solution.py:370
  44.8 6.8 %collective-permute-start = (s32[2,2048]{1,0:T(2,128)S(1)}, s32[2,2048]{1,0:T(2,128)S(1)}, u32[]{:S(2)}, u32[]{:S(2)}) collective-permute-start(s32[2,2048]{1,0:T(2,128)S(1)} %copy-done.9), channel_id=1, source_target_pairs={{0,1},{4,5},{9,10},{13,14},{18,19},{22,23},{27,24},{31,28}} | collective-permute-start | bytes 49160 | tf_op jit(solution)/shard_map/ppermute | solution.py:370
  46.1 6.8 %collective-permute-start.2 = (s32[2,2048]{1,0:T(2,128)S(1)}, s32[2,2048]{1,0:T(2,128)S(1)}, u32[]{:S(2)}, u32[]{:S(2)}) collective-permute-start(s32[2,2048]{1,0:T(2,128)S(1)} %copy-done.9), channel_id=1, source_target_pairs={{0,3},{4,7},{9,8},{13,12},{18,17},{22,21},{27,26},{31,30}} | collective-permute-start | bytes 49160 | tf_op jit(solution)/shard_map/ppermute | solution.py:370
  48.1 5.4 %collective-permute-start.17 = (f32[1,2048]{1,0:T(1,128)S(1)}, f32[1,2048]{1,0:T(1,128)S(1)}, u32[]{:S(2)}, u32[]{:S(2)}) collective-permute-start(f32[1,2048]{1,0:T(1,128)S(1)} %fusion.4.mean_ref), channel_id=1, source_target_pairs={{0,3},{4,7},{9,8},{13,12},{18,17},{22,21},{27,26},{31,30}} | collective-permute-start | bytes 24584 | tf_op jit(solution)/shard_map/ppermute | solution.py:370
  63.7 148.6 %all-gather.11.cloned.1.call-start = ((), (), s32[]{:S(2)}) async-start(), calls=%async_computation.2 | async-start | bytes 2621440 | tf_op jit(solution)/shard_map/all_gather | solution.py:415
  63.8 28.4 %collective-permute-start.5 = (s16[3,1500,128]{2,1,0:T(8,128)(2,1)S(1)}, s16[3,1500,128]{2,1,0:T(8,128)(2,1)S(1)}, u32[]{:S(2)}, u32[]{:S(2)}) collective-permute-start(s16[3,1500,128]{2,1,0:T(8,128)(2,1)S(1)} %fusion), channel_id=1, source_target_pairs={{0,16},{4,20},{8,24},{12,28},{16,0},{20,4},{24,8},{28,12},{1,17},{... | collective-permute-start | bytes 3456008 | tf_op jit(solution)/shard_map/ppermute | solution.py:349
  69.2 47.7 %collective-permute-start.19 = (bf16[2048,512]{1,0:T(8,128)(2,1)}, bf16[2048,512]{1,0:T(8,128)(2,1)}, u32[]{:S(2)}, u32[]{:S(2)}) collective-permute-start(bf16[2048,512]{1,0:T(8,128)(2,1)} %shard_map.61.rest_4_.rest_1_), channel_id=1, source_target_pairs={{0,8},{4,12},{8,0},{12,4},{16,24},{20,28},{24,16},{28,20},{1,9},{5... | collective-permute-start | bytes 6291464 | tf_op jit(solution)/shard_map/ppermute | solution.py:349
  72.2 65.0 %collective-permute-start.21 = (bf16[2048,512]{1,0:T(8,128)(2,1)}, bf16[2048,512]{1,0:T(8,128)(2,1)}, u32[]{:S(2)}, u32[]{:S(2)}) collective-permute-start(bf16[2048,512]{1,0:T(8,128)(2,1)} %shard_map.61.rest_4_.rest_1_), channel_id=1, source_target_pairs={{0,16},{4,20},{8,24},{12,28},{16,0},{20,4},{24,8},{28,12},{1,17},{... | collective-permute-start | bytes 6291464 | tf_op jit(solution)/shard_map/ppermute | solution.py:349
  103.8 150.1 %all-gather.7.cloned.1.call-start = ((), (), s32[]{:S(2)}) async-start(), calls=%async_computation | async-start | bytes 2621440 | tf_op jit(solution)/shard_map/all_gather | solution.py:415
  118.4 56.3 %collective-permute-start.23 = (bf16[1024,512]{1,0:T(8,128)(2,1)S(1)}, bf16[1024,512]{1,0:T(8,128)(2,1)S(1)}, u32[]{:S(2)}, u32[]{:S(2)}) collective-permute-start(bf16[1024,512]{1,0:T(8,128)(2,1)S(1)} %slice.53), channel_id=1, source_target_pairs={{0,16},{4,20},{8,24},{12,28},{16,0},{20,4},{24,8},{28,12},{1,17},{... | collective-permute-start | bytes 3145736 | tf_op jit(solution)/shard_map/ppermute | solution.py:349
  138.5 37.4 %collective-permute-start.24 = (bf16[1024,512]{1,0:T(8,128)(2,1)S(1)}, bf16[1024,512]{1,0:T(8,128)(2,1)S(1)}, u32[]{:S(2)}, u32[]{:S(2)}) collective-permute-start(bf16[1024,512]{1,0:T(8,128)(2,1)S(1)} %slice.54), channel_id=1, source_target_pairs={{0,8},{4,12},{8,0},{12,4},{16,24},{20,28},{24,16},{28,20},{1,9},{5... | collective-permute-start | bytes 3145736 | tf_op jit(solution)/shard_map/ppermute | solution.py:349
  141.5 29.0 %collective-permute-start.4 = (s16[3,736,128]{2,1,0:T(8,128)(2,1)S(1)}, s16[3,736,128]{2,1,0:T(8,128)(2,1)S(1)}, u32[]{:S(2)}, u32[]{:S(2)}) collective-permute-start(s16[3,736,128]{2,1,0:T(8,128)(2,1)S(1)} %slice.44), channel_id=1, source_target_pairs={{0,16},{4,20},{8,24},{12,28},{16,0},{20,4},{24,8},{28,12},{1,17},{... | collective-permute-start | bytes 1695752 | tf_op jit(solution)/shard_map/ppermute | solution.py:349
  143.7 30.4 %collective-permute-start.6 = (s16[3,764,128]{2,1,0:T(8,128)(2,1)S(1)}, s16[3,764,128]{2,1,0:T(8,128)(2,1)S(1)}, u32[]{:S(2)}, u32[]{:S(2)}) collective-permute-start(s16[3,764,128]{2,1,0:T(8,128)(2,1)S(1)} %slice.45), channel_id=1, source_target_pairs={{0,8},{4,12},{8,0},{12,4},{16,24},{20,28},{24,16},{28,20},{1,9},{5... | collective-permute-start | bytes 1760264 | tf_op jit(solution)/shard_map/ppermute | solution.py:349
  143.8 68.5 %collective-permute-start.18 = (bf16[2048,512]{1,0:T(8,128)(2,1)S(1)}, bf16[2048,512]{1,0:T(8,128)(2,1)}, u32[]{:S(2)}, u32[]{:S(2)}) collective-permute-start(bf16[2048,512]{1,0:T(8,128)(2,1)S(1)} %copy-done), channel_id=1, source_target_pairs={{0,4},{4,0},{8,12},{12,8},{16,20},{20,16},{24,28},{28,24},{1,5},{5... | collective-permute-start | bytes 6291464 | tf_op jit(solution)/shard_map/ppermute | solution.py:349
  174.2 26.7 %collective-permute-start.7 = (s16[3,1500,128]{2,1,0:T(8,128)(2,1)S(1)}, s16[3,1500,128]{2,1,0:T(8,128)(2,1)}, u32[]{:S(2)}, u32[]{:S(2)}) collective-permute-start(s16[3,1500,128]{2,1,0:T(8,128)(2,1)S(1)} %constant_dynamic-update-slice_fusion.first_ref), channel_id=1, source_target_pairs={{0,4},{4,0},{8,12},{12,8},{16,20},{20,16},{24,28},{28,24},{1,5},{5... | collective-permute-start | bytes 3456008 | tf_op jit(solution)/shard_map/ppermute | solution.py:349
  174.2 38.0 %collective-permute-start.22 = (bf16[2048,512]{1,0:T(8,128)(2,1)}, bf16[2048,512]{1,0:T(8,128)(2,1)}, u32[]{:S(2)}, u32[]{:S(2)}) collective-permute-start(bf16[2048,512]{1,0:T(8,128)(2,1)} %collective-permute-done.21.rest_8_.rest_5_), channel_id=1, source_target_pairs={{0,4},{4,0},{8,12},{12,8},{16,20},{20,16},{24,28},{28,24},{1,5},{5... | collective-permute-start | bytes 6291464 | tf_op jit(solution)/shard_map/ppermute | solution.py:349
  174.7 37.5 %collective-permute-start.20 = (bf16[2048,512]{1,0:T(8,128)(2,1)}, bf16[2048,512]{1,0:T(8,128)(2,1)}, u32[]{:S(2)}, u32[]{:S(2)}) collective-permute-start(bf16[2048,512]{1,0:T(8,128)(2,1)} %collective-permute-done.19.rest_6_.rest_3_), channel_id=1, source_target_pairs={{0,4},{4,0},{8,12},{12,8},{16,20},{20,16},{24,28},{28,24},{1,5},{5... | collective-permute-start | bytes 6291464 | tf_op jit(solution)/shard_map/ppermute | solution.py:349
  177.0 35.3 %collective-permute-start.25 = (bf16[2048,512]{1,0:T(8,128)(2,1)}, bf16[2048,512]{1,0:T(8,128)(2,1)}, u32[]{:S(2)}, u32[]{:S(2)}) collective-permute-start(bf16[2048,512]{1,0:T(8,128)(2,1)} %constant_dynamic-update-slice_fusion.2.rest_10_.rest_7_), channel_id=1, source_target_pairs={{0,4},{4,0},{8,12},{12,8},{16,20},{20,16},{24,28},{28,24},{1,5},{5... | collective-permute-start | bytes 6291464 | tf_op jit(solution)/shard_map/ppermute | solution.py:349
  200.9 11.3 %collective-permute-start.26 = (bf16[1024,512]{1,0:T(8,128)(2,1)}, bf16[1024,512]{1,0:T(8,128)(2,1)S(1)}, u32[]{:S(2)}, u32[]{:S(2)}) collective-permute-start(bf16[1024,512]{1,0:T(8,128)(2,1)} %get-tuple-element.12), channel_id=1, source_target_pairs={{0,4},{4,0},{8,12},{12,8},{16,20},{20,16},{24,28},{28,24},{1,5},{5... | collective-permute-start | bytes 3145736 | tf_op jit(solution)/shard_map/ppermute | solution.py:349
  (22 other events, 201.3 us)
Sparse Core Ops, SparseCore 0:
  63.8 44.7 all-gather.8
  110.2 44.8 all-gather.10
  209.5 44.4 all-gather.6

commit v3 on v0

--- a/solution.py
+++ b/solution.py
@@ -1,9 +1,15 @@
+import functools
+
 import jax
 import jax.numpy as jnp
 from jax import lax
+from jax.experimental import pallas as pl
+from jax.experimental.pallas import tpu as pltpu
 from jax.sharding import PartitionSpec as P
 
 LAG = 384
+CHUNK = 128
+VMEM_LIMIT = 56 * 1024 * 1024
 
 
 def contact_values(coords, frame_scale, pairs):
@@ -38,7 +44,7 @@
     )
 
 
-def shards(coords, frame_scale, pairs, walker_lengths):
+def plain_shards(coords, frame_scale, pairs, walker_lengths):
     tm_count = lax.axis_size("tm")
     frames_dev = coords.shape[0]
     local_feats = pairs.shape[1]
@@ -60,11 +66,336 @@
     return (same / jnp.float32(frames_all), cross / npairs)
 
 
+def switch(squares, scale):
+    dist_sq = (scale * scale) * squares
+    return 1.0 / (1.0 + dist_sq * dist_sq * dist_sq)
+
+
+def as_column(row):
+    return jnp.broadcast_to(row, (CHUNK, row.shape[1])).T
+
+
+def gather_kernel(centered, coords_count, pairs_ref, scale_ref, *rest):
+    coords_refs, rest = rest[:coords_count], rest[coords_count:]
+    if centered:
+        mean_ref, out_ref, table, dense, part = rest
+    else:
+        out_ref, sums_ref, table, dense, part = rest
+    residues = coords_refs[0].shape[1]
+    chunks = 4 if coords_count == 1 else coords_count
+    stride = table.shape[0] // residues
+    block = part.shape[0]
+    group = dense.shape[0] // chunks
+    step = pl.program_id(0)
+
+    @pl.when(step == 0)
+    def _():
+        for k in range(3):
+            for c in range(chunks):
+                if coords_count == 1:
+                    plane = coords_refs[0][k, :, c * CHUNK : (c + 1) * CHUNK]
+                else:
+                    plane = coords_refs[c][k].astype(jnp.int32)
+                table[pl.ds(k * chunks + c, residues, stride=stride), :] = plane
+
+    if centered:
+        part[...] = as_column(mean_ref[...])
+    sublane = lax.broadcasted_iota(jnp.int32, (8, CHUNK), 0)
+    scale = scale_ref[...]
+
+    def squares(f):
+        first = pl.multiple_of(pairs_ref[0, f], 8)
+        second = pl.multiple_of(pairs_ref[1, f], 8)
+        diff = (table[pl.ds(first, stride), :] - table[pl.ds(second, stride), :]).astype(jnp.float32)
+        diff = diff * diff
+        if chunks == 4:
+            total = diff[0:8] + jnp.where(sublane < 4, diff[8:16], 0.0)
+            return total + pltpu.roll(total, 4, 0)
+        diff = jnp.where(sublane < 6, diff, 0.0)
+        total = diff + pltpu.roll(diff, 4, 0)
+        return total + pltpu.roll(total, 2, 0)
+
+    @pl.loop(0, block // group)
+    def _(g):
+        at = pl.multiple_of(g * group, group)
+        packed = 8 // chunks
+        for f in range(0, group, packed):
+            base = step * block + at + f
+            value = squares(base)
+            for i in range(1, packed):
+                value = jnp.where(sublane < i * chunks, value, squares(base + i))
+            dense[pl.ds(f * chunks, 8), :] = switch(value, scale)
+        for h in range(group // 16):
+            here = pl.ds(pl.multiple_of(at + h * 16, 16), 16)
+            total = jnp.zeros((16, CHUNK), jnp.float32)
+            for c in range(chunks):
+                contact = dense[pl.ds(h * 16 * chunks + c, 16, stride=chunks), :]
+                if not centered:
+                    out_ref[here, c * CHUNK : (c + 1) * CHUNK] = contact
+                    total = total + contact
+                elif coords_count == 1:
+                    out_ref[here, c * CHUNK : (c + 1) * CHUNK] = (contact - part[here, :]).astype(
+                        jnp.bfloat16
+                    )
+                else:
+                    out_ref[c, here, :] = (contact - part[here, :]).astype(jnp.bfloat16)
+            if not centered:
+                part[here, :] = total
+
+    if not centered:
+        sums_ref[...] = jnp.sum(part[...].T, axis=0, keepdims=True)
+
+
+def contacts(pairs, coords, scale, mean=None, block=512, group=32):
+    residues = coords[0].shape[1]
+    feats = pairs.shape[1]
+    chunks = scale.shape[0]
+    stride = -(-3 * chunks // 8) * 8
+    centered = mean is not None
+    row_spec = pl.BlockSpec((1, block), lambda n: (0, n))
+    in_specs = [pl.BlockSpec(memory_space=pltpu.SMEM), pl.BlockSpec((8, CHUNK), lambda n: (0, 0))]
+    in_specs += [pl.BlockSpec(x.shape, lambda n: (0, 0, 0), pipeline_mode=pl.Buffered(1)) for x in coords]
+    args = [pairs * stride, jnp.concatenate([scale] * (8 // chunks), axis=0), *coords]
+    if len(coords) == 1:
+        out_shape = jax.ShapeDtypeStruct((feats, chunks * CHUNK), jnp.bfloat16 if centered else jnp.float32)
+        out_specs = pl.BlockSpec((block, chunks * CHUNK), lambda n: (n, 0))
+    else:
+        out_shape = jax.ShapeDtypeStruct((chunks, feats, CHUNK), jnp.bfloat16)
+        out_specs = pl.BlockSpec((chunks, block, CHUNK), lambda n: (0, n, 0))
+    if centered:
+        in_specs.append(row_spec)
+        args.append(mean)
+    else:
+        out_shape = [out_shape, jax.ShapeDtypeStruct((1, feats), jnp.float32)]
+        out_specs = [out_specs, row_spec]
+    return pl.pallas_call(
+        functools.partial(gather_kernel, centered, len(coords)),
+        out_shape=out_shape,
+        grid=(feats // block,),
+        in_specs=in_specs,
+        out_specs=out_specs,
+        scratch_shapes=[
+            pltpu.VMEM((residues * stride, CHUNK), jnp.int32),
+            pltpu.VMEM((group * chunks, CHUNK), jnp.float32),
+            pltpu.VMEM((block, CHUNK), jnp.float32),
+        ],
+        compiler_params=pltpu.CompilerParams(vmem_limit_bytes=VMEM_LIMIT),
+        cost_estimate=pl.CostEstimate(
+            flops=40 * feats * chunks * CHUNK,
+            bytes_accessed=12 * residues * chunks * CHUNK + 4 * feats * chunks * CHUNK,
+            transcendentals=0,
+        ),
+    )(*args)
+
+
+def center_kernel(raw_ref, mean_ref, out_ref):
+    col = as_column(mean_ref[...])
+    for c in range(raw_ref.shape[1] // CHUNK):
+        lanes = slice(c * CHUNK, (c + 1) * CHUNK)
+        out_ref[:, lanes] = (raw_ref[:, lanes] - col).astype(jnp.bfloat16)
+
+
+def center(raw, mean, block=512):
+    feats, frames = raw.shape
+    return pl.pallas_call(
+        center_kernel,
+        out_shape=jax.ShapeDtypeStruct(raw.shape, jnp.bfloat16),
+        grid=(feats // block,),
+        in_specs=[
+            pl.BlockSpec((block, frames), lambda n: (n, 0)),
+            pl.BlockSpec((1, block), lambda n: (0, n)),
+        ],
+        out_specs=pl.BlockSpec((block, frames), lambda n: (n, 0)),
+        compiler_params=pltpu.CompilerParams(vmem_limit_bytes=VMEM_LIMIT),
+        cost_estimate=pl.CostEstimate(flops=2 * raw.size, bytes_accessed=6 * raw.size, transcendentals=0),
+    )(raw, mean)
+
+
+def product_kernel(sources, me_ref, mask_ref, factors_ref, *rest):
+    rows_refs, rest = rest[:5], rest[5:]
+    cols_refs, rest = rest[:8], rest[8:]
+    same_ref, cross_ref, left = rest[-3:]
+    feats = same_ref.shape[0]
+    frames = cols_refs[0].shape[1]
+    parts = frames // CHUNK
+    me = me_ref[0]
+
+    @pl.when(pl.program_id(0) == 0)
+    def _():
+        for d, (operand, block) in enumerate(sources):
+            j = me ^ d
+            after = me ^ lax.rem(j + 1, 8)
+            mask = mask_ref[j].astype(jnp.bfloat16)
+            ref = rows_refs[operand]
+            for c in range(parts):
+                inner = slice(c * CHUNK, (c + 1) * CHUNK)
+                value = ref[:, inner] if block is None else ref[c, block]
+                left[0:feats, d * frames + c * CHUNK : d * frames + (c + 1) * CHUNK] = value
+                to = c + LAG // CHUNK
+                start = (d if to < parts else after) * frames + (to % parts) * CHUNK
+                if to >= parts:
+                    start = pl.multiple_of(start, CHUNK)
+                left[feats : 2 * feats, pl.ds(start, CHUNK)] = value * mask[:, inner]
+
+    right = jnp.concatenate([ref[...] for ref in cols_refs], axis=1)
+    both = lax.dot_general(
+        left[...], right, (((1,), (1,)), ((), ())), preferred_element_type=jnp.float32
+    )
+    same_ref[...] = both[0:feats] * factors_ref[0]
+    cross_ref[...] = both[feats : 2 * feats] / factors_ref[1]
+
+
+def products(me, mask, factors, piece, pieces, near, gathered, cols, outs=(), block=512):
+    sources = ((0, None), (1, None), (2, None), (4, 0), (3, None), (4, 1), (4, 2), (4, 3))
+    feats, frames = cols[0].shape
+    row_feats = near[0].shape[0]
+    rows = row_feats // pieces
+    out = jax.ShapeDtypeStruct((row_feats, feats), jnp.float32)
+    whole = lambda x: pl.BlockSpec(x.shape, lambda n, s: (0,) * x.ndim, pipeline_mode=pl.Buffered(1))
+    inputs = [mask, factors, *near, gathered, *cols, *outs]
+    return pl.pallas_call(
+        functools.partial(product_kernel, sources),
+        out_shape=[out, out],
+        grid_spec=pltpu.PrefetchScalarGridSpec(
+            num_scalar_prefetch=1,
+            grid=(feats // block,),
+            in_specs=[whole(mask), pl.BlockSpec(memory_space=pltpu.SMEM)]
+            + [pl.BlockSpec((rows, frames), lambda n, s: (piece, 0), pipeline_mode=pl.Buffered(1))] * 4
+            + [whole(gathered)]
+            + [pl.BlockSpec((block, frames), lambda n, s: (n, 0))] * 8
+            + [pl.BlockSpec(memory_space=pl.ANY)] * len(outs),
+            out_specs=[pl.BlockSpec((rows, block), lambda n, s: (piece, n))] * 2,
+            scratch_shapes=[pltpu.VMEM((2 * rows, 8 * frames), jnp.bfloat16)],
+        ),
+        input_output_aliases={1 + len(inputs) - 2 + i: i for i in range(len(outs))},
+        compiler_params=pltpu.CompilerParams(vmem_limit_bytes=VMEM_LIMIT),
+        cost_estimate=pl.CostEstimate(
+            flops=4 * rows * feats * 8 * frames,
+            bytes_accessed=16 * frames * (rows + feats) + 8 * rows * feats,
+            transcendentals=0,
+        ),
+    )(me, *inputs)
+
+
+def swap(x, bits):
+    return lax.ppermute(x, "tm", [(i, i ^ bits) for i in range(8)])
+
+
+def corner(along_x, along_y, axis, half):
+    low = swap(lax.slice_in_dim(along_x, 0, half, axis=axis), 4)
+    high = swap(lax.slice_in_dim(along_y, half, along_y.shape[axis], axis=axis), 2)
+    return jnp.concatenate([low, high], axis=axis)
+
+
+def from_owner(x, feat_count, *after):
+    owner = lambda i: i * feat_count // 8
+    held = [jnp.where(lax.axis_index("feat") == owner(lax.axis_index("tm")), x, jnp.zeros_like(x))]
+    for s in range(1, feat_count):
+        perm = [
+            (i * feat_count + owner(i), i * feat_count + (owner(i) + s) % feat_count)
+            for i in range(8)
+        ]
+        held.append(lax.ppermute(x, ("tm", "feat"), perm))
+    if after:
+        held = tie(held, *after)
+    return sum(held[1:], held[0])
+
+
+def tie(x, *after):
+    return lax.optimization_barrier((x, after))[0]
+
+
+def shards(coords, frame_scale, pairs, walker_lengths):
+    tm_count = lax.axis_size("tm")
+    feat_count = lax.axis_size("feat")
+    frames_dev = coords.shape[0]
+    feats = pairs.shape[1]
+    frames_all = frames_dev * tm_count
+    row_feats = feats * feat_count // tm_count
+    parts = frames_dev // CHUNK
+    pieces = 2
+    tm = lax.axis_index("tm").astype(jnp.int32)
+    z = lax.axis_index("feat").astype(jnp.int32)
+    me = tm.reshape(1)
+    own_half = (tm % (feats // row_feats)) * row_feats
+
+    coords_t = jnp.transpose(coords, (1, 2, 0))
+    scale_own = frame_scale.reshape(parts, CHUNK)
+    quarter = lax.dynamic_slice_in_dim(coords_t, z * CHUNK, CHUNK, axis=2).astype(jnp.int16)
+    quarters = {3: swap(quarter, 3), 5: swap(quarter, 5)}
+
+    raw, sums = contacts(pairs, [coords_t], scale_own)
+    note = jnp.concatenate([sums, frame_scale.reshape(1, frames_dev)], axis=1)
+    notes = [note] + [swap(note, d) for d in range(1, 8)]
+
+    quarters = tie(quarters, sums)
+    quarters[7] = corner(quarters[3], quarters[5], 1, (coords_t.shape[1] // 32) * 16)
+    chip_pairs = from_owner(pairs, feat_count, sums)
+    row_pairs = lax.dynamic_slice_in_dim(chip_pairs, own_half, row_feats, axis=1)
+    near_pairs = jnp.concatenate([swap(row_pairs, 2), swap(row_pairs, 4)], axis=1)
+
+    totals = notes[0][:, :feats]
+    for other in notes[1:]:
+        totals = totals + other[:, :feats]
+    mean = totals / jnp.float32(frames_all)
+    chip_mean = from_owner(mean, feat_count)
+    row_mean = lax.dynamic_slice_in_dim(chip_mean, own_half, row_feats, axis=1)
+    scales = [lax.dynamic_slice_in_dim(n, feats + z * CHUNK, CHUNK, axis=1) for n in notes]
+    scale_of = lambda *d: jnp.concatenate([scales[i] for i in d], axis=0)
+
+    sent_near = contacts(row_pairs, [quarters[3], quarters[5]], scale_of(3, 5), row_mean)
+    raw = tie(raw, sent_near, quarters[7])
+    mine = center(raw, mean)
+    quarters[6] = swap(quarters[7], 1)
+    cols = {0: mine, 1: swap(mine, 1), 2: swap(mine, 2), 4: swap(mine, 4)}
+
+    far = tie([quarters[6], quarters[7]], mine)
+    sent_far = contacts(row_pairs, far, scale_of(6, 7), row_mean)
+    joined = []
+    for p in range(pieces):
+        cut = slice(p * row_feats // pieces, (p + 1) * row_feats // pieces)
+        joined.append(jnp.concatenate([sent_near[:, cut], sent_far[:, cut]], axis=0))
+    gathered = [lax.all_gather(x, "feat", axis=0, tiled=False) for x in joined]
+
+    near_mean = jnp.concatenate([swap(row_mean, 2), swap(row_mean, 4)], axis=1)
+    out_pairs = jnp.concatenate([near_pairs, chip_pairs], axis=1)
+    out_mean = jnp.concatenate([near_mean, chip_mean], axis=1)
+    out_pairs = tie(out_pairs, *joined)
+    sent = contacts(out_pairs, [coords_t], scale_own, out_mean)
+    rows_cut = lambda start: lax.dynamic_slice_in_dim(sent, start, row_feats, axis=0)
+    own = rows_cut(2 * row_feats + own_half)
+    partner = swap(rows_cut(3 * row_feats - own_half), 1)
+
+    cols = tie(cols, sent)
+    cols[6] = corner(cols[2], cols[4], 0, feats // 2)
+    from_x = swap(rows_cut(0), 2)
+    from_y = swap(rows_cut(row_feats), 4)
+    for d in (2, 4, 6):
+        cols[d + 1] = swap(cols[d], 1)
+    cols = [cols[d] for d in range(8)]
+
+    valid = walker_mask(walker_lengths, frames_all, frames_all)
+    mask = valid.astype(jnp.float32).reshape(tm_count, 1, frames_dev)
+    npairs = jnp.sum(jnp.maximum(walker_lengths - LAG, 0)).astype(jnp.float32)
+    factors = jnp.stack([jnp.float32(1.0 / frames_all), npairs])
+    outs = ()
+    for p in range(pieces):
+        outs = products(me, mask, factors, p, pieces, [own, partner, from_x, from_y], gathered[p], cols, outs)
+    return outs
+
+
 def solution(mesh):
-    return jax.shard_map(
-        shards,
-        mesh=mesh,
-        in_specs=(P("tm", None, None), P("tm"), P(None, "feat"), P()),
-        out_specs=(P("tm", "feat"), P("tm", "feat")),
-        check_vma=False,
-    )
+    def run(coords, frame_scale, pairs, walker_lengths):
+        tm_count, feat_count = mesh.shape["tm"], mesh.shape["feat"]
+        frames_dev = coords.shape[0] // tm_count
+        square = tm_count == 8 and feat_count == 4
+        fits = square and frames_dev == 4 * CHUNK and pairs.shape[1] == 16 * 512
+        return jax.shard_map(
+            shards if fits else plain_shards,
+            mesh=mesh,
+            in_specs=(P("tm", None, None), P("tm"), P(None, "feat"), P()),
+            out_specs=(P("tm", "feat"), P("tm", "feat")),
+            check_vma=False,
+        )(coords, frame_scale, pairs, walker_lengths)
+
+    return run

time: 595 us -> 281 us (0.47)
  waiting for transfers between devices: 307 us -> 80 us
  matrix products: 129 us -> 0 us
  Pallas kernels: 0 us -> 115 us
  local copies, waits for them, and re-layouts: 69.8 us -> 21.3 us
  other arithmetic: 47.5 us -> 11 us
  starting transfers between devices: 5.48 us -> 38.2 us
  blocking collectives: 15.5 us -> 0 us
    all_gather x2, waiting for transfers between devices: 306 us -> 0.04 us  [shards(): gathered = [lax.all_gather(x, 'feat', axis=0, tiled=False) for x in joined]]
    dot_general x3 -> x0, matrix products: 129 us -> none  [the longest x1 79.1 us: contact_values(): jnp.dot(flat, selector, precision=lax.Precision.HIGHEST, preferred_elemen...]
    pallas_call x0 -> x7, Pallas kernels: none -> 115 us  [the longest x4 59.1 us: contacts(): pl.pallas_call(functools.partial(gather_kernel, centered, len(coords)), o...]
    ppermute x0 -> x33, waiting for transfers between devices: none -> 79.9 us  [the longest x27 79.9 us: swap(): return lax.ppermute(x, 'tm', [(i, i ^ bits) for i in range(8)])]
    ppermute x0 -> x33, starting transfers between devices: none -> 37.9 us  [the longest x27 21.8 us: swap(): return lax.ppermute(x, 'tm', [(i, i ^ bits) for i in range(8)])]
    reshape x2 -> x0, local copies, waits for them, and re-layouts: 34.2 us -> none  [the longest x1 19.3 us: contact_values(): diff = diff.reshape(frames_dev, 3, pairs.shape[1])]
    add x1 -> x2, other arithmetic: 26.5 us -> 0.78 us  [from_owner(): return sum(held[1:], held[0])]
    psum x1 -> x0, blocking collectives: 15.5 us -> none  [shards(): totals = lax.psum(jnp.sum(contact, axis=0), 'tm')]
  transfers between devices with their start and end apart: 3 -> 35, of which waited for: 2 -> 7; matrix products, arithmetic and copies ran while one was open for 4% -> 10% of each run, Pallas kernels for 0% -> 32%
where the time goes in v3:
time: 281 us
  Pallas kernels  115 us (41%)
  waiting for transfers between devices  80 us (28%)
  starting transfers between devices  38.2 us (14%)
  local copies, waits for them, and re-layouts  21.3 us (8%)
  between operations  15.1 us (5%)
  other arithmetic  11 us (4%)
    ppermute x27, waiting for transfers between devices, swap(): return lax.ppermute(x, 'tm', [(i, i ^ bits) for i in range(8)])  79.9 us
    pallas_call x4, Pallas kernels, contacts(): pl.pallas_call(functools.partial(gather_kernel, centered, len(coords)), o...  59.1 us
    pallas_call x2, Pallas kernels, products(): pl.pallas_call(functools.partial(product_kernel, sources), out_shape=[out...  51.4 us
    ppermute x27, starting transfers between devices, swap(): return lax.ppermute(x, 'tm', [(i, i ^ bits) for i in range(8)])  21.8 us
    ppermute x6, starting transfers between devices, from_owner(): held.append(lax.ppermute(x, ('tm', 'feat'), perm))  16.1 us
  transfers between devices with their start and end apart: 35, of which 7 were waited for; matrix products, arithmetic and copies ran while one was open for 10% of the time, Pallas kernels for 32%

profile of v3, /device:TPU:0, one launch (start us, length us, event | category | flops | bytes accessed | tf_op | source)
XLA Modules:
  0.0 280.6 jit_solution(389539539930434562)
XLA Ops:
  9.0 2.5 collective-permute-start.8
  14.5 17.8 %shard_map.59 = (f32[2048,512]{1,0:T(8,128)}, f32[1,2048]{1,0:T(1,128)}) custom-call(s32[2,2048]{1,0:T(2,128)} %get-tuple-element.50.pairs_ref, f32[8,128]{1,0:T(8,128)} %pad_maximum_fusion.4.scale_ref, s32[3,1500,512]{2,1,0:T(8,128)} %bitcast.11), custom_call_target="tpu_custom_call" | custom-call | flops 41943040 | bytes 13410304 | tf_op jit(solution)/shard_map/pallas_call | solution.py:171
  33.1 2.3 collective-permute-start.12
  36.0 3.5 %collective-permute-done.13 = f32[1,2560]{1,0:T(1,128)S(1)} collective-permute-done((f32[1,2560]{1,0:T(1,128)S(1)}, f32[1,2560]{1,0:T(1,128)S(1)}, u32[]{:S(2)}, u32[]{:S(2)}) %collective-permute-start.13) | collective-permute-done | bytes 10272 | tf_op jit(solution)/shard_map/ppermute | solution.py:281
  43.2 3.4 %collective-permute-start = (s32[2,2048]{1,0:T(2,128)S(1)}, s32[2,2048]{1,0:T(2,128)S(1)}, u32[]{:S(2)}, u32[]{:S(2)}) collective-permute-start(s32[2,2048]{1,0:T(2,128)S(1)} %copy-done.7), channel_id=1, source_target_pairs={{0,1},{4,5},{9,10},{13,14},{18,19},{22,23},{27,24},{31,28}} | collective-permute-start | bytes 49160 | tf_op jit(solution)/shard_map/ppermute | solution.py:298
  46.6 2.3 collective-permute-start.1
  48.9 2.9 %collective-permute-start.2 = (s32[2,2048]{1,0:T(2,128)S(1)}, s32[2,2048]{1,0:T(2,128)}, u32[]{:S(2)}, u32[]{:S(2)}) collective-permute-start(s32[2,2048]{1,0:T(2,128)S(1)} %copy-done.7), channel_id=1, source_target_pairs={{0,3},{4,7},{9,8},{13,12},{18,17},{22,21},{27,26},{31,30}} | collective-permute-start | bytes 49160 | tf_op jit(solution)/shard_map/ppermute | solution.py:298
  56.9 5.0 %collective-permute-start.16 = (f32[1,2048]{1,0:T(1,128)S(1)}, f32[1,2048]{1,0:T(1,128)S(1)}, u32[]{:S(2)}, u32[]{:S(2)}) collective-permute-start(f32[1,2048]{1,0:T(1,128)S(1)} %fusion.4.mean_ref), channel_id=1, source_target_pairs={{0,3},{4,7},{9,8},{13,12},{18,17},{22,21},{27,26},{31,30}} | collective-permute-start | bytes 24584 | tf_op jit(solution)/shard_map/ppermute | solution.py:298
  65.2 3.5 %collective-permute-done.17 = s16[3,736,128]{2,1,0:T(8,128)(2,1)} collective-permute-done((s16[3,736,128]{2,1,0:T(8,128)(2,1)}, s16[3,736,128]{2,1,0:T(8,128)(2,1)}, u32[]{:S(2)}, u32[]{:S(2)}) %collective-permute-start.17) | collective-permute-done | bytes 565280 | tf_op jit(solution)/shard_map/ppermute | solution.py:281
  72.9 7.7 %shard_map.60 = bf16[2,1024,128]{2,1,0:T(8,128)(2,1)} custom-call(s32[2,1024]{1,0:T(2,128)} %get-tuple-element.40.pairs_ref, f32[8,128]{1,0:T(8,128)} %concatenate.38.scale_ref, s16[3,1500,128]{2,1,0:T(8,128)(2,1)} %copy-done.1, s16[3,1500,128]{2,1,0:T(8,128)(2,1)} %copy-done, f32[1,1024]{1,0:T(1,128)} %copy-done.6), custom_call_target="tpu_custom_call" | custom-call | flops 10485760 | bytes 5656576 | tf_op jit(solution)/shard_map/pallas_call | solution.py:171
  80.6 4.5 %shard_map.61.rest_5_ = bf16[2048,512]{1,0:T(8,128)(2,1)} custom-call(f32[2048,512]{1,0:T(8,128)} %get-tuple-element.28.raw_ref, f32[1,2048]{1,0:T(1,128)} %copy-done.5), custom_call_target="tpu_custom_call" | custom-call | flops 2097152 | bytes 6291456 | tf_op jit(solution)/shard_map/pallas_call | solution.py:200
  90.3 7.7 %shard_map.62 = bf16[2,1024,128]{2,1,0:T(8,128)(2,1)} custom-call(s32[2,1024]{1,0:T(2,128)} %get-tuple-element.40.pairs_ref, f32[8,128]{1,0:T(8,128)} %concatenate.39.scale_ref, s16[3,1500,128]{2,1,0:T(8,128)(2,1)} %copy-done.4, s16[3,1500,128]{2,1,0:T(8,128)(2,1)} %copy-done.2, f32[1,1024]{1,0:T(1,128)} %copy-done.6), custom_call_target="tpu_custom_call" | custom-call | flops 10485760 | bytes 5656576 | tf_op jit(solution)/shard_map/pallas_call | solution.py:171
  100.2 34.0 %collective-permute-done.3 = s32[2,1024]{1,0:T(2,128)S(1)} collective-permute-done((s32[2,1024]{1,0:T(2,128)S(1)}, s32[2,1024]{1,0:T(2,128)S(1)}, u32[]{:S(2)}, u32[]{:S(2)}) %collective-permute-start.3) | collective-permute-done | bytes 8224 | tf_op jit(solution)/shard_map/ppermute | solution.py:281
  135.7 25.9 %shard_map.63 = bf16[4096,512]{1,0:T(8,128)(2,1)} custom-call(s32[2,4096]{1,0:T(2,128)} %broadcast_multiply_fusion.pairs_ref, f32[8,128]{1,0:T(8,128)} %pad_maximum_fusion.4.scale_ref, s32[3,1500,512]{2,1,0:T(8,128)} %bitcast.12, f32[1,4096]{1,0:T(1,128)} %pad_maximum_fusion.2.rest_1_), custom_call_target="tpu_custom_call" | custom-call | flops 83886080 | bytes 17604608 | tf_op jit(solution)/shard_map/pallas_call | solution.py:171
  161.6 3.0 %slice.58 = bf16[1024,512]{1,0:T(8,128)(2,1)} slice(bf16[2048,512]{1,0:T(8,128)(2,1)} %collective-permute-done.26.rest_7_), slice={[0:1024], [0:512]} | slice | bytes 2097152 | tf_op jit(solution)/shard_map/slice | solution.py:285
  165.1 2.3 slice.59
  169.1 3.4 %fusion.5 = (bf16[1024,512]{1,0:T(8,128)(2,1)S(1)}, bf16[1024,512]{1,0:T(8,128)(2,1)S(1)}, bf16[1024,512]{1,0:T(8,128)(2,1)S(1)}, bf16[1024,512]{1,0:T(8,128)(2,1)}) fusion(bf16[4096,512]{1,0:T(8,128)(2,1)} %shard_map.63, s32[]{:T(128)S(6)} %select_n.57, s32[]{:T(128)S(6)} %select_n.56), kind=kLoop, calls=%fused_computation.44 | loop fusion | bytes 8388616 | tf_op jit(solution)/shard_map/dynamic_slice | solution.py:365
  174.6 16.4 %collective-permute-done.30 = bf16[1024,512]{1,0:T(8,128)(2,1)} collective-permute-done((bf16[1024,512]{1,0:T(8,128)(2,1)}, bf16[1024,512]{1,0:T(8,128)(2,1)}, u32[]{:S(2)}, u32[]{:S(2)}) %collective-permute-start.30) | collective-permute-done | bytes 1048608 | tf_op jit(solution)/shard_map/ppermute | solution.py:281
  191.1 2.3 constant_dynamic-update-slice_fusion.3
  193.3 2.3 constant_dynamic-update-slice_fusion.2.rest_11_
  197.4 13.6 %collective-permute-done.24.rest_3_ = bf16[1024,512]{1,0:T(8,128)(2,1)} collective-permute-done((bf16[1024,512]{1,0:T(8,128)(2,1)S(1)}, bf16[1024,512]{1,0:T(8,128)(2,1)}, u32[]{:S(2)}, u32[]{:S(2)}) %collective-permute-start.24) | collective-permute-done | bytes 1048608 | tf_op jit(solution)/shard_map/ppermute | solution.py:281
  213.9 7.4 %collective-permute-done.23.rest_2_ = bf16[1024,512]{1,0:T(8,128)(2,1)} collective-permute-done((bf16[1024,512]{1,0:T(8,128)(2,1)S(1)}, bf16[1024,512]{1,0:T(8,128)(2,1)}, u32[]{:S(2)}, u32[]{:S(2)}) %collective-permute-start.23) | collective-permute-done | bytes 1048608 | tf_op jit(solution)/shard_map/ppermute | solution.py:281
  222.3 25.6 %shard_map.64 = (f32[1024,2048]{1,0:T(8,128)}, f32[1024,2048]{1,0:T(8,128)}) custom-call(s32[1]{0:T(128)} %bitcast.me_ref, f32[8,1,512]{2,1,0:T(1,128)} %and_convert_fusion.mask_ref, f32[2]{0:T(128)} %pad_maximum_fusion.5.factors_ref, bf16[1024,512]{1,0:T(8,128)(2,1)} %get-tuple-element.45.rest_0_, bf16[1024,512]{1,0:T(8,128)(2,1)} %copy-done.11, ...), custom_call_target="tpu_custom_call" | custom-call | flops 17179869184 | bytes 29360128 | tf_op jit(solution)/shard_map/pallas_call | solution.py:256
  248.0 25.8 %shard_map.65 = (f32[1024,2048]{1,0:T(8,128)}, f32[1024,2048]{1,0:T(8,128)}) custom-call(s32[1]{0:T(128)} %bitcast.me_ref, f32[8,1,512]{2,1,0:T(1,128)} %and_convert_fusion.mask_ref, f32[2]{0:T(128)} %pad_maximum_fusion.5.factors_ref, bf16[1024,512]{1,0:T(8,128)(2,1)} %get-tuple-element.45.rest_0_, ...), custom_call_target="tpu_custom_call", output_to_operand_aliasing={{0}: (16, {}), {1}: (17, {})} | custom-call | flops 17179869184 | bytes 29360128 | tf_op jit(solution)/shard_map/pallas_call | solution.py:256
  (120 shorter events, 40.4 us)
Async XLA Ops:
  7.2 214.2 %all-gather.7.cloned.1.call-start = ((), (), s32[]{:S(2)}) async-start(), calls=%async_computation.1 | async-start | bytes 2621440 | tf_op jit(solution)/shard_map/all_gather | solution.py:358
  9.0 43.6 %collective-permute-start.8 = (s16[3,1500,128]{2,1,0:T(8,128)(2,1)S(1)}, s16[3,1500,128]{2,1,0:T(8,128)(2,1)S(1)}, u32[]{:S(2)}, u32[]{:S(2)}) collective-permute-start(s16[3,1500,128]{2,1,0:T(8,128)(2,1)S(1)} %fusion), channel_id=1, source_target_pairs={{0,20},{4,16},{8,28},{12,24},{16,4},{20,0},{24,12},{28,8},{1,21},{... | collective-permute-start | bytes 3456008 | tf_op jit(solution)/shard_map/ppermute | solution.py:281
  11.5 41.1 %collective-permute-start.7 = (s16[3,1500,128]{2,1,0:T(8,128)(2,1)S(1)}, s16[3,1500,128]{2,1,0:T(8,128)(2,1)S(1)}, u32[]{:S(2)}, u32[]{:S(2)}) collective-permute-start(s16[3,1500,128]{2,1,0:T(8,128)(2,1)S(1)} %fusion), channel_id=1, source_target_pairs={{0,12},{4,8},{8,4},{12,0},{16,28},{20,24},{24,20},{28,16},{1,13},{... | collective-permute-start | bytes 3456008 | tf_op jit(solution)/shard_map/ppermute | solution.py:281
  43.2 13.7 %collective-permute-start = (s32[2,2048]{1,0:T(2,128)S(1)}, s32[2,2048]{1,0:T(2,128)S(1)}, u32[]{:S(2)}, u32[]{:S(2)}) collective-permute-start(s32[2,2048]{1,0:T(2,128)S(1)} %copy-done.7), channel_id=1, source_target_pairs={{0,1},{4,5},{9,10},{13,14},{18,19},{22,23},{27,24},{31,28}} | collective-permute-start | bytes 49160 | tf_op jit(solution)/shard_map/ppermute | solution.py:298
  46.6 15.2 %collective-permute-start.1 = (s32[2,2048]{1,0:T(2,128)S(1)}, s32[2,2048]{1,0:T(2,128)}, u32[]{:S(2)}, u32[]{:S(2)}) collective-permute-start(s32[2,2048]{1,0:T(2,128)S(1)} %copy-done.7), channel_id=1, source_target_pairs={{0,2},{4,6},{9,11},{13,15},{18,16},{22,20},{27,25},{31,29}} | collective-permute-start | bytes 49160 | tf_op jit(solution)/shard_map/ppermute | solution.py:298
  48.9 14.2 %collective-permute-start.2 = (s32[2,2048]{1,0:T(2,128)S(1)}, s32[2,2048]{1,0:T(2,128)}, u32[]{:S(2)}, u32[]{:S(2)}) collective-permute-start(s32[2,2048]{1,0:T(2,128)S(1)} %copy-done.7), channel_id=1, source_target_pairs={{0,3},{4,7},{9,8},{13,12},{18,17},{22,21},{27,26},{31,30}} | collective-permute-start | bytes 49160 | tf_op jit(solution)/shard_map/ppermute | solution.py:298
  53.6 15.1 %collective-permute-start.17 = (s16[3,736,128]{2,1,0:T(8,128)(2,1)}, s16[3,736,128]{2,1,0:T(8,128)(2,1)}, u32[]{:S(2)}, u32[]{:S(2)}) collective-permute-start(s16[3,736,128]{2,1,0:T(8,128)(2,1)} %slice.53), channel_id=1, source_target_pairs={{0,16},{4,20},{8,24},{12,28},{16,0},{20,4},{24,8},{28,12},{1,17},{... | collective-permute-start | bytes 1695752 | tf_op jit(solution)/shard_map/ppermute | solution.py:281
  54.2 15.6 %collective-permute-start.18 = (s16[3,764,128]{2,1,0:T(8,128)(2,1)S(1)}, s16[3,764,128]{2,1,0:T(8,128)(2,1)S(1)}, u32[]{:S(2)}, u32[]{:S(2)}) collective-permute-start(s16[3,764,128]{2,1,0:T(8,128)(2,1)S(1)} %slice.54), channel_id=1, source_target_pairs={{0,8},{4,12},{8,0},{12,4},{16,24},{20,28},{24,16},{28,20},{1,9},{5... | collective-permute-start | bytes 1760264 | tf_op jit(solution)/shard_map/ppermute | solution.py:281
  69.9 19.3 %collective-permute-start.19 = (s16[3,1500,128]{2,1,0:T(8,128)(2,1)S(1)}, s16[3,1500,128]{2,1,0:T(8,128)(2,1)S(1)}, u32[]{:S(2)}, u32[]{:S(2)}) collective-permute-start(s16[3,1500,128]{2,1,0:T(8,128)(2,1)S(1)} %constant_dynamic-update-slice_fusion.rest_1_), channel_id=1, source_target_pairs={{0,4},{4,0},{8,12},{12,8},{16,20},{20,16},{24,28},{28,24},{1,5},{5... | collective-permute-start | bytes 3456008 | tf_op jit(solution)/shard_map/ppermute | solution.py:281
  70.1 16.8 %collective-permute-start.21 = (f32[1,1024]{1,0:T(1,128)S(1)}, f32[1,1024]{1,0:T(1,128)S(1)}, u32[]{:S(2)}, u32[]{:S(2)}) collective-permute-start(f32[1,1024]{1,0:T(1,128)S(1)} %constant_dynamic-slice_fusion.4.rest_2_), channel_id=1, source_target_pairs={{0,16},{4,20},{8,24},{12,28},{16,0},{20,4},{24,8},{28,12},{1,17},{... | collective-permute-start | bytes 12296 | tf_op jit(solution)/shard_map/ppermute | solution.py:281
  71.7 16.9 %collective-permute-start.20 = (f32[1,1024]{1,0:T(1,128)S(1)}, f32[1,1024]{1,0:T(1,128)S(1)}, u32[]{:S(2)}, u32[]{:S(2)}) collective-permute-start(f32[1,1024]{1,0:T(1,128)S(1)} %constant_dynamic-slice_fusion.4.rest_2_), channel_id=1, source_target_pairs={{0,8},{4,12},{8,0},{12,4},{16,24},{20,28},{24,16},{28,20},{1,9},{5... | collective-permute-start | bytes 12296 | tf_op jit(solution)/shard_map/ppermute | solution.py:281
  72.6 27.6 %collective-permute-start.4 = (s32[2,1024]{1,0:T(2,128)S(1)}, s32[2,1024]{1,0:T(2,128)S(1)}, u32[]{:S(2)}, u32[]{:S(2)}) collective-permute-start(s32[2,1024]{1,0:T(2,128)S(1)} %get-tuple-element.41), channel_id=1, source_target_pairs={{0,16},{4,20},{8,24},{12,28},{16,0},{20,4},{24,8},{28,12},{1,17},{... | collective-permute-start | bytes 24584 | tf_op jit(solution)/shard_map/ppermute | solution.py:281
  85.1 76.5 %collective-permute-start.27 = (bf16[2048,512]{1,0:T(8,128)(2,1)}, bf16[2048,512]{1,0:T(8,128)(2,1)}, u32[]{:S(2)}, u32[]{:S(2)}) collective-permute-start(bf16[2048,512]{1,0:T(8,128)(2,1)} %shard_map.61.rest_5_), channel_id=1, source_target_pairs={{0,16},{4,20},{8,24},{12,28},{16,0},{20,4},{24,8},{28,12},{1,17},{... | collective-permute-start | bytes 6291464 | tf_op jit(solution)/shard_map/ppermute | solution.py:281
  86.8 74.8 %collective-permute-start.26 = (bf16[2048,512]{1,0:T(8,128)(2,1)}, bf16[2048,512]{1,0:T(8,128)(2,1)}, u32[]{:S(2)}, u32[]{:S(2)}) collective-permute-start(bf16[2048,512]{1,0:T(8,128)(2,1)} %shard_map.61.rest_5_), channel_id=1, source_target_pairs={{0,8},{4,12},{8,0},{12,4},{16,24},{20,28},{24,16},{28,20},{1,9},{5... | collective-permute-start | bytes 6291464 | tf_op jit(solution)/shard_map/ppermute | solution.py:281
  88.6 73.0 %collective-permute-start.25 = (bf16[2048,512]{1,0:T(8,128)(2,1)}, bf16[2048,512]{1,0:T(8,128)(2,1)S(1)}, u32[]{:S(2)}, u32[]{:S(2)}) collective-permute-start(bf16[2048,512]{1,0:T(8,128)(2,1)} %shard_map.61.rest_5_), channel_id=1, source_target_pairs={{0,4},{4,0},{8,12},{12,8},{16,20},{20,16},{24,28},{28,24},{1,5},{5... | collective-permute-start | bytes 6291464 | tf_op jit(solution)/shard_map/ppermute | solution.py:281
  89.3 44.9 %collective-permute-start.3 = (s32[2,1024]{1,0:T(2,128)S(1)}, s32[2,1024]{1,0:T(2,128)S(1)}, u32[]{:S(2)}, u32[]{:S(2)}) collective-permute-start(s32[2,1024]{1,0:T(2,128)S(1)} %get-tuple-element.41), channel_id=1, source_target_pairs={{0,8},{4,12},{8,0},{12,4},{16,24},{20,28},{24,16},{28,20},{1,9},{5... | collective-permute-start | bytes 24584 | tf_op jit(solution)/shard_map/ppermute | solution.py:281
  99.9 148.0 %all-gather.5.cloned.1.call-start = ((), (), s32[]{:S(2)}) async-start(), calls=%async_computation | async-start | bytes 2621440 | tf_op jit(solution)/shard_map/all_gather | solution.py:358
  164.6 26.4 %collective-permute-start.30 = (bf16[1024,512]{1,0:T(8,128)(2,1)}, bf16[1024,512]{1,0:T(8,128)(2,1)}, u32[]{:S(2)}, u32[]{:S(2)}) collective-permute-start(bf16[1024,512]{1,0:T(8,128)(2,1)} %slice.58), channel_id=1, source_target_pairs={{0,16},{4,20},{8,24},{12,28},{16,0},{20,4},{24,8},{28,12},{1,17},{... | collective-permute-start | bytes 3145736 | tf_op jit(solution)/shard_map/ppermute | solution.py:281
  167.4 25.9 %collective-permute-start.31 = (bf16[1024,512]{1,0:T(8,128)(2,1)}, bf16[1024,512]{1,0:T(8,128)(2,1)}, u32[]{:S(2)}, u32[]{:S(2)}) collective-permute-start(bf16[1024,512]{1,0:T(8,128)(2,1)} %slice.59), channel_id=1, source_target_pairs={{0,8},{4,12},{8,0},{12,4},{16,24},{20,28},{24,16},{28,20},{1,9},{5... | collective-permute-start | bytes 3145736 | tf_op jit(solution)/shard_map/ppermute | solution.py:281
  172.6 38.5 %collective-permute-start.24 = (bf16[1024,512]{1,0:T(8,128)(2,1)S(1)}, bf16[1024,512]{1,0:T(8,128)(2,1)}, u32[]{:S(2)}, u32[]{:S(2)}) collective-permute-start(bf16[1024,512]{1,0:T(8,128)(2,1)S(1)} %get-tuple-element.42), channel_id=1, source_target_pairs={{0,16},{4,20},{8,24},{12,28},{16,0},{20,4},{24,8},{28,12},{1,17},{... | collective-permute-start | bytes 3145736 | tf_op jit(solution)/shard_map/ppermute | solution.py:281
  174.1 47.2 %collective-permute-start.28 = (bf16[2048,512]{1,0:T(8,128)(2,1)}, bf16[2048,512]{1,0:T(8,128)(2,1)}, u32[]{:S(2)}, u32[]{:S(2)}) collective-permute-start(bf16[2048,512]{1,0:T(8,128)(2,1)} %collective-permute-done.26.rest_7_), channel_id=1, source_target_pairs={{0,4},{4,0},{8,12},{12,8},{16,20},{20,16},{24,28},{28,24},{1,5},{5... | collective-permute-start | bytes 6291464 | tf_op jit(solution)/shard_map/ppermute | solution.py:281
  174.1 47.2 %collective-permute-start.29 = (bf16[2048,512]{1,0:T(8,128)(2,1)}, bf16[2048,512]{1,0:T(8,128)(2,1)}, u32[]{:S(2)}, u32[]{:S(2)}) collective-permute-start(bf16[2048,512]{1,0:T(8,128)(2,1)} %collective-permute-done.27.rest_9_), channel_id=1, source_target_pairs={{0,4},{4,0},{8,12},{12,8},{16,20},{20,16},{24,28},{28,24},{1,5},{5... | collective-permute-start | bytes 6291464 | tf_op jit(solution)/shard_map/ppermute | solution.py:281
  195.6 25.8 %collective-permute-start.32 = (bf16[2048,512]{1,0:T(8,128)(2,1)}, bf16[2048,512]{1,0:T(8,128)(2,1)}, u32[]{:S(2)}, u32[]{:S(2)}) collective-permute-start(bf16[2048,512]{1,0:T(8,128)(2,1)} %constant_dynamic-update-slice_fusion.2.rest_11_), channel_id=1, source_target_pairs={{0,4},{4,0},{8,12},{12,8},{16,20},{20,16},{24,28},{28,24},{1,5},{5... | collective-permute-start | bytes 6291464 | tf_op jit(solution)/shard_map/ppermute | solution.py:281
  195.6 25.7 %collective-permute-start.23 = (bf16[1024,512]{1,0:T(8,128)(2,1)S(1)}, bf16[1024,512]{1,0:T(8,128)(2,1)}, u32[]{:S(2)}, u32[]{:S(2)}) collective-permute-start(bf16[1024,512]{1,0:T(8,128)(2,1)S(1)} %get-tuple-element.43), channel_id=1, source_target_pairs={{0,8},{4,12},{8,0},{12,4},{16,24},{20,28},{24,16},{28,20},{1,9},{5... | collective-permute-start | bytes 3145736 | tf_op jit(solution)/shard_map/ppermute | solution.py:281
  (24 other events, 216.2 us)
Sparse Core Ops, SparseCore 0:
  100.0 44.7 all-gather.6
  195.7 45.4 all-gather.4

commit v4 on v3

--- a/solution.py
+++ b/solution.py
@@ -10,6 +10,8 @@
 LAG = 384
 CHUNK = 128
 VMEM_LIMIT = 56 * 1024 * 1024
+NEAR = (0, 1, 2, 4)
+FAR = (3, 5, 6, 7)
 
 
 def contact_values(coords, frame_scale, pairs):
@@ -36,6 +38,12 @@
     own = jnp.sum((times[:, None] >= ends[None, :]).astype(jnp.int32), axis=1)
     ahead = jnp.sum((later[:, None] >= ends[None, :]).astype(jnp.int32), axis=1)
     return (own == ahead) & (later < frames_all)
+
+
+def estimate(micros):
+    return pl.CostEstimate(
+        flops=int(micros * 1_000_000_000), bytes_accessed=int(micros * 3_690_000), transcendentals=0
+    )
 
 
 def contract(left, right):
@@ -78,9 +86,9 @@
 def gather_kernel(centered, coords_count, pairs_ref, scale_ref, *rest):
     coords_refs, rest = rest[:coords_count], rest[coords_count:]
     if centered:
-        mean_ref, out_ref, table, dense, part = rest
+        mean_ref, out_ref, table, dense, part, held, arrived = rest
     else:
-        out_ref, sums_ref, table, dense, part = rest
+        out_ref, sums_ref, table, dense, part, held, arrived = rest
     residues = coords_refs[0].shape[1]
     chunks = 4 if coords_count == 1 else coords_count
     stride = table.shape[0] // residues
@@ -90,12 +98,21 @@
 
     @pl.when(step == 0)
     def _():
+        copies = [
+            pltpu.make_async_copy(ref.at[k], held.at[n, k], arrived.at[n, k])
+            for k in range(3)
+            for n, ref in enumerate(coords_refs)
+        ]
+        for copy in copies:
+            copy.start()
         for k in range(3):
+            for n in range(coords_count):
+                copies[k * coords_count + n].wait()
             for c in range(chunks):
                 if coords_count == 1:
-                    plane = coords_refs[0][k, :, c * CHUNK : (c + 1) * CHUNK]
+                    plane = held[0, k, :, c * CHUNK : (c + 1) * CHUNK]
                 else:
-                    plane = coords_refs[c][k].astype(jnp.int32)
+                    plane = held[c, k].astype(jnp.int32)
                 table[pl.ds(k * chunks + c, residues, stride=stride), :] = plane
 
     if centered:
@@ -154,7 +171,7 @@
     centered = mean is not None
     row_spec = pl.BlockSpec((1, block), lambda n: (0, n))
     in_specs = [pl.BlockSpec(memory_space=pltpu.SMEM), pl.BlockSpec((8, CHUNK), lambda n: (0, 0))]
-    in_specs += [pl.BlockSpec(x.shape, lambda n: (0, 0, 0), pipeline_mode=pl.Buffered(1)) for x in coords]
+    in_specs += [pl.BlockSpec(memory_space=pl.ANY) for x in coords]
     args = [pairs * stride, jnp.concatenate([scale] * (8 // chunks), axis=0), *coords]
     if len(coords) == 1:
         out_shape = jax.ShapeDtypeStruct((feats, chunks * CHUNK), jnp.bfloat16 if centered else jnp.float32)
@@ -178,103 +195,106 @@
             pltpu.VMEM((residues * stride, CHUNK), jnp.int32),
             pltpu.VMEM((group * chunks, CHUNK), jnp.float32),
             pltpu.VMEM((block, CHUNK), jnp.float32),
+            pltpu.VMEM((len(coords),) + coords[0].shape, coords[0].dtype),
+            pltpu.SemaphoreType.DMA((len(coords), 3)),
         ],
         compiler_params=pltpu.CompilerParams(vmem_limit_bytes=VMEM_LIMIT),
-        cost_estimate=pl.CostEstimate(
-            flops=40 * feats * chunks * CHUNK,
-            bytes_accessed=12 * residues * chunks * CHUNK + 4 * feats * chunks * CHUNK,
-            transcendentals=0,
-        ),
+        cost_estimate=estimate(1),
     )(*args)
 
 
 def center_kernel(raw_ref, mean_ref, out_ref):
-    col = as_column(mean_ref[...])
     for c in range(raw_ref.shape[1] // CHUNK):
-        lanes = slice(c * CHUNK, (c + 1) * CHUNK)
-        out_ref[:, lanes] = (raw_ref[:, lanes] - col).astype(jnp.bfloat16)
+        frames = slice(c * CHUNK, (c + 1) * CHUNK)
+        out_ref[frames, :] = (raw_ref[:, frames].T - mean_ref[...]).astype(jnp.bfloat16)
 
 
 def center(raw, mean, block=512):
     feats, frames = raw.shape
     return pl.pallas_call(
         center_kernel,
-        out_shape=jax.ShapeDtypeStruct(raw.shape, jnp.bfloat16),
+        out_shape=jax.ShapeDtypeStruct((frames, feats), jnp.bfloat16),
         grid=(feats // block,),
         in_specs=[
             pl.BlockSpec((block, frames), lambda n: (n, 0)),
             pl.BlockSpec((1, block), lambda n: (0, n)),
         ],
-        out_specs=pl.BlockSpec((block, frames), lambda n: (n, 0)),
+        out_specs=pl.BlockSpec((frames, block), lambda n: (0, n)),
         compiler_params=pltpu.CompilerParams(vmem_limit_bytes=VMEM_LIMIT),
-        cost_estimate=pl.CostEstimate(flops=2 * raw.size, bytes_accessed=6 * raw.size, transcendentals=0),
+        cost_estimate=estimate(1),
     )(raw, mean)
 
 
-def product_kernel(sources, me_ref, mask_ref, factors_ref, *rest):
-    rows_refs, rest = rest[:5], rest[5:]
+def product_kernel(place_ref, mask_ref, factors_ref, *rest):
+    near_refs, rest = rest[: len(NEAR)], rest[len(NEAR) :]
+    far_refs, rest = rest[:7], rest[7:]
     cols_refs, rest = rest[:8], rest[8:]
     same_ref, cross_ref, left = rest[-3:]
     feats = same_ref.shape[0]
-    frames = cols_refs[0].shape[1]
+    frames = cols_refs[0].shape[0]
     parts = frames // CHUNK
-    me = me_ref[0]
+    me, z = place_ref[0], place_ref[1]
+
+    def put(d, c, value):
+        j = me ^ d
+        after = me ^ lax.rem(j + 1, 8)
+        mask = mask_ref[j, c].astype(jnp.bfloat16)
+        at = pl.multiple_of(d * frames + c * CHUNK, CHUNK)
+        left[0:feats, pl.ds(at, CHUNK)] = value
+        to = c + LAG // CHUNK
+        at = jnp.where(to < parts, d * frames + to * CHUNK, after * frames + (to - parts) * CHUNK)
+        left[feats : 2 * feats, pl.ds(pl.multiple_of(at, CHUNK), CHUNK)] = value * mask
 
     @pl.when(pl.program_id(0) == 0)
     def _():
-        for d, (operand, block) in enumerate(sources):
-            j = me ^ d
-            after = me ^ lax.rem(j + 1, 8)
-            mask = mask_ref[j].astype(jnp.bfloat16)
-            ref = rows_refs[operand]
+        for d, ref in zip(NEAR, near_refs):
             for c in range(parts):
-                inner = slice(c * CHUNK, (c + 1) * CHUNK)
-                value = ref[:, inner] if block is None else ref[c, block]
-                left[0:feats, d * frames + c * CHUNK : d * frames + (c + 1) * CHUNK] = value
-                to = c + LAG // CHUNK
-                start = (d if to < parts else after) * frames + (to % parts) * CHUNK
-                if to >= parts:
-                    start = pl.multiple_of(start, CHUNK)
-                left[feats : 2 * feats, pl.ds(start, CHUNK)] = value * mask[:, inner]
-
-    right = jnp.concatenate([ref[...] for ref in cols_refs], axis=1)
-    both = lax.dot_general(
-        left[...], right, (((1,), (1,)), ((), ())), preferred_element_type=jnp.float32
-    )
+                put(d, c, ref[:, c * CHUNK : (c + 1) * CHUNK])
+        for n, ref in enumerate(far_refs):
+            hop = (n + 1) // 2
+            c = z - hop if n % 2 else z + hop
+
+            @pl.when((c >= 0) & (c < parts))
+            def _():
+                for i, d in enumerate(FAR):
+                    put(d, c, ref[0, i])
+
+    right = jnp.concatenate([ref[...] for ref in cols_refs], axis=0)
+    both = jnp.dot(left[...], right, preferred_element_type=jnp.float32)
     same_ref[...] = both[0:feats] * factors_ref[0]
     cross_ref[...] = both[feats : 2 * feats] / factors_ref[1]
 
 
-def products(me, mask, factors, piece, pieces, near, gathered, cols, outs=(), block=512):
-    sources = ((0, None), (1, None), (2, None), (4, 0), (3, None), (4, 1), (4, 2), (4, 3))
-    feats, frames = cols[0].shape
-    row_feats = near[0].shape[0]
-    rows = row_feats // pieces
+def products(place, mask, factors, piece, pieces, near, far, cols, outs=(), block=256):
+    frames, feats = cols[0][0].shape
+    rows = near[0].shape[0]
+    row_feats = rows * pieces
     out = jax.ShapeDtypeStruct((row_feats, feats), jnp.float32)
     whole = lambda x: pl.BlockSpec(x.shape, lambda n, s: (0,) * x.ndim, pipeline_mode=pl.Buffered(1))
-    inputs = [mask, factors, *near, gathered, *cols, *outs]
+    part = lambda x: pl.BlockSpec(
+        (1,) + x.shape[1:],
+        lambda n, s: (piece if x.shape[0] == pieces else 0, 0, 0, 0),
+        pipeline_mode=pl.Buffered(1),
+    )
+    inputs = [mask, factors, *near, *far, *[x for x, _ in cols], *outs]
     return pl.pallas_call(
-        functools.partial(product_kernel, sources),
+        product_kernel,
         out_shape=[out, out],
         grid_spec=pltpu.PrefetchScalarGridSpec(
             num_scalar_prefetch=1,
             grid=(feats // block,),
             in_specs=[whole(mask), pl.BlockSpec(memory_space=pltpu.SMEM)]
-            + [pl.BlockSpec((rows, frames), lambda n, s: (piece, 0), pipeline_mode=pl.Buffered(1))] * 4
-            + [whole(gathered)]
-            + [pl.BlockSpec((block, frames), lambda n, s: (n, 0))] * 8
+            + [whole(x) for x in near]
+            + [part(x) for x in far]
+            + [pl.BlockSpec((frames, block), lambda n, s, i=i: (i, n)) for _, i in cols]
             + [pl.BlockSpec(memory_space=pl.ANY)] * len(outs),
             out_specs=[pl.BlockSpec((rows, block), lambda n, s: (piece, n))] * 2,
             scratch_shapes=[pltpu.VMEM((2 * rows, 8 * frames), jnp.bfloat16)],
         ),
         input_output_aliases={1 + len(inputs) - 2 + i: i for i in range(len(outs))},
         compiler_params=pltpu.CompilerParams(vmem_limit_bytes=VMEM_LIMIT),
-        cost_estimate=pl.CostEstimate(
-            flops=4 * rows * feats * 8 * frames,
-            bytes_accessed=16 * frames * (rows + feats) + 8 * rows * feats,
-            transcendentals=0,
-        ),
-    )(me, *inputs)
+        cost_estimate=estimate(24),
+    )(place, *inputs)
 
 
 def swap(x, bits):
@@ -284,25 +304,22 @@
 def corner(along_x, along_y, axis, half):
     low = swap(lax.slice_in_dim(along_x, 0, half, axis=axis), 4)
     high = swap(lax.slice_in_dim(along_y, half, along_y.shape[axis], axis=axis), 2)
-    return jnp.concatenate([low, high], axis=axis)
-
-
-def from_owner(x, feat_count, *after):
-    owner = lambda i: i * feat_count // 8
-    held = [jnp.where(lax.axis_index("feat") == owner(lax.axis_index("tm")), x, jnp.zeros_like(x))]
-    for s in range(1, feat_count):
-        perm = [
-            (i * feat_count + owner(i), i * feat_count + (owner(i) + s) % feat_count)
-            for i in range(8)
-        ]
-        held.append(lax.ppermute(x, ("tm", "feat"), perm))
-    if after:
-        held = tie(held, *after)
-    return sum(held[1:], held[0])
-
-
-def tie(x, *after):
-    return lax.optimization_barrier((x, after))[0]
+    return low, high
+
+
+def line_gather(x, count):
+    shift = lambda s: [(i, (i + s) % count) for i in range(count)]
+    return jnp.stack([x] + [lax.ppermute(x, "feat", shift(s)) for s in range(1, count)])
+
+
+def line_hop(up, down, hop, count):
+    up = lax.ppermute(up, "feat", [(i, i + 1) for i in range(hop - 1, count - 1)])
+    down = lax.ppermute(down, "feat", [(i + 1, i) for i in range(count - hop)])
+    return up, down
+
+
+def together(*values):
+    return lax.optimization_barrier(values)
 
 
 def shards(coords, frame_scale, pairs, walker_lengths):
@@ -313,10 +330,10 @@
     frames_all = frames_dev * tm_count
     row_feats = feats * feat_count // tm_count
     parts = frames_dev // CHUNK
-    pieces = 2
+    pieces = 1
     tm = lax.axis_index("tm").astype(jnp.int32)
     z = lax.axis_index("feat").astype(jnp.int32)
-    me = tm.reshape(1)
+    place = jnp.stack([tm, z])
     own_half = (tm % (feats // row_feats)) * row_feats
 
     coords_t = jnp.transpose(coords, (1, 2, 0))
@@ -325,63 +342,70 @@
     quarters = {3: swap(quarter, 3), 5: swap(quarter, 5)}
 
     raw, sums = contacts(pairs, [coords_t], scale_own)
+    raw, sums, quarters = together(raw, sums, quarters)
+    halves = corner(quarters[3], quarters[5], 1, (coords_t.shape[1] // 32) * 16)
     note = jnp.concatenate([sums, frame_scale.reshape(1, frames_dev)], axis=1)
     notes = [note] + [swap(note, d) for d in range(1, 8)]
-
-    quarters = tie(quarters, sums)
-    quarters[7] = corner(quarters[3], quarters[5], 1, (coords_t.shape[1] // 32) * 16)
-    chip_pairs = from_owner(pairs, feat_count, sums)
-    row_pairs = lax.dynamic_slice_in_dim(chip_pairs, own_half, row_feats, axis=1)
-    near_pairs = jnp.concatenate([swap(row_pairs, 2), swap(row_pairs, 4)], axis=1)
 
     totals = notes[0][:, :feats]
     for other in notes[1:]:
         totals = totals + other[:, :feats]
     mean = totals / jnp.float32(frames_all)
-    chip_mean = from_owner(mean, feat_count)
-    row_mean = lax.dynamic_slice_in_dim(chip_mean, own_half, row_feats, axis=1)
     scales = [lax.dynamic_slice_in_dim(n, feats + z * CHUNK, CHUNK, axis=1) for n in notes]
     scale_of = lambda *d: jnp.concatenate([scales[i] for i in d], axis=0)
 
+    facts = line_gather(jnp.concatenate([mean, pairs.astype(jnp.float32)], axis=0), feat_count)
+    mine, facts, halves = together(center(raw, mean), facts, halves)
+    quarters[7] = jnp.concatenate(halves, axis=1)
+    cols = {0: mine, 2: swap(mine, 2), 4: swap(mine, 4)}
+    quarters[6] = swap(quarters[7], 1)
+
+    def facts_of(i, start, count):
+        back = (z - i * feat_count // tm_count) % feat_count
+        return lax.dynamic_slice(facts, (back, 0, start), (1, 3, count))[0]
+
+    row_facts = facts_of(tm, own_half, row_feats)
+    out_facts = jnp.concatenate(
+        [facts_of(tm ^ 2, own_half, row_feats), facts_of(tm ^ 4, own_half, row_feats), facts_of(tm, 0, feats)],
+        axis=1,
+    )
+    row_facts, out_facts, scales = together(row_facts, out_facts, scales)
+    row_mean, row_pairs = row_facts[0:1], row_facts[1:3].astype(jnp.int32)
+    out_mean, out_pairs = out_facts[0:1], out_facts[1:3].astype(jnp.int32)
+
     sent_near = contacts(row_pairs, [quarters[3], quarters[5]], scale_of(3, 5), row_mean)
-    raw = tie(raw, sent_near, quarters[7])
-    mine = center(raw, mean)
-    quarters[6] = swap(quarters[7], 1)
-    cols = {0: mine, 1: swap(mine, 1), 2: swap(mine, 2), 4: swap(mine, 4)}
-
-    far = tie([quarters[6], quarters[7]], mine)
-    sent_far = contacts(row_pairs, far, scale_of(6, 7), row_mean)
-    joined = []
-    for p in range(pieces):
-        cut = slice(p * row_feats // pieces, (p + 1) * row_feats // pieces)
-        joined.append(jnp.concatenate([sent_near[:, cut], sent_far[:, cut]], axis=0))
-    gathered = [lax.all_gather(x, "feat", axis=0, tiled=False) for x in joined]
-
-    near_mean = jnp.concatenate([swap(row_mean, 2), swap(row_mean, 4)], axis=1)
-    out_pairs = jnp.concatenate([near_pairs, chip_pairs], axis=1)
-    out_mean = jnp.concatenate([near_mean, chip_mean], axis=1)
-    out_pairs = tie(out_pairs, *joined)
-    sent = contacts(out_pairs, [coords_t], scale_own, out_mean)
-    rows_cut = lambda start: lax.dynamic_slice_in_dim(sent, start, row_feats, axis=0)
-    own = rows_cut(2 * row_feats + own_half)
-    partner = swap(rows_cut(3 * row_feats - own_half), 1)
-
-    cols = tie(cols, sent)
-    cols[6] = corner(cols[2], cols[4], 0, feats // 2)
-    from_x = swap(rows_cut(0), 2)
-    from_y = swap(rows_cut(row_feats), 4)
-    for d in (2, 4, 6):
-        cols[d + 1] = swap(cols[d], 1)
-    cols = [cols[d] for d in range(8)]
+    sent_near, quarters, mine = together(sent_near, quarters, mine)
+    cols[1] = swap(mine, 1)
+    sent_far = contacts(row_pairs, [quarters[6], quarters[7]], scale_of(6, 7), row_mean)
 
     valid = walker_mask(walker_lengths, frames_all, frames_all)
-    mask = valid.astype(jnp.float32).reshape(tm_count, 1, frames_dev)
+    mask = valid.astype(jnp.float32).reshape(tm_count, parts, 1, CHUNK)
     npairs = jnp.sum(jnp.maximum(walker_lengths - LAG, 0)).astype(jnp.float32)
     factors = jnp.stack([jnp.float32(1.0 / frames_all), npairs])
-    outs = ()
-    for p in range(pieces):
-        outs = products(me, mask, factors, p, pieces, [own, partner, from_x, from_y], gathered[p], cols, outs)
-    return outs
+
+    rows = row_feats // pieces
+    joined = jnp.concatenate([sent_near, sent_far], axis=0).reshape(len(FAR), pieces, rows, CHUNK)
+    joined = jnp.transpose(joined, (1, 0, 2, 3))
+    out_pairs, mask, factors, joined = together(out_pairs, mask, factors, joined)
+    up, down = line_hop(joined, joined, 1, feat_count)
+    sent = contacts(out_pairs, [coords_t], scale_own, out_mean)
+    sent, up, down = together(sent, up, down)
+    far = [joined, up, down]
+    up, down = line_hop(up, down, 2, feat_count)
+    cut = lambda start: lax.dynamic_slice_in_dim(sent, start, row_feats, axis=0)
+    own = cut(2 * row_feats + own_half)
+    partner = swap(cut(3 * row_feats - own_half), 1)
+    cols, sent = together(cols, sent)
+    low, high = corner(cols[2], cols[4], 0, frames_dev // 2)
+    low, high, up, down, sent = together(low, high, up, down, sent)
+    far_cols = jnp.concatenate([cols[2], cols[4], low, high], axis=0)
+    their_cols = swap(far_cols, 1)
+    far += [up, down, *line_hop(up, down, 3, feat_count)]
+    near = [own, partner, swap(cut(0), 2), swap(cut(row_feats), 4)]
+    cols = [(cols[0], 0), (cols[1], 0)]
+    for i in range(3):
+        cols += [(far_cols, i), (their_cols, i)]
+    return products(place, mask, factors, 0, pieces, near, far, cols)
 
 
 def solution(mesh):

time: 281 us -> 237 us (0.84)
  waiting for transfers between devices: 80 us -> 53.9 us
  between operations: 15.1 us -> 1.88 us
  local copies, waits for them, and re-layouts: 21.3 us -> 16.9 us
    ppermute x27 -> x21, waiting for transfers between devices: 79.9 us -> 14.5 us  [swap(): return lax.ppermute(x, 'tm', [(i, i ^ bits) for i in range(8)])]
    ppermute x6 -> x9, waiting for transfers between devices: 0.02 us -> 39.4 us  [the longest x3 39.4 us: line_hop(): down = lax.ppermute(down, 'feat', [(i + 1, i) for i in range(count - hop)])]
    unnamed x28 -> x38, local copies, waits for them, and re-layouts: 4.97 us -> 7.02 us
    ppermute x27 -> x21, starting transfers between devices: 21.8 us -> 20 us  [swap(): return lax.ppermute(x, 'tm', [(i, i ^ bits) for i in range(8)])]
    pallas_call x3 -> x2, Pallas kernels: 55.9 us -> 54.3 us  [the longest x1 49.4 us: products(): pl.pallas_call(product_kernel, out_shape=[out, out], grid_spec=pltpu.Pref...]
    ppermute x6 -> x9, starting transfers between devices: 16.1 us -> 16.8 us  [the longest x3 6.48 us: line_gather(): lax.ppermute(x, 'feat', shift(s))]
  transfers between devices with their start and end apart: 35 -> 30, of which waited for: 7 -> 8; matrix products, arithmetic and copies ran while one was open for 10% -> 10% of each run, Pallas kernels for 32% -> 27%
where the time goes in v4:
time: 237 us; the launch traced here: 235 us
  Pallas kernels  113 us (48%)
  waiting for transfers between devices  53.9 us (23%)
  starting transfers between devices  36.8 us (16%)
  local copies, waits for them, and re-layouts  16.9 us (7%)
  other arithmetic  12.1 us (5%)
    pallas_call x4, Pallas kernels, contacts(): pl.pallas_call(functools.partial(gather_kernel, centered, len(coords)), o...  58.8 us
    pallas_call x1, Pallas kernels, products(): pl.pallas_call(product_kernel, out_shape=[out, out], grid_spec=pltpu.Pref...  49.4 us
    ppermute x3, waiting for transfers between devices, line_hop(): down = lax.ppermute(down, 'feat', [(i + 1, i) for i in range(count - hop)])  39.4 us
    ppermute x21, starting transfers between devices, swap(): return lax.ppermute(x, 'tm', [(i, i ^ bits) for i in range(8)])  20 us
    ppermute x21, waiting for transfers between devices, swap(): return lax.ppermute(x, 'tm', [(i, i ^ bits) for i in range(8)])  14.5 us
    unnamed x38, local copies, waits for them, and re-layouts  7.02 us
    ppermute x3, starting transfers between devices, line_gather(): lax.ppermute(x, 'feat', shift(s))  6.48 us
    ppermute x3, starting transfers between devices, line_hop(): lax.ppermute(up, 'feat', [(i, i + 1) for i in range(hop - 1, count - 1)])  6.24 us
  transfers between devices with their start and end apart: 30, of which 8 were waited for; matrix products, arithmetic and copies ran while one was open for 10% of the time, Pallas kernels for 27%

profile of v4, /device:TPU:0, one launch (start us, length us, event | category | flops | bytes accessed | tf_op | source)
XLA Modules:
  0.0 234.8 jit_solution(442071628831321647)
XLA Ops:
  0.6 1.8 fusion
  2.4 2.5 %collective-permute-start.1 = (s16[3,1500,128]{2,1,0:T(8,128)(2,1)S(1)}, s16[3,1500,128]{2,1,0:T(8,128)(2,1)S(1)}, u32[]{:S(2)}, u32[]{:S(2)}) collective-permute-start(s16[3,1500,128]{2,1,0:T(8,128)(2,1)S(1)} %fusion), channel_id=1, source_target_pairs={{0,20},{4,16},{8,28},{12,24},{16,4},{20,0},{24,12},{28,8},{1,21},{... | collective-permute-start | bytes 3456008 | tf_op jit(solution)/shard_map/ppermute | solution.py:301
  4.9 1.8 collective-permute-start
  10.4 17.0 %shard_map.59 = (f32[2048,512]{1,0:T(8,128)}, f32[1,2048]{1,0:T(1,128)}) custom-call(s32[2,2048]{1,0:T(2,128)} %get-tuple-element.88.pairs_ref, f32[8,128]{1,0:T(8,128)} %pad_maximum_fusion.4.scale_ref, s32[3,1500,512]{2,1,0:T(8,128)} %bitcast.26), custom_call_target="tpu_custom_call" | custom-call | flops 1000000000 | bytes 3690000 | tf_op jit(solution)/shard_map/pallas_call | solution.py:188
  28.1 2.7 %collective-permute-done.1.rest_1_ = s16[3,1500,128]{2,1,0:T(8,128)(2,1)S(1)} collective-permute-done((s16[3,1500,128]{2,1,0:T(8,128)(2,1)S(1)}, s16[3,1500,128]{2,1,0:T(8,128)(2,1)S(1)}, u32[]{:S(2)}, u32[]{:S(2)}) %collective-permute-start.1) | collective-permute-done | bytes 1152032 | tf_op jit(solution)/shard_map/ppermute | solution.py:301
  32.7 2.0 collective-permute-start.8
  38.5 1.7 collective-permute-start.4
  45.8 2.7 %collective-permute-start.10 = (f32[3,2048]{1,0:T(4,128)S(1)}, f32[3,2048]{1,0:T(4,128)S(1)}, u32[]{:S(2)}, u32[]{:S(2)}) collective-permute-start(f32[3,2048]{1,0:T(4,128)S(1)} %get-tuple-element.86), channel_id=1, source_target_pairs={{0,2},{1,3},{2,0},{3,1},{4,6},{5,7},{6,4},{7,5},{8,10},{9,11},{10,... | collective-permute-start | bytes 73736 | tf_op jit(solution)/shard_map/ppermute | solution.py:312
  48.4 1.6 collective-permute-start.9
  50.0 2.2 collective-permute-start.11
  52.3 4.9 %shard_map.60.rest_11_ = bf16[512,2048]{1,0:T(8,128)(2,1)} custom-call(f32[2048,512]{1,0:T(8,128)} %get-tuple-element.41.raw_ref, f32[1,2048]{1,0:T(1,128)} %copy-done.4), custom_call_target="tpu_custom_call" | custom-call | flops 1000000000 | bytes 3690000 | tf_op jit(solution)/shard_map/pallas_call | solution.py:214
  64.3 8.2 %shard_map.61 = bf16[2,1024,128]{2,1,0:T(8,128)(2,1)} custom-call(s32[2,1024]{1,0:T(2,128)} %convert_multiply_fusion.pairs_ref, f32[8,128]{1,0:T(8,128)} %concatenate.36.scale_ref, s16[3,1500,128]{2,1,0:T(8,128)(2,1)} %collective-permute-done.rest_0_, s16[3,1500,128]{2,1,0:T(8,128)(2,1)} %copy-done.2, f32[1,1024]{1,0:T(1,128)} %slice.56.rest_2_), custom_call_target="tpu_custom_call" | custom-call | flops 1000000000 | bytes 3690000 | tf_op jit(solution)/shard_map/pallas_call | solution.py:188
  72.7 8.1 %shard_map.62 = bf16[2,1024,128]{2,1,0:T(8,128)(2,1)} custom-call(s32[2,1024]{1,0:T(2,128)} %convert_multiply_fusion.pairs_ref, f32[8,128]{1,0:T(8,128)} %concatenate.38.scale_ref, s16[3,1500,128]{2,1,0:T(8,128)(2,1)} %collective-permute-done.14.rest_0_, s16[3,1500,128]{2,1,0:T(8,128)(2,1)} %copy-done.3, f32[1,1024]{1,0:T(1,128)} %slice.56.rest_2_), custom_call_target="tpu_custom_call" | custom-call | flops 1000000000 | bytes 3690000 | tf_op jit(solution)/shard_map/pallas_call | solution.py:188
  83.4 4.8 %collective-permute-start.15 = (bf16[1,4,1024,128]{3,2,1,0:T(8,128)(2,1)S(1)}, bf16[1,4,1024,128]{3,2,1,0:T(8,128)(2,1)S(1)}, u32[]{:S(2)}, u32[]{:S(2)}) collective-permute-start(bf16[1,4,1024,128]{3,2,1,0:T(8,128)(2,1)S(1)} %maximum_bitcast_fusion.rest_4_), channel_id=1, source_target_pairs={{0,1},{1,2},{2,3},{4,5},{5,6},{6,7},{8,9},{9,10},{10,11},{12,13},{... | collective-permute-start | bytes 3145736 | tf_op jit(solution)/shard_map/ppermute | solution.py:316
  89.4 25.5 %shard_map.63 = bf16[4096,512]{1,0:T(8,128)(2,1)} custom-call(s32[2,4096]{1,0:T(2,128)} %broadcast_multiply_fusion.pairs_ref, f32[8,128]{1,0:T(8,128)} %pad_maximum_fusion.4.scale_ref, s32[3,1500,512]{2,1,0:T(8,128)} %bitcast.27, f32[1,4096]{1,0:T(1,128)} %slice.57.rest_1_), custom_call_target="tpu_custom_call" | custom-call | flops 1000000000 | bytes 3690000 | tf_op jit(solution)/shard_map/pallas_call | solution.py:188
  117.1 2.1 slice.58
  120.7 3.2 %constant_dynamic-update-slice_fusion.5 = bf16[1536,2048]{1,0:T(8,128)(2,1)} fusion(bf16[512,2048]{1,0:T(8,128)(2,1)} %collective-permute-done.19), kind=kLoop, calls=%fused_computation.23 | loop fusion | bytes 4194304
  125.5 19.5 %collective-permute-done.24.rest_8_ = bf16[1,4,1024,128]{3,2,1,0:T(8,128)(2,1)S(1)} collective-permute-done((bf16[1,4,1024,128]{3,2,1,0:T(8,128)(2,1)S(1)}, bf16[1,4,1024,128]{3,2,1,0:T(8,128)(2,1)S(1)}, u32[]{:S(2)}, u32[]{:S(2)}) %collective-permute-start.24) | collective-permute-done | bytes 1048608 | tf_op jit(solution)/shard_map/ppermute | solution.py:317
  147.3 2.8 %constant_dynamic-slice_fusion = (bf16[1024,512]{1,0:T(8,128)(2,1)S(1)}, bf16[1024,512]{1,0:T(8,128)(2,1)}) fusion(bf16[4096,512]{1,0:T(8,128)(2,1)} %shard_map.63, s32[]{:T(128)S(6)} %select_n.80, s32[]{:T(128)S(6)} %select_n.79), kind=kLoop, calls=%fused_computation.36 | loop fusion | bytes 4194312 | tf_op jit(solution)/shard_map/dynamic_slice | solution.py:395
  151.3 1.5 collective-permute-start.28
  153.8 5.1 %collective-permute-done.17.rest_1_ = bf16[1024,512]{1,0:T(8,128)(2,1)S(1)} collective-permute-done((bf16[1024,512]{1,0:T(8,128)(2,1)S(1)}, bf16[1024,512]{1,0:T(8,128)(2,1)S(1)}, u32[]{:S(2)}, u32[]{:S(2)}) %collective-permute-start.17) | collective-permute-done | bytes 1048608 | tf_op jit(solution)/shard_map/ppermute | solution.py:301
  160.5 19.8 %collective-permute-done.28.rest_10_ = bf16[1,4,1024,128]{3,2,1,0:T(8,128)(2,1)S(1)} collective-permute-done((bf16[1,4,1024,128]{3,2,1,0:T(8,128)(2,1)}, bf16[1,4,1024,128]{3,2,1,0:T(8,128)(2,1)S(1)}, u32[]{:S(2)}, u32[]{:S(2)}) %collective-permute-start.28) | collective-permute-done | bytes 1048608 | tf_op jit(solution)/shard_map/ppermute | solution.py:317
  180.3 3.8 %collective-permute-done.25.rest_2_ = bf16[1024,512]{1,0:T(8,128)(2,1)S(1)} collective-permute-done((bf16[1024,512]{1,0:T(8,128)(2,1)S(1)}, bf16[1024,512]{1,0:T(8,128)(2,1)S(1)}, u32[]{:S(2)}, u32[]{:S(2)}) %collective-permute-start.25) | collective-permute-done | bytes 1048608 | tf_op jit(solution)/shard_map/ppermute | solution.py:301
  185.2 49.4 %shard_map.64 = (f32[1024,2048]{1,0:T(8,128)}, f32[1024,2048]{1,0:T(8,128)}) custom-call(s32[2]{0:T(128)} %pad_add_fusion.place_ref, f32[8,4,1,128]{3,2,1,0:T(1,128)} %fusion.1.mask_ref, f32[2]{0:T(128)} %pad_maximum_fusion.5.factors_ref, bf16[1024,512]{1,0:T(8,128)(2,1)} %get-tuple-element.81.rest_0_, bf16[1024,512]{1,0:T(8,128)(2,1)} %copy-done.11, ...), custom_call_target="tpu_custom_call" | custom-call | flops 24000000000 | bytes 88560000 | tf_op jit(solution)/shard_map/pallas_call | solution.py:280
  (118 shorter events, 38.3 us)
Async XLA Ops:
  2.4 28.3 %collective-permute-start.1 = (s16[3,1500,128]{2,1,0:T(8,128)(2,1)S(1)}, s16[3,1500,128]{2,1,0:T(8,128)(2,1)S(1)}, u32[]{:S(2)}, u32[]{:S(2)}) collective-permute-start(s16[3,1500,128]{2,1,0:T(8,128)(2,1)S(1)} %fusion), channel_id=1, source_target_pairs={{0,20},{4,16},{8,28},{12,24},{16,4},{20,0},{24,12},{28,8},{1,21},{... | collective-permute-start | bytes 3456008 | tf_op jit(solution)/shard_map/ppermute | solution.py:301
  4.9 27.1 %collective-permute-start = (s16[3,1500,128]{2,1,0:T(8,128)(2,1)S(1)}, s16[3,1500,128]{2,1,0:T(8,128)(2,1)}, u32[]{:S(2)}, u32[]{:S(2)}) collective-permute-start(s16[3,1500,128]{2,1,0:T(8,128)(2,1)S(1)} %fusion), channel_id=1, source_target_pairs={{0,12},{4,8},{8,4},{12,0},{16,28},{20,24},{24,20},{28,16},{1,13},{... | collective-permute-start | bytes 3456008 | tf_op jit(solution)/shard_map/ppermute | solution.py:301
  32.7 7.5 %collective-permute-start.8 = (f32[1,2560]{1,0:T(1,128)S(1)}, f32[1,2560]{1,0:T(1,128)S(1)}, u32[]{:S(2)}, u32[]{:S(2)}) collective-permute-start(f32[1,2560]{1,0:T(1,128)S(1)} %pad_maximum_fusion.3), channel_id=1, source_target_pairs={{0,28},{4,24},{8,20},{12,16},{16,12},{20,8},{24,4},{28,0},{1,29},{... | collective-permute-start | bytes 30728 | tf_op jit(solution)/shard_map/ppermute | solution.py:301
  42.5 15.3 %collective-permute-start.12 = (s16[3,736,128]{2,1,0:T(8,128)(2,1)S(1)}, s16[3,736,128]{2,1,0:T(8,128)(2,1)S(1)}, u32[]{:S(2)}, u32[]{:S(2)}) collective-permute-start(s16[3,736,128]{2,1,0:T(8,128)(2,1)S(1)} %slice.52), channel_id=1, source_target_pairs={{0,16},{4,20},{8,24},{12,28},{16,0},{20,4},{24,8},{28,12},{1,17},{... | collective-permute-start | bytes 1695752 | tf_op jit(solution)/shard_map/ppermute | solution.py:301
  43.6 15.3 %collective-permute-start.13 = (s16[3,764,128]{2,1,0:T(8,128)(2,1)S(1)}, s16[3,764,128]{2,1,0:T(8,128)(2,1)S(1)}, u32[]{:S(2)}, u32[]{:S(2)}) collective-permute-start(s16[3,764,128]{2,1,0:T(8,128)(2,1)S(1)} %slice.53), channel_id=1, source_target_pairs={{0,8},{4,12},{8,0},{12,4},{16,24},{20,28},{24,16},{28,20},{1,9},{5... | collective-permute-start | bytes 1760264 | tf_op jit(solution)/shard_map/ppermute | solution.py:301
  45.8 11.4 %collective-permute-start.10 = (f32[3,2048]{1,0:T(4,128)S(1)}, f32[3,2048]{1,0:T(4,128)S(1)}, u32[]{:S(2)}, u32[]{:S(2)}) collective-permute-start(f32[3,2048]{1,0:T(4,128)S(1)} %get-tuple-element.86), channel_id=1, source_target_pairs={{0,2},{1,3},{2,0},{3,1},{4,6},{5,7},{6,4},{7,5},{8,10},{9,11},{10,... | collective-permute-start | bytes 73736 | tf_op jit(solution)/shard_map/ppermute | solution.py:312
  48.4 8.7 %collective-permute-start.9 = (f32[3,2048]{1,0:T(4,128)S(1)}, f32[3,2048]{1,0:T(4,128)S(1)}, u32[]{:S(2)}, u32[]{:S(2)}) collective-permute-start(f32[3,2048]{1,0:T(4,128)S(1)} %get-tuple-element.86), channel_id=1, source_target_pairs={{0,1},{1,2},{2,3},{3,0},{4,5},{5,6},{6,7},{7,4},{8,9},{9,10},{10,1... | collective-permute-start | bytes 73736 | tf_op jit(solution)/shard_map/ppermute | solution.py:312
  50.0 7.2 %collective-permute-start.11 = (f32[3,2048]{1,0:T(4,128)S(1)}, f32[3,2048]{1,0:T(4,128)S(1)}, u32[]{:S(2)}, u32[]{:S(2)}) collective-permute-start(f32[3,2048]{1,0:T(4,128)S(1)} %get-tuple-element.86), channel_id=1, source_target_pairs={{0,3},{1,0},{2,1},{3,2},{4,7},{5,4},{6,5},{7,6},{8,11},{9,8},{10,9... | collective-permute-start | bytes 73736 | tf_op jit(solution)/shard_map/ppermute | solution.py:312
  59.1 13.4 %collective-permute-start.14 = (s16[3,1500,128]{2,1,0:T(8,128)(2,1)S(1)}, s16[3,1500,128]{2,1,0:T(8,128)(2,1)}, u32[]{:S(2)}, u32[]{:S(2)}) collective-permute-start(s16[3,1500,128]{2,1,0:T(8,128)(2,1)S(1)} %constant_dynamic-update-slice_fusion.rest_1_), channel_id=1, source_target_pairs={{0,4},{4,0},{8,12},{12,8},{16,20},{20,16},{24,28},{28,24},{1,5},{5... | collective-permute-start | bytes 3456008 | tf_op jit(solution)/shard_map/ppermute | solution.py:301
  59.2 57.9 %collective-permute-start.20 = (bf16[512,2048]{1,0:T(8,128)(2,1)}, bf16[512,2048]{1,0:T(8,128)(2,1)S(1)}, u32[]{:S(2)}, u32[]{:S(2)}) collective-permute-start(bf16[512,2048]{1,0:T(8,128)(2,1)} %shard_map.60.rest_11_), channel_id=1, source_target_pairs={{0,16},{4,20},{8,24},{12,28},{16,0},{20,4},{24,8},{28,12},{1,17},{... | collective-permute-start | bytes 6291464 | tf_op jit(solution)/shard_map/ppermute | solution.py:301
  60.4 56.7 %collective-permute-start.19 = (bf16[512,2048]{1,0:T(8,128)(2,1)}, bf16[512,2048]{1,0:T(8,128)(2,1)}, u32[]{:S(2)}, u32[]{:S(2)}) collective-permute-start(bf16[512,2048]{1,0:T(8,128)(2,1)} %shard_map.60.rest_11_), channel_id=1, source_target_pairs={{0,8},{4,12},{8,0},{12,4},{16,24},{20,28},{24,16},{28,20},{1,9},{5... | collective-permute-start | bytes 6291464 | tf_op jit(solution)/shard_map/ppermute | solution.py:301
  72.5 44.5 %collective-permute-start.18 = (bf16[512,2048]{1,0:T(8,128)(2,1)}, bf16[512,2048]{1,0:T(8,128)(2,1)S(1)}, u32[]{:S(2)}, u32[]{:S(2)}) collective-permute-start(bf16[512,2048]{1,0:T(8,128)(2,1)} %shard_map.60.rest_11_), channel_id=1, source_target_pairs={{0,4},{4,0},{8,12},{12,8},{16,20},{20,16},{24,28},{28,24},{1,5},{5... | collective-permute-start | bytes 6291464 | tf_op jit(solution)/shard_map/ppermute | solution.py:301
  82.1 32.9 %collective-permute-start.16 = (bf16[1,4,1024,128]{3,2,1,0:T(8,128)(2,1)S(1)}, bf16[1,4,1024,128]{3,2,1,0:T(8,128)(2,1)S(1)}, u32[]{:S(2)}, u32[]{:S(2)}) collective-permute-start(bf16[1,4,1024,128]{3,2,1,0:T(8,128)(2,1)S(1)} %maximum_bitcast_fusion.rest_4_), channel_id=1, source_target_pairs={{1,0},{2,1},{3,2},{5,4},{6,5},{7,6},{9,8},{10,9},{11,10},{13,12},{... | collective-permute-start | bytes 3145736 | tf_op jit(solution)/shard_map/ppermute | solution.py:317
  83.4 31.6 %collective-permute-start.15 = (bf16[1,4,1024,128]{3,2,1,0:T(8,128)(2,1)S(1)}, bf16[1,4,1024,128]{3,2,1,0:T(8,128)(2,1)S(1)}, u32[]{:S(2)}, u32[]{:S(2)}) collective-permute-start(bf16[1,4,1024,128]{3,2,1,0:T(8,128)(2,1)S(1)} %maximum_bitcast_fusion.rest_4_), channel_id=1, source_target_pairs={{0,1},{1,2},{2,3},{4,5},{5,6},{6,7},{8,9},{9,10},{10,11},{12,13},{... | collective-permute-start | bytes 3145736 | tf_op jit(solution)/shard_map/ppermute | solution.py:316
  115.0 10.5 %collective-permute-start.23 = (bf16[1,4,1024,128]{3,2,1,0:T(8,128)(2,1)S(1)}, bf16[1,4,1024,128]{3,2,1,0:T(8,128)(2,1)S(1)}, u32[]{:S(2)}, u32[]{:S(2)}) collective-permute-start(bf16[1,4,1024,128]{3,2,1,0:T(8,128)(2,1)S(1)} %collective-permute-done.15.rest_5_), channel_id=1, source_target_pairs={{1,2},{2,3},{5,6},{6,7},{9,10},{10,11},{13,14},{14,15},{17,18},{18... | collective-permute-start | bytes 3145736 | tf_op jit(solution)/shard_map/ppermute | solution.py:316
  115.7 29.3 %collective-permute-start.24 = (bf16[1,4,1024,128]{3,2,1,0:T(8,128)(2,1)S(1)}, bf16[1,4,1024,128]{3,2,1,0:T(8,128)(2,1)S(1)}, u32[]{:S(2)}, u32[]{:S(2)}) collective-permute-start(bf16[1,4,1024,128]{3,2,1,0:T(8,128)(2,1)S(1)} %collective-permute-done.16.rest_6_), channel_id=1, source_target_pairs={{1,0},{2,1},{5,4},{6,5},{9,8},{10,9},{13,12},{14,13},{17,16},{18,1... | collective-permute-start | bytes 3145736 | tf_op jit(solution)/shard_map/ppermute | solution.py:317
  119.2 25.8 %collective-permute-start.22 = (bf16[256,2048]{1,0:T(8,128)(2,1)S(1)}, bf16[256,2048]{1,0:T(8,128)(2,1)S(1)}, u32[]{:S(2)}, u32[]{:S(2)}) collective-permute-start(bf16[256,2048]{1,0:T(8,128)(2,1)S(1)} %slice.59), channel_id=1, source_target_pairs={{0,8},{4,12},{8,0},{12,4},{16,24},{20,28},{24,16},{28,20},{1,9},{5... | collective-permute-start | bytes 3145736 | tf_op jit(solution)/shard_map/ppermute | solution.py:301
  119.8 25.2 %collective-permute-start.21 = (bf16[256,2048]{1,0:T(8,128)(2,1)S(1)}, bf16[256,2048]{1,0:T(8,128)(2,1)S(1)}, u32[]{:S(2)}, u32[]{:S(2)}) collective-permute-start(bf16[256,2048]{1,0:T(8,128)(2,1)S(1)} %slice.58), channel_id=1, source_target_pairs={{0,16},{4,20},{8,24},{12,28},{16,0},{20,4},{24,8},{28,12},{1,17},{... | collective-permute-start | bytes 3145736 | tf_op jit(solution)/shard_map/ppermute | solution.py:301
  147.2 36.9 %collective-permute-start.29 = (bf16[1536,2048]{1,0:T(8,128)(2,1)}, bf16[1536,2048]{1,0:T(8,128)(2,1)}, u32[]{:S(2)}, u32[]{:S(2)}) collective-permute-start(bf16[1536,2048]{1,0:T(8,128)(2,1)} %constant_dynamic-update-slice_fusion.2.rest_13_.rest_15_.rest_17_), channel_id=1, source_target_pairs={{0,4},{4,0},{8,12},{12,8},{16,20},{20,16},{24,28},{28,24},{1,5},{5... | collective-permute-start | bytes 18874376 | tf_op jit(solution)/shard_map/ppermute | solution.py:301
  150.1 8.8 %collective-permute-start.17 = (bf16[1024,512]{1,0:T(8,128)(2,1)S(1)}, bf16[1024,512]{1,0:T(8,128)(2,1)S(1)}, u32[]{:S(2)}, u32[]{:S(2)}) collective-permute-start(bf16[1024,512]{1,0:T(8,128)(2,1)S(1)} %get-tuple-element.80), channel_id=1, source_target_pairs={{0,4},{4,0},{8,12},{12,8},{16,20},{20,16},{24,28},{28,24},{1,5},{5... | collective-permute-start | bytes 3145736 | tf_op jit(solution)/shard_map/ppermute | solution.py:301
  150.6 9.9 %collective-permute-start.27 = (bf16[1,4,1024,128]{3,2,1,0:T(8,128)(2,1)}, bf16[1,4,1024,128]{3,2,1,0:T(8,128)(2,1)S(1)}, u32[]{:S(2)}, u32[]{:S(2)}) collective-permute-start(bf16[1,4,1024,128]{3,2,1,0:T(8,128)(2,1)} %copy-done.9), channel_id=1, source_target_pairs={{2,3},{6,7},{10,11},{14,15},{18,19},{22,23},{26,27},{30,31}} | collective-permute-start | bytes 3145736 | tf_op jit(solution)/shard_map/ppermute | solution.py:316
  151.3 29.0 %collective-permute-start.28 = (bf16[1,4,1024,128]{3,2,1,0:T(8,128)(2,1)}, bf16[1,4,1024,128]{3,2,1,0:T(8,128)(2,1)S(1)}, u32[]{:S(2)}, u32[]{:S(2)}) collective-permute-start(bf16[1,4,1024,128]{3,2,1,0:T(8,128)(2,1)} %copy-done.10), channel_id=1, source_target_pairs={{1,0},{5,4},{9,8},{13,12},{17,16},{21,20},{25,24},{29,28}} | collective-permute-start | bytes 3145736 | tf_op jit(solution)/shard_map/ppermute | solution.py:317
  153.0 27.3 %collective-permute-start.26 = (bf16[1024,512]{1,0:T(8,128)(2,1)S(1)}, bf16[1024,512]{1,0:T(8,128)(2,1)S(1)}, u32[]{:S(2)}, u32[]{:S(2)}) collective-permute-start(bf16[1024,512]{1,0:T(8,128)(2,1)S(1)} %get-tuple-element.78), channel_id=1, source_target_pairs={{0,16},{4,20},{8,24},{12,28},{16,0},{20,4},{24,8},{28,12},{1,17},{... | collective-permute-start | bytes 3145736 | tf_op jit(solution)/shard_map/ppermute | solution.py:301
  158.9 25.2 %collective-permute-start.25 = (bf16[1024,512]{1,0:T(8,128)(2,1)S(1)}, bf16[1024,512]{1,0:T(8,128)(2,1)S(1)}, u32[]{:S(2)}, u32[]{:S(2)}) collective-permute-start(bf16[1024,512]{1,0:T(8,128)(2,1)S(1)} %get-tuple-element.79), channel_id=1, source_target_pairs={{0,8},{4,12},{8,0},{12,4},{16,24},{20,28},{24,16},{28,20},{1,9},{5... | collective-permute-start | bytes 3145736 | tf_op jit(solution)/shard_map/ppermute | solution.py:301
  (23 other events, 271.1 us)

commit v5 on v4

--- a/solution.py
+++ b/solution.py
@@ -83,121 +83,135 @@
     return jnp.broadcast_to(row, (CHUNK, row.shape[1])).T
 
 
-def gather_kernel(centered, coords_count, pairs_ref, scale_ref, *rest):
-    coords_refs, rest = rest[:coords_count], rest[coords_count:]
-    if centered:
+def gather_kernel(form, chunks, count, pairs_ref, scale_ref, *rest):
+    sources, rest = rest[:count], rest[count:]
+    if form == "first":
+        out_ref, sums_ref, table_out, table, dense, part, held, arrived, left = rest
+    elif form == "own":
+        mean_ref, out_ref, table, dense, part, arrived = rest
+    else:
         mean_ref, out_ref, table, dense, part, held, arrived = rest
-    else:
-        out_ref, sums_ref, table, dense, part, held, arrived = rest
-    residues = coords_refs[0].shape[1]
-    chunks = 4 if coords_count == 1 else coords_count
-    stride = table.shape[0] // residues
     block = part.shape[0]
+    stride = -(-3 * chunks // 8) * 8
+    residues = table.shape[0] // stride
     group = dense.shape[0] // chunks
     step = pl.program_id(0)
 
     @pl.when(step == 0)
     def _():
+        if form == "own":
+            copy = pltpu.make_async_copy(sources[0], table, arrived)
+            copy.start()
+            copy.wait()
+            return
         copies = [
             pltpu.make_async_copy(ref.at[k], held.at[n, k], arrived.at[n, k])
             for k in range(3)
-            for n, ref in enumerate(coords_refs)
+            for n, ref in enumerate(sources)
         ]
         for copy in copies:
             copy.start()
         for k in range(3):
-            for n in range(coords_count):
-                copies[k * coords_count + n].wait()
+            for n in range(count):
+                copies[k * count + n].wait()
             for c in range(chunks):
-                if coords_count == 1:
+                if form == "first":
                     plane = held[0, k, :, c * CHUNK : (c + 1) * CHUNK]
                 else:
                     plane = held[c, k].astype(jnp.int32)
                 table[pl.ds(k * chunks + c, residues, stride=stride), :] = plane
-
-    if centered:
+        if form == "first":
+            pltpu.make_async_copy(table, table_out, left).start()
+
+    if form != "first":
         part[...] = as_column(mean_ref[...])
     sublane = lax.broadcasted_iota(jnp.int32, (8, CHUNK), 0)
-    scale = scale_ref[...]
+    scale = jnp.concatenate([scale_ref[...]] * (8 // chunks), axis=0)
 
     def squares(f):
         first = pl.multiple_of(pairs_ref[0, f], 8)
         second = pl.multiple_of(pairs_ref[1, f], 8)
         diff = (table[pl.ds(first, stride), :] - table[pl.ds(second, stride), :]).astype(jnp.float32)
         diff = diff * diff
-        if chunks == 4:
-            total = diff[0:8] + jnp.where(sublane < 4, diff[8:16], 0.0)
-            return total + pltpu.roll(total, 4, 0)
-        diff = jnp.where(sublane < 6, diff, 0.0)
-        total = diff + pltpu.roll(diff, 4, 0)
-        return total + pltpu.roll(total, 2, 0)
+        total = diff[0:8] + jnp.where(sublane < 4, diff[8:16], 0.0)
+        return total + pltpu.roll(total, 4, 0)
 
     @pl.loop(0, block // group)
     def _(g):
         at = pl.multiple_of(g * group, group)
-        packed = 8 // chunks
-        for f in range(0, group, packed):
+        for f in range(0, group, 2):
             base = step * block + at + f
-            value = squares(base)
-            for i in range(1, packed):
-                value = jnp.where(sublane < i * chunks, value, squares(base + i))
+            value = jnp.where(sublane < 4, squares(base), squares(base + 1))
             dense[pl.ds(f * chunks, 8), :] = switch(value, scale)
         for h in range(group // 16):
             here = pl.ds(pl.multiple_of(at + h * 16, 16), 16)
             total = jnp.zeros((16, CHUNK), jnp.float32)
             for c in range(chunks):
                 contact = dense[pl.ds(h * 16 * chunks + c, 16, stride=chunks), :]
-                if not centered:
-                    out_ref[here, c * CHUNK : (c + 1) * CHUNK] = contact
+                lanes = slice(c * CHUNK, (c + 1) * CHUNK)
+                if form == "first":
+                    out_ref[here, lanes] = contact
                     total = total + contact
-                elif coords_count == 1:
-                    out_ref[here, c * CHUNK : (c + 1) * CHUNK] = (contact - part[here, :]).astype(
-                        jnp.bfloat16
-                    )
+                elif form == "own":
+                    out_ref[here, lanes] = (contact - part[here, :]).astype(jnp.bfloat16)
                 else:
                     out_ref[c, here, :] = (contact - part[here, :]).astype(jnp.bfloat16)
-            if not centered:
+            if form == "first":
                 part[here, :] = total
 
-    if not centered:
+    if form == "first":
         sums_ref[...] = jnp.sum(part[...].T, axis=0, keepdims=True)
 
-
-def contacts(pairs, coords, scale, mean=None, block=512, group=32):
-    residues = coords[0].shape[1]
+        @pl.when(step == pl.num_programs(0) - 1)
+        def _():
+            pltpu.make_async_copy(table, table_out, left).wait()
+
+
+def contacts(form, pairs, sources, scale, mean=None, block=512, group=32):
     feats = pairs.shape[1]
     chunks = scale.shape[0]
     stride = -(-3 * chunks // 8) * 8
-    centered = mean is not None
+    rows = sources[0].shape[0] if form == "own" else sources[0].shape[1] * stride
     row_spec = pl.BlockSpec((1, block), lambda n: (0, n))
-    in_specs = [pl.BlockSpec(memory_space=pltpu.SMEM), pl.BlockSpec((8, CHUNK), lambda n: (0, 0))]
-    in_specs += [pl.BlockSpec(memory_space=pl.ANY) for x in coords]
-    args = [pairs * stride, jnp.concatenate([scale] * (8 // chunks), axis=0), *coords]
-    if len(coords) == 1:
-        out_shape = jax.ShapeDtypeStruct((feats, chunks * CHUNK), jnp.bfloat16 if centered else jnp.float32)
-        out_specs = pl.BlockSpec((block, chunks * CHUNK), lambda n: (n, 0))
-    else:
+    any_spec = pl.BlockSpec(memory_space=pl.ANY)
+    in_specs = [pl.BlockSpec(memory_space=pltpu.SMEM), pl.BlockSpec((chunks, CHUNK), lambda n: (0, 0))]
+    in_specs += [any_spec] * len(sources)
+    args = [pairs * stride, scale, *sources]
+    scratch = [
+        pltpu.VMEM((rows, CHUNK), jnp.int32),
+        pltpu.VMEM((group * chunks, CHUNK), jnp.float32),
+        pltpu.VMEM((block, CHUNK), jnp.float32),
+    ]
+    if form == "sent":
         out_shape = jax.ShapeDtypeStruct((chunks, feats, CHUNK), jnp.bfloat16)
         out_specs = pl.BlockSpec((chunks, block, CHUNK), lambda n: (0, n, 0))
-    if centered:
+    else:
+        dtype = jnp.bfloat16 if form == "own" else jnp.float32
+        out_shape = jax.ShapeDtypeStruct((feats, chunks * CHUNK), dtype)
+        out_specs = pl.BlockSpec((block, chunks * CHUNK), lambda n: (n, 0))
+    if form == "own":
+        scratch.append(pltpu.SemaphoreType.DMA)
+    else:
+        scratch.append(pltpu.VMEM((len(sources),) + sources[0].shape, sources[0].dtype))
+        scratch.append(pltpu.SemaphoreType.DMA((len(sources), 3)))
+    if form == "first":
+        out_shape = [
+            out_shape,
+            jax.ShapeDtypeStruct((1, feats), jnp.float32),
+            jax.ShapeDtypeStruct((rows, CHUNK), jnp.int32),
+        ]
+        out_specs = [out_specs, row_spec, any_spec]
+        scratch.append(pltpu.SemaphoreType.DMA)
+    else:
         in_specs.append(row_spec)
         args.append(mean)
-    else:
-        out_shape = [out_shape, jax.ShapeDtypeStruct((1, feats), jnp.float32)]
-        out_specs = [out_specs, row_spec]
     return pl.pallas_call(
-        functools.partial(gather_kernel, centered, len(coords)),
+        functools.partial(gather_kernel, form, chunks, len(sources)),
         out_shape=out_shape,
         grid=(feats // block,),
         in_specs=in_specs,
         out_specs=out_specs,
-        scratch_shapes=[
-            pltpu.VMEM((residues * stride, CHUNK), jnp.int32),
-            pltpu.VMEM((group * chunks, CHUNK), jnp.float32),
-            pltpu.VMEM((block, CHUNK), jnp.float32),
-            pltpu.VMEM((len(coords),) + coords[0].shape, coords[0].dtype),
-            pltpu.SemaphoreType.DMA((len(coords), 3)),
-        ],
+        scratch_shapes=scratch,
         compiler_params=pltpu.CompilerParams(vmem_limit_bytes=VMEM_LIMIT),
         cost_estimate=estimate(1),
     )(*args)
@@ -257,7 +271,7 @@
             @pl.when((c >= 0) & (c < parts))
             def _():
                 for i, d in enumerate(FAR):
-                    put(d, c, ref[0, i])
+                    put(d, c, ref[i])
 
     right = jnp.concatenate([ref[...] for ref in cols_refs], axis=0)
     both = jnp.dot(left[...], right, preferred_element_type=jnp.float32)
@@ -265,18 +279,12 @@
     cross_ref[...] = both[feats : 2 * feats] / factors_ref[1]
 
 
-def products(place, mask, factors, piece, pieces, near, far, cols, outs=(), block=256):
+def products(place, mask, factors, near, far, cols, block=256):
     frames, feats = cols[0][0].shape
     rows = near[0].shape[0]
-    row_feats = rows * pieces
-    out = jax.ShapeDtypeStruct((row_feats, feats), jnp.float32)
+    out = jax.ShapeDtypeStruct((rows, feats), jnp.float32)
     whole = lambda x: pl.BlockSpec(x.shape, lambda n, s: (0,) * x.ndim, pipeline_mode=pl.Buffered(1))
-    part = lambda x: pl.BlockSpec(
-        (1,) + x.shape[1:],
-        lambda n, s: (piece if x.shape[0] == pieces else 0, 0, 0, 0),
-        pipeline_mode=pl.Buffered(1),
-    )
-    inputs = [mask, factors, *near, *far, *[x for x, _ in cols], *outs]
+    inputs = [mask, factors, *near, *far, *[x for x, _ in cols]]
     return pl.pallas_call(
         product_kernel,
         out_shape=[out, out],
@@ -284,14 +292,11 @@
             num_scalar_prefetch=1,
             grid=(feats // block,),
             in_specs=[whole(mask), pl.BlockSpec(memory_space=pltpu.SMEM)]
-            + [whole(x) for x in near]
-            + [part(x) for x in far]
-            + [pl.BlockSpec((frames, block), lambda n, s, i=i: (i, n)) for _, i in cols]
-            + [pl.BlockSpec(memory_space=pl.ANY)] * len(outs),
-            out_specs=[pl.BlockSpec((rows, block), lambda n, s: (piece, n))] * 2,
+            + [whole(x) for x in (*near, *far)]
+            + [pl.BlockSpec((frames, block), lambda n, s, i=i: (i, n)) for _, i in cols],
+            out_specs=[pl.BlockSpec((rows, block), lambda n, s: (0, n))] * 2,
             scratch_shapes=[pltpu.VMEM((2 * rows, 8 * frames), jnp.bfloat16)],
         ),
-        input_output_aliases={1 + len(inputs) - 2 + i: i for i in range(len(outs))},
         compiler_params=pltpu.CompilerParams(vmem_limit_bytes=VMEM_LIMIT),
         cost_estimate=estimate(24),
     )(place, *inputs)
@@ -301,10 +306,10 @@
     return lax.ppermute(x, "tm", [(i, i ^ bits) for i in range(8)])
 
 
-def corner(along_x, along_y, axis, half):
-    low = swap(lax.slice_in_dim(along_x, 0, half, axis=axis), 4)
-    high = swap(lax.slice_in_dim(along_y, half, along_y.shape[axis], axis=axis), 2)
-    return low, high
+def corner(along_x, along_y):
+    over_y = lax.ppermute(along_x, "tm", [(i, i ^ 4) for i in range(0, 8, 2)])
+    over_x = lax.ppermute(along_y, "tm", [(i, i ^ 2) for i in range(1, 8, 2)])
+    return over_y, over_x
 
 
 def line_gather(x, count):
@@ -330,7 +335,6 @@
     frames_all = frames_dev * tm_count
     row_feats = feats * feat_count // tm_count
     parts = frames_dev // CHUNK
-    pieces = 1
     tm = lax.axis_index("tm").astype(jnp.int32)
     z = lax.axis_index("feat").astype(jnp.int32)
     place = jnp.stack([tm, z])
@@ -341,9 +345,9 @@
     quarter = lax.dynamic_slice_in_dim(coords_t, z * CHUNK, CHUNK, axis=2).astype(jnp.int16)
     quarters = {3: swap(quarter, 3), 5: swap(quarter, 5)}
 
-    raw, sums = contacts(pairs, [coords_t], scale_own)
+    raw, sums, table = contacts("first", pairs, [coords_t], scale_own)
     raw, sums, quarters = together(raw, sums, quarters)
-    halves = corner(quarters[3], quarters[5], 1, (coords_t.shape[1] // 32) * 16)
+    across = corner(quarters[3], quarters[5])
     note = jnp.concatenate([sums, frame_scale.reshape(1, frames_dev)], axis=1)
     notes = [note] + [swap(note, d) for d in range(1, 8)]
 
@@ -355,8 +359,8 @@
     scale_of = lambda *d: jnp.concatenate([scales[i] for i in d], axis=0)
 
     facts = line_gather(jnp.concatenate([mean, pairs.astype(jnp.float32)], axis=0), feat_count)
-    mine, facts, halves = together(center(raw, mean), facts, halves)
-    quarters[7] = jnp.concatenate(halves, axis=1)
+    mine, facts, across = together(center(raw, mean), facts, across)
+    quarters[7] = across[0] + across[1]
     cols = {0: mine, 2: swap(mine, 2), 4: swap(mine, 4)}
     quarters[6] = swap(quarters[7], 1)
 
@@ -373,39 +377,40 @@
     row_mean, row_pairs = row_facts[0:1], row_facts[1:3].astype(jnp.int32)
     out_mean, out_pairs = out_facts[0:1], out_facts[1:3].astype(jnp.int32)
 
-    sent_near = contacts(row_pairs, [quarters[3], quarters[5]], scale_of(3, 5), row_mean)
-    sent_near, quarters, mine = together(sent_near, quarters, mine)
+    row_pairs, mine, quarters = together(row_pairs, mine, quarters)
     cols[1] = swap(mine, 1)
-    sent_far = contacts(row_pairs, [quarters[6], quarters[7]], scale_of(6, 7), row_mean)
-
+    mixed = contacts("sent", row_pairs, [quarters[d] for d in FAR], scale_of(*FAR), row_mean)
+
+    out_pairs, mixed, walker_lengths = together(out_pairs, mixed, walker_lengths)
+    up, down = line_hop(mixed, mixed, 1, feat_count)
     valid = walker_mask(walker_lengths, frames_all, frames_all)
     mask = valid.astype(jnp.float32).reshape(tm_count, parts, 1, CHUNK)
     npairs = jnp.sum(jnp.maximum(walker_lengths - LAG, 0)).astype(jnp.float32)
     factors = jnp.stack([jnp.float32(1.0 / frames_all), npairs])
-
-    rows = row_feats // pieces
-    joined = jnp.concatenate([sent_near, sent_far], axis=0).reshape(len(FAR), pieces, rows, CHUNK)
-    joined = jnp.transpose(joined, (1, 0, 2, 3))
-    out_pairs, mask, factors, joined = together(out_pairs, mask, factors, joined)
-    up, down = line_hop(joined, joined, 1, feat_count)
-    sent = contacts(out_pairs, [coords_t], scale_own, out_mean)
-    sent, up, down = together(sent, up, down)
-    far = [joined, up, down]
+    near_rows = contacts("own", out_pairs[:, :feats], [table], scale_own, out_mean[:, :feats])
+    near_rows, mask, factors, up, down, cols = together(near_rows, mask, factors, up, down, cols)
+    far = [mixed, up, down]
+
     up, down = line_hop(up, down, 2, feat_count)
-    cut = lambda start: lax.dynamic_slice_in_dim(sent, start, row_feats, axis=0)
-    own = cut(2 * row_feats + own_half)
-    partner = swap(cut(3 * row_feats - own_half), 1)
-    cols, sent = together(cols, sent)
-    low, high = corner(cols[2], cols[4], 0, frames_dev // 2)
-    low, high, up, down, sent = together(low, high, up, down, sent)
-    far_cols = jnp.concatenate([cols[2], cols[4], low, high], axis=0)
-    their_cols = swap(far_cols, 1)
+    across = corner(cols[2], cols[4])
+    side_cols = jnp.concatenate([cols[2], cols[4]], axis=0)
+    their_side_cols = swap(side_cols, 1)
+    chip_pairs, side_cols = together(out_pairs[:, feats:], side_cols)
+    chip_rows = contacts("own", chip_pairs, [table], scale_own, out_mean[:, feats:])
+    chip_rows, across, up, down, their_side_cols = together(chip_rows, across, up, down, their_side_cols)
+
     far += [up, down, *line_hop(up, down, 3, feat_count)]
-    near = [own, partner, swap(cut(0), 2), swap(cut(row_feats), 4)]
+    far_cols = across[0] + across[1]
+    their_far_cols = swap(far_cols, 1)
+    near_rows, far_cols = together(near_rows, far_cols)
+    cut = lambda x, start: lax.dynamic_slice_in_dim(x, start, row_feats, axis=0)
+    own = cut(chip_rows, own_half)
+    partner = swap(cut(chip_rows, row_feats - own_half), 1)
+    near = [own, partner, swap(near_rows[:row_feats], 2), swap(near_rows[row_feats:], 4)]
     cols = [(cols[0], 0), (cols[1], 0)]
-    for i in range(3):
-        cols += [(far_cols, i), (their_cols, i)]
-    return products(place, mask, factors, 0, pieces, near, far, cols)
+    cols += [(side_cols, 0), (their_side_cols, 0), (side_cols, 1), (their_side_cols, 1)]
+    cols += [(far_cols, 0), (their_far_cols, 0)]
+    return products(place, mask, factors, near, far, cols)
 
 
 def solution(mesh):

time: 237 us -> 236 us (level)
  starting transfers between devices: 36.8 us -> 42.8 us
  local copies, waits for them, and re-layouts: 16.9 us -> 12.8 us
  waiting for transfers between devices: 53.9 us -> 51.1 us
    ppermute x0 -> x4, starting transfers between devices: none -> 8.54 us  [the longest x2 5.83 us: corner(): over_y = lax.ppermute(along_x, 'tm', [(i, i ^ 4) for i in range(0, 8, 2)])]
    ppermute x21 -> x18, starting transfers between devices: 20 us -> 15.8 us  [swap(): return lax.ppermute(x, 'tm', [(i, i ^ bits) for i in range(8)])]
    ppermute x3, waiting for transfers between devices: 39.4 us -> 35.3 us  [line_hop(): down = lax.ppermute(down, 'feat', [(i + 1, i) for i in range(count - hop)])]
    slice x5 -> x2, local copies, waits for them, and re-layouts: 3.87 us -> 0.74 us  [the longest x1 0.61 us: shards(): out_mean[:, feats:]]
    add x0 -> x2, other arithmetic: none -> 2.93 us  [the longest x1 2.54 us: shards(): far_cols = across[0] + across[1]]
    unnamed x38 -> x35, local copies, waits for them, and re-layouts: 7.02 us -> 5.44 us
    ppermute x21 -> x18, waiting for transfers between devices: 14.5 us -> 13.6 us  [swap(): return lax.ppermute(x, 'tm', [(i, i ^ bits) for i in range(8)])]
  transfers between devices with their start and end apart: 30 -> 31, of which waited for: 8 -> 9; matrix products, arithmetic and copies ran while one was open for 10% -> 5% of each run, Pallas kernels for 27% -> 27%
where the time goes in v5:
time: 236 us; the launch traced here: 235 us
  Pallas kernels  114 us (48%)
  waiting for transfers between devices  51.1 us (22%)
  starting transfers between devices  42.8 us (18%)
  local copies, waits for them, and re-layouts  12.8 us (5%)
  other arithmetic  12.1 us (5%)
    pallas_call x4, Pallas kernels, contacts(): pl.pallas_call(functools.partial(gather_kernel, form, chunks, len(sources...  59.5 us
    pallas_call x1, Pallas kernels, products(): pl.pallas_call(product_kernel, out_shape=[out, out], grid_spec=pltpu.Pref...  49.4 us
    ppermute x3, waiting for transfers between devices, line_hop(): down = lax.ppermute(down, 'feat', [(i + 1, i) for i in range(count - hop)])  35.3 us
    ppermute x18, starting transfers between devices, swap(): return lax.ppermute(x, 'tm', [(i, i ^ bits) for i in range(8)])  15.8 us
    ppermute x18, waiting for transfers between devices, swap(): return lax.ppermute(x, 'tm', [(i, i ^ bits) for i in range(8)])  13.6 us
    ppermute x3, starting transfers between devices, line_hop(): lax.ppermute(up, 'feat', [(i, i + 1) for i in range(hop - 1, count - 1)])  7.91 us
    ppermute x3, starting transfers between devices, line_gather(): lax.ppermute(x, 'feat', shift(s))  6.45 us
    ppermute x2, starting transfers between devices, corner(): over_y = lax.ppermute(along_x, 'tm', [(i, i ^ 4) for i in range(0, 8, 2)])  5.83 us
  transfers between devices with their start and end apart: 31, of which 9 were waited for; matrix products, arithmetic and copies ran while one was open for 5% of the time, Pallas kernels for 27%

profile of v5, /device:TPU:0, one launch (start us, length us, event | category | flops | bytes accessed | tf_op | source)
XLA Modules:
  0.0 234.6 jit_solution(18444102813448826600)
XLA Ops:
  0.6 1.8 fusion
  2.5 2.5 %collective-permute-start.1 = (s16[3,1500,128]{2,1,0:T(8,128)(2,1)S(1)}, s16[3,1500,128]{2,1,0:T(8,128)(2,1)S(1)}, u32[]{:S(2)}, u32[]{:S(2)}) collective-permute-start(s16[3,1500,128]{2,1,0:T(8,128)(2,1)S(1)} %fusion), channel_id=1, source_target_pairs={{0,20},{4,16},{8,28},{12,24},{16,4},{20,0},{24,12},{28,8},{1,21},{... | collective-permute-start | bytes 3456008 | tf_op jit(solution)/shard_map/ppermute | solution.py:306
  7.3 18.1 %shard_map.59 = (f32[2048,512]{1,0:T(8,128)}, f32[1,2048]{1,0:T(1,128)}, s32[24000,128]{1,0:T(8,128)}) custom-call(s32[2,2048]{1,0:T(2,128)} %get-tuple-element.108.pairs_ref, f32[4,128]{1,0:T(4,128)} %bitcast.25, s32[3,1500,512]{2,1,0:T(8,128)} %bitcast.24), custom_call_target="tpu_custom_call" | custom-call | flops 1000000000 | bytes 3690000 | tf_op jit(solution)/shard_map/pallas_call | solution.py:208
  25.4 5.4 %collective-permute-done.1.rest_1_ = s16[3,1500,128]{2,1,0:T(8,128)(2,1)S(1)} collective-permute-done((s16[3,1500,128]{2,1,0:T(8,128)(2,1)S(1)}, s16[3,1500,128]{2,1,0:T(8,128)(2,1)S(1)}, u32[]{:S(2)}, u32[]{:S(2)}) %collective-permute-start.1) | collective-permute-done | bytes 1152032 | tf_op jit(solution)/shard_map/ppermute | solution.py:306
  32.7 2.0 collective-permute-start.8
  39.6 2.9 %collective-permute-start.12 = (s16[3,1500,128]{2,1,0:T(8,128)(2,1)}, s16[3,1500,128]{2,1,0:T(8,128)(2,1)S(1)}, u32[]{:S(2)}, u32[]{:S(2)}) collective-permute-start(s16[3,1500,128]{2,1,0:T(8,128)(2,1)} %collective-permute-done.rest_0_), channel_id=1, source_target_pairs={{0,16},{8,24},{16,0},{24,8},{1,17},{9,25},{17,1},{25,9},{2,18},{10... | collective-permute-start | bytes 3456008 | tf_op jit(solution)/shard_map/ppermute | solution.py:310
  44.0 2.6 %collective-permute-start.10 = (f32[3,2048]{1,0:T(4,128)S(1)}, f32[3,2048]{1,0:T(4,128)S(1)}, u32[]{:S(2)}, u32[]{:S(2)}) collective-permute-start(f32[3,2048]{1,0:T(4,128)S(1)} %get-tuple-element.106), channel_id=1, source_target_pairs={{0,2},{1,3},{2,0},{3,1},{4,6},{5,7},{6,4},{7,5},{8,10},{9,11},{10,... | collective-permute-start | bytes 73736 | tf_op jit(solution)/shard_map/ppermute | solution.py:317
  48.2 2.2 collective-permute-start.11
  50.5 4.9 %shard_map.60.rest_11_ = bf16[512,2048]{1,0:T(8,128)(2,1)} custom-call(f32[2048,512]{1,0:T(8,128)} %get-tuple-element.49.raw_ref, f32[1,2048]{1,0:T(1,128)} %copy-done.6), custom_call_target="tpu_custom_call" | custom-call | flops 1000000000 | bytes 3690000 | tf_op jit(solution)/shard_map/pallas_call | solution.py:228
  55.5 2.2 collective-permute-done.12
  63.6 12.1 %shard_map.61.rest_4_ = bf16[4,1024,128]{2,1,0:T(8,128)(2,1)} custom-call(s32[2,1024]{1,0:T(2,128)} %broadcast_multiply_fusion.2.pairs_ref, f32[4,128]{1,0:T(4,128)} %pad_maximum_fusion.4.scale_ref, s16[3,1500,128]{2,1,0:T(8,128)(2,1)} %collective-permute-done.rest_0_, s16[3,1500,128]{2,1,0:T(8,128)(2,1)} %copy-done.4, s16[3,1500,128]{2,1,0:T(8,128)(2,1)} %copy-done.5, ...), custom_call_target="tpu_custom_call" | custom-call | flops 1000000000 | bytes 3690000 | tf_op jit(solution)/shard_map/pallas_call | solution.py:208
  77.0 5.6 %collective-permute-start.15 = (bf16[4,1024,128]{2,1,0:T(8,128)(2,1)}, bf16[4,1024,128]{2,1,0:T(8,128)(2,1)}, u32[]{:S(2)}, u32[]{:S(2)}) collective-permute-start(bf16[4,1024,128]{2,1,0:T(8,128)(2,1)} %shard_map.61.rest_4_), channel_id=1, source_target_pairs={{0,1},{1,2},{2,3},{4,5},{5,6},{6,7},{8,9},{9,10},{10,11},{12,13},{... | collective-permute-start | bytes 3145736 | tf_op jit(solution)/shard_map/ppermute | solution.py:321
  84.8 14.6 %shard_map.62 = bf16[2048,512]{1,0:T(8,128)(2,1)} custom-call(s32[2,2048]{1,0:T(2,128)} %get-tuple-element.104.pairs_ref, f32[4,128]{1,0:T(4,128)} %bitcast.26, s32[24000,128]{1,0:T(8,128)} %get-tuple-element.69.rest_0_, f32[1,2048]{1,0:T(1,128)} %get-tuple-element.102.rest_1_), custom_call_target="tpu_custom_call" | custom-call | flops 1000000000 | bytes 3690000 | tf_op jit(solution)/shard_map/pallas_call | solution.py:208
  100.7 5.6 %collective-permute-done.19 = bf16[512,2048]{1,0:T(8,128)(2,1)} collective-permute-done((bf16[512,2048]{1,0:T(8,128)(2,1)S(1)}, bf16[512,2048]{1,0:T(8,128)(2,1)}, u32[]{:S(2)}, u32[]{:S(2)}) %collective-permute-start.19) | collective-permute-done | bytes 2097184 | tf_op jit(solution)/shard_map/ppermute | solution.py:306
  107.0 3.5 %constant_dynamic-update-slice_fusion.1 = bf16[1024,2048]{1,0:T(8,128)(2,1)} fusion(bf16[512,2048]{1,0:T(8,128)(2,1)} %collective-permute-done.18), kind=kLoop, calls=%fused_computation.30 | loop fusion | bytes 4194304
  110.5 3.1 %constant_dynamic-update-slice_fusion.rest_13_.rest_15_ = bf16[1024,2048]{1,0:T(8,128)(2,1)} fusion(bf16[1024,2048]{1,0:T(8,128)(2,1)} %constant_dynamic-update-slice_fusion.1, bf16[512,2048]{1,0:T(8,128)(2,1)} %collective-permute-done.19), kind=kLoop, calls=%fused_computation.29 | loop fusion | bytes 4194304 | tf_op jit(solution)/shard_map/concatenate | solution.py:396
  113.7 3.0 %collective-permute-start.20 = (bf16[512,2048]{1,0:T(8,128)(2,1)}, bf16[512,2048]{1,0:T(8,128)(2,1)S(1)}, u32[]{:S(2)}, u32[]{:S(2)}) collective-permute-start(bf16[512,2048]{1,0:T(8,128)(2,1)} %collective-permute-done.18), channel_id=1, source_target_pairs={{0,16},{8,24},{16,0},{24,8},{1,17},{9,25},{17,1},{25,9},{2,18},{10... | collective-permute-start | bytes 6291464 | tf_op jit(solution)/shard_map/ppermute | solution.py:310
  116.6 2.0 collective-permute-start.21
  122.3 14.6 %shard_map.63 = bf16[2048,512]{1,0:T(8,128)(2,1)} custom-call(s32[2,2048]{1,0:T(2,128)} %broadcast_multiply_fusion.pairs_ref, f32[4,128]{1,0:T(4,128)} %bitcast.27, s32[24000,128]{1,0:T(8,128)} %get-tuple-element.69.rest_0_, f32[1,2048]{1,0:T(1,128)} %get-tuple-element.101.rest_1_), custom_call_target="tpu_custom_call" | custom-call | flops 1000000000 | bytes 3690000 | tf_op jit(solution)/shard_map/pallas_call | solution.py:208
  137.0 12.0 %collective-permute-done.23.rest_8_ = bf16[4,1024,128]{2,1,0:T(8,128)(2,1)} collective-permute-done((bf16[4,1024,128]{2,1,0:T(8,128)(2,1)S(1)}, bf16[4,1024,128]{2,1,0:T(8,128)(2,1)}, u32[]{:S(2)}, u32[]{:S(2)}) %collective-permute-start.23) | collective-permute-done | bytes 1048608 | tf_op jit(solution)/shard_map/ppermute | solution.py:322
  149.0 2.8 %constant_dynamic-slice_fusion = (bf16[1024,512]{1,0:T(8,128)(2,1)S(1)}, bf16[1024,512]{1,0:T(8,128)(2,1)}) fusion(bf16[2048,512]{1,0:T(8,128)(2,1)} %shard_map.63, s32[]{:T(128)S(6)} %select_n.77, s32[]{:T(128)S(6)} %select_n.69), kind=kLoop, calls=%fused_computation.32 | loop fusion | bytes 4194312 | tf_op jit(solution)/shard_map/dynamic_slice | solution.py:406
  151.7 2.5 %add.150.rest_17_ = bf16[512,2048]{1,0:T(8,128)(2,1)S(1)} add(bf16[512,2048]{1,0:T(8,128)(2,1)S(1)} %collective-permute-done.20, bf16[512,2048]{1,0:T(8,128)(2,1)} %collective-permute-done.21) | non-fusion elementwise | flops 1048576 | bytes 6291456 | tf_op jit(solution)/shard_map/add | solution.py:403
  159.4 23.3 %collective-permute-done.29.rest_10_ = bf16[4,1024,128]{2,1,0:T(8,128)(2,1)S(1)} collective-permute-done((bf16[4,1024,128]{2,1,0:T(8,128)(2,1)}, bf16[4,1024,128]{2,1,0:T(8,128)(2,1)S(1)}, u32[]{:S(2)}, u32[]{:S(2)}) %collective-permute-start.29) | collective-permute-done | bytes 1048608 | tf_op jit(solution)/shard_map/ppermute | solution.py:322
  185.0 49.4 %shard_map.64 = (f32[1024,2048]{1,0:T(8,128)}, f32[1024,2048]{1,0:T(8,128)}) custom-call(s32[2]{0:T(128)} %pad_add_fusion.place_ref, f32[8,4,1,128]{3,2,1,0:T(1,128)} %fusion.1.mask_ref, f32[2]{0:T(128)} %pad_maximum_fusion.5.factors_ref, bf16[1024,512]{1,0:T(8,128)(2,1)} %get-tuple-element.97.rest_0_, bf16[1024,512]{1,0:T(8,128)(2,1)} %copy-done.11, ...), custom_call_target="tpu_custom_call" | custom-call | flops 24000000000 | bytes 88560000 | tf_op jit(solution)/shard_map/pallas_call | solution.py:288
  (113 shorter events, 34.0 us)
Async XLA Ops:
  2.5 28.3 %collective-permute-start.1 = (s16[3,1500,128]{2,1,0:T(8,128)(2,1)S(1)}, s16[3,1500,128]{2,1,0:T(8,128)(2,1)S(1)}, u32[]{:S(2)}, u32[]{:S(2)}) collective-permute-start(s16[3,1500,128]{2,1,0:T(8,128)(2,1)S(1)} %fusion), channel_id=1, source_target_pairs={{0,20},{4,16},{8,28},{12,24},{16,4},{20,0},{24,12},{28,8},{1,21},{... | collective-permute-start | bytes 3456008 | tf_op jit(solution)/shard_map/ppermute | solution.py:306
  4.9 27.1 %collective-permute-start = (s16[3,1500,128]{2,1,0:T(8,128)(2,1)S(1)}, s16[3,1500,128]{2,1,0:T(8,128)(2,1)}, u32[]{:S(2)}, u32[]{:S(2)}) collective-permute-start(s16[3,1500,128]{2,1,0:T(8,128)(2,1)S(1)} %fusion), channel_id=1, source_target_pairs={{0,12},{4,8},{8,4},{12,0},{16,28},{20,24},{24,20},{28,16},{1,13},{... | collective-permute-start | bytes 3456008 | tf_op jit(solution)/shard_map/ppermute | solution.py:306
  32.7 6.2 %collective-permute-start.8 = (f32[1,2560]{1,0:T(1,128)S(1)}, f32[1,2560]{1,0:T(1,128)S(1)}, u32[]{:S(2)}, u32[]{:S(2)}) collective-permute-start(f32[1,2560]{1,0:T(1,128)S(1)} %pad_maximum_fusion.3), channel_id=1, source_target_pairs={{0,28},{4,24},{8,20},{12,16},{16,12},{20,8},{24,4},{28,0},{1,29},{... | collective-permute-start | bytes 30728 | tf_op jit(solution)/shard_map/ppermute | solution.py:306
  37.2 6.0 %collective-permute-start.4 = (f32[1,2560]{1,0:T(1,128)S(1)}, f32[1,2560]{1,0:T(1,128)S(1)}, u32[]{:S(2)}, u32[]{:S(2)}) collective-permute-start(f32[1,2560]{1,0:T(1,128)S(1)} %pad_maximum_fusion.3), channel_id=1, source_target_pairs={{0,12},{4,8},{8,4},{12,0},{16,28},{20,24},{24,20},{28,16},{1,13},{... | collective-permute-start | bytes 30728 | tf_op jit(solution)/shard_map/ppermute | solution.py:306
  39.6 18.0 %collective-permute-start.12 = (s16[3,1500,128]{2,1,0:T(8,128)(2,1)}, s16[3,1500,128]{2,1,0:T(8,128)(2,1)S(1)}, u32[]{:S(2)}, u32[]{:S(2)}) collective-permute-start(s16[3,1500,128]{2,1,0:T(8,128)(2,1)} %collective-permute-done.rest_0_), channel_id=1, source_target_pairs={{0,16},{8,24},{16,0},{24,8},{1,17},{9,25},{17,1},{25,9},{2,18},{10... | collective-permute-start | bytes 3456008 | tf_op jit(solution)/shard_map/ppermute | solution.py:310
  42.5 15.2 %collective-permute-start.13 = (s16[3,1500,128]{2,1,0:T(8,128)(2,1)S(1)}, s16[3,1500,128]{2,1,0:T(8,128)(2,1)S(1)}, u32[]{:S(2)}, u32[]{:S(2)}) collective-permute-start(s16[3,1500,128]{2,1,0:T(8,128)(2,1)S(1)} %collective-permute-done.1.rest_1_), channel_id=1, source_target_pairs={{4,12},{12,4},{20,28},{28,20},{5,13},{13,5},{21,29},{29,21},{6,14}... | collective-permute-start | bytes 3456008 | tf_op jit(solution)/shard_map/ppermute | solution.py:311
  44.0 11.4 %collective-permute-start.10 = (f32[3,2048]{1,0:T(4,128)S(1)}, f32[3,2048]{1,0:T(4,128)S(1)}, u32[]{:S(2)}, u32[]{:S(2)}) collective-permute-start(f32[3,2048]{1,0:T(4,128)S(1)} %get-tuple-element.106), channel_id=1, source_target_pairs={{0,2},{1,3},{2,0},{3,1},{4,6},{5,7},{6,4},{7,5},{8,10},{9,11},{10,... | collective-permute-start | bytes 73736 | tf_op jit(solution)/shard_map/ppermute | solution.py:317
  46.6 8.8 %collective-permute-start.9 = (f32[3,2048]{1,0:T(4,128)S(1)}, f32[3,2048]{1,0:T(4,128)S(1)}, u32[]{:S(2)}, u32[]{:S(2)}) collective-permute-start(f32[3,2048]{1,0:T(4,128)S(1)} %get-tuple-element.106), channel_id=1, source_target_pairs={{0,1},{1,2},{2,3},{3,0},{4,5},{5,6},{6,7},{7,4},{8,9},{9,10},{10,1... | collective-permute-start | bytes 73736 | tf_op jit(solution)/shard_map/ppermute | solution.py:317
  48.2 7.2 %collective-permute-start.11 = (f32[3,2048]{1,0:T(4,128)S(1)}, f32[3,2048]{1,0:T(4,128)S(1)}, u32[]{:S(2)}, u32[]{:S(2)}) collective-permute-start(f32[3,2048]{1,0:T(4,128)S(1)} %get-tuple-element.106), channel_id=1, source_target_pairs={{0,3},{1,0},{2,1},{3,2},{4,7},{5,4},{6,5},{7,6},{8,11},{9,8},{10,9... | collective-permute-start | bytes 73736 | tf_op jit(solution)/shard_map/ppermute | solution.py:317
  58.2 48.1 %collective-permute-start.19 = (bf16[512,2048]{1,0:T(8,128)(2,1)S(1)}, bf16[512,2048]{1,0:T(8,128)(2,1)}, u32[]{:S(2)}, u32[]{:S(2)}) collective-permute-start(bf16[512,2048]{1,0:T(8,128)(2,1)S(1)} %copy-done.3), channel_id=1, source_target_pairs={{0,16},{4,20},{8,24},{12,28},{16,0},{20,4},{24,8},{28,12},{1,17},{... | collective-permute-start | bytes 6291464 | tf_op jit(solution)/shard_map/ppermute | solution.py:306
  59.2 47.7 %collective-permute-start.18 = (bf16[512,2048]{1,0:T(8,128)(2,1)S(1)}, bf16[512,2048]{1,0:T(8,128)(2,1)}, u32[]{:S(2)}, u32[]{:S(2)}) collective-permute-start(bf16[512,2048]{1,0:T(8,128)(2,1)S(1)} %copy-done.3), channel_id=1, source_target_pairs={{0,8},{4,12},{8,0},{12,4},{16,24},{20,28},{24,16},{28,20},{1,9},{5... | collective-permute-start | bytes 6291464 | tf_op jit(solution)/shard_map/ppermute | solution.py:306
  60.9 46.0 %collective-permute-start.17 = (bf16[512,2048]{1,0:T(8,128)(2,1)S(1)}, bf16[512,2048]{1,0:T(8,128)(2,1)}, u32[]{:S(2)}, u32[]{:S(2)}) collective-permute-start(bf16[512,2048]{1,0:T(8,128)(2,1)S(1)} %copy-done.3), channel_id=1, source_target_pairs={{0,4},{4,0},{8,12},{12,8},{16,20},{20,16},{24,28},{28,24},{1,5},{5... | collective-permute-start | bytes 6291464 | tf_op jit(solution)/shard_map/ppermute | solution.py:306
  75.7 31.2 %collective-permute-start.16 = (bf16[4,1024,128]{2,1,0:T(8,128)(2,1)}, bf16[4,1024,128]{2,1,0:T(8,128)(2,1)S(1)}, u32[]{:S(2)}, u32[]{:S(2)}) collective-permute-start(bf16[4,1024,128]{2,1,0:T(8,128)(2,1)} %shard_map.61.rest_4_), channel_id=1, source_target_pairs={{1,0},{2,1},{3,2},{5,4},{6,5},{7,6},{9,8},{10,9},{11,10},{13,12},{... | collective-permute-start | bytes 3145736 | tf_op jit(solution)/shard_map/ppermute | solution.py:322
  77.0 29.9 %collective-permute-start.15 = (bf16[4,1024,128]{2,1,0:T(8,128)(2,1)}, bf16[4,1024,128]{2,1,0:T(8,128)(2,1)}, u32[]{:S(2)}, u32[]{:S(2)}) collective-permute-start(bf16[4,1024,128]{2,1,0:T(8,128)(2,1)} %shard_map.61.rest_4_), channel_id=1, source_target_pairs={{0,1},{1,2},{2,3},{4,5},{5,6},{6,7},{8,9},{9,10},{10,11},{12,13},{... | collective-permute-start | bytes 3145736 | tf_op jit(solution)/shard_map/ppermute | solution.py:321
  113.7 35.3 %collective-permute-start.24 = (bf16[1024,2048]{1,0:T(8,128)(2,1)}, bf16[1024,2048]{1,0:T(8,128)(2,1)}, u32[]{:S(2)}, u32[]{:S(2)}) collective-permute-start(bf16[1024,2048]{1,0:T(8,128)(2,1)} %constant_dynamic-update-slice_fusion.rest_13_.rest_15_), channel_id=1, source_target_pairs={{0,4},{4,0},{8,12},{12,8},{16,20},{20,16},{24,28},{28,24},{1,5},{5... | collective-permute-start | bytes 12582920 | tf_op jit(solution)/shard_map/ppermute | solution.py:306
  113.7 35.3 %collective-permute-start.20 = (bf16[512,2048]{1,0:T(8,128)(2,1)}, bf16[512,2048]{1,0:T(8,128)(2,1)S(1)}, u32[]{:S(2)}, u32[]{:S(2)}) collective-permute-start(bf16[512,2048]{1,0:T(8,128)(2,1)} %collective-permute-done.18), channel_id=1, source_target_pairs={{0,16},{8,24},{16,0},{24,8},{1,17},{9,25},{17,1},{25,9},{2,18},{10... | collective-permute-start | bytes 6291464 | tf_op jit(solution)/shard_map/ppermute | solution.py:310
  116.6 32.3 %collective-permute-start.21 = (bf16[512,2048]{1,0:T(8,128)(2,1)}, bf16[512,2048]{1,0:T(8,128)(2,1)}, u32[]{:S(2)}, u32[]{:S(2)}) collective-permute-start(bf16[512,2048]{1,0:T(8,128)(2,1)} %collective-permute-done.19), channel_id=1, source_target_pairs={{4,12},{12,4},{20,28},{28,20},{5,13},{13,5},{21,29},{29,21},{6,14}... | collective-permute-start | bytes 6291464 | tf_op jit(solution)/shard_map/ppermute | solution.py:311
  118.6 18.4 %collective-permute-start.22 = (bf16[4,1024,128]{2,1,0:T(8,128)(2,1)}, bf16[4,1024,128]{2,1,0:T(8,128)(2,1)}, u32[]{:S(2)}, u32[]{:S(2)}) collective-permute-start(bf16[4,1024,128]{2,1,0:T(8,128)(2,1)} %collective-permute-done.15.rest_5_), channel_id=1, source_target_pairs={{1,2},{2,3},{5,6},{6,7},{9,10},{10,11},{13,14},{14,15},{17,18},{18... | collective-permute-start | bytes 3145736 | tf_op jit(solution)/shard_map/ppermute | solution.py:321
  120.2 28.7 %collective-permute-start.23 = (bf16[4,1024,128]{2,1,0:T(8,128)(2,1)S(1)}, bf16[4,1024,128]{2,1,0:T(8,128)(2,1)}, u32[]{:S(2)}, u32[]{:S(2)}) collective-permute-start(bf16[4,1024,128]{2,1,0:T(8,128)(2,1)S(1)} %collective-permute-done.16.rest_6_), channel_id=1, source_target_pairs={{1,0},{2,1},{5,4},{6,5},{9,8},{10,9},{13,12},{14,13},{17,16},{18,1... | collective-permute-start | bytes 3145736 | tf_op jit(solution)/shard_map/ppermute | solution.py:322
  151.7 6.5 %collective-permute-start.25 = (bf16[1024,512]{1,0:T(8,128)(2,1)S(1)}, bf16[1024,512]{1,0:T(8,128)(2,1)S(1)}, u32[]{:S(2)}, u32[]{:S(2)}) collective-permute-start(bf16[1024,512]{1,0:T(8,128)(2,1)S(1)} %get-tuple-element.96), channel_id=1, source_target_pairs={{0,4},{4,0},{8,12},{12,8},{16,20},{20,16},{24,28},{28,24},{1,5},{5... | collective-permute-start | bytes 3145736 | tf_op jit(solution)/shard_map/ppermute | solution.py:306
  154.3 28.9 %collective-permute-start.30 = (bf16[512,2048]{1,0:T(8,128)(2,1)S(1)}, bf16[512,2048]{1,0:T(8,128)(2,1)S(1)}, u32[]{:S(2)}, u32[]{:S(2)}) collective-permute-start(bf16[512,2048]{1,0:T(8,128)(2,1)S(1)} %add.150.rest_17_), channel_id=1, source_target_pairs={{0,4},{4,0},{8,12},{12,8},{16,20},{20,16},{24,28},{28,24},{1,5},{5... | collective-permute-start | bytes 6291464 | tf_op jit(solution)/shard_map/ppermute | solution.py:306
  155.4 27.3 %collective-permute-start.29 = (bf16[4,1024,128]{2,1,0:T(8,128)(2,1)}, bf16[4,1024,128]{2,1,0:T(8,128)(2,1)S(1)}, u32[]{:S(2)}, u32[]{:S(2)}) collective-permute-start(bf16[4,1024,128]{2,1,0:T(8,128)(2,1)} %collective-permute-done.23.rest_8_), channel_id=1, source_target_pairs={{1,0},{5,4},{9,8},{13,12},{17,16},{21,20},{25,24},{29,28}} | collective-permute-start | bytes 3145736 | tf_op jit(solution)/shard_map/ppermute | solution.py:322
  156.9 25.9 %collective-permute-start.27 = (bf16[1024,512]{1,0:T(8,128)(2,1)S(1)}, bf16[1024,512]{1,0:T(8,128)(2,1)S(1)}, u32[]{:S(2)}, u32[]{:S(2)}) collective-permute-start(bf16[1024,512]{1,0:T(8,128)(2,1)S(1)} %get-tuple-element.94), channel_id=1, source_target_pairs={{0,16},{4,20},{8,24},{12,28},{16,0},{20,4},{24,8},{28,12},{1,17},{... | collective-permute-start | bytes 3145736 | tf_op jit(solution)/shard_map/ppermute | solution.py:306
  158.2 24.9 %collective-permute-start.26 = (bf16[1024,512]{1,0:T(8,128)(2,1)S(1)}, bf16[1024,512]{1,0:T(8,128)(2,1)S(1)}, u32[]{:S(2)}, u32[]{:S(2)}) collective-permute-start(bf16[1024,512]{1,0:T(8,128)(2,1)S(1)} %get-tuple-element.95), channel_id=1, source_target_pairs={{0,8},{4,12},{8,0},{12,4},{16,24},{20,28},{24,16},{28,20},{1,9},{5... | collective-permute-start | bytes 3145736 | tf_op jit(solution)/shard_map/ppermute | solution.py:306
  (24 other events, 197.0 us)

commit v6 on v5

--- a/solution.py
+++ b/solution.py
@@ -243,7 +243,7 @@
     near_refs, rest = rest[: len(NEAR)], rest[len(NEAR) :]
     far_refs, rest = rest[:7], rest[7:]
     cols_refs, rest = rest[:8], rest[8:]
-    same_ref, cross_ref, left = rest[-3:]
+    same_ref, cross_ref, left, near_held, far_held, arrived = rest
     feats = same_ref.shape[0]
     frames = cols_refs[0].shape[0]
     parts = frames // CHUNK
@@ -261,41 +261,64 @@
 
     @pl.when(pl.program_id(0) == 0)
     def _():
-        for d, ref in zip(NEAR, near_refs):
+        copies = [
+            pltpu.make_async_copy(ref, near_held.at[n], arrived.at[n]) for n, ref in enumerate(near_refs)
+        ]
+        copies += [
+            pltpu.make_async_copy(ref, far_held.at[n], arrived.at[len(NEAR) + n])
+            for n, ref in enumerate(far_refs)
+        ]
+        for copy in copies:
+            copy.start()
+        for n, d in enumerate(NEAR):
+            copies[n].wait()
             for c in range(parts):
-                put(d, c, ref[:, c * CHUNK : (c + 1) * CHUNK])
-        for n, ref in enumerate(far_refs):
+                put(d, c, near_held[n, :, c * CHUNK : (c + 1) * CHUNK])
+        for n in range(len(far_refs)):
+            copies[len(NEAR) + n].wait()
             hop = (n + 1) // 2
             c = z - hop if n % 2 else z + hop
 
             @pl.when((c >= 0) & (c < parts))
             def _():
                 for i, d in enumerate(FAR):
-                    put(d, c, ref[i])
+                    put(d, c, far_held[n, i])
 
     right = jnp.concatenate([ref[...] for ref in cols_refs], axis=0)
-    both = jnp.dot(left[...], right, preferred_element_type=jnp.float32)
-    same_ref[...] = both[0:feats] * factors_ref[0]
-    cross_ref[...] = both[feats : 2 * feats] / factors_ref[1]
+    for m in range(0, feats, 512):
+        here = slice(m, m + 512)
+        same = jnp.dot(left[here, :], right, preferred_element_type=jnp.float32)
+        same_ref[here, :] = same * factors_ref[0]
+    for m in range(0, feats, 512):
+        here = slice(m, m + 512)
+        cross = jnp.dot(left[feats + m : feats + m + 512, :], right, preferred_element_type=jnp.float32)
+        cross_ref[here, :] = cross / factors_ref[1]
 
 
 def products(place, mask, factors, near, far, cols, block=256):
-    frames, feats = cols[0][0].shape
+    frames, feats = cols[0].shape
     rows = near[0].shape[0]
     out = jax.ShapeDtypeStruct((rows, feats), jnp.float32)
-    whole = lambda x: pl.BlockSpec(x.shape, lambda n, s: (0,) * x.ndim, pipeline_mode=pl.Buffered(1))
-    inputs = [mask, factors, *near, *far, *[x for x, _ in cols]]
+    inputs = [mask, factors, *near, *far, *cols]
     return pl.pallas_call(
         product_kernel,
         out_shape=[out, out],
         grid_spec=pltpu.PrefetchScalarGridSpec(
             num_scalar_prefetch=1,
             grid=(feats // block,),
-            in_specs=[whole(mask), pl.BlockSpec(memory_space=pltpu.SMEM)]
-            + [whole(x) for x in (*near, *far)]
-            + [pl.BlockSpec((frames, block), lambda n, s, i=i: (i, n)) for _, i in cols],
+            in_specs=[
+                pl.BlockSpec(mask.shape, lambda n, s: (0,) * mask.ndim),
+                pl.BlockSpec(memory_space=pltpu.SMEM),
+            ]
+            + [pl.BlockSpec(memory_space=pl.ANY)] * (len(near) + len(far))
+            + [pl.BlockSpec((frames, block), lambda n, s: (0, n))] * 8,
             out_specs=[pl.BlockSpec((rows, block), lambda n, s: (0, n))] * 2,
-            scratch_shapes=[pltpu.VMEM((2 * rows, 8 * frames), jnp.bfloat16)],
+            scratch_shapes=[
+                pltpu.VMEM((2 * rows, 8 * frames), jnp.bfloat16),
+                pltpu.VMEM((len(near),) + near[0].shape, jnp.bfloat16),
+                pltpu.VMEM((len(far),) + far[0].shape, jnp.bfloat16),
+                pltpu.SemaphoreType.DMA((len(near) + len(far),)),
+            ],
         ),
         compiler_params=pltpu.CompilerParams(vmem_limit_bytes=VMEM_LIMIT),
         cost_estimate=estimate(24),
@@ -307,9 +330,9 @@
 
 
 def corner(along_x, along_y):
-    over_y = lax.ppermute(along_x, "tm", [(i, i ^ 4) for i in range(0, 8, 2)])
-    over_x = lax.ppermute(along_y, "tm", [(i, i ^ 2) for i in range(1, 8, 2)])
-    return over_y, over_x
+    even = lax.axis_index("tm") % 2 == 0
+    forwarded = jnp.where(even, along_x, along_y)
+    return lax.ppermute(forwarded, "tm", [(i, i ^ (2 if i % 2 else 4)) for i in range(8)])
 
 
 def line_gather(x, count):
@@ -346,8 +369,8 @@
     quarters = {3: swap(quarter, 3), 5: swap(quarter, 5)}
 
     raw, sums, table = contacts("first", pairs, [coords_t], scale_own)
-    raw, sums, quarters = together(raw, sums, quarters)
-    across = corner(quarters[3], quarters[5])
+    quarters, _ = together(quarters, sums)
+    quarters[7] = corner(quarters[3], quarters[5])
     note = jnp.concatenate([sums, frame_scale.reshape(1, frames_dev)], axis=1)
     notes = [note] + [swap(note, d) for d in range(1, 8)]
 
@@ -359,8 +382,7 @@
     scale_of = lambda *d: jnp.concatenate([scales[i] for i in d], axis=0)
 
     facts = line_gather(jnp.concatenate([mean, pairs.astype(jnp.float32)], axis=0), feat_count)
-    mine, facts, across = together(center(raw, mean), facts, across)
-    quarters[7] = across[0] + across[1]
+    mine, facts, quarters = together(center(raw, mean), facts, quarters)
     cols = {0: mine, 2: swap(mine, 2), 4: swap(mine, 4)}
     quarters[6] = swap(quarters[7], 1)
 
@@ -387,29 +409,26 @@
     mask = valid.astype(jnp.float32).reshape(tm_count, parts, 1, CHUNK)
     npairs = jnp.sum(jnp.maximum(walker_lengths - LAG, 0)).astype(jnp.float32)
     factors = jnp.stack([jnp.float32(1.0 / frames_all), npairs])
-    near_rows = contacts("own", out_pairs[:, :feats], [table], scale_own, out_mean[:, :feats])
-    near_rows, mask, factors, up, down, cols = together(near_rows, mask, factors, up, down, cols)
+    chip_rows = contacts("own", out_pairs[:, feats:], [table], scale_own, out_mean[:, feats:])
+    chip_rows, mask, factors, up, down = together(chip_rows, mask, factors, up, down)
     far = [mixed, up, down]
 
     up, down = line_hop(up, down, 2, feat_count)
-    across = corner(cols[2], cols[4])
-    side_cols = jnp.concatenate([cols[2], cols[4]], axis=0)
-    their_side_cols = swap(side_cols, 1)
-    chip_pairs, side_cols = together(out_pairs[:, feats:], side_cols)
-    chip_rows = contacts("own", chip_pairs, [table], scale_own, out_mean[:, feats:])
-    chip_rows, across, up, down, their_side_cols = together(chip_rows, across, up, down, their_side_cols)
-
-    far += [up, down, *line_hop(up, down, 3, feat_count)]
-    far_cols = across[0] + across[1]
-    their_far_cols = swap(far_cols, 1)
-    near_rows, far_cols = together(near_rows, far_cols)
     cut = lambda x, start: lax.dynamic_slice_in_dim(x, start, row_feats, axis=0)
     own = cut(chip_rows, own_half)
     partner = swap(cut(chip_rows, row_feats - own_half), 1)
+    cols, own, partner = together(cols, own, partner)
+    cols[6] = corner(cols[2], cols[4])
+    for d in (2, 4):
+        cols[d + 1] = swap(cols[d], 1)
+    near_pairs, _ = together(out_pairs[:, :feats], own)
+    near_rows = contacts("own", near_pairs, [table], scale_own, out_mean[:, :feats])
+    near_rows, cols, up, down = together(near_rows, cols, up, down)
+
+    far += [up, down, *line_hop(up, down, 3, feat_count)]
+    cols[7] = swap(cols[6], 1)
     near = [own, partner, swap(near_rows[:row_feats], 2), swap(near_rows[row_feats:], 4)]
-    cols = [(cols[0], 0), (cols[1], 0)]
-    cols += [(side_cols, 0), (their_side_cols, 0), (side_cols, 1), (their_side_cols, 1)]
-    cols += [(far_cols, 0), (their_far_cols, 0)]
+    cols = [cols[d] for d in range(8)]
     return products(place, mask, factors, near, far, cols)
 
 

time: 236 us -> 221 us (0.936)
  starting transfers between devices: 42.8 us -> 35.6 us
  Pallas kernels: 114 us -> 110 us
    ppermute x3, waiting for transfers between devices: 35.3 us -> 18.1 us  [line_hop(): down = lax.ppermute(down, 'feat', [(i + 1, i) for i in range(count - hop)])]
    ppermute x18 -> x19, waiting for transfers between devices: 13.6 us -> 29.1 us  [swap(): return lax.ppermute(x, 'tm', [(i, i ^ bits) for i in range(8)])]
    ppermute x4 -> x2, starting transfers between devices: 8.54 us -> 2.1 us  [corner(): lax.ppermute(forwarded, 'tm', [(i, i ^ (2 if i % 2 else 4)) for i in rang...]
    pallas_call x1, Pallas kernels: 49.4 us -> 46 us  [products(): pl.pallas_call(product_kernel, out_shape=[out, out], grid_spec=pltpu.Pref...]
    concatenate x1 -> x0, local copies, waits for them, and re-layouts: 3.14 us -> none  [shards(): side_cols = jnp.concatenate([cols[2], cols[4]], axis=0)]
    add x2 -> x0, other arithmetic: 2.93 us -> none  [the longest x1 2.54 us: shards(): far_cols = across[0] + across[1]]
    ppermute x18 -> x19, starting transfers between devices: 15.8 us -> 15.1 us  [swap(): return lax.ppermute(x, 'tm', [(i, i ^ bits) for i in range(8)])]
    unnamed x35 -> x36, local copies, waits for them, and re-layouts: 5.44 us -> 4.96 us
  transfers between devices with their start and end apart: 31 -> 30, of which waited for: 9 -> 12; matrix products, arithmetic and copies ran while one was open for 5% -> 7% of each run, Pallas kernels for 27% -> 29%
where the time goes in v6:
time: 221 us; the launch traced here: 220 us
  Pallas kernels  110 us (50%)
  waiting for transfers between devices  49.1 us (22%)
  starting transfers between devices  35.6 us (16%)
  local copies, waits for them, and re-layouts  11.8 us (5%)
  other arithmetic  11.5 us (5%)
    pallas_call x4, Pallas kernels, contacts(): pl.pallas_call(functools.partial(gather_kernel, form, chunks, len(sources...  59.6 us
    pallas_call x1, Pallas kernels, products(): pl.pallas_call(product_kernel, out_shape=[out, out], grid_spec=pltpu.Pref...  46 us
    ppermute x19, waiting for transfers between devices, swap(): return lax.ppermute(x, 'tm', [(i, i ^ bits) for i in range(8)])  29.1 us
    ppermute x3, waiting for transfers between devices, line_hop(): down = lax.ppermute(down, 'feat', [(i + 1, i) for i in range(count - hop)])  18.1 us
    ppermute x19, starting transfers between devices, swap(): return lax.ppermute(x, 'tm', [(i, i ^ bits) for i in range(8)])  15.1 us
    ppermute x3, starting transfers between devices, line_hop(): lax.ppermute(up, 'feat', [(i, i + 1) for i in range(hop - 1, count - 1)])  7.9 us
    ppermute x3, starting transfers between devices, line_gather(): lax.ppermute(x, 'feat', shift(s))  6.48 us
    unnamed x36, local copies, waits for them, and re-layouts  4.96 us
  transfers between devices with their start and end apart: 30, of which 12 were waited for; matrix products, arithmetic and copies ran while one was open for 7% of the time, Pallas kernels for 29%

profile of v6, /device:TPU:0, one launch (start us, length us, event | category | flops | bytes accessed | tf_op | source)
XLA Modules:
  0.0 220.2 jit_solution(15023568711170614705)
XLA Ops:
  0.6 1.8 fusion
  2.5 2.5 %collective-permute-start.11 = (s16[3,1500,128]{2,1,0:T(8,128)(2,1)S(1)}, s16[3,1500,128]{2,1,0:T(8,128)(2,1)S(1)}, u32[]{:S(2)}, u32[]{:S(2)}) collective-permute-start(s16[3,1500,128]{2,1,0:T(8,128)(2,1)S(1)} %fusion), channel_id=1, source_target_pairs={{0,20},{4,16},{8,28},{12,24},{16,4},{20,0},{24,12},{28,8},{1,21},{... | collective-permute-start | bytes 3456008 | tf_op jit(solution)/shard_map/ppermute | solution.py:329
  4.9 1.8 collective-permute-start.10
  7.3 18.1 %shard_map.59 = (f32[2048,512]{1,0:T(8,128)}, f32[1,2048]{1,0:T(1,128)}, s32[24000,128]{1,0:T(8,128)}) custom-call(s32[2,2048]{1,0:T(2,128)} %get-tuple-element.112.pairs_ref, f32[4,128]{1,0:T(4,128)} %bitcast.25, s32[3,1500,512]{2,1,0:T(8,128)} %bitcast.24), custom_call_target="tpu_custom_call" | custom-call | flops 1000000000 | bytes 3690000 | tf_op jit(solution)/shard_map/pallas_call | solution.py:208
  26.3 2.3 %collective-permute-start.5 = (f32[1,2560]{1,0:T(1,128)S(1)}, f32[1,2560]{1,0:T(1,128)S(1)}, u32[]{:S(2)}, u32[]{:S(2)}) collective-permute-start(f32[1,2560]{1,0:T(1,128)S(1)} %pad_maximum_fusion.3), channel_id=1, source_target_pairs={{0,24},{4,28},{8,16},{12,20},{16,8},{20,12},{24,0},{28,4},{1,25},{... | collective-permute-start | bytes 30728 | tf_op jit(solution)/shard_map/ppermute | solution.py:329
  29.1 1.6 collective-permute-done.11.rest_1_
  30.8 2.5 %collective-permute-start.3 = (f32[1,2560]{1,0:T(1,128)S(1)}, f32[1,2560]{1,0:T(1,128)S(1)}, u32[]{:S(2)}, u32[]{:S(2)}) collective-permute-start(f32[1,2560]{1,0:T(1,128)S(1)} %pad_maximum_fusion.3), channel_id=1, source_target_pairs={{0,16},{4,20},{8,24},{12,28},{16,0},{20,4},{24,8},{28,12},{1,17},{... | collective-permute-start | bytes 30728 | tf_op jit(solution)/shard_map/ppermute | solution.py:329
  36.3 1.6 collective-permute-done.1
  38.7 2.7 %collective-permute-start.8 = (f32[3,2048]{1,0:T(4,128)S(1)}, f32[3,2048]{1,0:T(4,128)S(1)}, u32[]{:S(2)}, u32[]{:S(2)}) collective-permute-start(f32[3,2048]{1,0:T(4,128)S(1)} %get-tuple-element.110), channel_id=1, source_target_pairs={{0,2},{1,3},{2,0},{3,1},{4,6},{5,7},{6,4},{7,5},{8,10},{9,11},{10,... | collective-permute-start | bytes 73736 | tf_op jit(solution)/shard_map/ppermute | solution.py:340
  43.0 2.2 %collective-permute-start.9 = (f32[3,2048]{1,0:T(4,128)S(1)}, f32[3,2048]{1,0:T(4,128)S(1)}, u32[]{:S(2)}, u32[]{:S(2)}) collective-permute-start(f32[3,2048]{1,0:T(4,128)S(1)} %get-tuple-element.110), channel_id=1, source_target_pairs={{0,3},{1,0},{2,1},{3,2},{4,7},{5,4},{6,5},{7,6},{8,11},{9,8},{10,9... | collective-permute-start | bytes 73736 | tf_op jit(solution)/shard_map/ppermute | solution.py:340
  45.9 4.9 %shard_map.60.rest_11_ = bf16[512,2048]{1,0:T(8,128)(2,1)} custom-call(f32[2048,512]{1,0:T(8,128)} %get-tuple-element.49.raw_ref, f32[1,2048]{1,0:T(1,128)} %copy-done.5), custom_call_target="tpu_custom_call" | custom-call | flops 1000000000 | bytes 3690000 | tf_op jit(solution)/shard_map/pallas_call | solution.py:228
  57.9 12.2 %shard_map.61.rest_4_ = bf16[4,1024,128]{2,1,0:T(8,128)(2,1)} custom-call(s32[2,1024]{1,0:T(2,128)} %broadcast_multiply_fusion.2.pairs_ref, f32[4,128]{1,0:T(4,128)} %pad_maximum_fusion.4.scale_ref, s16[3,1500,128]{2,1,0:T(8,128)(2,1)} %copy-done.1, s16[3,1500,128]{2,1,0:T(8,128)(2,1)} %copy-done, s16[3,1500,128]{2,1,0:T(8,128)(2,1)} %copy-done.4, ...), custom_call_target="tpu_custom_call" | custom-call | flops 1000000000 | bytes 3690000 | tf_op jit(solution)/shard_map/pallas_call | solution.py:208
  71.4 5.6 %collective-permute-start.14 = (bf16[4,1024,128]{2,1,0:T(8,128)(2,1)}, bf16[4,1024,128]{2,1,0:T(8,128)(2,1)}, u32[]{:S(2)}, u32[]{:S(2)}) collective-permute-start(bf16[4,1024,128]{2,1,0:T(8,128)(2,1)} %shard_map.61.rest_4_), channel_id=1, source_target_pairs={{0,1},{1,2},{2,3},{4,5},{5,6},{6,7},{8,9},{9,10},{10,11},{12,13},{... | collective-permute-start | bytes 3145736 | tf_op jit(solution)/shard_map/ppermute | solution.py:344
  79.3 14.6 %shard_map.62 = bf16[2048,512]{1,0:T(8,128)(2,1)} custom-call(s32[2,2048]{1,0:T(2,128)} %get-tuple-element.108.pairs_ref, f32[4,128]{1,0:T(4,128)} %bitcast.26, s32[24000,128]{1,0:T(8,128)} %get-tuple-element.70.rest_0_, f32[1,2048]{1,0:T(1,128)} %get-tuple-element.106.rest_1_), custom_call_target="tpu_custom_call" | custom-call | flops 1000000000 | bytes 3690000 | tf_op jit(solution)/shard_map/pallas_call | solution.py:208
  95.1 2.4 %collective-permute-done.15.rest_6_ = bf16[4,1024,128]{2,1,0:T(8,128)(2,1)S(1)} collective-permute-done((bf16[4,1024,128]{2,1,0:T(8,128)(2,1)}, bf16[4,1024,128]{2,1,0:T(8,128)(2,1)S(1)}, u32[]{:S(2)}, u32[]{:S(2)}) %collective-permute-start.15) | collective-permute-done | bytes 1048608 | tf_op jit(solution)/shard_map/ppermute | solution.py:345
  98.7 2.6 %constant_dynamic-slice_fusion = (bf16[1024,512]{1,0:T(8,128)(2,1)S(1)}, bf16[1024,512]{1,0:T(8,128)(2,1)}) fusion(bf16[2048,512]{1,0:T(8,128)(2,1)} %shard_map.62, s32[]{:T(128)S(6)} %select_n.99, s32[]{:T(128)S(6)} %select_n.91), kind=kLoop, calls=%fused_computation.32 | loop fusion | bytes 4194312 | tf_op jit(solution)/shard_map/dynamic_slice | solution.py:417
  101.4 2.6 %collective-permute-done.19.rest_1_ = bf16[1024,512]{1,0:T(8,128)(2,1)S(1)} collective-permute-done((bf16[1024,512]{1,0:T(8,128)(2,1)S(1)}, bf16[1024,512]{1,0:T(8,128)(2,1)S(1)}, u32[]{:S(2)}, u32[]{:S(2)}) %collective-permute-start.19) | collective-permute-done | bytes 1048608 | tf_op jit(solution)/shard_map/ppermute | solution.py:329
  105.0 1.8 broadcast_select_fusion
  112.5 14.6 %shard_map.63 = bf16[2048,512]{1,0:T(8,128)(2,1)} custom-call(s32[2,2048]{1,0:T(2,128)} %broadcast_multiply_fusion.pairs_ref, f32[4,128]{1,0:T(4,128)} %bitcast.27, s32[24000,128]{1,0:T(8,128)} %get-tuple-element.70.rest_0_, f32[1,2048]{1,0:T(1,128)} %get-tuple-element.105.rest_1_), custom_call_target="tpu_custom_call" | custom-call | flops 1000000000 | bytes 3690000 | tf_op jit(solution)/shard_map/pallas_call | solution.py:208
  127.2 13.8 %collective-permute-done.24.rest_8_ = bf16[4,1024,128]{2,1,0:T(8,128)(2,1)} collective-permute-done((bf16[4,1024,128]{2,1,0:T(8,128)(2,1)S(1)}, bf16[4,1024,128]{2,1,0:T(8,128)(2,1)}, u32[]{:S(2)}, u32[]{:S(2)}) %collective-permute-start.24) | collective-permute-done | bytes 1048608 | tf_op jit(solution)/shard_map/ppermute | solution.py:345
  141.1 2.4 %fusion.4 = (bf16[1024,512]{1,0:T(8,128)(2,1)S(1)}, bf16[1024,512]{1,0:T(8,128)(2,1)S(1)}) fusion(bf16[2048,512]{1,0:T(8,128)(2,1)} %shard_map.63), kind=kLoop, calls=%fused_computation.43 | loop fusion | bytes 4194304 | tf_op jit(solution)/shard_map/slice | solution.py:430
  147.4 21.0 %collective-permute-done.26.rest_3_ = bf16[1024,512]{1,0:T(8,128)(2,1)S(1)} collective-permute-done((bf16[1024,512]{1,0:T(8,128)(2,1)S(1)}, bf16[1024,512]{1,0:T(8,128)(2,1)S(1)}, u32[]{:S(2)}, u32[]{:S(2)}) %collective-permute-start.26) | collective-permute-done | bytes 1048608 | tf_op jit(solution)/shard_map/ppermute | solution.py:329
  169.7 1.9 collective-permute-done.28.rest_10_
  174.1 46.0 %shard_map.64 = (f32[1024,2048]{1,0:T(8,128)}, f32[1024,2048]{1,0:T(8,128)}) custom-call(s32[2]{0:T(128)} %pad_add_fusion.place_ref, f32[8,4,1,128]{3,2,1,0:T(1,128)} %fusion.1.mask_ref, f32[2]{0:T(128)} %pad_maximum_fusion.5.factors_ref, bf16[1024,512]{1,0:T(8,128)(2,1)} %get-tuple-element.77.rest_0_, bf16[1024,512]{1,0:T(8,128)(2,1)} %copy-done.12, ...), custom_call_target="tpu_custom_call" | custom-call | flops 24000000000 | bytes 88560000 | tf_op jit(solution)/shard_map/pallas_call | solution.py:303
  (111 shorter events, 34.9 us)
Async XLA Ops:
  2.5 28.3 %collective-permute-start.11 = (s16[3,1500,128]{2,1,0:T(8,128)(2,1)S(1)}, s16[3,1500,128]{2,1,0:T(8,128)(2,1)S(1)}, u32[]{:S(2)}, u32[]{:S(2)}) collective-permute-start(s16[3,1500,128]{2,1,0:T(8,128)(2,1)S(1)} %fusion), channel_id=1, source_target_pairs={{0,20},{4,16},{8,28},{12,24},{16,4},{20,0},{24,12},{28,8},{1,21},{... | collective-permute-start | bytes 3456008 | tf_op jit(solution)/shard_map/ppermute | solution.py:329
  4.9 28.3 %collective-permute-start.10 = (s16[3,1500,128]{2,1,0:T(8,128)(2,1)S(1)}, s16[3,1500,128]{2,1,0:T(8,128)(2,1)S(1)}, u32[]{:S(2)}, u32[]{:S(2)}) collective-permute-start(s16[3,1500,128]{2,1,0:T(8,128)(2,1)S(1)} %fusion), channel_id=1, source_target_pairs={{0,12},{4,8},{8,4},{12,0},{16,28},{20,24},{24,20},{28,16},{1,13},{... | collective-permute-start | bytes 3456008 | tf_op jit(solution)/shard_map/ppermute | solution.py:329
  26.2 8.1 %collective-permute-start.6 = (f32[1,2560]{1,0:T(1,128)S(1)}, f32[1,2560]{1,0:T(1,128)S(1)}, u32[]{:S(2)}, u32[]{:S(2)}) collective-permute-start(f32[1,2560]{1,0:T(1,128)S(1)} %pad_maximum_fusion.3), channel_id=1, source_target_pairs={{0,28},{4,24},{8,20},{12,16},{16,12},{20,8},{24,4},{28,0},{1,29},{... | collective-permute-start | bytes 30728 | tf_op jit(solution)/shard_map/ppermute | solution.py:329
  26.3 8.5 %collective-permute-start.5 = (f32[1,2560]{1,0:T(1,128)S(1)}, f32[1,2560]{1,0:T(1,128)S(1)}, u32[]{:S(2)}, u32[]{:S(2)}) collective-permute-start(f32[1,2560]{1,0:T(1,128)S(1)} %pad_maximum_fusion.3), channel_id=1, source_target_pairs={{0,24},{4,28},{8,16},{12,20},{16,8},{20,12},{24,0},{28,4},{1,25},{... | collective-permute-start | bytes 30728 | tf_op jit(solution)/shard_map/ppermute | solution.py:329
  28.6 6.8 %collective-permute-start.4 = (f32[1,2560]{1,0:T(1,128)S(1)}, f32[1,2560]{1,0:T(1,128)}, u32[]{:S(2)}, u32[]{:S(2)}) collective-permute-start(f32[1,2560]{1,0:T(1,128)S(1)} %pad_maximum_fusion.3), channel_id=1, source_target_pairs={{0,20},{4,16},{8,28},{12,24},{16,4},{20,0},{24,12},{28,8},{1,21},{... | collective-permute-start | bytes 30728 | tf_op jit(solution)/shard_map/ppermute | solution.py:329
  35.5 16.0 %collective-permute-start.12 = (s16[3,1500,128]{2,1,0:T(8,128)(2,1)S(1)}, s16[3,1500,128]{2,1,0:T(8,128)(2,1)S(1)}, u32[]{:S(2)}, u32[]{:S(2)}) collective-permute-start(s16[3,1500,128]{2,1,0:T(8,128)(2,1)S(1)} %broadcast_select_fusion.1), channel_id=1, source_target_pairs={{0,16},{4,12},{8,24},{12,4},{16,0},{20,28},{24,8},{28,20},{1,17},{... | collective-permute-start | bytes 3456008 | tf_op jit(solution)/shard_map/ppermute | solution.py:335
  38.7 12.0 %collective-permute-start.8 = (f32[3,2048]{1,0:T(4,128)S(1)}, f32[3,2048]{1,0:T(4,128)S(1)}, u32[]{:S(2)}, u32[]{:S(2)}) collective-permute-start(f32[3,2048]{1,0:T(4,128)S(1)} %get-tuple-element.110), channel_id=1, source_target_pairs={{0,2},{1,3},{2,0},{3,1},{4,6},{5,7},{6,4},{7,5},{8,10},{9,11},{10,... | collective-permute-start | bytes 73736 | tf_op jit(solution)/shard_map/ppermute | solution.py:340
  41.4 9.3 %collective-permute-start.7 = (f32[3,2048]{1,0:T(4,128)S(1)}, f32[3,2048]{1,0:T(4,128)S(1)}, u32[]{:S(2)}, u32[]{:S(2)}) collective-permute-start(f32[3,2048]{1,0:T(4,128)S(1)} %get-tuple-element.110), channel_id=1, source_target_pairs={{0,1},{1,2},{2,3},{3,0},{4,5},{5,6},{6,7},{7,4},{8,9},{9,10},{10,1... | collective-permute-start | bytes 73736 | tf_op jit(solution)/shard_map/ppermute | solution.py:340
  43.0 7.8 %collective-permute-start.9 = (f32[3,2048]{1,0:T(4,128)S(1)}, f32[3,2048]{1,0:T(4,128)S(1)}, u32[]{:S(2)}, u32[]{:S(2)}) collective-permute-start(f32[3,2048]{1,0:T(4,128)S(1)} %get-tuple-element.110), channel_id=1, source_target_pairs={{0,3},{1,0},{2,1},{3,2},{4,7},{5,4},{6,5},{7,6},{8,11},{9,8},{10,9... | collective-permute-start | bytes 73736 | tf_op jit(solution)/shard_map/ppermute | solution.py:340
  51.5 49.9 %collective-permute-start.18 = (bf16[512,2048]{1,0:T(8,128)(2,1)}, bf16[512,2048]{1,0:T(8,128)(2,1)S(1)}, u32[]{:S(2)}, u32[]{:S(2)}) collective-permute-start(bf16[512,2048]{1,0:T(8,128)(2,1)} %shard_map.60.rest_11_), channel_id=1, source_target_pairs={{0,16},{4,20},{8,24},{12,28},{16,0},{20,4},{24,8},{28,12},{1,17},{... | collective-permute-start | bytes 6291464 | tf_op jit(solution)/shard_map/ppermute | solution.py:329
  51.9 49.5 %collective-permute-start.17 = (bf16[512,2048]{1,0:T(8,128)(2,1)}, bf16[512,2048]{1,0:T(8,128)(2,1)}, u32[]{:S(2)}, u32[]{:S(2)}) collective-permute-start(bf16[512,2048]{1,0:T(8,128)(2,1)} %shard_map.60.rest_11_), channel_id=1, source_target_pairs={{0,8},{4,12},{8,0},{12,4},{16,24},{20,28},{24,16},{28,20},{1,9},{5... | collective-permute-start | bytes 6291464 | tf_op jit(solution)/shard_map/ppermute | solution.py:329
  70.1 27.3 %collective-permute-start.15 = (bf16[4,1024,128]{2,1,0:T(8,128)(2,1)}, bf16[4,1024,128]{2,1,0:T(8,128)(2,1)S(1)}, u32[]{:S(2)}, u32[]{:S(2)}) collective-permute-start(bf16[4,1024,128]{2,1,0:T(8,128)(2,1)} %shard_map.61.rest_4_), channel_id=1, source_target_pairs={{1,0},{2,1},{3,2},{5,4},{6,5},{7,6},{9,8},{10,9},{11,10},{13,12},{... | collective-permute-start | bytes 3145736 | tf_op jit(solution)/shard_map/ppermute | solution.py:345
  71.4 27.3 %collective-permute-start.14 = (bf16[4,1024,128]{2,1,0:T(8,128)(2,1)}, bf16[4,1024,128]{2,1,0:T(8,128)(2,1)}, u32[]{:S(2)}, u32[]{:S(2)}) collective-permute-start(bf16[4,1024,128]{2,1,0:T(8,128)(2,1)} %shard_map.61.rest_4_), channel_id=1, source_target_pairs={{0,1},{1,2},{2,3},{4,5},{5,6},{6,7},{8,9},{9,10},{10,11},{12,13},{... | collective-permute-start | bytes 3145736 | tf_op jit(solution)/shard_map/ppermute | solution.py:344
  77.2 26.9 %collective-permute-start.16 = (bf16[512,2048]{1,0:T(8,128)(2,1)}, bf16[512,2048]{1,0:T(8,128)(2,1)}, u32[]{:S(2)}, u32[]{:S(2)}) collective-permute-start(bf16[512,2048]{1,0:T(8,128)(2,1)} %shard_map.60.rest_11_), channel_id=1, source_target_pairs={{0,4},{4,0},{8,12},{12,8},{16,20},{20,16},{24,28},{28,24},{1,5},{5... | collective-permute-start | bytes 6291464 | tf_op jit(solution)/shard_map/ppermute | solution.py:329
  106.9 34.1 %collective-permute-start.22 = (bf16[512,2048]{1,0:T(8,128)(2,1)S(1)}, bf16[512,2048]{1,0:T(8,128)(2,1)S(1)}, u32[]{:S(2)}, u32[]{:S(2)}) collective-permute-start(bf16[512,2048]{1,0:T(8,128)(2,1)S(1)} %broadcast_select_fusion), channel_id=1, source_target_pairs={{0,16},{4,12},{8,24},{12,4},{16,0},{20,28},{24,8},{28,20},{1,17},{... | collective-permute-start | bytes 6291464 | tf_op jit(solution)/shard_map/ppermute | solution.py:335
  108.5 32.5 %collective-permute-start.20 = (bf16[512,2048]{1,0:T(8,128)(2,1)}, bf16[512,2048]{1,0:T(8,128)(2,1)}, u32[]{:S(2)}, u32[]{:S(2)}) collective-permute-start(bf16[512,2048]{1,0:T(8,128)(2,1)} %collective-permute-done.17.rest_13_), channel_id=1, source_target_pairs={{0,4},{4,0},{8,12},{12,8},{16,20},{20,16},{24,28},{28,24},{1,5},{5... | collective-permute-start | bytes 6291464 | tf_op jit(solution)/shard_map/ppermute | solution.py:329
  108.5 32.5 %collective-permute-start.21 = (bf16[512,2048]{1,0:T(8,128)(2,1)S(1)}, bf16[512,2048]{1,0:T(8,128)(2,1)}, u32[]{:S(2)}, u32[]{:S(2)}) collective-permute-start(bf16[512,2048]{1,0:T(8,128)(2,1)S(1)} %collective-permute-done.18.rest_15_), channel_id=1, source_target_pairs={{0,4},{4,0},{8,12},{12,8},{16,20},{20,16},{24,28},{28,24},{1,5},{5... | collective-permute-start | bytes 6291464 | tf_op jit(solution)/shard_map/ppermute | solution.py:329
  109.0 18.2 %collective-permute-start.23 = (bf16[4,1024,128]{2,1,0:T(8,128)(2,1)}, bf16[4,1024,128]{2,1,0:T(8,128)(2,1)}, u32[]{:S(2)}, u32[]{:S(2)}) collective-permute-start(bf16[4,1024,128]{2,1,0:T(8,128)(2,1)} %collective-permute-done.14.rest_5_), channel_id=1, source_target_pairs={{1,2},{2,3},{5,6},{6,7},{9,10},{10,11},{13,14},{14,15},{17,18},{18... | collective-permute-start | bytes 3145736 | tf_op jit(solution)/shard_map/ppermute | solution.py:344
  110.6 30.3 %collective-permute-start.24 = (bf16[4,1024,128]{2,1,0:T(8,128)(2,1)S(1)}, bf16[4,1024,128]{2,1,0:T(8,128)(2,1)}, u32[]{:S(2)}, u32[]{:S(2)}) collective-permute-start(bf16[4,1024,128]{2,1,0:T(8,128)(2,1)S(1)} %collective-permute-done.15.rest_6_), channel_id=1, source_target_pairs={{1,0},{2,1},{5,4},{6,5},{9,8},{10,9},{13,12},{14,13},{17,16},{18,1... | collective-permute-start | bytes 3145736 | tf_op jit(solution)/shard_map/ppermute | solution.py:345
  141.0 31.7 %collective-permute-start.29 = (bf16[512,2048]{1,0:T(8,128)(2,1)S(1)}, bf16[512,2048]{1,0:T(8,128)(2,1)S(1)}, u32[]{:S(2)}, u32[]{:S(2)}) collective-permute-start(bf16[512,2048]{1,0:T(8,128)(2,1)S(1)} %collective-permute-done.22.rest_17_), channel_id=1, source_target_pairs={{0,4},{4,0},{8,12},{12,8},{16,20},{20,16},{24,28},{28,24},{1,5},{5... | collective-permute-start | bytes 6291464 | tf_op jit(solution)/shard_map/ppermute | solution.py:329
  143.4 25.0 %collective-permute-start.26 = (bf16[1024,512]{1,0:T(8,128)(2,1)S(1)}, bf16[1024,512]{1,0:T(8,128)(2,1)S(1)}, u32[]{:S(2)}, u32[]{:S(2)}) collective-permute-start(bf16[1024,512]{1,0:T(8,128)(2,1)S(1)} %get-tuple-element.98), channel_id=1, source_target_pairs={{0,16},{4,20},{8,24},{12,28},{16,0},{20,4},{24,8},{28,12},{1,17},{... | collective-permute-start | bytes 3145736 | tf_op jit(solution)/shard_map/ppermute | solution.py:329
  144.0 24.6 %collective-permute-start.25 = (bf16[1024,512]{1,0:T(8,128)(2,1)S(1)}, bf16[1024,512]{1,0:T(8,128)(2,1)S(1)}, u32[]{:S(2)}, u32[]{:S(2)}) collective-permute-start(bf16[1024,512]{1,0:T(8,128)(2,1)S(1)} %get-tuple-element.99), channel_id=1, source_target_pairs={{0,8},{4,12},{8,0},{12,4},{16,24},{20,28},{24,16},{28,20},{1,9},{5... | collective-permute-start | bytes 3145736 | tf_op jit(solution)/shard_map/ppermute | solution.py:329
  144.5 24.1 %collective-permute-start.27 = (bf16[4,1024,128]{2,1,0:T(8,128)(2,1)}, bf16[4,1024,128]{2,1,0:T(8,128)(2,1)S(1)}, u32[]{:S(2)}, u32[]{:S(2)}) collective-permute-start(bf16[4,1024,128]{2,1,0:T(8,128)(2,1)} %collective-permute-done.23.rest_7_), channel_id=1, source_target_pairs={{2,3},{6,7},{10,11},{14,15},{18,19},{22,23},{26,27},{30,31}} | collective-permute-start | bytes 3145736 | tf_op jit(solution)/shard_map/ppermute | solution.py:344
  145.2 26.4 %collective-permute-start.28 = (bf16[4,1024,128]{2,1,0:T(8,128)(2,1)}, bf16[4,1024,128]{2,1,0:T(8,128)(2,1)S(1)}, u32[]{:S(2)}, u32[]{:S(2)}) collective-permute-start(bf16[4,1024,128]{2,1,0:T(8,128)(2,1)} %collective-permute-done.24.rest_8_), channel_id=1, source_target_pairs={{1,0},{5,4},{9,8},{13,12},{17,16},{21,20},{25,24},{29,28}} | collective-permute-start | bytes 3145736 | tf_op jit(solution)/shard_map/ppermute | solution.py:345
  (24 other events, 161.6 us)

commit v7 on v6

--- a/solution.py
+++ b/solution.py
@@ -10,8 +10,9 @@
 LAG = 384
 CHUNK = 128
 VMEM_LIMIT = 56 * 1024 * 1024
-NEAR = (0, 1, 2, 4)
+LATE = (2, 4)
 FAR = (3, 5, 6, 7)
+EARLY = (0, 1) + FAR
 
 
 def contact_values(coords, frame_scale, pairs):
@@ -239,43 +240,52 @@
     )(raw, mean)
 
 
-def product_kernel(place_ref, mask_ref, factors_ref, *rest):
-    near_refs, rest = rest[: len(NEAR)], rest[len(NEAR) :]
-    far_refs, rest = rest[:7], rest[7:]
-    cols_refs, rest = rest[:8], rest[8:]
-    same_ref, cross_ref, left, near_held, far_held, arrived = rest
-    feats = same_ref.shape[0]
+def fetch(sources, held, arrived):
+    copies = [pltpu.make_async_copy(ref, held.at[n], arrived.at[n]) for n, ref in enumerate(sources)]
+    for copy in copies:
+        copy.start()
+    return copies
+
+
+def multiply(left, right, ahead, rows=512):
+    feats = left.shape[1]
+    for m in range(0, feats, rows):
+        here = slice(m, m + rows)
+        same = jnp.dot(left[0, here, :], right, preferred_element_type=jnp.float32)
+        cross = jnp.dot(left[1, here, :], ahead, preferred_element_type=jnp.float32)
+        yield here, same, cross
+
+
+def first_product_kernel(place_ref, mask_ref, *rest):
+    rows_refs, cols_refs = rest[:7], rest[7:15]
+    same_ref, cross_ref, left, right, ahead, near_held, far_held, near_arrived, far_arrived = rest[15:]
     frames = cols_refs[0].shape[0]
     parts = frames // CHUNK
+    kept = frames - LAG
     me, z = place_ref[0], place_ref[1]
 
     def put(d, c, value):
-        j = me ^ d
-        after = me ^ lax.rem(j + 1, 8)
-        mask = mask_ref[j, c].astype(jnp.bfloat16)
-        at = pl.multiple_of(d * frames + c * CHUNK, CHUNK)
-        left[0:feats, pl.ds(at, CHUNK)] = value
-        to = c + LAG // CHUNK
-        at = jnp.where(to < parts, d * frames + to * CHUNK, after * frames + (to - parts) * CHUNK)
-        left[feats : 2 * feats, pl.ds(pl.multiple_of(at, CHUNK), CHUNK)] = value * mask
+        at = pl.multiple_of(EARLY.index(d) * frames + c * CHUNK, CHUNK)
+        left[0, :, pl.ds(at, CHUNK)] = value
+        left[1, :, pl.ds(at, CHUNK)] = value * mask_ref[me ^ d, c].astype(jnp.bfloat16)
 
     @pl.when(pl.program_id(0) == 0)
     def _():
-        copies = [
-            pltpu.make_async_copy(ref, near_held.at[n], arrived.at[n]) for n, ref in enumerate(near_refs)
-        ]
-        copies += [
-            pltpu.make_async_copy(ref, far_held.at[n], arrived.at[len(NEAR) + n])
-            for n, ref in enumerate(far_refs)
-        ]
-        for copy in copies:
-            copy.start()
-        for n, d in enumerate(NEAR):
-            copies[n].wait()
+        near = fetch(rows_refs[:2], near_held, near_arrived)
+        far = fetch(rows_refs[2:], far_held, far_arrived)
+        ahead[...] = jnp.zeros_like(ahead)
+
+        @pl.when((z == 0) | (z == parts - 1))
+        def _():
+            for d in FAR:
+                put(d, parts - 1 - z, jnp.zeros((left.shape[1], CHUNK), jnp.bfloat16))
+
+        for d in range(2):
+            near[d].wait()
             for c in range(parts):
-                put(d, c, near_held[n, :, c * CHUNK : (c + 1) * CHUNK])
-        for n in range(len(far_refs)):
-            copies[len(NEAR) + n].wait()
+                put(d, c, near_held[d, :, c * CHUNK : (c + 1) * CHUNK])
+        for n, copy in enumerate(far):
+            copy.wait()
             hop = (n + 1) // 2
             c = z - hop if n % 2 else z + hop
 
@@ -284,42 +294,115 @@
                 for i, d in enumerate(FAR):
                     put(d, c, far_held[n, i])
 
-    right = jnp.concatenate([ref[...] for ref in cols_refs], axis=0)
-    for m in range(0, feats, 512):
-        here = slice(m, m + 512)
-        same = jnp.dot(left[here, :], right, preferred_element_type=jnp.float32)
-        same_ref[here, :] = same * factors_ref[0]
-    for m in range(0, feats, 512):
-        here = slice(m, m + 512)
-        cross = jnp.dot(left[feats + m : feats + m + 512, :], right, preferred_element_type=jnp.float32)
-        cross_ref[here, :] = cross / factors_ref[1]
-
-
-def products(place, mask, factors, near, far, cols, block=256):
+    for s, d in enumerate(EARLY):
+        right[s * frames : (s + 1) * frames, :] = cols_refs[d][...]
+        ahead[s * frames : s * frames + kept, :] = cols_refs[d][LAG:, :]
+    for d in range(8):
+        j = me ^ d
+        before = me ^ (j - 1)
+        for s, e in enumerate(EARLY):
+
+            @pl.when((j > 0) & (before == e))
+            def _():
+                ahead[s * frames + kept : (s + 1) * frames, :] = cols_refs[d][:LAG, :]
+
+    for here, same, cross in multiply(left, right[...], ahead[...]):
+        same_ref[here, :] = same
+        cross_ref[here, :] = cross
+
+
+def second_product_kernel(place_ref, mask_ref, factors_ref, *rest):
+    rows_refs, cols_refs, sums_refs = rest[:4], rest[4:12], rest[12:14]
+    same_ref, cross_ref, left, right, ahead, near_held, far_held, near_arrived, far_arrived = rest[14:]
+    frames = cols_refs[0].shape[0]
+    parts = frames // CHUNK
+    kept = frames - LAG
+    me, z = place_ref[0], place_ref[1]
+    quarter = jnp.where(z == 0, parts - 1, 0)
+    base = len(LATE) * frames
+
+    def put(at, d, c, value):
+        left[0, :, at : at + CHUNK] = value
+        left[1, :, at : at + CHUNK] = value * mask_ref[me ^ d, c].astype(jnp.bfloat16)
+
+    @pl.when(pl.program_id(0) == 0)
+    def _():
+        near = fetch(rows_refs[:2], near_held, near_arrived)
+        far = fetch(rows_refs[2:], far_held, far_arrived)
+        ahead[...] = jnp.zeros_like(ahead)
+        for s, d in enumerate(LATE):
+            near[s].wait()
+            for c in range(parts):
+                put(s * frames + c * CHUNK, d, c, near_held[s, :, c * CHUNK : (c + 1) * CHUNK])
+        for copy in far:
+            copy.wait()
+        for i, d in enumerate(FAR):
+            put(base + i * CHUNK, d, quarter, far_held[0, i] + far_held[1, i])
+
+    for s, d in enumerate(LATE):
+        right[s * frames : (s + 1) * frames, :] = cols_refs[d][...]
+        ahead[s * frames : s * frames + kept, :] = cols_refs[d][LAG:, :]
+    for i, d in enumerate(FAR):
+        at = slice(base + i * CHUNK, base + (i + 1) * CHUNK)
+        right[at, :] = cols_refs[d][pl.ds(pl.multiple_of(quarter * CHUNK, CHUNK), CHUNK), :]
+
+        @pl.when(quarter == 0)
+        def _():
+            ahead[at, :] = cols_refs[d][LAG:, :]
+
+    for d in range(8):
+        j = me ^ d
+        before = me ^ (j - 1)
+        for s, e in enumerate(LATE):
+
+            @pl.when((j > 0) & (before == e))
+            def _():
+                ahead[s * frames + kept : (s + 1) * frames, :] = cols_refs[d][:LAG, :]
+
+        for i, e in enumerate(FAR):
+
+            @pl.when((j > 0) & (before == e) & (quarter > 0))
+            def _():
+                at = slice(base + i * CHUNK, base + (i + 1) * CHUNK)
+                ahead[at, :] = cols_refs[d][LAG - CHUNK : LAG, :]
+
+    for here, same, cross in multiply(left, right[...], ahead[...]):
+        same_ref[here, :] = (same + sums_refs[0][here, :]) * factors_ref[0]
+        cross_ref[here, :] = (cross + sums_refs[1][here, :]) / factors_ref[1]
+
+
+def products(place, mask, near, far, cols, factors=None, sums=(), block=256):
     frames, feats = cols[0].shape
     rows = near[0].shape[0]
+    depth = len(EARLY if factors is None else LATE) * frames + (0 if factors is None else len(FAR) * CHUNK)
     out = jax.ShapeDtypeStruct((rows, feats), jnp.float32)
-    inputs = [mask, factors, *near, *far, *cols]
+    tile = pl.BlockSpec((rows, block), lambda n, s: (0, n))
+    any_spec = pl.BlockSpec(memory_space=pl.ANY)
+    last = factors is not None
+    inputs = [mask] + [factors] * last + [*near, *far, *cols, *sums]
     return pl.pallas_call(
-        product_kernel,
+        second_product_kernel if last else first_product_kernel,
         out_shape=[out, out],
         grid_spec=pltpu.PrefetchScalarGridSpec(
             num_scalar_prefetch=1,
             grid=(feats // block,),
-            in_specs=[
-                pl.BlockSpec(mask.shape, lambda n, s: (0,) * mask.ndim),
-                pl.BlockSpec(memory_space=pltpu.SMEM),
-            ]
-            + [pl.BlockSpec(memory_space=pl.ANY)] * (len(near) + len(far))
-            + [pl.BlockSpec((frames, block), lambda n, s: (0, n))] * 8,
-            out_specs=[pl.BlockSpec((rows, block), lambda n, s: (0, n))] * 2,
+            in_specs=[pl.BlockSpec(mask.shape, lambda n, s: (0,) * mask.ndim)]
+            + [pl.BlockSpec(memory_space=pltpu.SMEM)] * last
+            + [any_spec] * (len(near) + len(far))
+            + [pl.BlockSpec((frames, block), lambda n, s: (0, n))] * 8
+            + [tile] * len(sums),
+            out_specs=[tile] * 2,
             scratch_shapes=[
-                pltpu.VMEM((2 * rows, 8 * frames), jnp.bfloat16),
+                pltpu.VMEM((2, rows, depth), jnp.bfloat16),
+                pltpu.VMEM((depth, block), jnp.bfloat16),
+                pltpu.VMEM((depth, block), jnp.bfloat16),
                 pltpu.VMEM((len(near),) + near[0].shape, jnp.bfloat16),
                 pltpu.VMEM((len(far),) + far[0].shape, jnp.bfloat16),
-                pltpu.SemaphoreType.DMA((len(near) + len(far),)),
+                pltpu.SemaphoreType.DMA((len(near),)),
+                pltpu.SemaphoreType.DMA((len(far),)),
             ],
         ),
+        input_output_aliases={len(inputs) - 1 + i: i for i in range(2)} if sums else {},
         compiler_params=pltpu.CompilerParams(vmem_limit_bytes=VMEM_LIMIT),
         cost_estimate=estimate(24),
     )(place, *inputs)
@@ -424,12 +507,14 @@
     near_pairs, _ = together(out_pairs[:, :feats], own)
     near_rows = contacts("own", near_pairs, [table], scale_own, out_mean[:, :feats])
     near_rows, cols, up, down = together(near_rows, cols, up, down)
-
-    far += [up, down, *line_hop(up, down, 3, feat_count)]
     cols[7] = swap(cols[6], 1)
-    near = [own, partner, swap(near_rows[:row_feats], 2), swap(near_rows[row_feats:], 4)]
     cols = [cols[d] for d in range(8)]
-    return products(place, mask, factors, near, far, cols)
+    late = [swap(near_rows[:row_feats], 2), swap(near_rows[row_feats:], 4)]
+    far += [up, down]
+    sums = products(place, mask, [own, partner], far, cols)
+    last = line_hop(up, down, 3, feat_count)
+    sums, late, last = together(sums, late, last)
+    return products(place, mask, late, last, cols, factors, sums)
 
 
 def solution(mesh):

time: 221 us -> 220 us (level)
  waiting for transfers between devices: 49.1 us -> 26 us
  Pallas kernels: 110 us -> 132 us
    pallas_call x1 -> x2, Pallas kernels: 46 us -> 67.9 us  [products(): pl.pallas_call(second_product_kernel if last else first_product_kernel, o...]
    ppermute x19, waiting for transfers between devices: 29.1 us -> 7.91 us  [swap(): return lax.ppermute(x, 'tm', [(i, i ^ bits) for i in range(8)])]
    unnamed x36 -> x30, local copies, waits for them, and re-layouts: 4.96 us -> 3.78 us
  transfers between devices with their start and end apart: 30 -> 30, of which waited for: 12 -> 9; matrix products, arithmetic and copies ran while one was open for 7% -> 7% of each run, Pallas kernels for 29% -> 48%
where the time goes in v7:
time: 220 us; the launch traced here: 218 us
  Pallas kernels  132 us (60%)
  starting transfers between devices  36.5 us (17%)
  waiting for transfers between devices  26 us (12%)
  other arithmetic  11.7 us (5%)
  local copies, waits for them, and re-layouts  9.95 us (5%)
    pallas_call x2, Pallas kernels, products(): pl.pallas_call(second_product_kernel if last else first_product_kernel, o...  67.9 us
    pallas_call x4, Pallas kernels, contacts(): pl.pallas_call(functools.partial(gather_kernel, form, chunks, len(sources...  59.6 us
    ppermute x3, waiting for transfers between devices, line_hop(): down = lax.ppermute(down, 'feat', [(i + 1, i) for i in range(count - hop)])  16.1 us
    ppermute x19, starting transfers between devices, swap(): return lax.ppermute(x, 'tm', [(i, i ^ bits) for i in range(8)])  15.1 us
    ppermute x3, starting transfers between devices, line_hop(): lax.ppermute(up, 'feat', [(i, i + 1) for i in range(hop - 1, count - 1)])  8.84 us
    ppermute x19, waiting for transfers between devices, swap(): return lax.ppermute(x, 'tm', [(i, i ^ bits) for i in range(8)])  7.91 us
    ppermute x3, starting transfers between devices, line_gather(): lax.ppermute(x, 'feat', shift(s))  6.48 us
    pallas_call x1, Pallas kernels, center(): pl.pallas_call(center_kernel, out_shape=jax.ShapeDtypeStruct((frames, fea...  4.87 us
  transfers between devices with their start and end apart: 30, of which 9 were waited for; matrix products, arithmetic and copies ran while one was open for 7% of the time, Pallas kernels for 48%

profile of v7, /device:TPU:0, one launch (start us, length us, event | category | flops | bytes accessed | tf_op | source)
XLA Modules:
  0.0 218.3 jit_solution(17099796683141844690)
XLA Ops:
  0.6 1.8 fusion
  2.5 2.5 %collective-permute-start.11 = (s16[3,1500,128]{2,1,0:T(8,128)(2,1)S(1)}, s16[3,1500,128]{2,1,0:T(8,128)(2,1)S(1)}, u32[]{:S(2)}, u32[]{:S(2)}) collective-permute-start(s16[3,1500,128]{2,1,0:T(8,128)(2,1)S(1)} %fusion), channel_id=1, source_target_pairs={{0,20},{4,16},{8,28},{12,24},{16,4},{20,0},{24,12},{28,8},{1,21},{... | collective-permute-start | bytes 3456008 | tf_op jit(solution)/shard_map/ppermute | solution.py:412
  4.9 1.8 collective-permute-start.10
  7.3 18.1 %shard_map.59 = (f32[2048,512]{1,0:T(8,128)}, f32[1,2048]{1,0:T(1,128)}, s32[24000,128]{1,0:T(8,128)}) custom-call(s32[2,2048]{1,0:T(2,128)} %get-tuple-element.128.pairs_ref, f32[4,128]{1,0:T(4,128)} %bitcast.25, s32[3,1500,512]{2,1,0:T(8,128)} %bitcast.24), custom_call_target="tpu_custom_call" | custom-call | flops 1000000000 | bytes 3690000 | tf_op jit(solution)/shard_map/pallas_call | solution.py:209
  26.3 2.3 %collective-permute-start.5 = (f32[1,2560]{1,0:T(1,128)S(1)}, f32[1,2560]{1,0:T(1,128)S(1)}, u32[]{:S(2)}, u32[]{:S(2)}) collective-permute-start(f32[1,2560]{1,0:T(1,128)S(1)} %pad_maximum_fusion.3), channel_id=1, source_target_pairs={{0,24},{4,28},{8,16},{12,20},{16,8},{20,12},{24,0},{28,4},{1,25},{... | collective-permute-start | bytes 30728 | tf_op jit(solution)/shard_map/ppermute | solution.py:412
  30.8 2.5 %collective-permute-start.3 = (f32[1,2560]{1,0:T(1,128)S(1)}, f32[1,2560]{1,0:T(1,128)S(1)}, u32[]{:S(2)}, u32[]{:S(2)}) collective-permute-start(f32[1,2560]{1,0:T(1,128)S(1)} %pad_maximum_fusion.3), channel_id=1, source_target_pairs={{0,16},{4,20},{8,24},{12,28},{16,0},{20,4},{24,8},{28,12},{1,17},{... | collective-permute-start | bytes 30728 | tf_op jit(solution)/shard_map/ppermute | solution.py:412
  36.3 1.6 collective-permute-done.1
  38.7 2.7 %collective-permute-start.8 = (f32[3,2048]{1,0:T(4,128)S(1)}, f32[3,2048]{1,0:T(4,128)S(1)}, u32[]{:S(2)}, u32[]{:S(2)}) collective-permute-start(f32[3,2048]{1,0:T(4,128)S(1)} %get-tuple-element.126), channel_id=1, source_target_pairs={{0,2},{1,3},{2,0},{3,1},{4,6},{5,7},{6,4},{7,5},{8,10},{9,11},{10,... | collective-permute-start | bytes 73736 | tf_op jit(solution)/shard_map/ppermute | solution.py:423
  43.0 2.2 %collective-permute-start.9 = (f32[3,2048]{1,0:T(4,128)S(1)}, f32[3,2048]{1,0:T(4,128)S(1)}, u32[]{:S(2)}, u32[]{:S(2)}) collective-permute-start(f32[3,2048]{1,0:T(4,128)S(1)} %get-tuple-element.126), channel_id=1, source_target_pairs={{0,3},{1,0},{2,1},{3,2},{4,7},{5,4},{6,5},{7,6},{8,11},{9,8},{10,9... | collective-permute-start | bytes 73736 | tf_op jit(solution)/shard_map/ppermute | solution.py:423
  45.8 4.9 %shard_map.60.rest_7_.rest_4_ = bf16[512,2048]{1,0:T(8,128)(2,1)} custom-call(f32[2048,512]{1,0:T(8,128)} %get-tuple-element.57.raw_ref, f32[1,2048]{1,0:T(1,128)} %copy-done.5), custom_call_target="tpu_custom_call" | custom-call | flops 1000000000 | bytes 3690000 | tf_op jit(solution)/shard_map/pallas_call | solution.py:229
  57.9 12.3 %shard_map.61.rest_2_ = bf16[4,1024,128]{2,1,0:T(8,128)(2,1)} custom-call(s32[2,1024]{1,0:T(2,128)} %broadcast_multiply_fusion.2.pairs_ref, f32[4,128]{1,0:T(4,128)} %pad_maximum_fusion.4.scale_ref, s16[3,1500,128]{2,1,0:T(8,128)(2,1)} %copy-done.1, s16[3,1500,128]{2,1,0:T(8,128)(2,1)} %copy-done, s16[3,1500,128]{2,1,0:T(8,128)(2,1)} %copy-done.4, ...), custom_call_target="tpu_custom_call" | custom-call | flops 1000000000 | bytes 3690000 | tf_op jit(solution)/shard_map/pallas_call | solution.py:209
  71.5 5.5 %collective-permute-start.14 = (bf16[4,1024,128]{2,1,0:T(8,128)(2,1)}, bf16[4,1024,128]{2,1,0:T(8,128)(2,1)}, u32[]{:S(2)}, u32[]{:S(2)}) collective-permute-start(bf16[4,1024,128]{2,1,0:T(8,128)(2,1)} %shard_map.61.rest_2_), channel_id=1, source_target_pairs={{0,1},{1,2},{2,3},{4,5},{5,6},{6,7},{8,9},{9,10},{10,11},{12,13},{... | collective-permute-start | bytes 3145736 | tf_op jit(solution)/shard_map/ppermute | solution.py:427
  79.3 14.6 %shard_map.62 = bf16[2048,512]{1,0:T(8,128)(2,1)} custom-call(s32[2,2048]{1,0:T(2,128)} %get-tuple-element.124.pairs_ref, f32[4,128]{1,0:T(4,128)} %bitcast.26, s32[24000,128]{1,0:T(8,128)} %get-tuple-element.78.rest_0_, f32[1,2048]{1,0:T(1,128)} %get-tuple-element.122.rest_1_), custom_call_target="tpu_custom_call" | custom-call | flops 1000000000 | bytes 3690000 | tf_op jit(solution)/shard_map/pallas_call | solution.py:209
  95.1 2.3 %collective-permute-done.15.rest_4_ = bf16[4,1024,128]{2,1,0:T(8,128)(2,1)S(1)} collective-permute-done((bf16[4,1024,128]{2,1,0:T(8,128)(2,1)}, bf16[4,1024,128]{2,1,0:T(8,128)(2,1)S(1)}, u32[]{:S(2)}, u32[]{:S(2)}) %collective-permute-start.15) | collective-permute-done | bytes 1048608 | tf_op jit(solution)/shard_map/ppermute | solution.py:428
  98.8 2.7 %constant_dynamic-slice_fusion = (bf16[1024,512]{1,0:T(8,128)(2,1)S(1)}, bf16[1024,512]{1,0:T(8,128)(2,1)}) fusion(bf16[2048,512]{1,0:T(8,128)(2,1)} %shard_map.62, s32[]{:T(128)S(6)} %select_n.99, s32[]{:T(128)S(6)} %select_n.91), kind=kLoop, calls=%fused_computation.32 | loop fusion | bytes 4194312 | tf_op jit(solution)/shard_map/dynamic_slice | solution.py:500
  101.4 2.6 %collective-permute-done.19.rest_1_ = bf16[1024,512]{1,0:T(8,128)(2,1)S(1)} collective-permute-done((bf16[1024,512]{1,0:T(8,128)(2,1)S(1)}, bf16[1024,512]{1,0:T(8,128)(2,1)S(1)}, u32[]{:S(2)}, u32[]{:S(2)}) %collective-permute-start.19) | collective-permute-done | bytes 1048608 | tf_op jit(solution)/shard_map/ppermute | solution.py:412
  105.1 1.8 broadcast_select_fusion
  109.1 1.6 collective-permute-start.23
  112.6 14.6 %shard_map.63 = bf16[2048,512]{1,0:T(8,128)(2,1)} custom-call(s32[2,2048]{1,0:T(2,128)} %broadcast_multiply_fusion.pairs_ref, f32[4,128]{1,0:T(4,128)} %bitcast.27, s32[24000,128]{1,0:T(8,128)} %get-tuple-element.78.rest_0_, f32[1,2048]{1,0:T(1,128)} %get-tuple-element.121.rest_1_), custom_call_target="tpu_custom_call" | custom-call | flops 1000000000 | bytes 3690000 | tf_op jit(solution)/shard_map/pallas_call | solution.py:209
  127.3 13.8 %collective-permute-done.24.rest_6_ = bf16[4,1024,128]{2,1,0:T(8,128)(2,1)} collective-permute-done((bf16[4,1024,128]{2,1,0:T(8,128)(2,1)S(1)}, bf16[4,1024,128]{2,1,0:T(8,128)(2,1)}, u32[]{:S(2)}, u32[]{:S(2)}) %collective-permute-start.24) | collective-permute-done | bytes 1048608 | tf_op jit(solution)/shard_map/ppermute | solution.py:428
  142.0 1.7 fusion.4
  144.7 1.7 collective-permute-start.28
  149.2 40.1 %shard_map.64 = (f32[1024,2048]{1,0:T(8,128)}, f32[1024,2048]{1,0:T(8,128)}) custom-call(s32[2]{0:T(128)} %pad_add_fusion.place_ref, f32[8,4,1,128]{3,2,1,0:T(1,128)} %fusion.1.mask_ref, bf16[1024,512]{1,0:T(8,128)(2,1)} %get-tuple-element.85.rest_0_, bf16[1024,512]{1,0:T(8,128)(2,1)} %copy-done.12, bf16[4,1024,128]{2,1,0:T(8,128)(2,1)} %shard_map.61.rest_2_, ...), custom_call_target="tpu_custom_call" | custom-call | flops 24000000000 | bytes 88560000 | tf_op jit(solution)/shard_map/pallas_call | solution.py:383
  190.4 27.8 %shard_map.65 = (f32[1024,2048]{1,0:T(8,128)}, f32[1024,2048]{1,0:T(8,128)}) custom-call(s32[2]{0:T(128)} %pad_add_fusion.place_ref, f32[8,4,1,128]{3,2,1,0:T(1,128)} %fusion.1.mask_ref, f32[2]{0:T(128)} %pad_maximum_fusion.5.factors_ref, bf16[1024,512]{1,0:T(8,128)(2,1)} %collective-permute-done.26.rest_0_, ...), custom_call_target="tpu_custom_call", output_to_operand_aliasing={{0}: (15, {}), {1}: (16, {})} | custom-call | flops 24000000000 | bytes 88560000 | tf_op jit(solution)/shard_map/pallas_call | solution.py:383
  (106 shorter events, 33.1 us)
Async XLA Ops:
  2.5 28.3 %collective-permute-start.11 = (s16[3,1500,128]{2,1,0:T(8,128)(2,1)S(1)}, s16[3,1500,128]{2,1,0:T(8,128)(2,1)S(1)}, u32[]{:S(2)}, u32[]{:S(2)}) collective-permute-start(s16[3,1500,128]{2,1,0:T(8,128)(2,1)S(1)} %fusion), channel_id=1, source_target_pairs={{0,20},{4,16},{8,28},{12,24},{16,4},{20,0},{24,12},{28,8},{1,21},{... | collective-permute-start | bytes 3456008 | tf_op jit(solution)/shard_map/ppermute | solution.py:412
  4.9 28.3 %collective-permute-start.10 = (s16[3,1500,128]{2,1,0:T(8,128)(2,1)S(1)}, s16[3,1500,128]{2,1,0:T(8,128)(2,1)S(1)}, u32[]{:S(2)}, u32[]{:S(2)}) collective-permute-start(s16[3,1500,128]{2,1,0:T(8,128)(2,1)S(1)} %fusion), channel_id=1, source_target_pairs={{0,12},{4,8},{8,4},{12,0},{16,28},{20,24},{24,20},{28,16},{1,13},{... | collective-permute-start | bytes 3456008 | tf_op jit(solution)/shard_map/ppermute | solution.py:412
  26.2 8.1 %collective-permute-start.6 = (f32[1,2560]{1,0:T(1,128)S(1)}, f32[1,2560]{1,0:T(1,128)S(1)}, u32[]{:S(2)}, u32[]{:S(2)}) collective-permute-start(f32[1,2560]{1,0:T(1,128)S(1)} %pad_maximum_fusion.3), channel_id=1, source_target_pairs={{0,28},{4,24},{8,20},{12,16},{16,12},{20,8},{24,4},{28,0},{1,29},{... | collective-permute-start | bytes 30728 | tf_op jit(solution)/shard_map/ppermute | solution.py:412
  26.3 8.5 %collective-permute-start.5 = (f32[1,2560]{1,0:T(1,128)S(1)}, f32[1,2560]{1,0:T(1,128)S(1)}, u32[]{:S(2)}, u32[]{:S(2)}) collective-permute-start(f32[1,2560]{1,0:T(1,128)S(1)} %pad_maximum_fusion.3), channel_id=1, source_target_pairs={{0,24},{4,28},{8,16},{12,20},{16,8},{20,12},{24,0},{28,4},{1,25},{... | collective-permute-start | bytes 30728 | tf_op jit(solution)/shard_map/ppermute | solution.py:412
  28.6 6.8 %collective-permute-start.4 = (f32[1,2560]{1,0:T(1,128)S(1)}, f32[1,2560]{1,0:T(1,128)}, u32[]{:S(2)}, u32[]{:S(2)}) collective-permute-start(f32[1,2560]{1,0:T(1,128)S(1)} %pad_maximum_fusion.3), channel_id=1, source_target_pairs={{0,20},{4,16},{8,28},{12,24},{16,4},{20,0},{24,12},{28,8},{1,21},{... | collective-permute-start | bytes 30728 | tf_op jit(solution)/shard_map/ppermute | solution.py:412
  35.5 16.0 %collective-permute-start.12 = (s16[3,1500,128]{2,1,0:T(8,128)(2,1)S(1)}, s16[3,1500,128]{2,1,0:T(8,128)(2,1)S(1)}, u32[]{:S(2)}, u32[]{:S(2)}) collective-permute-start(s16[3,1500,128]{2,1,0:T(8,128)(2,1)S(1)} %broadcast_select_fusion.1), channel_id=1, source_target_pairs={{0,16},{4,12},{8,24},{12,4},{16,0},{20,28},{24,8},{28,20},{1,17},{... | collective-permute-start | bytes 3456008 | tf_op jit(solution)/shard_map/ppermute | solution.py:418
  38.7 12.0 %collective-permute-start.8 = (f32[3,2048]{1,0:T(4,128)S(1)}, f32[3,2048]{1,0:T(4,128)S(1)}, u32[]{:S(2)}, u32[]{:S(2)}) collective-permute-start(f32[3,2048]{1,0:T(4,128)S(1)} %get-tuple-element.126), channel_id=1, source_target_pairs={{0,2},{1,3},{2,0},{3,1},{4,6},{5,7},{6,4},{7,5},{8,10},{9,11},{10,... | collective-permute-start | bytes 73736 | tf_op jit(solution)/shard_map/ppermute | solution.py:423
  41.4 9.3 %collective-permute-start.7 = (f32[3,2048]{1,0:T(4,128)S(1)}, f32[3,2048]{1,0:T(4,128)S(1)}, u32[]{:S(2)}, u32[]{:S(2)}) collective-permute-start(f32[3,2048]{1,0:T(4,128)S(1)} %get-tuple-element.126), channel_id=1, source_target_pairs={{0,1},{1,2},{2,3},{3,0},{4,5},{5,6},{6,7},{7,4},{8,9},{9,10},{10,1... | collective-permute-start | bytes 73736 | tf_op jit(solution)/shard_map/ppermute | solution.py:423
  43.0 7.8 %collective-permute-start.9 = (f32[3,2048]{1,0:T(4,128)S(1)}, f32[3,2048]{1,0:T(4,128)S(1)}, u32[]{:S(2)}, u32[]{:S(2)}) collective-permute-start(f32[3,2048]{1,0:T(4,128)S(1)} %get-tuple-element.126), channel_id=1, source_target_pairs={{0,3},{1,0},{2,1},{3,2},{4,7},{5,4},{6,5},{7,6},{8,11},{9,8},{10,9... | collective-permute-start | bytes 73736 | tf_op jit(solution)/shard_map/ppermute | solution.py:423
  51.5 50.0 %collective-permute-start.18 = (bf16[512,2048]{1,0:T(8,128)(2,1)}, bf16[512,2048]{1,0:T(8,128)(2,1)S(1)}, u32[]{:S(2)}, u32[]{:S(2)}) collective-permute-start(bf16[512,2048]{1,0:T(8,128)(2,1)} %shard_map.60.rest_7_.rest_4_), channel_id=1, source_target_pairs={{0,16},{4,20},{8,24},{12,28},{16,0},{20,4},{24,8},{28,12},{1,17},{... | collective-permute-start | bytes 6291464 | tf_op jit(solution)/shard_map/ppermute | solution.py:412
  51.9 49.6 %collective-permute-start.17 = (bf16[512,2048]{1,0:T(8,128)(2,1)}, bf16[512,2048]{1,0:T(8,128)(2,1)}, u32[]{:S(2)}, u32[]{:S(2)}) collective-permute-start(bf16[512,2048]{1,0:T(8,128)(2,1)} %shard_map.60.rest_7_.rest_4_), channel_id=1, source_target_pairs={{0,8},{4,12},{8,0},{12,4},{16,24},{20,28},{24,16},{28,20},{1,9},{5... | collective-permute-start | bytes 6291464 | tf_op jit(solution)/shard_map/ppermute | solution.py:412
  70.2 27.3 %collective-permute-start.15 = (bf16[4,1024,128]{2,1,0:T(8,128)(2,1)}, bf16[4,1024,128]{2,1,0:T(8,128)(2,1)S(1)}, u32[]{:S(2)}, u32[]{:S(2)}) collective-permute-start(bf16[4,1024,128]{2,1,0:T(8,128)(2,1)} %shard_map.61.rest_2_), channel_id=1, source_target_pairs={{1,0},{2,1},{3,2},{5,4},{6,5},{7,6},{9,8},{10,9},{11,10},{13,12},{... | collective-permute-start | bytes 3145736 | tf_op jit(solution)/shard_map/ppermute | solution.py:428
  71.5 27.3 %collective-permute-start.14 = (bf16[4,1024,128]{2,1,0:T(8,128)(2,1)}, bf16[4,1024,128]{2,1,0:T(8,128)(2,1)}, u32[]{:S(2)}, u32[]{:S(2)}) collective-permute-start(bf16[4,1024,128]{2,1,0:T(8,128)(2,1)} %shard_map.61.rest_2_), channel_id=1, source_target_pairs={{0,1},{1,2},{2,3},{4,5},{5,6},{6,7},{8,9},{9,10},{10,11},{12,13},{... | collective-permute-start | bytes 3145736 | tf_op jit(solution)/shard_map/ppermute | solution.py:427
  77.2 26.9 %collective-permute-start.16 = (bf16[512,2048]{1,0:T(8,128)(2,1)}, bf16[512,2048]{1,0:T(8,128)(2,1)}, u32[]{:S(2)}, u32[]{:S(2)}) collective-permute-start(bf16[512,2048]{1,0:T(8,128)(2,1)} %shard_map.60.rest_7_.rest_4_), channel_id=1, source_target_pairs={{0,4},{4,0},{8,12},{12,8},{16,20},{20,16},{24,28},{28,24},{1,5},{5... | collective-permute-start | bytes 6291464 | tf_op jit(solution)/shard_map/ppermute | solution.py:412
  106.9 34.1 %collective-permute-start.22 = (bf16[512,2048]{1,0:T(8,128)(2,1)S(1)}, bf16[512,2048]{1,0:T(8,128)(2,1)S(1)}, u32[]{:S(2)}, u32[]{:S(2)}) collective-permute-start(bf16[512,2048]{1,0:T(8,128)(2,1)S(1)} %broadcast_select_fusion), channel_id=1, source_target_pairs={{0,16},{4,12},{8,24},{12,4},{16,0},{20,28},{24,8},{28,20},{1,17},{... | collective-permute-start | bytes 6291464 | tf_op jit(solution)/shard_map/ppermute | solution.py:418
  108.6 32.5 %collective-permute-start.20 = (bf16[512,2048]{1,0:T(8,128)(2,1)}, bf16[512,2048]{1,0:T(8,128)(2,1)}, u32[]{:S(2)}, u32[]{:S(2)}) collective-permute-start(bf16[512,2048]{1,0:T(8,128)(2,1)} %collective-permute-done.17.rest_9_.rest_6_), channel_id=1, source_target_pairs={{0,4},{4,0},{8,12},{12,8},{16,20},{20,16},{24,28},{28,24},{1,5},{5... | collective-permute-start | bytes 6291464 | tf_op jit(solution)/shard_map/ppermute | solution.py:412
  108.6 32.5 %collective-permute-start.21 = (bf16[512,2048]{1,0:T(8,128)(2,1)S(1)}, bf16[512,2048]{1,0:T(8,128)(2,1)}, u32[]{:S(2)}, u32[]{:S(2)}) collective-permute-start(bf16[512,2048]{1,0:T(8,128)(2,1)S(1)} %collective-permute-done.18.rest_11_.rest_8_), channel_id=1, source_target_pairs={{0,4},{4,0},{8,12},{12,8},{16,20},{20,16},{24,28},{28,24},{1,5},{5... | collective-permute-start | bytes 6291464 | tf_op jit(solution)/shard_map/ppermute | solution.py:412
  109.1 18.2 %collective-permute-start.23 = (bf16[4,1024,128]{2,1,0:T(8,128)(2,1)}, bf16[4,1024,128]{2,1,0:T(8,128)(2,1)}, u32[]{:S(2)}, u32[]{:S(2)}) collective-permute-start(bf16[4,1024,128]{2,1,0:T(8,128)(2,1)} %collective-permute-done.14.rest_3_), channel_id=1, source_target_pairs={{1,2},{2,3},{5,6},{6,7},{9,10},{10,11},{13,14},{14,15},{17,18},{18... | collective-permute-start | bytes 3145736 | tf_op jit(solution)/shard_map/ppermute | solution.py:427
  110.7 30.3 %collective-permute-start.24 = (bf16[4,1024,128]{2,1,0:T(8,128)(2,1)S(1)}, bf16[4,1024,128]{2,1,0:T(8,128)(2,1)}, u32[]{:S(2)}, u32[]{:S(2)}) collective-permute-start(bf16[4,1024,128]{2,1,0:T(8,128)(2,1)S(1)} %collective-permute-done.15.rest_4_), channel_id=1, source_target_pairs={{1,0},{2,1},{5,4},{6,5},{9,8},{10,9},{13,12},{14,13},{17,16},{18,1... | collective-permute-start | bytes 3145736 | tf_op jit(solution)/shard_map/ppermute | solution.py:428
  141.1 6.8 %collective-permute-start.25 = (bf16[512,2048]{1,0:T(8,128)(2,1)S(1)}, bf16[512,2048]{1,0:T(8,128)(2,1)S(1)}, u32[]{:S(2)}, u32[]{:S(2)}) collective-permute-start(bf16[512,2048]{1,0:T(8,128)(2,1)S(1)} %collective-permute-done.22.rest_13_.rest_10_), channel_id=1, source_target_pairs={{0,4},{4,0},{8,12},{12,8},{16,20},{20,16},{24,28},{28,24},{1,5},{5... | collective-permute-start | bytes 6291464 | tf_op jit(solution)/shard_map/ppermute | solution.py:412
  143.7 45.6 %collective-permute-start.27 = (bf16[1024,512]{1,0:T(8,128)(2,1)S(1)}, bf16[1024,512]{1,0:T(8,128)(2,1)S(1)}, u32[]{:S(2)}, u32[]{:S(2)}) collective-permute-start(bf16[1024,512]{1,0:T(8,128)(2,1)S(1)} %get-tuple-element.114), channel_id=1, source_target_pairs={{0,16},{4,20},{8,24},{12,28},{16,0},{20,4},{24,8},{28,12},{1,17},{... | collective-permute-start | bytes 3145736 | tf_op jit(solution)/shard_map/ppermute | solution.py:412
  144.2 45.1 %collective-permute-start.26 = (bf16[1024,512]{1,0:T(8,128)(2,1)S(1)}, bf16[1024,512]{1,0:T(8,128)(2,1)}, u32[]{:S(2)}, u32[]{:S(2)}) collective-permute-start(bf16[1024,512]{1,0:T(8,128)(2,1)S(1)} %get-tuple-element.115), channel_id=1, source_target_pairs={{0,8},{4,12},{8,0},{12,4},{16,24},{20,28},{24,16},{28,20},{1,9},{5... | collective-permute-start | bytes 3145736 | tf_op jit(solution)/shard_map/ppermute | solution.py:412
  144.7 44.6 %collective-permute-start.28 = (bf16[4,1024,128]{2,1,0:T(8,128)(2,1)}, bf16[4,1024,128]{2,1,0:T(8,128)(2,1)}, u32[]{:S(2)}, u32[]{:S(2)}) collective-permute-start(bf16[4,1024,128]{2,1,0:T(8,128)(2,1)} %collective-permute-done.23.rest_5_), channel_id=1, source_target_pairs={{2,3},{6,7},{10,11},{14,15},{18,19},{22,23},{26,27},{30,31}} | collective-permute-start | bytes 3145736 | tf_op jit(solution)/shard_map/ppermute | solution.py:427
  146.4 42.9 %collective-permute-start.29 = (bf16[4,1024,128]{2,1,0:T(8,128)(2,1)}, bf16[4,1024,128]{2,1,0:T(8,128)(2,1)}, u32[]{:S(2)}, u32[]{:S(2)}) collective-permute-start(bf16[4,1024,128]{2,1,0:T(8,128)(2,1)} %collective-permute-done.24.rest_6_), channel_id=1, source_target_pairs={{1,0},{5,4},{9,8},{13,12},{17,16},{21,20},{25,24},{29,28}} | collective-permute-start | bytes 3145736 | tf_op jit(solution)/shard_map/ppermute | solution.py:428
  (21 other events, 154.5 us)

commit v8 on v6

--- a/solution.py
+++ b/solution.py
@@ -12,6 +12,7 @@
 VMEM_LIMIT = 56 * 1024 * 1024
 NEAR = (0, 1, 2, 4)
 FAR = (3, 5, 6, 7)
+PIECES = 2
 
 
 def contact_values(coords, frame_scale, pairs):
@@ -213,7 +214,7 @@
         out_specs=out_specs,
         scratch_shapes=scratch,
         compiler_params=pltpu.CompilerParams(vmem_limit_bytes=VMEM_LIMIT),
-        cost_estimate=estimate(1),
+        cost_estimate=estimate(0.01),
     )(*args)
 
 
@@ -235,73 +236,69 @@
         ],
         out_specs=pl.BlockSpec((frames, block), lambda n: (0, n)),
         compiler_params=pltpu.CompilerParams(vmem_limit_bytes=VMEM_LIMIT),
-        cost_estimate=estimate(1),
+        cost_estimate=estimate(0.01),
     )(raw, mean)
 
 
-def product_kernel(place_ref, mask_ref, factors_ref, *rest):
+def product_kernel(piece, place_ref, mask_ref, factors_ref, *rest):
     near_refs, rest = rest[: len(NEAR)], rest[len(NEAR) :]
-    far_refs, rest = rest[:7], rest[7:]
-    cols_refs, rest = rest[:8], rest[8:]
-    same_ref, cross_ref, left, near_held, far_held, arrived = rest
+    far_ref, cols_refs = rest[0], rest[1:9]
+    same_ref, cross_ref, left, near_held, far_held, arrived = rest[-6:]
     feats = same_ref.shape[0]
     frames = cols_refs[0].shape[0]
     parts = frames // CHUNK
-    me, z = place_ref[0], place_ref[1]
+    me = place_ref[0]
 
     def put(d, c, value):
         j = me ^ d
         after = me ^ lax.rem(j + 1, 8)
-        mask = mask_ref[j, c].astype(jnp.bfloat16)
-        at = pl.multiple_of(d * frames + c * CHUNK, CHUNK)
-        left[0:feats, pl.ds(at, CHUNK)] = value
+        left[0:feats, d * frames + c * CHUNK : d * frames + (c + 1) * CHUNK] = value
         to = c + LAG // CHUNK
-        at = jnp.where(to < parts, d * frames + to * CHUNK, after * frames + (to - parts) * CHUNK)
-        left[feats : 2 * feats, pl.ds(pl.multiple_of(at, CHUNK), CHUNK)] = value * mask
+        if to < parts:
+            at = d * frames + to * CHUNK
+        else:
+            at = pl.multiple_of(after * frames + (to - parts) * CHUNK, CHUNK)
+        left[feats : 2 * feats, pl.ds(at, CHUNK)] = value * mask_ref[j, c].astype(jnp.bfloat16)
 
     @pl.when(pl.program_id(0) == 0)
     def _():
-        copies = [
-            pltpu.make_async_copy(ref, near_held.at[n], arrived.at[n]) for n, ref in enumerate(near_refs)
-        ]
-        copies += [
-            pltpu.make_async_copy(ref, far_held.at[n], arrived.at[len(NEAR) + n])
-            for n, ref in enumerate(far_refs)
-        ]
+        copies = []
+        for n, ref in enumerate(near_refs):
+            start = piece * feats if ref.shape[0] > feats else 0
+            copies.append(
+                pltpu.make_async_copy(ref.at[pl.ds(start, feats), :], near_held.at[n], arrived.at[n])
+            )
+        for c in range(parts):
+            copies.append(
+                pltpu.make_async_copy(far_ref.at[c], far_held.at[c], arrived.at[len(NEAR) + c])
+            )
         for copy in copies:
             copy.start()
         for n, d in enumerate(NEAR):
             copies[n].wait()
             for c in range(parts):
                 put(d, c, near_held[n, :, c * CHUNK : (c + 1) * CHUNK])
-        for n in range(len(far_refs)):
-            copies[len(NEAR) + n].wait()
-            hop = (n + 1) // 2
-            c = z - hop if n % 2 else z + hop
-
-            @pl.when((c >= 0) & (c < parts))
-            def _():
-                for i, d in enumerate(FAR):
-                    put(d, c, far_held[n, i])
+        for c in range(parts):
+            copies[len(NEAR) + c].wait()
+            for i, d in enumerate(FAR):
+                put(d, c, far_held[c, i])
 
     right = jnp.concatenate([ref[...] for ref in cols_refs], axis=0)
-    for m in range(0, feats, 512):
-        here = slice(m, m + 512)
-        same = jnp.dot(left[here, :], right, preferred_element_type=jnp.float32)
-        same_ref[here, :] = same * factors_ref[0]
-    for m in range(0, feats, 512):
-        here = slice(m, m + 512)
-        cross = jnp.dot(left[feats + m : feats + m + 512, :], right, preferred_element_type=jnp.float32)
-        cross_ref[here, :] = cross / factors_ref[1]
-
-
-def products(place, mask, factors, near, far, cols, block=256):
+    same = jnp.dot(left[0:feats, :], right, preferred_element_type=jnp.float32)
+    same_ref[...] = same * factors_ref[0]
+    cross = jnp.dot(left[feats : 2 * feats, :], right, preferred_element_type=jnp.float32)
+    cross_ref[...] = cross / factors_ref[1]
+
+
+def products(place, mask, factors, piece, near, far, cols, outs=(), block=512):
     frames, feats = cols[0].shape
-    rows = near[0].shape[0]
-    out = jax.ShapeDtypeStruct((rows, feats), jnp.float32)
-    inputs = [mask, factors, *near, *far, *cols]
+    row_feats = near[0].shape[0]
+    rows = row_feats // PIECES
+    out = jax.ShapeDtypeStruct((row_feats, feats), jnp.float32)
+    any_spec = pl.BlockSpec(memory_space=pl.ANY)
+    inputs = [mask, factors, *near, far, *cols, *outs]
     return pl.pallas_call(
-        product_kernel,
+        functools.partial(product_kernel, piece),
         out_shape=[out, out],
         grid_spec=pltpu.PrefetchScalarGridSpec(
             num_scalar_prefetch=1,
@@ -310,18 +307,20 @@
                 pl.BlockSpec(mask.shape, lambda n, s: (0,) * mask.ndim),
                 pl.BlockSpec(memory_space=pltpu.SMEM),
             ]
-            + [pl.BlockSpec(memory_space=pl.ANY)] * (len(near) + len(far))
-            + [pl.BlockSpec((frames, block), lambda n, s: (0, n))] * 8,
-            out_specs=[pl.BlockSpec((rows, block), lambda n, s: (0, n))] * 2,
+            + [any_spec] * (len(near) + 1)
+            + [pl.BlockSpec((frames, block), lambda n, s: (0, n))] * 8
+            + [any_spec] * len(outs),
+            out_specs=[pl.BlockSpec((rows, block), lambda n, s: (piece, n))] * 2,
             scratch_shapes=[
                 pltpu.VMEM((2 * rows, 8 * frames), jnp.bfloat16),
-                pltpu.VMEM((len(near),) + near[0].shape, jnp.bfloat16),
-                pltpu.VMEM((len(far),) + far[0].shape, jnp.bfloat16),
-                pltpu.SemaphoreType.DMA((len(near) + len(far),)),
+                pltpu.VMEM((len(near), rows, frames), jnp.bfloat16),
+                pltpu.VMEM(far.shape, jnp.bfloat16),
+                pltpu.SemaphoreType.DMA((len(near) + far.shape[0],)),
             ],
         ),
+        input_output_aliases={len(inputs) - 1 + i: i for i in range(len(outs))},
         compiler_params=pltpu.CompilerParams(vmem_limit_bytes=VMEM_LIMIT),
-        cost_estimate=estimate(24),
+        cost_estimate=estimate(0.01),
     )(place, *inputs)
 
 
@@ -338,12 +337,6 @@
 def line_gather(x, count):
     shift = lambda s: [(i, (i + s) % count) for i in range(count)]
     return jnp.stack([x] + [lax.ppermute(x, "feat", shift(s)) for s in range(1, count)])
-
-
-def line_hop(up, down, hop, count):
-    up = lax.ppermute(up, "feat", [(i, i + 1) for i in range(hop - 1, count - 1)])
-    down = lax.ppermute(down, "feat", [(i + 1, i) for i in range(count - hop)])
-    return up, down
 
 
 def together(*values):
@@ -403,33 +396,37 @@
     cols[1] = swap(mine, 1)
     mixed = contacts("sent", row_pairs, [quarters[d] for d in FAR], scale_of(*FAR), row_mean)
 
-    out_pairs, mixed, walker_lengths = together(out_pairs, mixed, walker_lengths)
-    up, down = line_hop(mixed, mixed, 1, feat_count)
+    rows = row_feats // PIECES
+    pieces = [mixed[:, p * rows : (p + 1) * rows] for p in range(PIECES)]
+    far = [lax.all_gather(x, "feat", axis=0, tiled=False) for x in pieces]
+
+    out_pairs, pieces, walker_lengths = together(out_pairs, pieces, walker_lengths)
     valid = walker_mask(walker_lengths, frames_all, frames_all)
     mask = valid.astype(jnp.float32).reshape(tm_count, parts, 1, CHUNK)
     npairs = jnp.sum(jnp.maximum(walker_lengths - LAG, 0)).astype(jnp.float32)
     factors = jnp.stack([jnp.float32(1.0 / frames_all), npairs])
-    chip_rows = contacts("own", out_pairs[:, feats:], [table], scale_own, out_mean[:, feats:])
-    chip_rows, mask, factors, up, down = together(chip_rows, mask, factors, up, down)
-    far = [mixed, up, down]
-
-    up, down = line_hop(up, down, 2, feat_count)
-    cut = lambda x, start: lax.dynamic_slice_in_dim(x, start, row_feats, axis=0)
-    own = cut(chip_rows, own_half)
-    partner = swap(cut(chip_rows, row_feats - own_half), 1)
-    cols, own, partner = together(cols, own, partner)
+    near_rows = contacts("own", out_pairs[:, :feats], [table], scale_own, out_mean[:, :feats])
+    chip_pairs, near_rows = together(out_pairs[:, feats:], near_rows)
+    chip_rows = contacts("own", chip_pairs, [table], scale_own, out_mean[:, feats:])
+    chip_rows, cols, near_rows, mask, factors = together(chip_rows, cols, near_rows, mask, factors)
+
     cols[6] = corner(cols[2], cols[4])
     for d in (2, 4):
         cols[d + 1] = swap(cols[d], 1)
-    near_pairs, _ = together(out_pairs[:, :feats], own)
-    near_rows = contacts("own", near_pairs, [table], scale_own, out_mean[:, :feats])
-    near_rows, cols, up, down = together(near_rows, cols, up, down)
-
-    far += [up, down, *line_hop(up, down, 3, feat_count)]
+    cut = lambda x, start, count: lax.dynamic_slice_in_dim(x, start, count, axis=0)
+    own = cut(chip_rows, own_half, row_feats)
+    partner = swap(cut(chip_rows, row_feats - own_half, row_feats), 1)
+    cols, partner, near_rows = together(cols, partner, near_rows)
+    direct = [
+        [swap(cut(near_rows, start + p * rows, rows), bit) for bit, start in ((2, 0), (4, row_feats))]
+        for p in range(PIECES)
+    ]
     cols[7] = swap(cols[6], 1)
-    near = [own, partner, swap(near_rows[:row_feats], 2), swap(near_rows[row_feats:], 4)]
     cols = [cols[d] for d in range(8)]
-    return products(place, mask, factors, near, far, cols)
+    outs = ()
+    for p in range(PIECES):
+        outs = products(place, mask, factors, p, [own, partner, *direct[p]], far[p], cols, outs)
+    return outs
 
 
 def solution(mesh):

time: 221 us -> 224 us (1.014)
  between operations: 1.73 us -> 15 us
  waiting for transfers between devices: 49.1 us -> 39 us
  starting transfers between devices: 35.6 us -> 26.9 us
  Pallas kernels: 110 us -> 116 us
    ppermute x6 -> x0, waiting for transfers between devices: 19.3 us -> none  [the longest x3 18.1 us: line_hop(): down = lax.ppermute(down, 'feat', [(i + 1, i) for i in range(count - hop)])]
    ppermute x2, waiting for transfers between devices: 0.67 us -> 16.6 us  [corner(): lax.ppermute(forwarded, 'tm', [(i, i ^ (2 if i % 2 else 4)) for i in rang...]
    ppermute x6 -> x0, starting transfers between devices: 11.9 us -> none  [the longest x3 7.9 us: line_hop(): lax.ppermute(up, 'feat', [(i, i + 1) for i in range(hop - 1, count - 1)])]
    ppermute x19 -> x21, waiting for transfers between devices: 29.1 us -> 22.3 us  [swap(): return lax.ppermute(x, 'tm', [(i, i ^ bits) for i in range(8)])]
    pallas_call x1 -> x2, Pallas kernels: 46 us -> 51.5 us  [products(): pl.pallas_call(functools.partial(product_kernel, piece), out_shape=[out,...]
    dynamic_slice x1 -> x2, local copies, waits for them, and re-layouts: 2.65 us -> 5.9 us  [shards(): lax.dynamic_slice_in_dim(x, start, count, axis=0)]
    unnamed x36 -> x28, local copies, waits for them, and re-layouts: 4.96 us -> 1.79 us
    ppermute x19 -> x21, starting transfers between devices: 15.1 us -> 18.2 us  [swap(): return lax.ppermute(x, 'tm', [(i, i ^ bits) for i in range(8)])]
  transfers between devices with their start and end apart: 30 -> 28, of which waited for: 12 -> 9; matrix products, arithmetic and copies ran while one was open for 7% -> 10% of each run, Pallas kernels for 29% -> 41%
where the time goes in v8:
time: 224 us; the launch traced here: 223 us
  Pallas kernels  116 us (52%)
  waiting for transfers between devices  39 us (17%)
  starting transfers between devices  26.9 us (12%)
  between operations  15 us (7%)
  other arithmetic  13.6 us (6%)
  local copies, waits for them, and re-layouts  11.9 us (5%)
    pallas_call x4, Pallas kernels, contacts(): pl.pallas_call(functools.partial(gather_kernel, form, chunks, len(sources...  60 us
    pallas_call x2, Pallas kernels, products(): pl.pallas_call(functools.partial(product_kernel, piece), out_shape=[out,...  51.5 us
    ppermute x21, waiting for transfers between devices, swap(): return lax.ppermute(x, 'tm', [(i, i ^ bits) for i in range(8)])  22.3 us
    ppermute x21, starting transfers between devices, swap(): return lax.ppermute(x, 'tm', [(i, i ^ bits) for i in range(8)])  18.2 us
    ppermute x2, waiting for transfers between devices, corner(): lax.ppermute(forwarded, 'tm', [(i, i ^ (2 if i % 2 else 4)) for i in rang...  16.6 us
    ppermute x3, starting transfers between devices, line_gather(): lax.ppermute(x, 'feat', shift(s))  6.48 us
    dynamic_slice x2, local copies, waits for them, and re-layouts, shards(): lax.dynamic_slice_in_dim(x, start, count, axis=0)  5.9 us
    pallas_call x1, Pallas kernels, center(): pl.pallas_call(center_kernel, out_shape=jax.ShapeDtypeStruct((frames, fea...  4.87 us
  transfers between devices with their start and end apart: 28, of which 9 were waited for; matrix products, arithmetic and copies ran while one was open for 10% of the time, Pallas kernels for 41%

profile of v8, /device:TPU:0, one launch (start us, length us, event | category | flops | bytes accessed | tf_op | source)
XLA Modules:
  0.0 222.8 jit_solution(1026081383594177893)
XLA Ops:
  7.2 1.8 fusion
  9.0 2.5 %collective-permute-start.11 = (s16[3,1500,128]{2,1,0:T(8,128)(2,1)S(1)}, s16[3,1500,128]{2,1,0:T(8,128)(2,1)S(1)}, u32[]{:S(2)}, u32[]{:S(2)}) collective-permute-start(s16[3,1500,128]{2,1,0:T(8,128)(2,1)S(1)} %fusion), channel_id=1, source_target_pairs={{0,20},{4,16},{8,28},{12,24},{16,4},{20,0},{24,12},{28,8},{1,21},{... | collective-permute-start | bytes 3456008 | tf_op jit(solution)/shard_map/ppermute | solution.py:328
  11.5 1.8 collective-permute-start.10
  13.9 18.1 %shard_map.59 = (f32[2048,512]{1,0:T(8,128)}, f32[1,2048]{1,0:T(1,128)}, s32[24000,128]{1,0:T(8,128)}) custom-call(s32[2,2048]{1,0:T(2,128)} %get-tuple-element.112.pairs_ref, f32[4,128]{1,0:T(4,128)} %bitcast.29, s32[3,1500,512]{2,1,0:T(8,128)} %bitcast.26), custom_call_target="tpu_custom_call" | custom-call | flops 10000000 | bytes 36900 | tf_op jit(solution)/shard_map/pallas_call | solution.py:209
  32.9 2.3 %collective-permute-start.5 = (f32[1,2560]{1,0:T(1,128)S(1)}, f32[1,2560]{1,0:T(1,128)S(1)}, u32[]{:S(2)}, u32[]{:S(2)}) collective-permute-start(f32[1,2560]{1,0:T(1,128)S(1)} %pad_maximum_fusion.3), channel_id=1, source_target_pairs={{0,24},{4,28},{8,16},{12,20},{16,8},{20,12},{24,0},{28,4},{1,25},{... | collective-permute-start | bytes 30728 | tf_op jit(solution)/shard_map/ppermute | solution.py:328
  35.7 1.6 collective-permute-done.11.rest_1_
  37.3 2.5 %collective-permute-start.3 = (f32[1,2560]{1,0:T(1,128)S(1)}, f32[1,2560]{1,0:T(1,128)S(1)}, u32[]{:S(2)}, u32[]{:S(2)}) collective-permute-start(f32[1,2560]{1,0:T(1,128)S(1)} %pad_maximum_fusion.3), channel_id=1, source_target_pairs={{0,16},{4,20},{8,24},{12,28},{16,0},{20,4},{24,8},{28,12},{1,17},{... | collective-permute-start | bytes 30728 | tf_op jit(solution)/shard_map/ppermute | solution.py:328
  42.9 1.6 collective-permute-done.1
  45.3 2.7 %collective-permute-start.8 = (f32[3,2048]{1,0:T(4,128)S(1)}, f32[3,2048]{1,0:T(4,128)S(1)}, u32[]{:S(2)}, u32[]{:S(2)}) collective-permute-start(f32[3,2048]{1,0:T(4,128)S(1)} %get-tuple-element.110), channel_id=1, source_target_pairs={{0,2},{1,3},{2,0},{3,1},{4,6},{5,7},{6,4},{7,5},{8,10},{9,11},{10,... | collective-permute-start | bytes 73736 | tf_op jit(solution)/shard_map/ppermute | solution.py:339
  49.5 2.2 %collective-permute-start.9 = (f32[3,2048]{1,0:T(4,128)S(1)}, f32[3,2048]{1,0:T(4,128)S(1)}, u32[]{:S(2)}, u32[]{:S(2)}) collective-permute-start(f32[3,2048]{1,0:T(4,128)S(1)} %get-tuple-element.110), channel_id=1, source_target_pairs={{0,3},{1,0},{2,1},{3,2},{4,7},{5,4},{6,5},{7,6},{8,11},{9,8},{10,9... | collective-permute-start | bytes 73736 | tf_op jit(solution)/shard_map/ppermute | solution.py:339
  52.4 4.9 %shard_map.60.rest_5_ = bf16[512,2048]{1,0:T(8,128)(2,1)} custom-call(f32[2048,512]{1,0:T(8,128)} %get-tuple-element.47.raw_ref, f32[1,2048]{1,0:T(1,128)} %copy-done.9), custom_call_target="tpu_custom_call" | custom-call | flops 10000000 | bytes 36900 | tf_op jit(solution)/shard_map/pallas_call | solution.py:229
  63.9 12.3 %shard_map.61 = bf16[4,1024,128]{2,1,0:T(8,128)(2,1)} custom-call(s32[2,1024]{1,0:T(2,128)} %broadcast_multiply_fusion.2.pairs_ref, f32[4,128]{1,0:T(4,128)} %pad_maximum_fusion.4.scale_ref, s16[3,1500,128]{2,1,0:T(8,128)(2,1)} %copy-done.3, s16[3,1500,128]{2,1,0:T(8,128)(2,1)} %copy-done.2, s16[3,1500,128]{2,1,0:T(8,128)(2,1)} %copy-done.6, ...), custom_call_target="tpu_custom_call" | custom-call | flops 10000000 | bytes 36900 | tf_op jit(solution)/shard_map/pallas_call | solution.py:209
  76.2 2.4 %fusion.5 = (bf16[4,512,128]{2,1,0:T(8,128)(2,1)}, bf16[4,512,128]{2,1,0:T(8,128)(2,1)}) fusion(bf16[4,1024,128]{2,1,0:T(8,128)(2,1)} %shard_map.61), kind=kLoop, calls=%fused_computation.44 | loop fusion | bytes 2097152 | tf_op jit(solution)/shard_map/slice | solution.py:400
  81.5 15.0 %shard_map.62 = bf16[2048,512]{1,0:T(8,128)(2,1)} custom-call(s32[2,2048]{1,0:T(2,128)} %get-tuple-element.107.pairs_ref, f32[4,128]{1,0:T(4,128)} %bitcast.30, s32[24000,128]{1,0:T(8,128)} %get-tuple-element.68.rest_0_, f32[1,2048]{1,0:T(1,128)} %get-tuple-element.106.rest_1_), custom_call_target="tpu_custom_call" | custom-call | flops 10000000 | bytes 36900 | tf_op jit(solution)/shard_map/pallas_call | solution.py:209
  97.2 14.7 %shard_map.63 = bf16[2048,512]{1,0:T(8,128)(2,1)} custom-call(s32[2,2048]{1,0:T(2,128)} %broadcast_multiply_fusion.pairs_ref, f32[4,128]{1,0:T(4,128)} %bitcast.31, s32[24000,128]{1,0:T(8,128)} %get-tuple-element.68.rest_0_, f32[1,2048]{1,0:T(1,128)} %get-tuple-element.105.rest_1_), custom_call_target="tpu_custom_call" | custom-call | flops 10000000 | bytes 36900 | tf_op jit(solution)/shard_map/pallas_call | solution.py:209
  113.2 3.9 %broadcast_select_fusion = bf16[512,2048]{1,0:T(8,128)(2,1)} fusion(bf16[512,2048]{1,0:T(8,128)(2,1)} %collective-permute-done.15.rest_7_, bf16[512,2048]{1,0:T(8,128)(2,1)S(1)} %collective-permute-done.16.rest_9_, pred[]{:T(512)S(6)} %eq.25), kind=kLoop, calls=%fused_computation.1 | loop fusion | flops 1048576 | bytes 6291457 | tf_op jit(solution)/shard_map/jit(_where)/select_n | solution.py:333
  119.1 3.0 %constant_dynamic-slice_fusion = (bf16[1024,512]{1,0:T(8,128)(2,1)}, bf16[1024,512]{1,0:T(8,128)(2,1)}) fusion(bf16[2048,512]{1,0:T(8,128)(2,1)} %shard_map.63, s32[]{:T(128)S(6)} %select_n.101, s32[]{:T(128)S(6)} %select_n.91), kind=kLoop, calls=%fused_computation.32 | loop fusion | bytes 4194312 | tf_op jit(solution)/shard_map/dynamic_slice | solution.py:416
  122.2 5.3 %collective-permute-done.20.rest_1_ = bf16[1024,512]{1,0:T(8,128)(2,1)S(1)} collective-permute-done((bf16[1024,512]{1,0:T(8,128)(2,1)}, bf16[1024,512]{1,0:T(8,128)(2,1)S(1)}, u32[]{:S(2)}, u32[]{:S(2)}) %collective-permute-start.20) | collective-permute-done | bytes 1048608 | tf_op jit(solution)/shard_map/ppermute | solution.py:328
  127.5 16.0 %collective-permute-done.19.rest_11_ = bf16[512,2048]{1,0:T(8,128)(2,1)} collective-permute-done((bf16[512,2048]{1,0:T(8,128)(2,1)}, bf16[512,2048]{1,0:T(8,128)(2,1)}, u32[]{:S(2)}, u32[]{:S(2)}) %collective-permute-start.19) | collective-permute-done | bytes 2097184 | tf_op jit(solution)/shard_map/ppermute | solution.py:334
  143.5 2.9 %fusion.4 = (bf16[512,512]{1,0:T(8,128)(2,1)}, bf16[512,512]{1,0:T(8,128)(2,1)}, bf16[512,512]{1,0:T(8,128)(2,1)}, bf16[512,512]{1,0:T(8,128)(2,1)}) fusion(bf16[2048,512]{1,0:T(8,128)(2,1)} %shard_map.62), kind=kLoop, calls=%fused_computation.43 | loop fusion | bytes 4194304 | tf_op jit(solution)/shard_map/dynamic_slice | solution.py:416
  148.6 1.8 collective-permute-start.21
  151.1 10.2 %collective-permute-done.25.rest_3_ = bf16[512,512]{1,0:T(8,128)(2,1)S(1)} collective-permute-done((bf16[512,512]{1,0:T(8,128)(2,1)}, bf16[512,512]{1,0:T(8,128)(2,1)S(1)}, u32[]{:S(2)}, u32[]{:S(2)}) %collective-permute-start.25) | collective-permute-done | bytes 524320 | tf_op jit(solution)/shard_map/ppermute | solution.py:328
  164.4 25.7 %shard_map.64 = (f32[1024,2048]{1,0:T(8,128)}, f32[1024,2048]{1,0:T(8,128)}) custom-call(s32[2]{0:T(128)} %pad_add_fusion.place_ref, f32[8,4,1,128]{3,2,1,0:T(1,128)} %fusion.1.mask_ref, f32[2]{0:T(128)} %pad_maximum_fusion.5.factors_ref, bf16[1024,512]{1,0:T(8,128)(2,1)} %get-tuple-element.99.rest_0_, bf16[1024,512]{1,0:T(8,128)(2,1)} %copy-done.4, ...), custom_call_target="tpu_custom_call" | custom-call | flops 10000000 | bytes 36900 | tf_op jit(solution)/shard_map/pallas_call | solution.py:300
  190.2 25.8 %shard_map.65 = (f32[1024,2048]{1,0:T(8,128)}, f32[1024,2048]{1,0:T(8,128)}) custom-call(s32[2]{0:T(128)} %pad_add_fusion.place_ref, f32[8,4,1,128]{3,2,1,0:T(1,128)} %fusion.1.mask_ref, f32[2]{0:T(128)} %pad_maximum_fusion.5.factors_ref, bf16[1024,512]{1,0:T(8,128)(2,1)} %get-tuple-element.99.rest_0_, ...), custom_call_target="tpu_custom_call", output_to_operand_aliasing={{0}: (16, {}), {1}: (17, {})} | custom-call | flops 10000000 | bytes 36900 | tf_op jit(solution)/shard_map/pallas_call | solution.py:300
  (103 shorter events, 26.9 us)
Async XLA Ops:
  7.2 143.9 %all-gather.7.cloned.1.call-start = ((), (), s32[]{:S(2)}) async-start(), calls=%async_computation.1 | async-start | bytes 2621440 | tf_op jit(solution)/shard_map/all_gather | solution.py:401
  9.0 28.3 %collective-permute-start.11 = (s16[3,1500,128]{2,1,0:T(8,128)(2,1)S(1)}, s16[3,1500,128]{2,1,0:T(8,128)(2,1)S(1)}, u32[]{:S(2)}, u32[]{:S(2)}) collective-permute-start(s16[3,1500,128]{2,1,0:T(8,128)(2,1)S(1)} %fusion), channel_id=1, source_target_pairs={{0,20},{4,16},{8,28},{12,24},{16,4},{20,0},{24,12},{28,8},{1,21},{... | collective-permute-start | bytes 3456008 | tf_op jit(solution)/shard_map/ppermute | solution.py:328
  11.5 28.3 %collective-permute-start.10 = (s16[3,1500,128]{2,1,0:T(8,128)(2,1)S(1)}, s16[3,1500,128]{2,1,0:T(8,128)(2,1)S(1)}, u32[]{:S(2)}, u32[]{:S(2)}) collective-permute-start(s16[3,1500,128]{2,1,0:T(8,128)(2,1)S(1)} %fusion), channel_id=1, source_target_pairs={{0,12},{4,8},{8,4},{12,0},{16,28},{20,24},{24,20},{28,16},{1,13},{... | collective-permute-start | bytes 3456008 | tf_op jit(solution)/shard_map/ppermute | solution.py:328
  32.8 8.1 %collective-permute-start.6 = (f32[1,2560]{1,0:T(1,128)S(1)}, f32[1,2560]{1,0:T(1,128)S(1)}, u32[]{:S(2)}, u32[]{:S(2)}) collective-permute-start(f32[1,2560]{1,0:T(1,128)S(1)} %pad_maximum_fusion.3), channel_id=1, source_target_pairs={{0,28},{4,24},{8,20},{12,16},{16,12},{20,8},{24,4},{28,0},{1,29},{... | collective-permute-start | bytes 30728 | tf_op jit(solution)/shard_map/ppermute | solution.py:328
  32.9 8.5 %collective-permute-start.5 = (f32[1,2560]{1,0:T(1,128)S(1)}, f32[1,2560]{1,0:T(1,128)S(1)}, u32[]{:S(2)}, u32[]{:S(2)}) collective-permute-start(f32[1,2560]{1,0:T(1,128)S(1)} %pad_maximum_fusion.3), channel_id=1, source_target_pairs={{0,24},{4,28},{8,16},{12,20},{16,8},{20,12},{24,0},{28,4},{1,25},{... | collective-permute-start | bytes 30728 | tf_op jit(solution)/shard_map/ppermute | solution.py:328
  35.2 6.8 %collective-permute-start.4 = (f32[1,2560]{1,0:T(1,128)S(1)}, f32[1,2560]{1,0:T(1,128)}, u32[]{:S(2)}, u32[]{:S(2)}) collective-permute-start(f32[1,2560]{1,0:T(1,128)S(1)} %pad_maximum_fusion.3), channel_id=1, source_target_pairs={{0,20},{4,16},{8,28},{12,24},{16,4},{20,0},{24,12},{28,8},{1,21},{... | collective-permute-start | bytes 30728 | tf_op jit(solution)/shard_map/ppermute | solution.py:328
  37.3 5.2 %collective-permute-start.3 = (f32[1,2560]{1,0:T(1,128)S(1)}, f32[1,2560]{1,0:T(1,128)S(1)}, u32[]{:S(2)}, u32[]{:S(2)}) collective-permute-start(f32[1,2560]{1,0:T(1,128)S(1)} %pad_maximum_fusion.3), channel_id=1, source_target_pairs={{0,16},{4,20},{8,24},{12,28},{16,0},{20,4},{24,8},{28,12},{1,17},{... | collective-permute-start | bytes 30728 | tf_op jit(solution)/shard_map/ppermute | solution.py:328
  42.0 16.0 %collective-permute-start.12 = (s16[3,1500,128]{2,1,0:T(8,128)(2,1)S(1)}, s16[3,1500,128]{2,1,0:T(8,128)(2,1)S(1)}, u32[]{:S(2)}, u32[]{:S(2)}) collective-permute-start(s16[3,1500,128]{2,1,0:T(8,128)(2,1)S(1)} %broadcast_select_fusion.1), channel_id=1, source_target_pairs={{0,16},{4,12},{8,24},{12,4},{16,0},{20,28},{24,8},{28,20},{1,17},{... | collective-permute-start | bytes 3456008 | tf_op jit(solution)/shard_map/ppermute | solution.py:334
  45.3 12.0 %collective-permute-start.8 = (f32[3,2048]{1,0:T(4,128)S(1)}, f32[3,2048]{1,0:T(4,128)S(1)}, u32[]{:S(2)}, u32[]{:S(2)}) collective-permute-start(f32[3,2048]{1,0:T(4,128)S(1)} %get-tuple-element.110), channel_id=1, source_target_pairs={{0,2},{1,3},{2,0},{3,1},{4,6},{5,7},{6,4},{7,5},{8,10},{9,11},{10,... | collective-permute-start | bytes 73736 | tf_op jit(solution)/shard_map/ppermute | solution.py:339
  48.0 9.3 %collective-permute-start.7 = (f32[3,2048]{1,0:T(4,128)S(1)}, f32[3,2048]{1,0:T(4,128)S(1)}, u32[]{:S(2)}, u32[]{:S(2)}) collective-permute-start(f32[3,2048]{1,0:T(4,128)S(1)} %get-tuple-element.110), channel_id=1, source_target_pairs={{0,1},{1,2},{2,3},{3,0},{4,5},{5,6},{6,7},{7,4},{8,9},{9,10},{10,1... | collective-permute-start | bytes 73736 | tf_op jit(solution)/shard_map/ppermute | solution.py:339
  49.5 7.8 %collective-permute-start.9 = (f32[3,2048]{1,0:T(4,128)S(1)}, f32[3,2048]{1,0:T(4,128)S(1)}, u32[]{:S(2)}, u32[]{:S(2)}) collective-permute-start(f32[3,2048]{1,0:T(4,128)S(1)} %get-tuple-element.110), channel_id=1, source_target_pairs={{0,3},{1,0},{2,1},{3,2},{4,7},{5,4},{6,5},{7,6},{8,11},{9,8},{10,9... | collective-permute-start | bytes 73736 | tf_op jit(solution)/shard_map/ppermute | solution.py:339
  58.0 55.1 %collective-permute-start.16 = (bf16[512,2048]{1,0:T(8,128)(2,1)}, bf16[512,2048]{1,0:T(8,128)(2,1)S(1)}, u32[]{:S(2)}, u32[]{:S(2)}) collective-permute-start(bf16[512,2048]{1,0:T(8,128)(2,1)} %shard_map.60.rest_5_), channel_id=1, source_target_pairs={{0,16},{4,20},{8,24},{12,28},{16,0},{20,4},{24,8},{28,12},{1,17},{... | collective-permute-start | bytes 6291464 | tf_op jit(solution)/shard_map/ppermute | solution.py:328
  58.4 54.7 %collective-permute-start.15 = (bf16[512,2048]{1,0:T(8,128)(2,1)}, bf16[512,2048]{1,0:T(8,128)(2,1)}, u32[]{:S(2)}, u32[]{:S(2)}) collective-permute-start(bf16[512,2048]{1,0:T(8,128)(2,1)} %shard_map.60.rest_5_), channel_id=1, source_target_pairs={{0,8},{4,12},{8,0},{12,4},{16,24},{20,28},{24,16},{28,20},{1,9},{5... | collective-permute-start | bytes 6291464 | tf_op jit(solution)/shard_map/ppermute | solution.py:328
  63.5 49.6 %collective-permute-start.14 = (bf16[512,2048]{1,0:T(8,128)(2,1)}, bf16[512,2048]{1,0:T(8,128)(2,1)}, u32[]{:S(2)}, u32[]{:S(2)}) collective-permute-start(bf16[512,2048]{1,0:T(8,128)(2,1)} %shard_map.60.rest_5_), channel_id=1, source_target_pairs={{0,4},{4,0},{8,12},{12,8},{16,20},{20,16},{24,28},{28,24},{1,5},{5... | collective-permute-start | bytes 6291464 | tf_op jit(solution)/shard_map/ppermute | solution.py:328
  78.6 111.6 %all-gather.5.cloned.1.call-start = ((), (), s32[]{:S(2)}) async-start(), calls=%async_computation | async-start | bytes 2621440 | tf_op jit(solution)/shard_map/all_gather | solution.py:401
  117.1 26.4 %collective-permute-start.19 = (bf16[512,2048]{1,0:T(8,128)(2,1)}, bf16[512,2048]{1,0:T(8,128)(2,1)}, u32[]{:S(2)}, u32[]{:S(2)}) collective-permute-start(bf16[512,2048]{1,0:T(8,128)(2,1)} %broadcast_select_fusion), channel_id=1, source_target_pairs={{0,16},{4,12},{8,24},{12,4},{16,0},{20,28},{24,8},{28,20},{1,17},{... | collective-permute-start | bytes 6291464 | tf_op jit(solution)/shard_map/ppermute | solution.py:334
  118.6 24.9 %collective-permute-start.17 = (bf16[512,2048]{1,0:T(8,128)(2,1)}, bf16[512,2048]{1,0:T(8,128)(2,1)}, u32[]{:S(2)}, u32[]{:S(2)}) collective-permute-start(bf16[512,2048]{1,0:T(8,128)(2,1)} %collective-permute-done.15.rest_7_), channel_id=1, source_target_pairs={{0,4},{4,0},{8,12},{12,8},{16,20},{20,16},{24,28},{28,24},{1,5},{5... | collective-permute-start | bytes 6291464 | tf_op jit(solution)/shard_map/ppermute | solution.py:328
  118.6 24.9 %collective-permute-start.18 = (bf16[512,2048]{1,0:T(8,128)(2,1)S(1)}, bf16[512,2048]{1,0:T(8,128)(2,1)}, u32[]{:S(2)}, u32[]{:S(2)}) collective-permute-start(bf16[512,2048]{1,0:T(8,128)(2,1)S(1)} %collective-permute-done.16.rest_9_), channel_id=1, source_target_pairs={{0,4},{4,0},{8,12},{12,8},{16,20},{20,16},{24,28},{28,24},{1,5},{5... | collective-permute-start | bytes 6291464 | tf_op jit(solution)/shard_map/ppermute | solution.py:328
  122.2 5.3 %collective-permute-start.20 = (bf16[1024,512]{1,0:T(8,128)(2,1)}, bf16[1024,512]{1,0:T(8,128)(2,1)S(1)}, u32[]{:S(2)}, u32[]{:S(2)}) collective-permute-start(bf16[1024,512]{1,0:T(8,128)(2,1)} %get-tuple-element.98), channel_id=1, source_target_pairs={{0,4},{4,0},{8,12},{12,8},{16,20},{20,16},{24,28},{28,24},{1,5},{5... | collective-permute-start | bytes 3145736 | tf_op jit(solution)/shard_map/ppermute | solution.py:328
  143.5 19.4 %collective-permute-start.23 = (bf16[512,2048]{1,0:T(8,128)(2,1)}, bf16[512,2048]{1,0:T(8,128)(2,1)S(1)}, u32[]{:S(2)}, u32[]{:S(2)}) collective-permute-start(bf16[512,2048]{1,0:T(8,128)(2,1)} %collective-permute-done.19.rest_11_), channel_id=1, source_target_pairs={{0,4},{4,0},{8,12},{12,8},{16,20},{20,16},{24,28},{28,24},{1,5},{5... | collective-permute-start | bytes 6291464 | tf_op jit(solution)/shard_map/ppermute | solution.py:328
  146.4 14.9 %collective-permute-start.25 = (bf16[512,512]{1,0:T(8,128)(2,1)}, bf16[512,512]{1,0:T(8,128)(2,1)S(1)}, u32[]{:S(2)}, u32[]{:S(2)}) collective-permute-start(bf16[512,512]{1,0:T(8,128)(2,1)} %get-tuple-element.94), channel_id=1, source_target_pairs={{0,16},{4,20},{8,24},{12,28},{16,0},{20,4},{24,8},{28,12},{1,17},{... | collective-permute-start | bytes 1572872 | tf_op jit(solution)/shard_map/ppermute | solution.py:328
  147.9 15.0 %collective-permute-start.24 = (bf16[512,512]{1,0:T(8,128)(2,1)}, bf16[512,512]{1,0:T(8,128)(2,1)S(1)}, u32[]{:S(2)}, u32[]{:S(2)}) collective-permute-start(bf16[512,512]{1,0:T(8,128)(2,1)} %get-tuple-element.95), channel_id=1, source_target_pairs={{0,8},{4,12},{8,0},{12,4},{16,24},{20,28},{24,16},{28,20},{1,9},{5... | collective-permute-start | bytes 1572872 | tf_op jit(solution)/shard_map/ppermute | solution.py:328
  148.2 41.9 %collective-permute-start.22 = (bf16[512,512]{1,0:T(8,128)(2,1)}, bf16[512,512]{1,0:T(8,128)(2,1)}, u32[]{:S(2)}, u32[]{:S(2)}) collective-permute-start(bf16[512,512]{1,0:T(8,128)(2,1)} %get-tuple-element.96), channel_id=1, source_target_pairs={{0,16},{4,20},{8,24},{12,28},{16,0},{20,4},{24,8},{28,12},{1,17},{... | collective-permute-start | bytes 1572872 | tf_op jit(solution)/shard_map/ppermute | solution.py:328
  148.6 41.6 %collective-permute-start.21 = (bf16[512,512]{1,0:T(8,128)(2,1)}, bf16[512,512]{1,0:T(8,128)(2,1)}, u32[]{:S(2)}, u32[]{:S(2)}) collective-permute-start(bf16[512,512]{1,0:T(8,128)(2,1)} %get-tuple-element.97), channel_id=1, source_target_pairs={{0,8},{4,12},{8,0},{12,4},{16,24},{20,28},{24,16},{28,20},{1,9},{5... | collective-permute-start | bytes 1572872 | tf_op jit(solution)/shard_map/ppermute | solution.py:328
  (18 other events, 132.3 us)
Sparse Core Ops, SparseCore 0:
  78.7 46.2 all-gather.6
  126.6 44.6 all-gather.4

commit v9 on v8

--- a/solution.py
+++ b/solution.py
@@ -365,18 +365,22 @@
     quarters, _ = together(quarters, sums)
     quarters[7] = corner(quarters[3], quarters[5])
     note = jnp.concatenate([sums, frame_scale.reshape(1, frames_dev)], axis=1)
-    notes = [note] + [swap(note, d) for d in range(1, 8)]
-
+    other = swap(note, 1)
+    note = jnp.concatenate([sums + other[:, :feats], note[:, feats:], other[:, feats:]], axis=1)
+    notes = [note] + [swap(note, d) for d in (2, 4, 6)]
     totals = notes[0][:, :feats]
     for other in notes[1:]:
         totals = totals + other[:, :feats]
     mean = totals / jnp.float32(frames_all)
-    scales = [lax.dynamic_slice_in_dim(n, feats + z * CHUNK, CHUNK, axis=1) for n in notes]
+    scales = [
+        lax.dynamic_slice_in_dim(notes[d // 2], feats + d % 2 * frames_dev + z * CHUNK, CHUNK, axis=1)
+        for d in range(8)
+    ]
     scale_of = lambda *d: jnp.concatenate([scales[i] for i in d], axis=0)
 
+    mine, mean = together(center(raw, mean), mean)
+    cols = {0: mine, 2: swap(mine, 2), 4: swap(mine, 4)}
     facts = line_gather(jnp.concatenate([mean, pairs.astype(jnp.float32)], axis=0), feat_count)
-    mine, facts, quarters = together(center(raw, mean), facts, quarters)
-    cols = {0: mine, 2: swap(mine, 2), 4: swap(mine, 4)}
     quarters[6] = swap(quarters[7], 1)
 
     def facts_of(i, start, count):
@@ -406,17 +410,17 @@
     npairs = jnp.sum(jnp.maximum(walker_lengths - LAG, 0)).astype(jnp.float32)
     factors = jnp.stack([jnp.float32(1.0 / frames_all), npairs])
     near_rows = contacts("own", out_pairs[:, :feats], [table], scale_own, out_mean[:, :feats])
-    chip_pairs, near_rows = together(out_pairs[:, feats:], near_rows)
-    chip_rows = contacts("own", chip_pairs, [table], scale_own, out_mean[:, feats:])
-    chip_rows, cols, near_rows, mask, factors = together(chip_rows, cols, near_rows, mask, factors)
-
+    chip_pairs = out_pairs[:, feats:]
+    cols, near_rows, mask, factors, chip_pairs = together(cols, near_rows, mask, factors, chip_pairs)
     cols[6] = corner(cols[2], cols[4])
     for d in (2, 4):
         cols[d + 1] = swap(cols[d], 1)
+    chip_rows = contacts("own", chip_pairs, [table], scale_own, out_mean[:, feats:])
+    chip_rows, cols, near_rows = together(chip_rows, cols, near_rows)
+
     cut = lambda x, start, count: lax.dynamic_slice_in_dim(x, start, count, axis=0)
     own = cut(chip_rows, own_half, row_feats)
     partner = swap(cut(chip_rows, row_feats - own_half, row_feats), 1)
-    cols, partner, near_rows = together(cols, partner, near_rows)
     direct = [
         [swap(cut(near_rows, start + p * rows, rows), bit) for bit, start in ((2, 0), (4, row_feats))]
         for p in range(PIECES)

time: 224 us -> 229 us (1.022)
  waiting for transfers between devices: 39 us -> 45.8 us
    ppermute x21 -> x18, waiting for transfers between devices: 22.3 us -> 36.2 us  [swap(): return lax.ppermute(x, 'tm', [(i, i ^ bits) for i in range(8)])]
    ppermute x2, waiting for transfers between devices: 16.6 us -> 9.55 us  [corner(): lax.ppermute(forwarded, 'tm', [(i, i ^ (2 if i % 2 else 4)) for i in rang...]
    ppermute x21 -> x18, starting transfers between devices: 18.2 us -> 16.9 us  [swap(): return lax.ppermute(x, 'tm', [(i, i ^ bits) for i in range(8)])]
  transfers between devices with their start and end apart: 28 -> 25, of which waited for: 9 -> 10; matrix products, arithmetic and copies ran while one was open for 10% -> 9% of each run, Pallas kernels for 41% -> 40%
where the time goes in v9:
time: 229 us; the launch traced here: 228 us
  Pallas kernels  116 us (51%)
  waiting for transfers between devices  45.8 us (20%)
  starting transfers between devices  26 us (11%)
  between operations  15 us (7%)
  other arithmetic  14.1 us (6%)
  local copies, waits for them, and re-layouts  10.6 us (5%)
    pallas_call x4, Pallas kernels, contacts(): pl.pallas_call(functools.partial(gather_kernel, form, chunks, len(sources...  60 us
    pallas_call x2, Pallas kernels, products(): pl.pallas_call(functools.partial(product_kernel, piece), out_shape=[out,...  51.5 us
    ppermute x18, waiting for transfers between devices, swap(): return lax.ppermute(x, 'tm', [(i, i ^ bits) for i in range(8)])  36.2 us
    ppermute x18, starting transfers between devices, swap(): return lax.ppermute(x, 'tm', [(i, i ^ bits) for i in range(8)])  16.9 us
    ppermute x2, waiting for transfers between devices, corner(): lax.ppermute(forwarded, 'tm', [(i, i ^ (2 if i % 2 else 4)) for i in rang...  9.55 us
    ppermute x3, starting transfers between devices, line_gather(): lax.ppermute(x, 'feat', shift(s))  6.48 us
    pallas_call x1, Pallas kernels, center(): pl.pallas_call(center_kernel, out_shape=jax.ShapeDtypeStruct((frames, fea...  4.94 us
  transfers between devices with their start and end apart: 25, of which 10 were waited for; matrix products, arithmetic and copies ran while one was open for 9% of the time, Pallas kernels for 40%

profile of v9, /device:TPU:0, one launch (start us, length us, event | category | flops | bytes accessed | tf_op | source)
XLA Modules:
  0.0 228.0 jit_solution(7915499802394611295)
XLA Ops:
  7.2 1.8 fusion
  9.0 2.5 %collective-permute-start.8 = (s16[3,1500,128]{2,1,0:T(8,128)(2,1)S(1)}, s16[3,1500,128]{2,1,0:T(8,128)(2,1)S(1)}, u32[]{:S(2)}, u32[]{:S(2)}) collective-permute-start(s16[3,1500,128]{2,1,0:T(8,128)(2,1)S(1)} %fusion), channel_id=1, source_target_pairs={{0,20},{4,16},{8,28},{12,24},{16,4},{20,0},{24,12},{28,8},{1,21},{... | collective-permute-start | bytes 3456008 | tf_op jit(solution)/shard_map/ppermute | solution.py:328
  11.5 1.8 collective-permute-start.7
  13.9 18.1 %shard_map.59 = (f32[2048,512]{1,0:T(8,128)}, f32[1,2048]{1,0:T(1,128)}, s32[24000,128]{1,0:T(8,128)}) custom-call(s32[2,2048]{1,0:T(2,128)} %get-tuple-element.102.pairs_ref, f32[4,128]{1,0:T(4,128)} %bitcast.29, s32[3,1500,512]{2,1,0:T(8,128)} %bitcast.26), custom_call_target="tpu_custom_call" | custom-call | flops 10000000 | bytes 36900 | tf_op jit(solution)/shard_map/pallas_call | solution.py:209
  34.7 2.7 %collective-permute-done.8.rest_1_ = s16[3,1500,128]{2,1,0:T(8,128)(2,1)S(1)} collective-permute-done((s16[3,1500,128]{2,1,0:T(8,128)(2,1)S(1)}, s16[3,1500,128]{2,1,0:T(8,128)(2,1)S(1)}, u32[]{:S(2)}, u32[]{:S(2)}) %collective-permute-start.8) | collective-permute-done | bytes 1152032 | tf_op jit(solution)/shard_map/ppermute | solution.py:328
  40.3 1.6 collective-permute-start.3
  45.1 10.3 %collective-permute-done.2 = f32[1,3072]{1,0:T(1,128)} collective-permute-done((f32[1,3072]{1,0:T(1,128)S(1)}, f32[1,3072]{1,0:T(1,128)}, u32[]{:S(2)}, u32[]{:S(2)}) %collective-permute-start.2) | collective-permute-done | bytes 12320 | tf_op jit(solution)/shard_map/ppermute | solution.py:328
  56.8 4.9 %shard_map.60.rest_5_ = bf16[512,2048]{1,0:T(8,128)(2,1)} custom-call(f32[2048,512]{1,0:T(8,128)} %get-tuple-element.42.raw_ref, f32[1,2048]{1,0:T(1,128)} %fusion.2.mean_ref), custom_call_target="tpu_custom_call" | custom-call | flops 10000000 | bytes 36900 | tf_op jit(solution)/shard_map/pallas_call | solution.py:229
  61.8 2.7 %collective-permute-start.5 = (f32[3,2048]{1,0:T(4,128)S(1)}, f32[3,2048]{1,0:T(4,128)S(1)}, u32[]{:S(2)}, u32[]{:S(2)}) collective-permute-start(f32[3,2048]{1,0:T(4,128)S(1)} %get-tuple-element.100), channel_id=1, source_target_pairs={{0,2},{1,3},{2,0},{3,1},{4,6},{5,7},{6,4},{7,5},{8,10},{9,11},{10,... | collective-permute-start | bytes 73736 | tf_op jit(solution)/shard_map/ppermute | solution.py:339
  64.4 1.6 collective-permute-start.4
  66.0 2.2 collective-permute-start.6
  70.2 1.6 collective-permute-start.12
  73.1 1.7 collective-permute-done.10.rest_2_
  75.8 12.2 %shard_map.61 = bf16[4,1024,128]{2,1,0:T(8,128)(2,1)} custom-call(s32[2,1024]{1,0:T(2,128)} %broadcast_multiply_fusion.2.pairs_ref, f32[4,128]{1,0:T(4,128)} %pad_maximum_fusion.5.scale_ref, s16[3,1500,128]{2,1,0:T(8,128)(2,1)} %copy-done.4, s16[3,1500,128]{2,1,0:T(8,128)(2,1)} %copy-done.3, s16[3,1500,128]{2,1,0:T(8,128)(2,1)} %copy-done.6, ...), custom_call_target="tpu_custom_call" | custom-call | flops 10000000 | bytes 36900 | tf_op jit(solution)/shard_map/pallas_call | solution.py:209
  88.0 2.3 %fusion.5 = (bf16[4,512,128]{2,1,0:T(8,128)(2,1)}, bf16[4,512,128]{2,1,0:T(8,128)(2,1)}) fusion(bf16[4,1024,128]{2,1,0:T(8,128)(2,1)} %shard_map.61), kind=kLoop, calls=%fused_computation.42 | loop fusion | bytes 2097152 | tf_op jit(solution)/shard_map/slice | solution.py:404
  93.7 15.0 %shard_map.62 = bf16[2048,512]{1,0:T(8,128)(2,1)} custom-call(s32[2,2048]{1,0:T(2,128)} %get-tuple-element.98.pairs_ref, f32[4,128]{1,0:T(4,128)} %bitcast.30, s32[24000,128]{1,0:T(8,128)} %get-tuple-element.61.rest_0_, f32[1,2048]{1,0:T(1,128)} %get-tuple-element.96.rest_1_), custom_call_target="tpu_custom_call" | custom-call | flops 10000000 | bytes 36900 | tf_op jit(solution)/shard_map/pallas_call | solution.py:209
  110.0 4.9 %collective-permute-done.13.rest_9_ = bf16[512,2048]{1,0:T(8,128)(2,1)S(1)} collective-permute-done((bf16[512,2048]{1,0:T(8,128)(2,1)}, bf16[512,2048]{1,0:T(8,128)(2,1)S(1)}, u32[]{:S(2)}, u32[]{:S(2)}) %collective-permute-start.13) | collective-permute-done | bytes 2097184 | tf_op jit(solution)/shard_map/ppermute | solution.py:328
  116.5 3.1 %broadcast_select_fusion = bf16[512,2048]{1,0:T(8,128)(2,1)} fusion(bf16[512,2048]{1,0:T(8,128)(2,1)} %collective-permute-done.12.rest_7_, bf16[512,2048]{1,0:T(8,128)(2,1)S(1)} %collective-permute-done.13.rest_9_, pred[]{:T(512)S(6)} %eq.25), kind=kLoop, calls=%fused_computation.1 | loop fusion | flops 1048576 | bytes 6291457 | tf_op jit(solution)/shard_map/jit(_where)/select_n | solution.py:333
  121.7 14.7 %shard_map.63 = bf16[2048,512]{1,0:T(8,128)(2,1)} custom-call(s32[2,2048]{1,0:T(2,128)} %broadcast_multiply_fusion.pairs_ref, f32[4,128]{1,0:T(4,128)} %bitcast.31, s32[24000,128]{1,0:T(8,128)} %get-tuple-element.61.rest_0_, f32[1,2048]{1,0:T(1,128)} %get-tuple-element.95.rest_1_), custom_call_target="tpu_custom_call" | custom-call | flops 10000000 | bytes 36900 | tf_op jit(solution)/shard_map/pallas_call | solution.py:209
  136.4 9.5 %collective-permute-done.16.rest_11_ = bf16[512,2048]{1,0:T(8,128)(2,1)} collective-permute-done((bf16[512,2048]{1,0:T(8,128)(2,1)}, bf16[512,2048]{1,0:T(8,128)(2,1)}, u32[]{:S(2)}, u32[]{:S(2)}) %collective-permute-start.16) | collective-permute-done | bytes 2097184 | tf_op jit(solution)/shard_map/ppermute | solution.py:334
  145.9 3.2 %constant_dynamic-slice_fusion = (bf16[1024,512]{1,0:T(8,128)(2,1)}, bf16[1024,512]{1,0:T(8,128)(2,1)}) fusion(bf16[2048,512]{1,0:T(8,128)(2,1)} %shard_map.63, s32[]{:T(128)S(6)} %select_n.104, s32[]{:T(128)S(6)} %select_n.90), kind=kLoop, calls=%fused_computation.30 | loop fusion | bytes 4194312 | tf_op jit(solution)/shard_map/dynamic_slice | solution.py:421
  154.3 11.4 %collective-permute-done.22.rest_3_ = bf16[512,512]{1,0:T(8,128)(2,1)} collective-permute-done((bf16[512,512]{1,0:T(8,128)(2,1)S(1)}, bf16[512,512]{1,0:T(8,128)(2,1)}, u32[]{:S(2)}, u32[]{:S(2)}) %collective-permute-start.22) | collective-permute-done | bytes 524320 | tf_op jit(solution)/shard_map/ppermute | solution.py:328
  169.5 25.7 %shard_map.64 = (f32[1024,2048]{1,0:T(8,128)}, f32[1024,2048]{1,0:T(8,128)}) custom-call(s32[2]{0:T(128)} %pad_add_fusion.place_ref, f32[8,4,1,128]{3,2,1,0:T(1,128)} %fusion.1.mask_ref, f32[2]{0:T(128)} %pad_maximum_fusion.6.factors_ref, bf16[1024,512]{1,0:T(8,128)(2,1)} %get-tuple-element.89.rest_0_, bf16[1024,512]{1,0:T(8,128)(2,1)} %copy-done.5, ...), custom_call_target="tpu_custom_call" | custom-call | flops 10000000 | bytes 36900 | tf_op jit(solution)/shard_map/pallas_call | solution.py:300
  195.4 25.8 %shard_map.65 = (f32[1024,2048]{1,0:T(8,128)}, f32[1024,2048]{1,0:T(8,128)}) custom-call(s32[2]{0:T(128)} %pad_add_fusion.place_ref, f32[8,4,1,128]{3,2,1,0:T(1,128)} %fusion.1.mask_ref, f32[2]{0:T(128)} %pad_maximum_fusion.6.factors_ref, bf16[1024,512]{1,0:T(8,128)(2,1)} %get-tuple-element.89.rest_0_, ...), custom_call_target="tpu_custom_call", output_to_operand_aliasing={{0}: (16, {}), {1}: (17, {})} | custom-call | flops 10000000 | bytes 36900 | tf_op jit(solution)/shard_map/pallas_call | solution.py:300
  (93 shorter events, 31.7 us)
Async XLA Ops:
  7.2 160.6 %all-gather.7.cloned.1.call-start = ((), (), s32[]{:S(2)}) async-start(), calls=%async_computation.1 | async-start | bytes 2621440 | tf_op jit(solution)/shard_map/all_gather | solution.py:405
  9.0 28.3 %collective-permute-start.8 = (s16[3,1500,128]{2,1,0:T(8,128)(2,1)S(1)}, s16[3,1500,128]{2,1,0:T(8,128)(2,1)S(1)}, u32[]{:S(2)}, u32[]{:S(2)}) collective-permute-start(s16[3,1500,128]{2,1,0:T(8,128)(2,1)S(1)} %fusion), channel_id=1, source_target_pairs={{0,20},{4,16},{8,28},{12,24},{16,4},{20,0},{24,12},{28,8},{1,21},{... | collective-permute-start | bytes 3456008 | tf_op jit(solution)/shard_map/ppermute | solution.py:328
  11.5 27.0 %collective-permute-start.7 = (s16[3,1500,128]{2,1,0:T(8,128)(2,1)S(1)}, s16[3,1500,128]{2,1,0:T(8,128)(2,1)S(1)}, u32[]{:S(2)}, u32[]{:S(2)}) collective-permute-start(s16[3,1500,128]{2,1,0:T(8,128)(2,1)S(1)} %fusion), channel_id=1, source_target_pairs={{0,12},{4,8},{8,4},{12,0},{16,28},{20,24},{24,20},{28,16},{1,13},{... | collective-permute-start | bytes 3456008 | tf_op jit(solution)/shard_map/ppermute | solution.py:328
  38.8 32.9 %collective-permute-start.9 = (s16[3,1500,128]{2,1,0:T(8,128)(2,1)S(1)}, s16[3,1500,128]{2,1,0:T(8,128)(2,1)}, u32[]{:S(2)}, u32[]{:S(2)}) collective-permute-start(s16[3,1500,128]{2,1,0:T(8,128)(2,1)S(1)} %broadcast_select_fusion.1), channel_id=1, source_target_pairs={{0,16},{4,12},{8,24},{12,4},{16,0},{20,28},{24,8},{28,20},{1,17},{... | collective-permute-start | bytes 3456008 | tf_op jit(solution)/shard_map/ppermute | solution.py:334
  40.3 4.9 %collective-permute-start.3 = (f32[1,3072]{1,0:T(1,128)S(1)}, f32[1,3072]{1,0:T(1,128)S(1)}, u32[]{:S(2)}, u32[]{:S(2)}) collective-permute-start(f32[1,3072]{1,0:T(1,128)S(1)} %pad_maximum_fusion.3), channel_id=1, source_target_pairs={{0,24},{4,28},{8,16},{12,20},{16,8},{20,12},{24,0},{28,4},{1,25},{... | collective-permute-start | bytes 36872 | tf_op jit(solution)/shard_map/ppermute | solution.py:328
  41.9 13.6 %collective-permute-start.2 = (f32[1,3072]{1,0:T(1,128)S(1)}, f32[1,3072]{1,0:T(1,128)}, u32[]{:S(2)}, u32[]{:S(2)}) collective-permute-start(f32[1,3072]{1,0:T(1,128)S(1)} %pad_maximum_fusion.3), channel_id=1, source_target_pairs={{0,16},{4,20},{8,24},{12,28},{16,0},{20,4},{24,8},{28,12},{1,17},{... | collective-permute-start | bytes 36872 | tf_op jit(solution)/shard_map/ppermute | solution.py:328
  43.3 12.2 %collective-permute-start.1 = (f32[1,3072]{1,0:T(1,128)S(1)}, f32[1,3072]{1,0:T(1,128)S(1)}, u32[]{:S(2)}, u32[]{:S(2)}) collective-permute-start(f32[1,3072]{1,0:T(1,128)S(1)} %pad_maximum_fusion.3), channel_id=1, source_target_pairs={{0,8},{4,12},{8,0},{12,4},{16,24},{20,28},{24,16},{28,20},{1,9},{5... | collective-permute-start | bytes 36872 | tf_op jit(solution)/shard_map/ppermute | solution.py:328
  61.8 8.4 %collective-permute-start.5 = (f32[3,2048]{1,0:T(4,128)S(1)}, f32[3,2048]{1,0:T(4,128)S(1)}, u32[]{:S(2)}, u32[]{:S(2)}) collective-permute-start(f32[3,2048]{1,0:T(4,128)S(1)} %get-tuple-element.100), channel_id=1, source_target_pairs={{0,2},{1,3},{2,0},{3,1},{4,6},{5,7},{6,4},{7,5},{8,10},{9,11},{10,... | collective-permute-start | bytes 73736 | tf_op jit(solution)/shard_map/ppermute | solution.py:339
  64.4 7.3 %collective-permute-start.4 = (f32[3,2048]{1,0:T(4,128)S(1)}, f32[3,2048]{1,0:T(4,128)S(1)}, u32[]{:S(2)}, u32[]{:S(2)}) collective-permute-start(f32[3,2048]{1,0:T(4,128)S(1)} %get-tuple-element.100), channel_id=1, source_target_pairs={{0,1},{1,2},{2,3},{3,0},{4,5},{5,6},{6,7},{7,4},{8,9},{9,10},{10,1... | collective-permute-start | bytes 73736 | tf_op jit(solution)/shard_map/ppermute | solution.py:339
  66.0 5.8 %collective-permute-start.6 = (f32[3,2048]{1,0:T(4,128)S(1)}, f32[3,2048]{1,0:T(4,128)S(1)}, u32[]{:S(2)}, u32[]{:S(2)}) collective-permute-start(f32[3,2048]{1,0:T(4,128)S(1)} %get-tuple-element.100), channel_id=1, source_target_pairs={{0,3},{1,0},{2,1},{3,2},{4,7},{5,4},{6,5},{7,6},{8,11},{9,8},{10,9... | collective-permute-start | bytes 73736 | tf_op jit(solution)/shard_map/ppermute | solution.py:339
  68.2 46.7 %collective-permute-start.13 = (bf16[512,2048]{1,0:T(8,128)(2,1)}, bf16[512,2048]{1,0:T(8,128)(2,1)S(1)}, u32[]{:S(2)}, u32[]{:S(2)}) collective-permute-start(bf16[512,2048]{1,0:T(8,128)(2,1)} %shard_map.60.rest_5_), channel_id=1, source_target_pairs={{0,16},{4,20},{8,24},{12,28},{16,0},{20,4},{24,8},{28,12},{1,17},{... | collective-permute-start | bytes 6291464 | tf_op jit(solution)/shard_map/ppermute | solution.py:328
  70.2 46.3 %collective-permute-start.12 = (bf16[512,2048]{1,0:T(8,128)(2,1)}, bf16[512,2048]{1,0:T(8,128)(2,1)}, u32[]{:S(2)}, u32[]{:S(2)}) collective-permute-start(bf16[512,2048]{1,0:T(8,128)(2,1)} %shard_map.60.rest_5_), channel_id=1, source_target_pairs={{0,8},{4,12},{8,0},{12,4},{16,24},{20,28},{24,16},{28,20},{1,9},{5... | collective-permute-start | bytes 6291464 | tf_op jit(solution)/shard_map/ppermute | solution.py:328
  71.7 3.0 %collective-permute-start.10 = (s16[3,1500,128]{2,1,0:T(8,128)(2,1)}, s16[3,1500,128]{2,1,0:T(8,128)(2,1)S(1)}, u32[]{:S(2)}, u32[]{:S(2)}) collective-permute-start(s16[3,1500,128]{2,1,0:T(8,128)(2,1)} %collective-permute-done.9.rest_3_), channel_id=1, source_target_pairs={{0,4},{4,0},{8,12},{12,8},{16,20},{20,16},{24,28},{28,24},{1,5},{5... | collective-permute-start | bytes 3456008 | tf_op jit(solution)/shard_map/ppermute | solution.py:328
  90.3 105.0 %all-gather.5.cloned.1.call-start = ((), (), s32[]{:S(2)}) async-start(), calls=%async_computation | async-start | bytes 2621440 | tf_op jit(solution)/shard_map/all_gather | solution.py:405
  90.6 25.9 %collective-permute-start.11 = (bf16[512,2048]{1,0:T(8,128)(2,1)}, bf16[512,2048]{1,0:T(8,128)(2,1)}, u32[]{:S(2)}, u32[]{:S(2)}) collective-permute-start(bf16[512,2048]{1,0:T(8,128)(2,1)} %shard_map.60.rest_5_), channel_id=1, source_target_pairs={{0,4},{4,0},{8,12},{12,8},{16,20},{20,16},{24,28},{28,24},{1,5},{5... | collective-permute-start | bytes 6291464 | tf_op jit(solution)/shard_map/ppermute | solution.py:328
  119.6 26.4 %collective-permute-start.16 = (bf16[512,2048]{1,0:T(8,128)(2,1)}, bf16[512,2048]{1,0:T(8,128)(2,1)}, u32[]{:S(2)}, u32[]{:S(2)}) collective-permute-start(bf16[512,2048]{1,0:T(8,128)(2,1)} %broadcast_select_fusion), channel_id=1, source_target_pairs={{0,16},{4,12},{8,24},{12,4},{16,0},{20,28},{24,8},{28,20},{1,17},{... | collective-permute-start | bytes 6291464 | tf_op jit(solution)/shard_map/ppermute | solution.py:334
  120.6 25.4 %collective-permute-start.14 = (bf16[512,2048]{1,0:T(8,128)(2,1)}, bf16[512,2048]{1,0:T(8,128)(2,1)}, u32[]{:S(2)}, u32[]{:S(2)}) collective-permute-start(bf16[512,2048]{1,0:T(8,128)(2,1)} %collective-permute-done.12.rest_7_), channel_id=1, source_target_pairs={{0,4},{4,0},{8,12},{12,8},{16,20},{20,16},{24,28},{28,24},{1,5},{5... | collective-permute-start | bytes 6291464 | tf_op jit(solution)/shard_map/ppermute | solution.py:328
  120.6 25.4 %collective-permute-start.15 = (bf16[512,2048]{1,0:T(8,128)(2,1)S(1)}, bf16[512,2048]{1,0:T(8,128)(2,1)}, u32[]{:S(2)}, u32[]{:S(2)}) collective-permute-start(bf16[512,2048]{1,0:T(8,128)(2,1)S(1)} %collective-permute-done.13.rest_9_), channel_id=1, source_target_pairs={{0,4},{4,0},{8,12},{12,8},{16,20},{20,16},{24,28},{28,24},{1,5},{5... | collective-permute-start | bytes 6291464 | tf_op jit(solution)/shard_map/ppermute | solution.py:328
  145.9 21.9 %collective-permute-start.20 = (bf16[512,2048]{1,0:T(8,128)(2,1)}, bf16[512,2048]{1,0:T(8,128)(2,1)S(1)}, u32[]{:S(2)}, u32[]{:S(2)}) collective-permute-start(bf16[512,2048]{1,0:T(8,128)(2,1)} %collective-permute-done.16.rest_11_), channel_id=1, source_target_pairs={{0,4},{4,0},{8,12},{12,8},{16,20},{20,16},{24,28},{28,24},{1,5},{5... | collective-permute-start | bytes 6291464 | tf_op jit(solution)/shard_map/ppermute | solution.py:328
  149.1 18.7 %collective-permute-start.17 = (bf16[1024,512]{1,0:T(8,128)(2,1)}, bf16[1024,512]{1,0:T(8,128)(2,1)S(1)}, u32[]{:S(2)}, u32[]{:S(2)}) collective-permute-start(bf16[1024,512]{1,0:T(8,128)(2,1)} %get-tuple-element.88), channel_id=1, source_target_pairs={{0,4},{4,0},{8,12},{12,8},{16,20},{20,16},{24,28},{28,24},{1,5},{5... | collective-permute-start | bytes 3145736 | tf_op jit(solution)/shard_map/ppermute | solution.py:328
  150.8 14.9 %collective-permute-start.22 = (bf16[512,512]{1,0:T(8,128)(2,1)S(1)}, bf16[512,512]{1,0:T(8,128)(2,1)}, u32[]{:S(2)}, u32[]{:S(2)}) collective-permute-start(bf16[512,512]{1,0:T(8,128)(2,1)S(1)} %get-tuple-element.84), channel_id=1, source_target_pairs={{0,16},{4,20},{8,24},{12,28},{16,0},{20,4},{24,8},{28,12},{1,17},{... | collective-permute-start | bytes 1572872 | tf_op jit(solution)/shard_map/ppermute | solution.py:328
  151.7 16.0 %collective-permute-start.21 = (bf16[512,512]{1,0:T(8,128)(2,1)}, bf16[512,512]{1,0:T(8,128)(2,1)}, u32[]{:S(2)}, u32[]{:S(2)}) collective-permute-start(bf16[512,512]{1,0:T(8,128)(2,1)} %get-tuple-element.85), channel_id=1, source_target_pairs={{0,8},{4,12},{8,0},{12,4},{16,24},{20,28},{24,16},{28,20},{1,9},{5... | collective-permute-start | bytes 1572872 | tf_op jit(solution)/shard_map/ppermute | solution.py:328
  153.2 42.1 %collective-permute-start.19 = (bf16[512,512]{1,0:T(8,128)(2,1)}, bf16[512,512]{1,0:T(8,128)(2,1)}, u32[]{:S(2)}, u32[]{:S(2)}) collective-permute-start(bf16[512,512]{1,0:T(8,128)(2,1)} %get-tuple-element.86), channel_id=1, source_target_pairs={{0,16},{4,20},{8,24},{12,28},{16,0},{20,4},{24,8},{28,12},{1,17},{... | collective-permute-start | bytes 1572872 | tf_op jit(solution)/shard_map/ppermute | solution.py:328
  165.7 29.7 %collective-permute-start.18 = (bf16[512,512]{1,0:T(8,128)(2,1)}, bf16[512,512]{1,0:T(8,128)(2,1)}, u32[]{:S(2)}, u32[]{:S(2)}) collective-permute-start(bf16[512,512]{1,0:T(8,128)(2,1)} %get-tuple-element.87), channel_id=1, source_target_pairs={{0,8},{4,12},{8,0},{12,4},{16,24},{20,28},{24,16},{28,20},{1,9},{5... | collective-permute-start | bytes 1572872 | tf_op jit(solution)/shard_map/ppermute | solution.py:328
  (12 other events, 94.5 us)
Sparse Core Ops, SparseCore 0:
  90.5 43.8 all-gather.6
  136.0 44.6 all-gather.4

commit v10 on v9

--- a/solution.py
+++ b/solution.py
@@ -91,7 +91,8 @@
     elif form == "own":
         mean_ref, out_ref, table, dense, part, arrived = rest
     else:
-        mean_ref, out_ref, table, dense, part, held, arrived = rest
+        mean_ref, *piece_refs, table, dense, part, held, arrived = rest
+        out_ref = None
     block = part.shape[0]
     stride = -(-3 * chunks // 8) * 8
     residues = table.shape[0] // stride
@@ -137,8 +138,7 @@
         total = diff[0:8] + jnp.where(sublane < 4, diff[8:16], 0.0)
         return total + pltpu.roll(total, 4, 0)
 
-    @pl.loop(0, block // group)
-    def _(g):
+    def one_group(g, out_ref):
         at = pl.multiple_of(g * group, group)
         for f in range(0, group, 2):
             base = step * block + at + f
@@ -160,6 +160,12 @@
             if form == "first":
                 part[here, :] = total
 
+    if form == "sent":
+        for p, ref in enumerate(piece_refs):
+            pl.when(step == p)(lambda ref=ref: pl.loop(0, block // group)(lambda g: one_group(g, ref)))
+    else:
+        pl.loop(0, block // group)(lambda g: one_group(g, out_ref))
+
     if form == "first":
         sums_ref[...] = jnp.sum(part[...].T, axis=0, keepdims=True)
 
@@ -184,8 +190,8 @@
         pltpu.VMEM((block, CHUNK), jnp.float32),
     ]
     if form == "sent":
-        out_shape = jax.ShapeDtypeStruct((chunks, feats, CHUNK), jnp.bfloat16)
-        out_specs = pl.BlockSpec((chunks, block, CHUNK), lambda n: (0, n, 0))
+        out_shape = [jax.ShapeDtypeStruct((chunks, block, CHUNK), jnp.bfloat16)] * (feats // block)
+        out_specs = [pl.BlockSpec((chunks, block, CHUNK), lambda n: (0, 0, 0))] * (feats // block)
     else:
         dtype = jnp.bfloat16 if form == "own" else jnp.float32
         out_shape = jax.ShapeDtypeStruct((feats, chunks * CHUNK), dtype)
@@ -362,11 +368,10 @@
     quarters = {3: swap(quarter, 3), 5: swap(quarter, 5)}
 
     raw, sums, table = contacts("first", pairs, [coords_t], scale_own)
-    quarters, _ = together(quarters, sums)
-    quarters[7] = corner(quarters[3], quarters[5])
     note = jnp.concatenate([sums, frame_scale.reshape(1, frames_dev)], axis=1)
     other = swap(note, 1)
     note = jnp.concatenate([sums + other[:, :feats], note[:, feats:], other[:, feats:]], axis=1)
+    note, quarters = together(note, quarters)
     notes = [note] + [swap(note, d) for d in (2, 4, 6)]
     totals = notes[0][:, :feats]
     for other in notes[1:]:
@@ -378,6 +383,8 @@
     ]
     scale_of = lambda *d: jnp.concatenate([scales[i] for i in d], axis=0)
 
+    quarters, mean = together(quarters, mean)
+    quarters[7] = corner(quarters[3], quarters[5])
     mine, mean = together(center(raw, mean), mean)
     cols = {0: mine, 2: swap(mine, 2), 4: swap(mine, 4)}
     facts = line_gather(jnp.concatenate([mean, pairs.astype(jnp.float32)], axis=0), feat_count)
@@ -398,10 +405,8 @@
 
     row_pairs, mine, quarters = together(row_pairs, mine, quarters)
     cols[1] = swap(mine, 1)
-    mixed = contacts("sent", row_pairs, [quarters[d] for d in FAR], scale_of(*FAR), row_mean)
-
     rows = row_feats // PIECES
-    pieces = [mixed[:, p * rows : (p + 1) * rows] for p in range(PIECES)]
+    pieces = contacts("sent", row_pairs, [quarters[d] for d in FAR], scale_of(*FAR), row_mean, block=rows)
     far = [lax.all_gather(x, "feat", axis=0, tiled=False) for x in pieces]
 
     out_pairs, pieces, walker_lengths = together(out_pairs, pieces, walker_lengths)

time: 229 us -> 220 us (0.961)
  starting transfers between devices: 26 us -> 22.8 us
  waiting for transfers between devices: 45.8 us -> 42.6 us
  local copies, waits for them, and re-layouts: 10.6 us -> 7.81 us
    ppermute x18, waiting for transfers between devices: 36.2 us -> 27.9 us  [swap(): return lax.ppermute(x, 'tm', [(i, i ^ bits) for i in range(8)])]
    ppermute x2, waiting for transfers between devices: 9.55 us -> 14.6 us  [corner(): lax.ppermute(forwarded, 'tm', [(i, i ^ (2 if i % 2 else 4)) for i in rang...]
    ppermute x18, starting transfers between devices: 16.9 us -> 13.2 us  [swap(): return lax.ppermute(x, 'tm', [(i, i ^ bits) for i in range(8)])]
    slice x1 -> x0, local copies, waits for them, and re-layouts: 2.29 us -> none  [shards(): pieces = [mixed[:, p * rows:(p + 1) * rows] for p in range(PIECES)]]
  transfers between devices with their start and end apart: 25 -> 25, of which waited for: 10 -> 11; matrix products, arithmetic and copies ran while one was open for 9% -> 8% of each run, Pallas kernels for 40% -> 41%
where the time goes in v10:
time: 220 us
  Pallas kernels  116 us (53%)
  waiting for transfers between devices  42.6 us (19%)
  starting transfers between devices  22.8 us (10%)
  other arithmetic  15.2 us (7%)
  between operations  15 us (7%)
  local copies, waits for them, and re-layouts  7.81 us (4%)
    pallas_call x4, Pallas kernels, contacts(): pl.pallas_call(functools.partial(gather_kernel, form, chunks, len(sources...  59.8 us
    pallas_call x2, Pallas kernels, products(): pl.pallas_call(functools.partial(product_kernel, piece), out_shape=[out,...  51.5 us
    ppermute x18, waiting for transfers between devices, swap(): return lax.ppermute(x, 'tm', [(i, i ^ bits) for i in range(8)])  27.9 us
    ppermute x2, waiting for transfers between devices, corner(): lax.ppermute(forwarded, 'tm', [(i, i ^ (2 if i % 2 else 4)) for i in rang...  14.6 us
    ppermute x18, starting transfers between devices, swap(): return lax.ppermute(x, 'tm', [(i, i ^ bits) for i in range(8)])  13.2 us
    ppermute x3, starting transfers between devices, line_gather(): lax.ppermute(x, 'feat', shift(s))  6.48 us
    select_n x2, other arithmetic, corner(): forwarded = jnp.where(even, along_x, along_y)  5.24 us
    pallas_call x1, Pallas kernels, center(): pl.pallas_call(center_kernel, out_shape=jax.ShapeDtypeStruct((frames, fea...  4.93 us
  transfers between devices with their start and end apart: 25, of which 11 were waited for; matrix products, arithmetic and copies ran while one was open for 8% of the time, Pallas kernels for 41%

profile of v10, /device:TPU:0, one launch (start us, length us, event | category | flops | bytes accessed | tf_op | source)
XLA Modules:
  0.0 219.6 jit_solution(14453225004314159210)
XLA Ops:
  7.2 1.8 fusion
  9.0 2.5 %collective-permute-start.2 = (s16[3,1500,128]{2,1,0:T(8,128)(2,1)S(1)}, s16[3,1500,128]{2,1,0:T(8,128)(2,1)S(1)}, u32[]{:S(2)}, u32[]{:S(2)}) collective-permute-start(s16[3,1500,128]{2,1,0:T(8,128)(2,1)S(1)} %fusion), channel_id=1, source_target_pairs={{0,20},{4,16},{8,28},{12,24},{16,4},{20,0},{24,12},{28,8},{1,21},{... | collective-permute-start | bytes 3456008 | tf_op jit(solution)/shard_map/ppermute | solution.py:334
  11.5 1.8 collective-permute-start.1
  13.9 18.1 %shard_map.59 = (f32[2048,512]{1,0:T(8,128)}, f32[1,2048]{1,0:T(1,128)}, s32[24000,128]{1,0:T(8,128)}) custom-call(s32[2,2048]{1,0:T(2,128)} %get-tuple-element.112.pairs_ref, f32[4,128]{1,0:T(4,128)} %bitcast.29, s32[3,1500,512]{2,1,0:T(8,128)} %bitcast.26), custom_call_target="tpu_custom_call" | custom-call | flops 10000000 | bytes 36900 | tf_op jit(solution)/shard_map/pallas_call | solution.py:215
  34.7 2.7 %collective-permute-done.2.rest_1_ = s16[3,1500,128]{2,1,0:T(8,128)(2,1)S(1)} collective-permute-done((s16[3,1500,128]{2,1,0:T(8,128)(2,1)S(1)}, s16[3,1500,128]{2,1,0:T(8,128)(2,1)S(1)}, u32[]{:S(2)}, u32[]{:S(2)}) %collective-permute-start.2) | collective-permute-done | bytes 1152032 | tf_op jit(solution)/shard_map/ppermute | solution.py:334
  38.5 2.3 %collective-permute-start.5 = (f32[1,3072]{1,0:T(1,128)S(1)}, f32[1,3072]{1,0:T(1,128)S(1)}, u32[]{:S(2)}, u32[]{:S(2)}) collective-permute-start(f32[1,3072]{1,0:T(1,128)S(1)} %pad_maximum_fusion.3), channel_id=1, source_target_pairs={{0,24},{4,28},{8,16},{12,20},{16,8},{20,12},{24,0},{28,4},{1,25},{... | collective-permute-start | bytes 36872 | tf_op jit(solution)/shard_map/ppermute | solution.py:334
  47.1 1.4 collective-permute-start.9
  48.5 4.9 %shard_map.60.rest_5_ = bf16[512,2048]{1,0:T(8,128)(2,1)} custom-call(f32[2048,512]{1,0:T(8,128)} %get-tuple-element.48.raw_ref, f32[1,2048]{1,0:T(1,128)} %fusion.2.mean_ref), custom_call_target="tpu_custom_call" | custom-call | flops 10000000 | bytes 36900 | tf_op jit(solution)/shard_map/pallas_call | solution.py:235
  53.5 2.7 %collective-permute-start.7 = (f32[3,2048]{1,0:T(4,128)S(1)}, f32[3,2048]{1,0:T(4,128)S(1)}, u32[]{:S(2)}, u32[]{:S(2)}) collective-permute-start(f32[3,2048]{1,0:T(4,128)S(1)} %get-tuple-element.110), channel_id=1, source_target_pairs={{0,2},{1,3},{2,0},{3,1},{4,6},{5,7},{6,4},{7,5},{8,10},{9,11},{10,... | collective-permute-start | bytes 73736 | tf_op jit(solution)/shard_map/ppermute | solution.py:345
  56.1 1.6 collective-permute-start.6
  57.7 2.2 %collective-permute-start.8 = (f32[3,2048]{1,0:T(4,128)S(1)}, f32[3,2048]{1,0:T(4,128)S(1)}, u32[]{:S(2)}, u32[]{:S(2)}) collective-permute-start(f32[3,2048]{1,0:T(4,128)S(1)} %get-tuple-element.110), channel_id=1, source_target_pairs={{0,3},{1,0},{2,1},{3,2},{4,7},{5,4},{6,5},{7,6},{8,11},{9,8},{10,9... | collective-permute-start | bytes 73736 | tf_op jit(solution)/shard_map/ppermute | solution.py:345
  61.2 5.5 %collective-permute-done.9.rest_3_ = s16[3,1500,128]{2,1,0:T(8,128)(2,1)} collective-permute-done((s16[3,1500,128]{2,1,0:T(8,128)(2,1)}, s16[3,1500,128]{2,1,0:T(8,128)(2,1)}, u32[]{:S(2)}, u32[]{:S(2)}) %collective-permute-start.9) | collective-permute-done | bytes 1152032 | tf_op jit(solution)/shard_map/ppermute | solution.py:340
  68.1 1.7 collective-permute-done.10.rest_2_
  70.8 12.4 %shard_map.61 = (bf16[4,512,128]{2,1,0:T(8,128)(2,1)}, bf16[4,512,128]{2,1,0:T(8,128)(2,1)}) custom-call(s32[2,1024]{1,0:T(2,128)} %broadcast_multiply_fusion.2.pairs_ref, f32[4,128]{1,0:T(4,128)} %pad_maximum_fusion.5.scale_ref, s16[3,1500,128]{2,1,0:T(8,128)(2,1)} %copy-done.4, s16[3,1500,128]{2,1,0:T(8,128)(2,1)} %copy-done.3, ...), custom_call_target="tpu_custom_call" | custom-call | flops 10000000 | bytes 36900 | tf_op jit(solution)/shard_map/pallas_call | solution.py:215
  86.5 14.6 %shard_map.62 = bf16[2048,512]{1,0:T(8,128)(2,1)} custom-call(s32[2,2048]{1,0:T(2,128)} %get-tuple-element.108.pairs_ref, f32[4,128]{1,0:T(4,128)} %bitcast.30, s32[24000,128]{1,0:T(8,128)} %get-tuple-element.73.rest_0_, f32[1,2048]{1,0:T(1,128)} %get-tuple-element.106.rest_1_), custom_call_target="tpu_custom_call" | custom-call | flops 10000000 | bytes 36900 | tf_op jit(solution)/shard_map/pallas_call | solution.py:215
  102.4 5.7 %collective-permute-done.13.rest_9_ = bf16[512,2048]{1,0:T(8,128)(2,1)S(1)} collective-permute-done((bf16[512,2048]{1,0:T(8,128)(2,1)}, bf16[512,2048]{1,0:T(8,128)(2,1)S(1)}, u32[]{:S(2)}, u32[]{:S(2)}) %collective-permute-start.13) | collective-permute-done | bytes 2097184 | tf_op jit(solution)/shard_map/ppermute | solution.py:334
  108.2 3.9 %broadcast_select_fusion = bf16[512,2048]{1,0:T(8,128)(2,1)} fusion(bf16[512,2048]{1,0:T(8,128)(2,1)} %collective-permute-done.12.rest_7_, bf16[512,2048]{1,0:T(8,128)(2,1)S(1)} %collective-permute-done.13.rest_9_, pred[]{:T(512)S(6)} %eq.25), kind=kLoop, calls=%fused_computation.1 | loop fusion | flops 1048576 | bytes 6291457 | tf_op jit(solution)/shard_map/jit(_where)/select_n | solution.py:339
  112.0 1.4 collective-permute-start.16
  114.6 14.7 %shard_map.63 = bf16[2048,512]{1,0:T(8,128)(2,1)} custom-call(s32[2,2048]{1,0:T(2,128)} %broadcast_multiply_fusion.pairs_ref, f32[4,128]{1,0:T(4,128)} %bitcast.31, s32[24000,128]{1,0:T(8,128)} %get-tuple-element.73.rest_0_, f32[1,2048]{1,0:T(1,128)} %get-tuple-element.105.rest_1_), custom_call_target="tpu_custom_call" | custom-call | flops 10000000 | bytes 36900 | tf_op jit(solution)/shard_map/pallas_call | solution.py:215
  129.3 9.1 %collective-permute-done.16.rest_11_ = bf16[512,2048]{1,0:T(8,128)(2,1)} collective-permute-done((bf16[512,2048]{1,0:T(8,128)(2,1)}, bf16[512,2048]{1,0:T(8,128)(2,1)}, u32[]{:S(2)}, u32[]{:S(2)}) %collective-permute-start.16) | collective-permute-done | bytes 2097184 | tf_op jit(solution)/shard_map/ppermute | solution.py:340
  138.4 3.2 %constant_dynamic-slice_fusion = (bf16[1024,512]{1,0:T(8,128)(2,1)}, bf16[1024,512]{1,0:T(8,128)(2,1)}) fusion(bf16[2048,512]{1,0:T(8,128)(2,1)} %shard_map.63, s32[]{:T(128)S(6)} %select_n.104, s32[]{:T(128)S(6)} %select_n.91), kind=kLoop, calls=%fused_computation.30 | loop fusion | bytes 4194312 | tf_op jit(solution)/shard_map/dynamic_slice | solution.py:426
  145.9 12.4 %collective-permute-done.22.rest_3_ = bf16[512,512]{1,0:T(8,128)(2,1)} collective-permute-done((bf16[512,512]{1,0:T(8,128)(2,1)S(1)}, bf16[512,512]{1,0:T(8,128)(2,1)}, u32[]{:S(2)}, u32[]{:S(2)}) %collective-permute-start.22) | collective-permute-done | bytes 524320 | tf_op jit(solution)/shard_map/ppermute | solution.py:334
  161.2 25.8 %shard_map.64 = (f32[1024,2048]{1,0:T(8,128)}, f32[1024,2048]{1,0:T(8,128)}) custom-call(s32[2]{0:T(128)} %pad_add_fusion.place_ref, f32[8,4,1,128]{3,2,1,0:T(1,128)} %fusion.1.mask_ref, f32[2]{0:T(128)} %pad_maximum_fusion.6.factors_ref, bf16[1024,512]{1,0:T(8,128)(2,1)} %get-tuple-element.101.rest_0_, bf16[1024,512]{1,0:T(8,128)(2,1)} %copy-done.5, ...), custom_call_target="tpu_custom_call" | custom-call | flops 10000000 | bytes 36900 | tf_op jit(solution)/shard_map/pallas_call | solution.py:306
  187.0 25.8 %shard_map.65 = (f32[1024,2048]{1,0:T(8,128)}, f32[1024,2048]{1,0:T(8,128)}) custom-call(s32[2]{0:T(128)} %pad_add_fusion.place_ref, f32[8,4,1,128]{3,2,1,0:T(1,128)} %fusion.1.mask_ref, f32[2]{0:T(128)} %pad_maximum_fusion.6.factors_ref, bf16[1024,512]{1,0:T(8,128)(2,1)} %get-tuple-element.101.rest_0_, ...), custom_call_target="tpu_custom_call", output_to_operand_aliasing={{0}: (16, {}), {1}: (17, {})} | custom-call | flops 10000000 | bytes 36900 | tf_op jit(solution)/shard_map/pallas_call | solution.py:306
  (92 shorter events, 26.5 us)
Async XLA Ops:
  7.2 152.2 %all-gather.7.cloned.1.call-start = ((), (), s32[]{:S(2)}) async-start(), calls=%async_computation.1 | async-start | bytes 2621440 | tf_op jit(solution)/shard_map/all_gather | solution.py:410
  9.0 28.3 %collective-permute-start.2 = (s16[3,1500,128]{2,1,0:T(8,128)(2,1)S(1)}, s16[3,1500,128]{2,1,0:T(8,128)(2,1)S(1)}, u32[]{:S(2)}, u32[]{:S(2)}) collective-permute-start(s16[3,1500,128]{2,1,0:T(8,128)(2,1)S(1)} %fusion), channel_id=1, source_target_pairs={{0,20},{4,16},{8,28},{12,24},{16,4},{20,0},{24,12},{28,8},{1,21},{... | collective-permute-start | bytes 3456008 | tf_op jit(solution)/shard_map/ppermute | solution.py:334
  11.5 27.0 %collective-permute-start.1 = (s16[3,1500,128]{2,1,0:T(8,128)(2,1)S(1)}, s16[3,1500,128]{2,1,0:T(8,128)(2,1)S(1)}, u32[]{:S(2)}, u32[]{:S(2)}) collective-permute-start(s16[3,1500,128]{2,1,0:T(8,128)(2,1)S(1)} %fusion), channel_id=1, source_target_pairs={{0,12},{4,8},{8,4},{12,0},{16,28},{20,24},{24,20},{28,16},{1,13},{... | collective-permute-start | bytes 3456008 | tf_op jit(solution)/shard_map/ppermute | solution.py:334
  38.5 4.6 %collective-permute-start.5 = (f32[1,3072]{1,0:T(1,128)S(1)}, f32[1,3072]{1,0:T(1,128)S(1)}, u32[]{:S(2)}, u32[]{:S(2)}) collective-permute-start(f32[1,3072]{1,0:T(1,128)S(1)} %pad_maximum_fusion.3), channel_id=1, source_target_pairs={{0,24},{4,28},{8,16},{12,20},{16,8},{20,12},{24,0},{28,4},{1,25},{... | collective-permute-start | bytes 36872 | tf_op jit(solution)/shard_map/ppermute | solution.py:334
  40.8 3.7 %collective-permute-start.4 = (f32[1,3072]{1,0:T(1,128)S(1)}, f32[1,3072]{1,0:T(1,128)S(1)}, u32[]{:S(2)}, u32[]{:S(2)}) collective-permute-start(f32[1,3072]{1,0:T(1,128)S(1)} %pad_maximum_fusion.3), channel_id=1, source_target_pairs={{0,16},{4,20},{8,24},{12,28},{16,0},{20,4},{24,8},{28,12},{1,17},{... | collective-permute-start | bytes 36872 | tf_op jit(solution)/shard_map/ppermute | solution.py:334
  41.4 3.7 %collective-permute-start.3 = (f32[1,3072]{1,0:T(1,128)S(1)}, f32[1,3072]{1,0:T(1,128)S(1)}, u32[]{:S(2)}, u32[]{:S(2)}) collective-permute-start(f32[1,3072]{1,0:T(1,128)S(1)} %pad_maximum_fusion.3), channel_id=1, source_target_pairs={{0,8},{4,12},{8,0},{12,4},{16,24},{20,28},{24,16},{28,20},{1,9},{5... | collective-permute-start | bytes 36872 | tf_op jit(solution)/shard_map/ppermute | solution.py:334
  47.1 19.7 %collective-permute-start.9 = (s16[3,1500,128]{2,1,0:T(8,128)(2,1)}, s16[3,1500,128]{2,1,0:T(8,128)(2,1)}, u32[]{:S(2)}, u32[]{:S(2)}) collective-permute-start(s16[3,1500,128]{2,1,0:T(8,128)(2,1)} %broadcast_select_fusion.1), channel_id=1, source_target_pairs={{0,16},{4,12},{8,24},{12,4},{16,0},{20,28},{24,8},{28,20},{1,17},{... | collective-permute-start | bytes 3456008 | tf_op jit(solution)/shard_map/ppermute | solution.py:340
  53.5 7.1 %collective-permute-start.7 = (f32[3,2048]{1,0:T(4,128)S(1)}, f32[3,2048]{1,0:T(4,128)S(1)}, u32[]{:S(2)}, u32[]{:S(2)}) collective-permute-start(f32[3,2048]{1,0:T(4,128)S(1)} %get-tuple-element.110), channel_id=1, source_target_pairs={{0,2},{1,3},{2,0},{3,1},{4,6},{5,7},{6,4},{7,5},{8,10},{9,11},{10,... | collective-permute-start | bytes 73736 | tf_op jit(solution)/shard_map/ppermute | solution.py:345
  56.1 10.6 %collective-permute-start.6 = (f32[3,2048]{1,0:T(4,128)S(1)}, f32[3,2048]{1,0:T(4,128)S(1)}, u32[]{:S(2)}, u32[]{:S(2)}) collective-permute-start(f32[3,2048]{1,0:T(4,128)S(1)} %get-tuple-element.110), channel_id=1, source_target_pairs={{0,1},{1,2},{2,3},{3,0},{4,5},{5,6},{6,7},{7,4},{8,9},{9,10},{10,1... | collective-permute-start | bytes 73736 | tf_op jit(solution)/shard_map/ppermute | solution.py:345
  57.7 9.0 %collective-permute-start.8 = (f32[3,2048]{1,0:T(4,128)S(1)}, f32[3,2048]{1,0:T(4,128)S(1)}, u32[]{:S(2)}, u32[]{:S(2)}) collective-permute-start(f32[3,2048]{1,0:T(4,128)S(1)} %get-tuple-element.110), channel_id=1, source_target_pairs={{0,3},{1,0},{2,1},{3,2},{4,7},{5,4},{6,5},{7,6},{8,11},{9,8},{10,9... | collective-permute-start | bytes 73736 | tf_op jit(solution)/shard_map/ppermute | solution.py:345
  59.9 48.2 %collective-permute-start.13 = (bf16[512,2048]{1,0:T(8,128)(2,1)}, bf16[512,2048]{1,0:T(8,128)(2,1)S(1)}, u32[]{:S(2)}, u32[]{:S(2)}) collective-permute-start(bf16[512,2048]{1,0:T(8,128)(2,1)} %shard_map.60.rest_5_), channel_id=1, source_target_pairs={{0,16},{4,20},{8,24},{12,28},{16,0},{20,4},{24,8},{28,12},{1,17},{... | collective-permute-start | bytes 6291464 | tf_op jit(solution)/shard_map/ppermute | solution.py:334
  60.5 47.6 %collective-permute-start.12 = (bf16[512,2048]{1,0:T(8,128)(2,1)}, bf16[512,2048]{1,0:T(8,128)(2,1)}, u32[]{:S(2)}, u32[]{:S(2)}) collective-permute-start(bf16[512,2048]{1,0:T(8,128)(2,1)} %shard_map.60.rest_5_), channel_id=1, source_target_pairs={{0,8},{4,12},{8,0},{12,4},{16,24},{20,28},{24,16},{28,20},{1,9},{5... | collective-permute-start | bytes 6291464 | tf_op jit(solution)/shard_map/ppermute | solution.py:334
  66.7 3.0 %collective-permute-start.10 = (s16[3,1500,128]{2,1,0:T(8,128)(2,1)}, s16[3,1500,128]{2,1,0:T(8,128)(2,1)S(1)}, u32[]{:S(2)}, u32[]{:S(2)}) collective-permute-start(s16[3,1500,128]{2,1,0:T(8,128)(2,1)} %collective-permute-done.9.rest_3_), channel_id=1, source_target_pairs={{0,4},{4,0},{8,12},{12,8},{16,20},{20,16},{24,28},{28,24},{1,5},{5... | collective-permute-start | bytes 3456008 | tf_op jit(solution)/shard_map/ppermute | solution.py:334
  83.2 103.8 %all-gather.5.cloned.1.call-start = ((), (), s32[]{:S(2)}) async-start(), calls=%async_computation | async-start | bytes 2621440 | tf_op jit(solution)/shard_map/all_gather | solution.py:410
  83.4 24.8 %collective-permute-start.11 = (bf16[512,2048]{1,0:T(8,128)(2,1)}, bf16[512,2048]{1,0:T(8,128)(2,1)}, u32[]{:S(2)}, u32[]{:S(2)}) collective-permute-start(bf16[512,2048]{1,0:T(8,128)(2,1)} %shard_map.60.rest_5_), channel_id=1, source_target_pairs={{0,4},{4,0},{8,12},{12,8},{16,20},{20,16},{24,28},{28,24},{1,5},{5... | collective-permute-start | bytes 6291464 | tf_op jit(solution)/shard_map/ppermute | solution.py:334
  112.0 26.4 %collective-permute-start.16 = (bf16[512,2048]{1,0:T(8,128)(2,1)}, bf16[512,2048]{1,0:T(8,128)(2,1)}, u32[]{:S(2)}, u32[]{:S(2)}) collective-permute-start(bf16[512,2048]{1,0:T(8,128)(2,1)} %broadcast_select_fusion), channel_id=1, source_target_pairs={{0,16},{4,12},{8,24},{12,4},{16,0},{20,28},{24,8},{28,20},{1,17},{... | collective-permute-start | bytes 6291464 | tf_op jit(solution)/shard_map/ppermute | solution.py:340
  113.5 24.9 %collective-permute-start.14 = (bf16[512,2048]{1,0:T(8,128)(2,1)}, bf16[512,2048]{1,0:T(8,128)(2,1)}, u32[]{:S(2)}, u32[]{:S(2)}) collective-permute-start(bf16[512,2048]{1,0:T(8,128)(2,1)} %collective-permute-done.12.rest_7_), channel_id=1, source_target_pairs={{0,4},{4,0},{8,12},{12,8},{16,20},{20,16},{24,28},{28,24},{1,5},{5... | collective-permute-start | bytes 6291464 | tf_op jit(solution)/shard_map/ppermute | solution.py:334
  113.5 24.9 %collective-permute-start.15 = (bf16[512,2048]{1,0:T(8,128)(2,1)S(1)}, bf16[512,2048]{1,0:T(8,128)(2,1)}, u32[]{:S(2)}, u32[]{:S(2)}) collective-permute-start(bf16[512,2048]{1,0:T(8,128)(2,1)S(1)} %collective-permute-done.13.rest_9_), channel_id=1, source_target_pairs={{0,4},{4,0},{8,12},{12,8},{16,20},{20,16},{24,28},{28,24},{1,5},{5... | collective-permute-start | bytes 6291464 | tf_op jit(solution)/shard_map/ppermute | solution.py:334
  138.4 21.0 %collective-permute-start.20 = (bf16[512,2048]{1,0:T(8,128)(2,1)}, bf16[512,2048]{1,0:T(8,128)(2,1)S(1)}, u32[]{:S(2)}, u32[]{:S(2)}) collective-permute-start(bf16[512,2048]{1,0:T(8,128)(2,1)} %collective-permute-done.16.rest_11_), channel_id=1, source_target_pairs={{0,4},{4,0},{8,12},{12,8},{16,20},{20,16},{24,28},{28,24},{1,5},{5... | collective-permute-start | bytes 6291464 | tf_op jit(solution)/shard_map/ppermute | solution.py:334
  141.7 17.7 %collective-permute-start.17 = (bf16[1024,512]{1,0:T(8,128)(2,1)}, bf16[1024,512]{1,0:T(8,128)(2,1)S(1)}, u32[]{:S(2)}, u32[]{:S(2)}) collective-permute-start(bf16[1024,512]{1,0:T(8,128)(2,1)} %get-tuple-element.100), channel_id=1, source_target_pairs={{0,4},{4,0},{8,12},{12,8},{16,20},{20,16},{24,28},{28,24},{1,5},{5... | collective-permute-start | bytes 3145736 | tf_op jit(solution)/shard_map/ppermute | solution.py:334
  143.4 14.9 %collective-permute-start.22 = (bf16[512,512]{1,0:T(8,128)(2,1)S(1)}, bf16[512,512]{1,0:T(8,128)(2,1)}, u32[]{:S(2)}, u32[]{:S(2)}) collective-permute-start(bf16[512,512]{1,0:T(8,128)(2,1)S(1)} %get-tuple-element.96), channel_id=1, source_target_pairs={{0,16},{4,20},{8,24},{12,28},{16,0},{20,4},{24,8},{28,12},{1,17},{... | collective-permute-start | bytes 1572872 | tf_op jit(solution)/shard_map/ppermute | solution.py:334
  144.7 14.6 %collective-permute-start.21 = (bf16[512,512]{1,0:T(8,128)(2,1)}, bf16[512,512]{1,0:T(8,128)(2,1)}, u32[]{:S(2)}, u32[]{:S(2)}) collective-permute-start(bf16[512,512]{1,0:T(8,128)(2,1)} %get-tuple-element.97), channel_id=1, source_target_pairs={{0,8},{4,12},{8,0},{12,4},{16,24},{20,28},{24,16},{28,20},{1,9},{5... | collective-permute-start | bytes 1572872 | tf_op jit(solution)/shard_map/ppermute | solution.py:334
  145.2 41.8 %collective-permute-start.19 = (bf16[512,512]{1,0:T(8,128)(2,1)}, bf16[512,512]{1,0:T(8,128)(2,1)}, u32[]{:S(2)}, u32[]{:S(2)}) collective-permute-start(bf16[512,512]{1,0:T(8,128)(2,1)} %get-tuple-element.98), channel_id=1, source_target_pairs={{0,16},{4,20},{8,24},{12,28},{16,0},{20,4},{24,8},{28,12},{1,17},{... | collective-permute-start | bytes 1572872 | tf_op jit(solution)/shard_map/ppermute | solution.py:334
  158.3 28.7 %collective-permute-start.18 = (bf16[512,512]{1,0:T(8,128)(2,1)}, bf16[512,512]{1,0:T(8,128)(2,1)}, u32[]{:S(2)}, u32[]{:S(2)}) collective-permute-start(bf16[512,512]{1,0:T(8,128)(2,1)} %get-tuple-element.99), channel_id=1, source_target_pairs={{0,8},{4,12},{8,0},{12,4},{16,24},{20,28},{24,16},{28,20},{1,9},{5... | collective-permute-start | bytes 1572872 | tf_op jit(solution)/shard_map/ppermute | solution.py:334
  (12 other events, 87.7 us)
Sparse Core Ops, SparseCore 0:
  83.3 49.7 all-gather.6
  134.7 44.5 all-gather.4

commit v11 on v8

--- a/solution.py
+++ b/solution.py
@@ -156,7 +156,7 @@
                 elif form == "own":
                     out_ref[here, lanes] = (contact - part[here, :]).astype(jnp.bfloat16)
                 else:
-                    out_ref[c, here, :] = (contact - part[here, :]).astype(jnp.bfloat16)
+                    out_ref[0, c, here, :] = (contact - part[here, :]).astype(jnp.bfloat16)
             if form == "first":
                 part[here, :] = total
 
@@ -184,8 +184,8 @@
         pltpu.VMEM((block, CHUNK), jnp.float32),
     ]
     if form == "sent":
-        out_shape = jax.ShapeDtypeStruct((chunks, feats, CHUNK), jnp.bfloat16)
-        out_specs = pl.BlockSpec((chunks, block, CHUNK), lambda n: (0, n, 0))
+        out_shape = jax.ShapeDtypeStruct((feats // block, chunks, block, CHUNK), jnp.bfloat16)
+        out_specs = pl.BlockSpec((1, chunks, block, CHUNK), lambda n: (n, 0, 0, 0))
     else:
         dtype = jnp.bfloat16 if form == "own" else jnp.float32
         out_shape = jax.ShapeDtypeStruct((feats, chunks * CHUNK), dtype)
@@ -242,23 +242,22 @@
 
 def product_kernel(piece, place_ref, mask_ref, factors_ref, *rest):
     near_refs, rest = rest[: len(NEAR)], rest[len(NEAR) :]
-    far_ref, cols_refs = rest[0], rest[1:9]
+    far_refs, cols_refs = rest[:7], rest[7:15]
     same_ref, cross_ref, left, near_held, far_held, arrived = rest[-6:]
     feats = same_ref.shape[0]
     frames = cols_refs[0].shape[0]
     parts = frames // CHUNK
-    me = place_ref[0]
+    me, z = place_ref[0], place_ref[1]
 
     def put(d, c, value):
         j = me ^ d
         after = me ^ lax.rem(j + 1, 8)
-        left[0:feats, d * frames + c * CHUNK : d * frames + (c + 1) * CHUNK] = value
+        mask = mask_ref[j, c].astype(jnp.bfloat16)
+        at = pl.multiple_of(d * frames + c * CHUNK, CHUNK)
+        left[0:feats, pl.ds(at, CHUNK)] = value
         to = c + LAG // CHUNK
-        if to < parts:
-            at = d * frames + to * CHUNK
-        else:
-            at = pl.multiple_of(after * frames + (to - parts) * CHUNK, CHUNK)
-        left[feats : 2 * feats, pl.ds(at, CHUNK)] = value * mask_ref[j, c].astype(jnp.bfloat16)
+        at = jnp.where(to < parts, d * frames + to * CHUNK, after * frames + (to - parts) * CHUNK)
+        left[feats : 2 * feats, pl.ds(pl.multiple_of(at, CHUNK), CHUNK)] = value * mask
 
     @pl.when(pl.program_id(0) == 0)
     def _():
@@ -268,20 +267,24 @@
             copies.append(
                 pltpu.make_async_copy(ref.at[pl.ds(start, feats), :], near_held.at[n], arrived.at[n])
             )
-        for c in range(parts):
-            copies.append(
-                pltpu.make_async_copy(far_ref.at[c], far_held.at[c], arrived.at[len(NEAR) + c])
-            )
+        for n, ref in enumerate(far_refs):
+            source = ref.at[piece if ref.shape[0] > 1 else 0]
+            copies.append(pltpu.make_async_copy(source, far_held.at[n], arrived.at[len(NEAR) + n]))
         for copy in copies:
             copy.start()
         for n, d in enumerate(NEAR):
             copies[n].wait()
             for c in range(parts):
                 put(d, c, near_held[n, :, c * CHUNK : (c + 1) * CHUNK])
-        for c in range(parts):
-            copies[len(NEAR) + c].wait()
-            for i, d in enumerate(FAR):
-                put(d, c, far_held[c, i])
+        for n in range(len(far_refs)):
+            copies[len(NEAR) + n].wait()
+            hop = (n + 1) // 2
+            c = z - hop if n % 2 else z + hop
+
+            @pl.when((c >= 0) & (c < parts))
+            def _():
+                for i, d in enumerate(FAR):
+                    put(d, c, far_held[n, i])
 
     right = jnp.concatenate([ref[...] for ref in cols_refs], axis=0)
     same = jnp.dot(left[0:feats, :], right, preferred_element_type=jnp.float32)
@@ -290,13 +293,13 @@
     cross_ref[...] = cross / factors_ref[1]
 
 
-def products(place, mask, factors, piece, near, far, cols, outs=(), block=512):
+def products(place, mask, factors, piece, near, far, cols, outs=(), block=256):
     frames, feats = cols[0].shape
     row_feats = near[0].shape[0]
     rows = row_feats // PIECES
     out = jax.ShapeDtypeStruct((row_feats, feats), jnp.float32)
     any_spec = pl.BlockSpec(memory_space=pl.ANY)
-    inputs = [mask, factors, *near, far, *cols, *outs]
+    inputs = [mask, factors, *near, *far, *cols, *outs]
     return pl.pallas_call(
         functools.partial(product_kernel, piece),
         out_shape=[out, out],
@@ -307,15 +310,15 @@
                 pl.BlockSpec(mask.shape, lambda n, s: (0,) * mask.ndim),
                 pl.BlockSpec(memory_space=pltpu.SMEM),
             ]
-            + [any_spec] * (len(near) + 1)
+            + [any_spec] * (len(near) + len(far))
             + [pl.BlockSpec((frames, block), lambda n, s: (0, n))] * 8
             + [any_spec] * len(outs),
             out_specs=[pl.BlockSpec((rows, block), lambda n, s: (piece, n))] * 2,
             scratch_shapes=[
                 pltpu.VMEM((2 * rows, 8 * frames), jnp.bfloat16),
                 pltpu.VMEM((len(near), rows, frames), jnp.bfloat16),
-                pltpu.VMEM(far.shape, jnp.bfloat16),
-                pltpu.SemaphoreType.DMA((len(near) + far.shape[0],)),
+                pltpu.VMEM((len(far), *far[0].shape[1:]), jnp.bfloat16),
+                pltpu.SemaphoreType.DMA((len(near) + len(far),)),
             ],
         ),
         input_output_aliases={len(inputs) - 1 + i: i for i in range(len(outs))},
@@ -337,6 +340,12 @@
 def line_gather(x, count):
     shift = lambda s: [(i, (i + s) % count) for i in range(count)]
     return jnp.stack([x] + [lax.ppermute(x, "feat", shift(s)) for s in range(1, count)])
+
+
+def line_hop(up, down, hop, count):
+    up = lax.ppermute(up, "feat", [(i, i + 1) for i in range(hop - 1, count - 1)])
+    down = lax.ppermute(down, "feat", [(i + 1, i) for i in range(count - hop)])
+    return up, down
 
 
 def together(*values):
@@ -396,36 +405,42 @@
     cols[1] = swap(mine, 1)
     mixed = contacts("sent", row_pairs, [quarters[d] for d in FAR], scale_of(*FAR), row_mean)
 
-    rows = row_feats // PIECES
-    pieces = [mixed[:, p * rows : (p + 1) * rows] for p in range(PIECES)]
-    far = [lax.all_gather(x, "feat", axis=0, tiled=False) for x in pieces]
-
-    out_pairs, pieces, walker_lengths = together(out_pairs, pieces, walker_lengths)
+    out_pairs, mixed, walker_lengths = together(out_pairs, mixed, walker_lengths)
+    up, down = line_hop(mixed, mixed, 1, feat_count)
     valid = walker_mask(walker_lengths, frames_all, frames_all)
     mask = valid.astype(jnp.float32).reshape(tm_count, parts, 1, CHUNK)
     npairs = jnp.sum(jnp.maximum(walker_lengths - LAG, 0)).astype(jnp.float32)
     factors = jnp.stack([jnp.float32(1.0 / frames_all), npairs])
     near_rows = contacts("own", out_pairs[:, :feats], [table], scale_own, out_mean[:, :feats])
-    chip_pairs, near_rows = together(out_pairs[:, feats:], near_rows)
-    chip_rows = contacts("own", chip_pairs, [table], scale_own, out_mean[:, feats:])
-    chip_rows, cols, near_rows, mask, factors = together(chip_rows, cols, near_rows, mask, factors)
+    near_rows, mask, factors, up, down, cols = together(near_rows, mask, factors, up, down, cols)
+    far = [mixed, up, down]
 
     cols[6] = corner(cols[2], cols[4])
+    up, down = line_hop(up, down, 2, feat_count)
     for d in (2, 4):
         cols[d + 1] = swap(cols[d], 1)
+    chip_pairs, _ = together(out_pairs[:, feats:], near_rows)
+    chip_rows = contacts("own", chip_pairs, [table], scale_own, out_mean[:, feats:])
+    chip_rows, near_rows, cols, up, down = together(chip_rows, near_rows, cols, up, down)
+    far += [up, down]
+
+    rows = row_feats // PIECES
     cut = lambda x, start, count: lax.dynamic_slice_in_dim(x, start, count, axis=0)
     own = cut(chip_rows, own_half, row_feats)
-    partner = swap(cut(chip_rows, row_feats - own_half, row_feats), 1)
-    cols, partner, near_rows = together(cols, partner, near_rows)
-    direct = [
-        [swap(cut(near_rows, start + p * rows, rows), bit) for bit, start in ((2, 0), (4, row_feats))]
-        for p in range(PIECES)
-    ]
     cols[7] = swap(cols[6], 1)
+    partner, cols = together(cut(chip_rows, row_feats - own_half, row_feats), cols)
+    partner = swap(partner, 1)
     cols = [cols[d] for d in range(8)]
+    arrived = []
+    for p in range(PIECES):
+        last = line_hop(up[p : p + 1], down[p : p + 1], 3, feat_count)
+        sides = [swap(cut(near_rows, start + p * rows, rows), bit) for bit, start in ((2, 0), (4, row_feats))]
+        if p < PIECES - 1:
+            last, sides, up, down, near_rows = together(last, sides, up, down, near_rows)
+        arrived.append((sides, last))
     outs = ()
-    for p in range(PIECES):
-        outs = products(place, mask, factors, p, [own, partner, *direct[p]], far[p], cols, outs)
+    for p, (sides, last) in enumerate(arrived):
+        outs = products(place, mask, factors, p, [own, partner, *sides], [*far, *last], cols, outs)
     return outs
 
 

time: 224 us -> 220 us (0.982)
  starting transfers between devices: 26.9 us -> 41.3 us
  between operations: 15 us -> 1.88 us
  waiting for transfers between devices: 39 us -> 33.7 us
    ppermute x0 -> x8, waiting for transfers between devices: none -> 19.1 us  [the longest x4 19.1 us: line_hop(): down = lax.ppermute(down, 'feat', [(i + 1, i) for i in range(count - hop)])]
    ppermute x2, waiting for transfers between devices: 16.6 us -> 0.5 us  [corner(): lax.ppermute(forwarded, 'tm', [(i, i ^ (2 if i % 2 else 4)) for i in rang...]
    ppermute x0 -> x8, starting transfers between devices: none -> 13.8 us  [the longest x4 8.62 us: line_hop(): lax.ppermute(up, 'feat', [(i, i + 1) for i in range(hop - 1, count - 1)])]
    ppermute x21, waiting for transfers between devices: 22.3 us -> 14.1 us  [swap(): return lax.ppermute(x, 'tm', [(i, i ^ bits) for i in range(8)])]
    dynamic_slice x2 -> x3, local copies, waits for them, and re-layouts: 5.9 us -> 5.07 us  [shards(): lax.dynamic_slice_in_dim(x, start, count, axis=0)]
  transfers between devices with their start and end apart: 28 -> 34, of which waited for: 9 -> 11; matrix products, arithmetic and copies ran while one was open for 10% -> 8% of each run, Pallas kernels for 41% -> 41%
where the time goes in v11:
time: 220 us; the launch traced here: 219 us
  Pallas kernels  116 us (53%)
  starting transfers between devices  41.3 us (19%)
  waiting for transfers between devices  33.7 us (15%)
  other arithmetic  13.7 us (6%)
  local copies, waits for them, and re-layouts  12.1 us (6%)
    pallas_call x4, Pallas kernels, contacts(): pl.pallas_call(functools.partial(gather_kernel, form, chunks, len(sources...  59.4 us
    pallas_call x2, Pallas kernels, products(): pl.pallas_call(functools.partial(product_kernel, piece), out_shape=[out,...  51.7 us
    ppermute x21, starting transfers between devices, swap(): return lax.ppermute(x, 'tm', [(i, i ^ bits) for i in range(8)])  19.5 us
    ppermute x4, waiting for transfers between devices, line_hop(): down = lax.ppermute(down, 'feat', [(i + 1, i) for i in range(count - hop)])  19.1 us
    ppermute x21, waiting for transfers between devices, swap(): return lax.ppermute(x, 'tm', [(i, i ^ bits) for i in range(8)])  14.1 us
    ppermute x4, starting transfers between devices, line_hop(): lax.ppermute(up, 'feat', [(i, i + 1) for i in range(hop - 1, count - 1)])  8.62 us
    ppermute x3, starting transfers between devices, line_gather(): lax.ppermute(x, 'feat', shift(s))  6.48 us
    ppermute x4, starting transfers between devices, line_hop(): down = lax.ppermute(down, 'feat', [(i + 1, i) for i in range(count - hop)])  5.16 us
  transfers between devices with their start and end apart: 34, of which 11 were waited for; matrix products, arithmetic and copies ran while one was open for 8% of the time, Pallas kernels for 41%

profile of v11, /device:TPU:0, one launch (start us, length us, event | category | flops | bytes accessed | tf_op | source)
XLA Modules:
  0.0 218.8 jit_solution(15003265109358902132)
XLA Ops:
  0.6 1.8 fusion
  2.5 2.5 %collective-permute-start.11 = (s16[3,1500,128]{2,1,0:T(8,128)(2,1)S(1)}, s16[3,1500,128]{2,1,0:T(8,128)(2,1)S(1)}, u32[]{:S(2)}, u32[]{:S(2)}) collective-permute-start(s16[3,1500,128]{2,1,0:T(8,128)(2,1)S(1)} %fusion), channel_id=1, source_target_pairs={{0,20},{4,16},{8,28},{12,24},{16,4},{20,0},{24,12},{28,8},{1,21},{... | collective-permute-start | bytes 3456008 | tf_op jit(solution)/shard_map/ppermute | solution.py:331
  4.9 1.8 collective-permute-start.10
  7.3 18.1 %shard_map.59 = (f32[2048,512]{1,0:T(8,128)}, f32[1,2048]{1,0:T(1,128)}, s32[24000,128]{1,0:T(8,128)}) custom-call(s32[2,2048]{1,0:T(2,128)} %get-tuple-element.148.pairs_ref, f32[4,128]{1,0:T(4,128)} %bitcast.25, s32[3,1500,512]{2,1,0:T(8,128)} %bitcast.24), custom_call_target="tpu_custom_call" | custom-call | flops 10000000 | bytes 36900 | tf_op jit(solution)/shard_map/pallas_call | solution.py:209
  26.3 2.3 %collective-permute-start.5 = (f32[1,2560]{1,0:T(1,128)S(1)}, f32[1,2560]{1,0:T(1,128)S(1)}, u32[]{:S(2)}, u32[]{:S(2)}) collective-permute-start(f32[1,2560]{1,0:T(1,128)S(1)} %pad_maximum_fusion.3), channel_id=1, source_target_pairs={{0,24},{4,28},{8,16},{12,20},{16,8},{20,12},{24,0},{28,4},{1,25},{... | collective-permute-start | bytes 30728 | tf_op jit(solution)/shard_map/ppermute | solution.py:331
  29.1 1.6 collective-permute-done.11.rest_1_
  30.8 2.5 %collective-permute-start.3 = (f32[1,2560]{1,0:T(1,128)S(1)}, f32[1,2560]{1,0:T(1,128)}, u32[]{:S(2)}, u32[]{:S(2)}) collective-permute-start(f32[1,2560]{1,0:T(1,128)S(1)} %pad_maximum_fusion.3), channel_id=1, source_target_pairs={{0,16},{4,20},{8,24},{12,28},{16,0},{20,4},{24,8},{28,12},{1,17},{... | collective-permute-start | bytes 30728 | tf_op jit(solution)/shard_map/ppermute | solution.py:331
  36.5 1.9 collective-permute-done.1
  39.2 2.7 %collective-permute-start.8 = (f32[3,2048]{1,0:T(4,128)S(1)}, f32[3,2048]{1,0:T(4,128)S(1)}, u32[]{:S(2)}, u32[]{:S(2)}) collective-permute-start(f32[3,2048]{1,0:T(4,128)S(1)} %get-tuple-element.146), channel_id=1, source_target_pairs={{0,2},{1,3},{2,0},{3,1},{4,6},{5,7},{6,4},{7,5},{8,10},{9,11},{10,... | collective-permute-start | bytes 73736 | tf_op jit(solution)/shard_map/ppermute | solution.py:342
  43.5 2.2 %collective-permute-start.9 = (f32[3,2048]{1,0:T(4,128)S(1)}, f32[3,2048]{1,0:T(4,128)S(1)}, u32[]{:S(2)}, u32[]{:S(2)}) collective-permute-start(f32[3,2048]{1,0:T(4,128)S(1)} %get-tuple-element.146), channel_id=1, source_target_pairs={{0,3},{1,0},{2,1},{3,2},{4,7},{5,4},{6,5},{7,6},{8,11},{9,8},{10,9... | collective-permute-start | bytes 73736 | tf_op jit(solution)/shard_map/ppermute | solution.py:342
  46.3 4.9 %shard_map.60.rest_11_ = bf16[512,2048]{1,0:T(8,128)(2,1)} custom-call(f32[2048,512]{1,0:T(8,128)} %get-tuple-element.66.raw_ref, f32[1,2048]{1,0:T(1,128)} %copy-done.16), custom_call_target="tpu_custom_call" | custom-call | flops 10000000 | bytes 36900 | tf_op jit(solution)/shard_map/pallas_call | solution.py:229
  56.9 12.1 %shard_map.61.rest_4_ = bf16[2,4,512,128]{3,2,1,0:T(8,128)(2,1)} custom-call(s32[2,1024]{1,0:T(2,128)} %broadcast_multiply_fusion.2.pairs_ref, f32[4,128]{1,0:T(4,128)} %pad_maximum_fusion.4.scale_ref, s16[3,1500,128]{2,1,0:T(8,128)(2,1)} %copy-done.8, s16[3,1500,128]{2,1,0:T(8,128)(2,1)} %copy-done.7, s16[3,1500,128]{2,1,0:T(8,128)(2,1)} %copy-done.11, ...), custom_call_target="tpu_custom_call" | custom-call | flops 10000000 | bytes 36900 | tf_op jit(solution)/shard_map/pallas_call | solution.py:209
  70.3 5.6 %collective-permute-start.14 = (bf16[2,4,512,128]{3,2,1,0:T(8,128)(2,1)}, bf16[2,4,512,128]{3,2,1,0:T(8,128)(2,1)}, u32[]{:S(2)}, u32[]{:S(2)}) collective-permute-start(bf16[2,4,512,128]{3,2,1,0:T(8,128)(2,1)} %shard_map.61.rest_4_), channel_id=1, source_target_pairs={{0,1},{1,2},{2,3},{4,5},{5,6},{6,7},{8,9},{9,10},{10,11},{12,13},{... | collective-permute-start | bytes 3145736 | tf_op jit(solution)/shard_map/ppermute | solution.py:346
  78.7 14.6 %shard_map.62 = bf16[2048,512]{1,0:T(8,128)(2,1)} custom-call(s32[2,2048]{1,0:T(2,128)} %get-tuple-element.144.pairs_ref, f32[4,128]{1,0:T(4,128)} %bitcast.26, s32[24000,128]{1,0:T(8,128)} %get-tuple-element.87.rest_0_, f32[1,2048]{1,0:T(1,128)} %get-tuple-element.142.rest_1_), custom_call_target="tpu_custom_call" | custom-call | flops 10000000 | bytes 36900 | tf_op jit(solution)/shard_map/pallas_call | solution.py:209
  94.6 6.0 %collective-permute-done.18.rest_15_ = bf16[512,2048]{1,0:T(8,128)(2,1)S(1)} collective-permute-done((bf16[512,2048]{1,0:T(8,128)(2,1)}, bf16[512,2048]{1,0:T(8,128)(2,1)S(1)}, u32[]{:S(2)}, u32[]{:S(2)}) %collective-permute-start.18) | collective-permute-done | bytes 2097184 | tf_op jit(solution)/shard_map/ppermute | solution.py:331
  100.9 4.0 %broadcast_select_fusion = bf16[512,2048]{1,0:T(8,128)(2,1)} fusion(bf16[512,2048]{1,0:T(8,128)(2,1)} %collective-permute-done.17.rest_13_, bf16[512,2048]{1,0:T(8,128)(2,1)S(1)} %collective-permute-done.18.rest_15_, pred[]{:T(512)S(6)} %eq.25), kind=kLoop, calls=%fused_computation.1 | loop fusion | flops 1048576 | bytes 6291457 | tf_op jit(solution)/shard_map/jit(_where)/select_n | solution.py:336
  109.2 14.6 %shard_map.63 = bf16[2048,512]{1,0:T(8,128)(2,1)} custom-call(s32[2,2048]{1,0:T(2,128)} %broadcast_multiply_fusion.pairs_ref, f32[4,128]{1,0:T(4,128)} %bitcast.27, s32[24000,128]{1,0:T(8,128)} %get-tuple-element.87.rest_0_, f32[1,2048]{1,0:T(1,128)} %get-tuple-element.141.rest_1_), custom_call_target="tpu_custom_call" | custom-call | flops 10000000 | bytes 36900 | tf_op jit(solution)/shard_map/pallas_call | solution.py:209
  123.9 13.0 %collective-permute-done.23.rest_8_ = bf16[2,4,512,128]{3,2,1,0:T(8,128)(2,1)S(1)} collective-permute-done((bf16[2,4,512,128]{3,2,1,0:T(8,128)(2,1)}, bf16[2,4,512,128]{3,2,1,0:T(8,128)(2,1)S(1)}, u32[]{:S(2)}, u32[]{:S(2)}) %collective-permute-start.23) | collective-permute-done | bytes 1048608 | tf_op jit(solution)/shard_map/ppermute | solution.py:347
  141.7 2.2 %fusion.5 = (bf16[512,512]{1,0:T(8,128)(2,1)}, bf16[512,512]{1,0:T(8,128)(2,1)}) fusion(bf16[2048,512]{1,0:T(8,128)(2,1)} %shard_map.62), kind=kLoop, calls=%fused_computation.44 | loop fusion | bytes 2097152 | tf_op jit(solution)/shard_map/dynamic_slice | solution.py:428
  146.3 2.8 %constant_dynamic-slice_fusion = (bf16[1024,512]{1,0:T(8,128)(2,1)S(1)}, bf16[1024,512]{1,0:T(8,128)(2,1)}) fusion(bf16[2048,512]{1,0:T(8,128)(2,1)} %shard_map.63, s32[]{:T(128)S(6)} %select_n.101, s32[]{:T(128)S(6)} %select_n.91), kind=kLoop, calls=%fused_computation.32 | loop fusion | bytes 4194312 | tf_op jit(solution)/shard_map/dynamic_slice | solution.py:428
  149.1 6.1 %collective-permute-done.27.rest_10_ = bf16[1,4,512,128]{3,2,1,0:T(8,128)(2,1)} collective-permute-done((bf16[1,4,512,128]{3,2,1,0:T(8,128)(2,1)}, bf16[1,4,512,128]{3,2,1,0:T(8,128)(2,1)}, u32[]{:S(2)}, u32[]{:S(2)}) %collective-permute-start.27) | collective-permute-done | bytes 524320 | tf_op jit(solution)/shard_map/ppermute | solution.py:347
  155.2 3.1 %collective-permute-done.29.rest_3_ = bf16[512,512]{1,0:T(8,128)(2,1)} collective-permute-done((bf16[512,512]{1,0:T(8,128)(2,1)}, bf16[512,512]{1,0:T(8,128)(2,1)}, u32[]{:S(2)}, u32[]{:S(2)}) %collective-permute-start.29) | collective-permute-done | bytes 524320 | tf_op jit(solution)/shard_map/ppermute | solution.py:331
  165.6 25.9 %shard_map.64 = (f32[1024,2048]{1,0:T(8,128)}, f32[1024,2048]{1,0:T(8,128)}) custom-call(s32[2]{0:T(128)} %pad_add_fusion.place_ref, f32[8,4,1,128]{3,2,1,0:T(1,128)} %fusion.1.mask_ref, f32[2]{0:T(128)} %pad_maximum_fusion.5.factors_ref, bf16[1024,512]{1,0:T(8,128)(2,1)} %get-tuple-element.137.rest_0_, bf16[1024,512]{1,0:T(8,128)(2,1)} %copy-done.10, ...), custom_call_target="tpu_custom_call" | custom-call | flops 10000000 | bytes 36900 | tf_op jit(solution)/shard_map/pallas_call | solution.py:303
  192.8 25.9 %shard_map.65 = (f32[1024,2048]{1,0:T(8,128)}, f32[1024,2048]{1,0:T(8,128)}) custom-call(s32[2]{0:T(128)} %pad_add_fusion.place_ref, f32[8,4,1,128]{3,2,1,0:T(1,128)} %fusion.1.mask_ref, f32[2]{0:T(128)} %pad_maximum_fusion.5.factors_ref, bf16[1024,512]{1,0:T(8,128)(2,1)} %get-tuple-element.137.rest_0_, ...), custom_call_target="tpu_custom_call", output_to_operand_aliasing={{0}: (22, {}), {1}: (23, {})} | custom-call | flops 10000000 | bytes 36900 | tf_op jit(solution)/shard_map/pallas_call | solution.py:303
  (133 shorter events, 38.9 us)
Async XLA Ops:
  2.5 28.3 %collective-permute-start.11 = (s16[3,1500,128]{2,1,0:T(8,128)(2,1)S(1)}, s16[3,1500,128]{2,1,0:T(8,128)(2,1)S(1)}, u32[]{:S(2)}, u32[]{:S(2)}) collective-permute-start(s16[3,1500,128]{2,1,0:T(8,128)(2,1)S(1)} %fusion), channel_id=1, source_target_pairs={{0,20},{4,16},{8,28},{12,24},{16,4},{20,0},{24,12},{28,8},{1,21},{... | collective-permute-start | bytes 3456008 | tf_op jit(solution)/shard_map/ppermute | solution.py:331
  4.9 28.3 %collective-permute-start.10 = (s16[3,1500,128]{2,1,0:T(8,128)(2,1)S(1)}, s16[3,1500,128]{2,1,0:T(8,128)(2,1)S(1)}, u32[]{:S(2)}, u32[]{:S(2)}) collective-permute-start(s16[3,1500,128]{2,1,0:T(8,128)(2,1)S(1)} %fusion), channel_id=1, source_target_pairs={{0,12},{4,8},{8,4},{12,0},{16,28},{20,24},{24,20},{28,16},{1,13},{... | collective-permute-start | bytes 3456008 | tf_op jit(solution)/shard_map/ppermute | solution.py:331
  35.7 16.0 %collective-permute-start.12 = (s16[3,1500,128]{2,1,0:T(8,128)(2,1)S(1)}, s16[3,1500,128]{2,1,0:T(8,128)(2,1)}, u32[]{:S(2)}, u32[]{:S(2)}) collective-permute-start(s16[3,1500,128]{2,1,0:T(8,128)(2,1)S(1)} %broadcast_select_fusion.1), channel_id=1, source_target_pairs={{0,16},{4,12},{8,24},{12,4},{16,0},{20,28},{24,8},{28,20},{1,17},{... | collective-permute-start | bytes 3456008 | tf_op jit(solution)/shard_map/ppermute | solution.py:337
  39.2 12.0 %collective-permute-start.8 = (f32[3,2048]{1,0:T(4,128)S(1)}, f32[3,2048]{1,0:T(4,128)S(1)}, u32[]{:S(2)}, u32[]{:S(2)}) collective-permute-start(f32[3,2048]{1,0:T(4,128)S(1)} %get-tuple-element.146), channel_id=1, source_target_pairs={{0,2},{1,3},{2,0},{3,1},{4,6},{5,7},{6,4},{7,5},{8,10},{9,11},{10,... | collective-permute-start | bytes 73736 | tf_op jit(solution)/shard_map/ppermute | solution.py:342
  52.4 48.3 %collective-permute-start.18 = (bf16[512,2048]{1,0:T(8,128)(2,1)}, bf16[512,2048]{1,0:T(8,128)(2,1)S(1)}, u32[]{:S(2)}, u32[]{:S(2)}) collective-permute-start(bf16[512,2048]{1,0:T(8,128)(2,1)} %shard_map.60.rest_11_), channel_id=1, source_target_pairs={{0,16},{4,20},{8,24},{12,28},{16,0},{20,4},{24,8},{28,12},{1,17},{... | collective-permute-start | bytes 6291464 | tf_op jit(solution)/shard_map/ppermute | solution.py:331
  52.8 48.1 %collective-permute-start.17 = (bf16[512,2048]{1,0:T(8,128)(2,1)}, bf16[512,2048]{1,0:T(8,128)(2,1)}, u32[]{:S(2)}, u32[]{:S(2)}) collective-permute-start(bf16[512,2048]{1,0:T(8,128)(2,1)} %shard_map.60.rest_11_), channel_id=1, source_target_pairs={{0,8},{4,12},{8,0},{12,4},{16,24},{20,28},{24,16},{28,20},{1,9},{5... | collective-permute-start | bytes 6291464 | tf_op jit(solution)/shard_map/ppermute | solution.py:331
  54.8 46.1 %collective-permute-start.16 = (bf16[512,2048]{1,0:T(8,128)(2,1)}, bf16[512,2048]{1,0:T(8,128)(2,1)}, u32[]{:S(2)}, u32[]{:S(2)}) collective-permute-start(bf16[512,2048]{1,0:T(8,128)(2,1)} %shard_map.60.rest_11_), channel_id=1, source_target_pairs={{0,4},{4,0},{8,12},{12,8},{16,20},{20,16},{24,28},{28,24},{1,5},{5... | collective-permute-start | bytes 6291464 | tf_op jit(solution)/shard_map/ppermute | solution.py:331
  69.0 31.9 %collective-permute-start.15 = (bf16[2,4,512,128]{3,2,1,0:T(8,128)(2,1)}, bf16[2,4,512,128]{3,2,1,0:T(8,128)(2,1)S(1)}, u32[]{:S(2)}, u32[]{:S(2)}) collective-permute-start(bf16[2,4,512,128]{3,2,1,0:T(8,128)(2,1)} %shard_map.61.rest_4_), channel_id=1, source_target_pairs={{1,0},{2,1},{3,2},{5,4},{6,5},{7,6},{9,8},{10,9},{11,10},{13,12},{... | collective-permute-start | bytes 3145736 | tf_op jit(solution)/shard_map/ppermute | solution.py:347
  70.3 30.6 %collective-permute-start.14 = (bf16[2,4,512,128]{3,2,1,0:T(8,128)(2,1)}, bf16[2,4,512,128]{3,2,1,0:T(8,128)(2,1)}, u32[]{:S(2)}, u32[]{:S(2)}) collective-permute-start(bf16[2,4,512,128]{3,2,1,0:T(8,128)(2,1)} %shard_map.61.rest_4_), channel_id=1, source_target_pairs={{0,1},{1,2},{2,3},{4,5},{5,6},{6,7},{8,9},{9,10},{10,11},{12,13},{... | collective-permute-start | bytes 3145736 | tf_op jit(solution)/shard_map/ppermute | solution.py:346
  105.0 31.9 %collective-permute-start.21 = (bf16[512,2048]{1,0:T(8,128)(2,1)}, bf16[512,2048]{1,0:T(8,128)(2,1)}, u32[]{:S(2)}, u32[]{:S(2)}) collective-permute-start(bf16[512,2048]{1,0:T(8,128)(2,1)} %broadcast_select_fusion), channel_id=1, source_target_pairs={{0,16},{4,12},{8,24},{12,4},{16,0},{20,28},{24,8},{28,20},{1,17},{... | collective-permute-start | bytes 6291464 | tf_op jit(solution)/shard_map/ppermute | solution.py:337
  106.1 30.8 %collective-permute-start.19 = (bf16[512,2048]{1,0:T(8,128)(2,1)}, bf16[512,2048]{1,0:T(8,128)(2,1)S(1)}, u32[]{:S(2)}, u32[]{:S(2)}) collective-permute-start(bf16[512,2048]{1,0:T(8,128)(2,1)} %collective-permute-done.17.rest_13_), channel_id=1, source_target_pairs={{0,4},{4,0},{8,12},{12,8},{16,20},{20,16},{24,28},{28,24},{1,5},{5... | collective-permute-start | bytes 6291464 | tf_op jit(solution)/shard_map/ppermute | solution.py:331
  106.1 30.8 %collective-permute-start.20 = (bf16[512,2048]{1,0:T(8,128)(2,1)S(1)}, bf16[512,2048]{1,0:T(8,128)(2,1)}, u32[]{:S(2)}, u32[]{:S(2)}) collective-permute-start(bf16[512,2048]{1,0:T(8,128)(2,1)S(1)} %collective-permute-done.18.rest_15_), channel_id=1, source_target_pairs={{0,4},{4,0},{8,12},{12,8},{16,20},{20,16},{24,28},{28,24},{1,5},{5... | collective-permute-start | bytes 6291464 | tf_op jit(solution)/shard_map/ppermute | solution.py:331
  106.6 17.3 %collective-permute-start.22 = (bf16[2,4,512,128]{3,2,1,0:T(8,128)(2,1)}, bf16[2,4,512,128]{3,2,1,0:T(8,128)(2,1)S(1)}, u32[]{:S(2)}, u32[]{:S(2)}) collective-permute-start(bf16[2,4,512,128]{3,2,1,0:T(8,128)(2,1)} %collective-permute-done.14.rest_5_), channel_id=1, source_target_pairs={{1,2},{2,3},{5,6},{6,7},{9,10},{10,11},{13,14},{14,15},{17,18},{18... | collective-permute-start | bytes 3145736 | tf_op jit(solution)/shard_map/ppermute | solution.py:346
  107.3 29.6 %collective-permute-start.23 = (bf16[2,4,512,128]{3,2,1,0:T(8,128)(2,1)}, bf16[2,4,512,128]{3,2,1,0:T(8,128)(2,1)S(1)}, u32[]{:S(2)}, u32[]{:S(2)}) collective-permute-start(bf16[2,4,512,128]{3,2,1,0:T(8,128)(2,1)} %copy-done.9), channel_id=1, source_target_pairs={{1,0},{2,1},{5,4},{6,5},{9,8},{10,9},{13,12},{14,13},{17,16},{18,1... | collective-permute-start | bytes 3145736 | tf_op jit(solution)/shard_map/ppermute | solution.py:347
  136.9 12.1 %collective-permute-start.24 = (bf16[512,2048]{1,0:T(8,128)(2,1)}, bf16[512,2048]{1,0:T(8,128)(2,1)S(1)}, u32[]{:S(2)}, u32[]{:S(2)}) collective-permute-start(bf16[512,2048]{1,0:T(8,128)(2,1)} %collective-permute-done.21.rest_17_), channel_id=1, source_target_pairs={{0,4},{4,0},{8,12},{12,8},{16,20},{20,16},{24,28},{28,24},{1,5},{5... | collective-permute-start | bytes 6291464 | tf_op jit(solution)/shard_map/ppermute | solution.py:331
  138.9 16.3 %collective-permute-start.27 = (bf16[1,4,512,128]{3,2,1,0:T(8,128)(2,1)}, bf16[1,4,512,128]{3,2,1,0:T(8,128)(2,1)}, u32[]{:S(2)}, u32[]{:S(2)}) collective-permute-start(bf16[1,4,512,128]{3,2,1,0:T(8,128)(2,1)} %slice.72), channel_id=1, source_target_pairs={{1,0},{5,4},{9,8},{13,12},{17,16},{21,20},{25,24},{29,28}} | collective-permute-start | bytes 1572872 | tf_op jit(solution)/shard_map/ppermute | solution.py:347
  140.2 15.0 %collective-permute-start.26 = (bf16[1,4,512,128]{3,2,1,0:T(8,128)(2,1)}, bf16[1,4,512,128]{3,2,1,0:T(8,128)(2,1)}, u32[]{:S(2)}, u32[]{:S(2)}) collective-permute-start(bf16[1,4,512,128]{3,2,1,0:T(8,128)(2,1)} %slice.71), channel_id=1, source_target_pairs={{2,3},{6,7},{10,11},{14,15},{18,19},{22,23},{26,27},{30,31}} | collective-permute-start | bytes 1572872 | tf_op jit(solution)/shard_map/ppermute | solution.py:346
  143.9 14.4 %collective-permute-start.29 = (bf16[512,512]{1,0:T(8,128)(2,1)}, bf16[512,512]{1,0:T(8,128)(2,1)}, u32[]{:S(2)}, u32[]{:S(2)}) collective-permute-start(bf16[512,512]{1,0:T(8,128)(2,1)} %get-tuple-element.134), channel_id=1, source_target_pairs={{0,16},{4,20},{8,24},{12,28},{16,0},{20,4},{24,8},{28,12},{1,17},{... | collective-permute-start | bytes 1572872 | tf_op jit(solution)/shard_map/ppermute | solution.py:331
  144.8 14.1 %collective-permute-start.28 = (bf16[512,512]{1,0:T(8,128)(2,1)}, bf16[512,512]{1,0:T(8,128)(2,1)}, u32[]{:S(2)}, u32[]{:S(2)}) collective-permute-start(bf16[512,512]{1,0:T(8,128)(2,1)} %get-tuple-element.135), channel_id=1, source_target_pairs={{0,8},{4,12},{8,0},{12,4},{16,24},{20,28},{24,16},{28,20},{1,9},{5... | collective-permute-start | bytes 1572872 | tf_op jit(solution)/shard_map/ppermute | solution.py:331
  149.1 15.5 %collective-permute-start.25 = (bf16[1024,512]{1,0:T(8,128)(2,1)S(1)}, bf16[1024,512]{1,0:T(8,128)(2,1)S(1)}, u32[]{:S(2)}, u32[]{:S(2)}) collective-permute-start(bf16[1024,512]{1,0:T(8,128)(2,1)S(1)} %get-tuple-element.109), channel_id=1, source_target_pairs={{0,4},{4,0},{8,12},{12,8},{16,20},{20,16},{24,28},{28,24},{1,5},{5... | collective-permute-start | bytes 3145736 | tf_op jit(solution)/shard_map/ppermute | solution.py:331
  159.0 32.5 %collective-permute-start.33 = (bf16[1,4,512,128]{3,2,1,0:T(8,128)(2,1)S(1)}, bf16[1,4,512,128]{3,2,1,0:T(8,128)(2,1)S(1)}, u32[]{:S(2)}, u32[]{:S(2)}) collective-permute-start(bf16[1,4,512,128]{3,2,1,0:T(8,128)(2,1)S(1)} %slice.74), channel_id=1, source_target_pairs={{1,0},{5,4},{9,8},{13,12},{17,16},{21,20},{25,24},{29,28}} | collective-permute-start | bytes 1572872 | tf_op jit(solution)/shard_map/ppermute | solution.py:347
  160.3 31.2 %collective-permute-start.32 = (bf16[1,4,512,128]{3,2,1,0:T(8,128)(2,1)S(1)}, bf16[1,4,512,128]{3,2,1,0:T(8,128)(2,1)S(1)}, u32[]{:S(2)}, u32[]{:S(2)}) collective-permute-start(bf16[1,4,512,128]{3,2,1,0:T(8,128)(2,1)S(1)} %slice.73), channel_id=1, source_target_pairs={{2,3},{6,7},{10,11},{14,15},{18,19},{22,23},{26,27},{30,31}} | collective-permute-start | bytes 1572872 | tf_op jit(solution)/shard_map/ppermute | solution.py:346
  161.3 30.2 %collective-permute-start.31 = (bf16[512,512]{1,0:T(8,128)(2,1)S(1)}, bf16[512,512]{1,0:T(8,128)(2,1)S(1)}, u32[]{:S(2)}, u32[]{:S(2)}) collective-permute-start(bf16[512,512]{1,0:T(8,128)(2,1)S(1)} %get-tuple-element.132), channel_id=1, source_target_pairs={{0,16},{4,20},{8,24},{12,28},{16,0},{20,4},{24,8},{28,12},{1,17},{... | collective-permute-start | bytes 1572872 | tf_op jit(solution)/shard_map/ppermute | solution.py:331
  162.5 29.0 %collective-permute-start.30 = (bf16[512,512]{1,0:T(8,128)(2,1)S(1)}, bf16[512,512]{1,0:T(8,128)(2,1)S(1)}, u32[]{:S(2)}, u32[]{:S(2)}) collective-permute-start(bf16[512,512]{1,0:T(8,128)(2,1)S(1)} %get-tuple-element.133), channel_id=1, source_target_pairs={{0,8},{4,12},{8,0},{12,4},{16,24},{20,28},{24,16},{28,20},{1,9},{5... | collective-permute-start | bytes 1572872 | tf_op jit(solution)/shard_map/ppermute | solution.py:331
  (32 other events, 265.8 us)

commit v12 on v6

--- a/solution.py
+++ b/solution.py
@@ -213,7 +213,7 @@
         out_specs=out_specs,
         scratch_shapes=scratch,
         compiler_params=pltpu.CompilerParams(vmem_limit_bytes=VMEM_LIMIT),
-        cost_estimate=estimate(1),
+        cost_estimate=estimate(0.01),
     )(*args)
 
 
@@ -235,28 +235,31 @@
         ],
         out_specs=pl.BlockSpec((frames, block), lambda n: (0, n)),
         compiler_params=pltpu.CompilerParams(vmem_limit_bytes=VMEM_LIMIT),
-        cost_estimate=estimate(1),
+        cost_estimate=estimate(0.01),
     )(raw, mean)
 
 
 def product_kernel(place_ref, mask_ref, factors_ref, *rest):
     near_refs, rest = rest[: len(NEAR)], rest[len(NEAR) :]
-    far_refs, rest = rest[:7], rest[7:]
-    cols_refs, rest = rest[:8], rest[8:]
-    same_ref, cross_ref, left, near_held, far_held, arrived = rest
+    far_refs, cols_refs = rest[:7], rest[7:15]
+    same_ref, cross_ref, left, near_held, far_held, arrived = rest[15:]
     feats = same_ref.shape[0]
     frames = cols_refs[0].shape[0]
     parts = frames // CHUNK
     me, z = place_ref[0], place_ref[1]
 
+    def slot_of(d):
+        crossed = (d >= 2) & (d <= 5) & ((d & 1) != (me & 1))
+        return jnp.where(crossed, 6 + 2 * (d & 1) - d, d)
+
     def put(d, c, value):
         j = me ^ d
-        after = me ^ lax.rem(j + 1, 8)
+        after = slot_of(me ^ lax.rem(j + 1, 8))
         mask = mask_ref[j, c].astype(jnp.bfloat16)
-        at = pl.multiple_of(d * frames + c * CHUNK, CHUNK)
-        left[0:feats, pl.ds(at, CHUNK)] = value
+        own = slot_of(jnp.int32(d)) * frames
+        left[0:feats, pl.ds(pl.multiple_of(own + c * CHUNK, CHUNK), CHUNK)] = value
         to = c + LAG // CHUNK
-        at = jnp.where(to < parts, d * frames + to * CHUNK, after * frames + (to - parts) * CHUNK)
+        at = jnp.where(to < parts, own + to * CHUNK, after * frames + (to - parts) * CHUNK)
         left[feats : 2 * feats, pl.ds(pl.multiple_of(at, CHUNK), CHUNK)] = value * mask
 
     @pl.when(pl.program_id(0) == 0)
@@ -321,7 +324,7 @@
             ],
         ),
         compiler_params=pltpu.CompilerParams(vmem_limit_bytes=VMEM_LIMIT),
-        cost_estimate=estimate(24),
+        cost_estimate=estimate(0.01),
     )(place, *inputs)
 
 
@@ -329,10 +332,13 @@
     return lax.ppermute(x, "tm", [(i, i ^ bits) for i in range(8)])
 
 
+def swap_by_parity(x, even, odd):
+    return lax.ppermute(x, "tm", [(i, i ^ (odd if i % 2 else even)) for i in range(8)])
+
+
 def corner(along_x, along_y):
     even = lax.axis_index("tm") % 2 == 0
-    forwarded = jnp.where(even, along_x, along_y)
-    return lax.ppermute(forwarded, "tm", [(i, i ^ (2 if i % 2 else 4)) for i in range(8)])
+    return swap_by_parity(jnp.where(even, along_x, along_y), 4, 2)
 
 
 def line_gather(x, count):
@@ -383,7 +389,7 @@
 
     facts = line_gather(jnp.concatenate([mean, pairs.astype(jnp.float32)], axis=0), feat_count)
     mine, facts, quarters = together(center(raw, mean), facts, quarters)
-    cols = {0: mine, 2: swap(mine, 2), 4: swap(mine, 4)}
+    cols = [mine, None, swap_by_parity(mine, 2, 4), None, swap_by_parity(mine, 4, 2)]
     quarters[6] = swap(quarters[7], 1)
 
     def facts_of(i, start, count):
@@ -409,26 +415,26 @@
     mask = valid.astype(jnp.float32).reshape(tm_count, parts, 1, CHUNK)
     npairs = jnp.sum(jnp.maximum(walker_lengths - LAG, 0)).astype(jnp.float32)
     factors = jnp.stack([jnp.float32(1.0 / frames_all), npairs])
-    chip_rows = contacts("own", out_pairs[:, feats:], [table], scale_own, out_mean[:, feats:])
-    chip_rows, mask, factors, up, down = together(chip_rows, mask, factors, up, down)
+    near_rows = contacts("own", out_pairs[:, :feats], [table], scale_own, out_mean[:, :feats])
+    near_x, near_y = near_rows[:row_feats], near_rows[row_feats:]
+    near_x, near_y, mask, factors, up, down, cols = together(near_x, near_y, mask, factors, up, down, cols)
     far = [mixed, up, down]
 
+    across = swap_by_parity(cols[2], 4, 2)
     up, down = line_hop(up, down, 2, feat_count)
+    cols[3] = swap(cols[2], 1)
+    their_last = swap(cols[4], 1)
+    chip_pairs, _ = together(out_pairs[:, feats:], near_x)
+    chip_rows = contacts("own", chip_pairs, [table], scale_own, out_mean[:, feats:])
+    cols += [their_last, across]
+    chip_rows, near_x, near_y, cols, up, down = together(chip_rows, near_x, near_y, cols, up, down)
+    far += [up, down, *line_hop(up, down, 3, feat_count)]
+
     cut = lambda x, start: lax.dynamic_slice_in_dim(x, start, row_feats, axis=0)
-    own = cut(chip_rows, own_half)
-    partner = swap(cut(chip_rows, row_feats - own_half), 1)
-    cols, own, partner = together(cols, own, partner)
-    cols[6] = corner(cols[2], cols[4])
-    for d in (2, 4):
-        cols[d + 1] = swap(cols[d], 1)
-    near_pairs, _ = together(out_pairs[:, :feats], own)
-    near_rows = contacts("own", near_pairs, [table], scale_own, out_mean[:, :feats])
-    near_rows, cols, up, down = together(near_rows, cols, up, down)
-
-    far += [up, down, *line_hop(up, down, 3, feat_count)]
-    cols[7] = swap(cols[6], 1)
-    near = [own, partner, swap(near_rows[:row_feats], 2), swap(near_rows[row_feats:], 4)]
-    cols = [cols[d] for d in range(8)]
+    near_x, near_y = swap(near_x, 2), swap(near_y, 4)
+    cols.append(swap(cols[6], 1))
+    partner, cols = together(cut(chip_rows, row_feats - own_half), cols)
+    near = [cut(chip_rows, own_half), swap(partner, 1), near_x, near_y]
     return products(place, mask, factors, near, far, cols)
 
 

time: 221 us -> 212 us (0.959)
  waiting for transfers between devices: 49.1 us -> 44.9 us
    ppermute x19 -> x17, waiting for transfers between devices: 29.1 us -> 24.3 us  [swap(): return lax.ppermute(x, 'tm', [(i, i ^ bits) for i in range(8)])]
    unnamed x36 -> x38, local copies, waits for them, and re-layouts: 4.96 us -> 3.08 us
    ppermute x19 -> x17, starting transfers between devices: 15.1 us -> 13.5 us  [swap(): return lax.ppermute(x, 'tm', [(i, i ^ bits) for i in range(8)])]
  transfers between devices with their start and end apart: 30 -> 30, of which waited for: 12 -> 9; matrix products, arithmetic and copies ran while one was open for 7% -> 7% of each run, Pallas kernels for 29% -> 30%
where the time goes in v12:
time: 212 us; the launch traced here: 211 us
  Pallas kernels  110 us (52%)
  waiting for transfers between devices  44.9 us (21%)
  starting transfers between devices  34.2 us (16%)
  local copies, waits for them, and re-layouts  10.2 us (5%)
  other arithmetic  9.81 us (5%)
    pallas_call x4, Pallas kernels, contacts(): pl.pallas_call(functools.partial(gather_kernel, form, chunks, len(sources...  59.5 us
    pallas_call x1, Pallas kernels, products(): pl.pallas_call(product_kernel, out_shape=[out, out], grid_spec=pltpu.Pref...  45.9 us
    ppermute x17, waiting for transfers between devices, swap(): return lax.ppermute(x, 'tm', [(i, i ^ bits) for i in range(8)])  24.3 us
    ppermute x3, waiting for transfers between devices, line_hop(): down = lax.ppermute(down, 'feat', [(i + 1, i) for i in range(count - hop)])  18.2 us
    ppermute x17, starting transfers between devices, swap(): return lax.ppermute(x, 'tm', [(i, i ^ bits) for i in range(8)])  13.5 us
    ppermute x3, starting transfers between devices, line_hop(): lax.ppermute(up, 'feat', [(i, i + 1) for i in range(hop - 1, count - 1)])  6.99 us
    ppermute x3, starting transfers between devices, line_gather(): lax.ppermute(x, 'feat', shift(s))  6.48 us
    pallas_call x1, Pallas kernels, center(): pl.pallas_call(center_kernel, out_shape=jax.ShapeDtypeStruct((frames, fea...  4.89 us
  transfers between devices with their start and end apart: 30, of which 9 were waited for; matrix products, arithmetic and copies ran while one was open for 7% of the time, Pallas kernels for 30%

profile of v12, /device:TPU:0, one launch (start us, length us, event | category | flops | bytes accessed | tf_op | source)
XLA Modules:
  0.0 211.2 jit_solution(8493758685397030680)
XLA Ops:
  0.6 1.8 fusion
  2.5 2.5 %collective-permute-start.11 = (s16[3,1500,128]{2,1,0:T(8,128)(2,1)S(1)}, s16[3,1500,128]{2,1,0:T(8,128)(2,1)S(1)}, u32[]{:S(2)}, u32[]{:S(2)}) collective-permute-start(s16[3,1500,128]{2,1,0:T(8,128)(2,1)S(1)} %fusion), channel_id=1, source_target_pairs={{0,20},{4,16},{8,28},{12,24},{16,4},{20,0},{24,12},{28,8},{1,21},{... | collective-permute-start | bytes 3456008 | tf_op jit(solution)/shard_map/ppermute | solution.py:332
  4.9 1.8 collective-permute-start.10
  7.3 18.1 %shard_map.59 = (f32[2048,512]{1,0:T(8,128)}, f32[1,2048]{1,0:T(1,128)}, s32[24000,128]{1,0:T(8,128)}) custom-call(s32[2,2048]{1,0:T(2,128)} %get-tuple-element.132.pairs_ref, f32[4,128]{1,0:T(4,128)} %bitcast.25, s32[3,1500,512]{2,1,0:T(8,128)} %bitcast.24), custom_call_target="tpu_custom_call" | custom-call | flops 10000000 | bytes 36900 | tf_op jit(solution)/shard_map/pallas_call | solution.py:208
  26.3 2.3 %collective-permute-start.5 = (f32[1,2560]{1,0:T(1,128)S(1)}, f32[1,2560]{1,0:T(1,128)S(1)}, u32[]{:S(2)}, u32[]{:S(2)}) collective-permute-start(f32[1,2560]{1,0:T(1,128)S(1)} %pad_maximum_fusion.3), channel_id=1, source_target_pairs={{0,24},{4,28},{8,16},{12,20},{16,8},{20,12},{24,0},{28,4},{1,25},{... | collective-permute-start | bytes 30728 | tf_op jit(solution)/shard_map/ppermute | solution.py:332
  29.1 1.6 collective-permute-done.11.rest_1_
  30.8 2.5 %collective-permute-start.3 = (f32[1,2560]{1,0:T(1,128)S(1)}, f32[1,2560]{1,0:T(1,128)S(1)}, u32[]{:S(2)}, u32[]{:S(2)}) collective-permute-start(f32[1,2560]{1,0:T(1,128)S(1)} %pad_maximum_fusion.3), channel_id=1, source_target_pairs={{0,16},{4,20},{8,24},{12,28},{16,0},{20,4},{24,8},{28,12},{1,17},{... | collective-permute-start | bytes 30728 | tf_op jit(solution)/shard_map/ppermute | solution.py:332
  36.3 1.6 collective-permute-done.1
  38.7 2.7 %collective-permute-start.8 = (f32[3,2048]{1,0:T(4,128)S(1)}, f32[3,2048]{1,0:T(4,128)S(1)}, u32[]{:S(2)}, u32[]{:S(2)}) collective-permute-start(f32[3,2048]{1,0:T(4,128)S(1)} %get-tuple-element.130), channel_id=1, source_target_pairs={{0,2},{1,3},{2,0},{3,1},{4,6},{5,7},{6,4},{7,5},{8,10},{9,11},{10,... | collective-permute-start | bytes 73736 | tf_op jit(solution)/shard_map/ppermute | solution.py:346
  41.4 1.6 collective-permute-start.7
  43.0 2.2 %collective-permute-start.9 = (f32[3,2048]{1,0:T(4,128)S(1)}, f32[3,2048]{1,0:T(4,128)S(1)}, u32[]{:S(2)}, u32[]{:S(2)}) collective-permute-start(f32[3,2048]{1,0:T(4,128)S(1)} %get-tuple-element.130), channel_id=1, source_target_pairs={{0,3},{1,0},{2,1},{3,2},{4,7},{5,4},{6,5},{7,6},{8,11},{9,8},{10,9... | collective-permute-start | bytes 73736 | tf_op jit(solution)/shard_map/ppermute | solution.py:346
  45.8 4.9 %shard_map.60.rest_11_ = bf16[512,2048]{1,0:T(8,128)(2,1)} custom-call(f32[2048,512]{1,0:T(8,128)} %get-tuple-element.59.raw_ref, f32[1,2048]{1,0:T(1,128)} %copy-done.14), custom_call_target="tpu_custom_call" | custom-call | flops 10000000 | bytes 36900 | tf_op jit(solution)/shard_map/pallas_call | solution.py:228
  54.1 2.1 collective-permute-done.13.rest_2_
  58.3 12.1 %shard_map.61.rest_4_ = bf16[4,1024,128]{2,1,0:T(8,128)(2,1)} custom-call(s32[2,1024]{1,0:T(2,128)} %broadcast_multiply_fusion.2.pairs_ref, f32[4,128]{1,0:T(4,128)} %pad_maximum_fusion.4.scale_ref, s16[3,1500,128]{2,1,0:T(8,128)(2,1)} %copy-done.1, s16[3,1500,128]{2,1,0:T(8,128)(2,1)} %copy-done, s16[3,1500,128]{2,1,0:T(8,128)(2,1)} %copy-done.6, ...), custom_call_target="tpu_custom_call" | custom-call | flops 10000000 | bytes 36900 | tf_op jit(solution)/shard_map/pallas_call | solution.py:208
  71.7 5.6 %collective-permute-start.14 = (bf16[4,1024,128]{2,1,0:T(8,128)(2,1)}, bf16[4,1024,128]{2,1,0:T(8,128)(2,1)}, u32[]{:S(2)}, u32[]{:S(2)}) collective-permute-start(bf16[4,1024,128]{2,1,0:T(8,128)(2,1)} %shard_map.61.rest_4_), channel_id=1, source_target_pairs={{0,1},{1,2},{2,3},{4,5},{5,6},{6,7},{8,9},{9,10},{10,11},{12,13},{... | collective-permute-start | bytes 3145736 | tf_op jit(solution)/shard_map/ppermute | solution.py:350
  79.6 14.6 %shard_map.62 = bf16[2048,512]{1,0:T(8,128)(2,1)} custom-call(s32[2,2048]{1,0:T(2,128)} %get-tuple-element.128.pairs_ref, f32[4,128]{1,0:T(4,128)} %bitcast.26, s32[24000,128]{1,0:T(8,128)} %get-tuple-element.80.rest_0_, f32[1,2048]{1,0:T(1,128)} %get-tuple-element.126.rest_1_), custom_call_target="tpu_custom_call" | custom-call | flops 10000000 | bytes 36900 | tf_op jit(solution)/shard_map/pallas_call | solution.py:208
  95.5 2.6 %fusion.4 = (bf16[1024,512]{1,0:T(8,128)(2,1)S(1)}, bf16[1024,512]{1,0:T(8,128)(2,1)}) fusion(bf16[2048,512]{1,0:T(8,128)(2,1)} %shard_map.62), kind=kLoop, calls=%fused_computation.42 | loop fusion | bytes 4194304 | tf_op jit(solution)/shard_map/slice | solution.py:419
  98.1 1.7 collective-permute-done.18.rest_15_
  103.4 14.6 %shard_map.63 = bf16[2048,512]{1,0:T(8,128)(2,1)} custom-call(s32[2,2048]{1,0:T(2,128)} %broadcast_multiply_fusion.pairs_ref, f32[4,128]{1,0:T(4,128)} %bitcast.27, s32[24000,128]{1,0:T(8,128)} %get-tuple-element.80.rest_0_, f32[1,2048]{1,0:T(1,128)} %get-tuple-element.125.rest_1_), custom_call_target="tpu_custom_call" | custom-call | flops 10000000 | bytes 36900 | tf_op jit(solution)/shard_map/pallas_call | solution.py:208
  118.1 14.4 %collective-permute-done.23.rest_8_ = bf16[4,1024,128]{2,1,0:T(8,128)(2,1)S(1)} collective-permute-done((bf16[4,1024,128]{2,1,0:T(8,128)(2,1)}, bf16[4,1024,128]{2,1,0:T(8,128)(2,1)S(1)}, u32[]{:S(2)}, u32[]{:S(2)}) %collective-permute-start.23) | collective-permute-done | bytes 1048608 | tf_op jit(solution)/shard_map/ppermute | solution.py:351
  138.2 2.7 %constant_dynamic-slice_fusion = (bf16[1024,512]{1,0:T(8,128)(2,1)S(1)}, bf16[1024,512]{1,0:T(8,128)(2,1)}) fusion(bf16[2048,512]{1,0:T(8,128)(2,1)} %shard_map.63, s32[]{:T(128)S(6)} %select_n.89, s32[]{:T(128)S(6)} %select_n.81), kind=kLoop, calls=%fused_computation.31 | loop fusion | bytes 4194312 | tf_op jit(solution)/shard_map/dynamic_slice | solution.py:433
  141.6 18.4 %collective-permute-done.26.rest_2_ = bf16[1024,512]{1,0:T(8,128)(2,1)S(1)} collective-permute-done((bf16[1024,512]{1,0:T(8,128)(2,1)}, bf16[1024,512]{1,0:T(8,128)(2,1)S(1)}, u32[]{:S(2)}, u32[]{:S(2)}) %collective-permute-start.26) | collective-permute-done | bytes 1048608 | tf_op jit(solution)/shard_map/ppermute | solution.py:332
  160.1 3.8 %collective-permute-done.29.rest_10_ = bf16[4,1024,128]{2,1,0:T(8,128)(2,1)S(1)} collective-permute-done((bf16[4,1024,128]{2,1,0:T(8,128)(2,1)}, bf16[4,1024,128]{2,1,0:T(8,128)(2,1)S(1)}, u32[]{:S(2)}, u32[]{:S(2)}) %collective-permute-start.29) | collective-permute-done | bytes 1048608 | tf_op jit(solution)/shard_map/ppermute | solution.py:351
  165.1 45.9 %shard_map.64 = (f32[1024,2048]{1,0:T(8,128)}, f32[1024,2048]{1,0:T(8,128)}) custom-call(s32[2]{0:T(128)} %pad_add_fusion.place_ref, f32[8,4,1,128]{3,2,1,0:T(1,128)} %fusion.1.mask_ref, f32[2]{0:T(128)} %pad_maximum_fusion.5.factors_ref, bf16[1024,512]{1,0:T(8,128)(2,1)} %get-tuple-element.119.rest_0_, bf16[1024,512]{1,0:T(8,128)(2,1)} %copy-done.13, ...), custom_call_target="tpu_custom_call" | custom-call | flops 10000000 | bytes 36900 | tf_op jit(solution)/shard_map/pallas_call | solution.py:306
  (112 shorter events, 27.3 us)
Async XLA Ops:
  2.5 28.3 %collective-permute-start.11 = (s16[3,1500,128]{2,1,0:T(8,128)(2,1)S(1)}, s16[3,1500,128]{2,1,0:T(8,128)(2,1)S(1)}, u32[]{:S(2)}, u32[]{:S(2)}) collective-permute-start(s16[3,1500,128]{2,1,0:T(8,128)(2,1)S(1)} %fusion), channel_id=1, source_target_pairs={{0,20},{4,16},{8,28},{12,24},{16,4},{20,0},{24,12},{28,8},{1,21},{... | collective-permute-start | bytes 3456008 | tf_op jit(solution)/shard_map/ppermute | solution.py:332
  4.9 28.3 %collective-permute-start.10 = (s16[3,1500,128]{2,1,0:T(8,128)(2,1)S(1)}, s16[3,1500,128]{2,1,0:T(8,128)(2,1)S(1)}, u32[]{:S(2)}, u32[]{:S(2)}) collective-permute-start(s16[3,1500,128]{2,1,0:T(8,128)(2,1)S(1)} %fusion), channel_id=1, source_target_pairs={{0,12},{4,8},{8,4},{12,0},{16,28},{20,24},{24,20},{28,16},{1,13},{... | collective-permute-start | bytes 3456008 | tf_op jit(solution)/shard_map/ppermute | solution.py:332
  26.2 8.1 %collective-permute-start.6 = (f32[1,2560]{1,0:T(1,128)S(1)}, f32[1,2560]{1,0:T(1,128)S(1)}, u32[]{:S(2)}, u32[]{:S(2)}) collective-permute-start(f32[1,2560]{1,0:T(1,128)S(1)} %pad_maximum_fusion.3), channel_id=1, source_target_pairs={{0,28},{4,24},{8,20},{12,16},{16,12},{20,8},{24,4},{28,0},{1,29},{... | collective-permute-start | bytes 30728 | tf_op jit(solution)/shard_map/ppermute | solution.py:332
  26.3 8.5 %collective-permute-start.5 = (f32[1,2560]{1,0:T(1,128)S(1)}, f32[1,2560]{1,0:T(1,128)S(1)}, u32[]{:S(2)}, u32[]{:S(2)}) collective-permute-start(f32[1,2560]{1,0:T(1,128)S(1)} %pad_maximum_fusion.3), channel_id=1, source_target_pairs={{0,24},{4,28},{8,16},{12,20},{16,8},{20,12},{24,0},{28,4},{1,25},{... | collective-permute-start | bytes 30728 | tf_op jit(solution)/shard_map/ppermute | solution.py:332
  28.6 6.8 %collective-permute-start.4 = (f32[1,2560]{1,0:T(1,128)S(1)}, f32[1,2560]{1,0:T(1,128)}, u32[]{:S(2)}, u32[]{:S(2)}) collective-permute-start(f32[1,2560]{1,0:T(1,128)S(1)} %pad_maximum_fusion.3), channel_id=1, source_target_pairs={{0,20},{4,16},{8,28},{12,24},{16,4},{20,0},{24,12},{28,8},{1,21},{... | collective-permute-start | bytes 30728 | tf_op jit(solution)/shard_map/ppermute | solution.py:332
  35.5 16.0 %collective-permute-start.12 = (s16[3,1500,128]{2,1,0:T(8,128)(2,1)S(1)}, s16[3,1500,128]{2,1,0:T(8,128)(2,1)S(1)}, u32[]{:S(2)}, u32[]{:S(2)}) collective-permute-start(s16[3,1500,128]{2,1,0:T(8,128)(2,1)S(1)} %broadcast_select_fusion), channel_id=1, source_target_pairs={{0,16},{4,12},{8,24},{12,4},{16,0},{20,28},{24,8},{28,20},{1,17},{... | collective-permute-start | bytes 3456008 | tf_op jit(solution)/shard_map/ppermute | solution.py:336
  38.7 12.0 %collective-permute-start.8 = (f32[3,2048]{1,0:T(4,128)S(1)}, f32[3,2048]{1,0:T(4,128)S(1)}, u32[]{:S(2)}, u32[]{:S(2)}) collective-permute-start(f32[3,2048]{1,0:T(4,128)S(1)} %get-tuple-element.130), channel_id=1, source_target_pairs={{0,2},{1,3},{2,0},{3,1},{4,6},{5,7},{6,4},{7,5},{8,10},{9,11},{10,... | collective-permute-start | bytes 73736 | tf_op jit(solution)/shard_map/ppermute | solution.py:346
  41.4 9.3 %collective-permute-start.7 = (f32[3,2048]{1,0:T(4,128)S(1)}, f32[3,2048]{1,0:T(4,128)S(1)}, u32[]{:S(2)}, u32[]{:S(2)}) collective-permute-start(f32[3,2048]{1,0:T(4,128)S(1)} %get-tuple-element.130), channel_id=1, source_target_pairs={{0,1},{1,2},{2,3},{3,0},{4,5},{5,6},{6,7},{7,4},{8,9},{9,10},{10,1... | collective-permute-start | bytes 73736 | tf_op jit(solution)/shard_map/ppermute | solution.py:346
  43.0 7.7 %collective-permute-start.9 = (f32[3,2048]{1,0:T(4,128)S(1)}, f32[3,2048]{1,0:T(4,128)S(1)}, u32[]{:S(2)}, u32[]{:S(2)}) collective-permute-start(f32[3,2048]{1,0:T(4,128)S(1)} %get-tuple-element.130), channel_id=1, source_target_pairs={{0,3},{1,0},{2,1},{3,2},{4,7},{5,4},{6,5},{7,6},{8,11},{9,8},{10,9... | collective-permute-start | bytes 73736 | tf_op jit(solution)/shard_map/ppermute | solution.py:346
  51.5 48.3 %collective-permute-start.18 = (bf16[512,2048]{1,0:T(8,128)(2,1)}, bf16[512,2048]{1,0:T(8,128)(2,1)S(1)}, u32[]{:S(2)}, u32[]{:S(2)}) collective-permute-start(bf16[512,2048]{1,0:T(8,128)(2,1)} %shard_map.60.rest_11_), channel_id=1, source_target_pairs={{0,16},{4,12},{8,24},{12,4},{16,0},{20,28},{24,8},{28,20},{1,17},{... | collective-permute-start | bytes 6291464 | tf_op jit(solution)/shard_map/ppermute | solution.py:336
  51.9 47.9 %collective-permute-start.17 = (bf16[512,2048]{1,0:T(8,128)(2,1)}, bf16[512,2048]{1,0:T(8,128)(2,1)}, u32[]{:S(2)}, u32[]{:S(2)}) collective-permute-start(bf16[512,2048]{1,0:T(8,128)(2,1)} %shard_map.60.rest_11_), channel_id=1, source_target_pairs={{0,8},{4,20},{8,0},{12,28},{16,24},{20,4},{24,16},{28,12},{1,9},{5... | collective-permute-start | bytes 6291464 | tf_op jit(solution)/shard_map/ppermute | solution.py:336
  56.2 43.6 %collective-permute-start.16 = (bf16[512,2048]{1,0:T(8,128)(2,1)}, bf16[512,2048]{1,0:T(8,128)(2,1)}, u32[]{:S(2)}, u32[]{:S(2)}) collective-permute-start(bf16[512,2048]{1,0:T(8,128)(2,1)} %shard_map.60.rest_11_), channel_id=1, source_target_pairs={{0,4},{4,0},{8,12},{12,8},{16,20},{20,16},{24,28},{28,24},{1,5},{5... | collective-permute-start | bytes 6291464 | tf_op jit(solution)/shard_map/ppermute | solution.py:332
  70.4 29.4 %collective-permute-start.15 = (bf16[4,1024,128]{2,1,0:T(8,128)(2,1)}, bf16[4,1024,128]{2,1,0:T(8,128)(2,1)}, u32[]{:S(2)}, u32[]{:S(2)}) collective-permute-start(bf16[4,1024,128]{2,1,0:T(8,128)(2,1)} %shard_map.61.rest_4_), channel_id=1, source_target_pairs={{1,0},{2,1},{3,2},{5,4},{6,5},{7,6},{9,8},{10,9},{11,10},{13,12},{... | collective-permute-start | bytes 3145736 | tf_op jit(solution)/shard_map/ppermute | solution.py:351
  71.7 28.1 %collective-permute-start.14 = (bf16[4,1024,128]{2,1,0:T(8,128)(2,1)}, bf16[4,1024,128]{2,1,0:T(8,128)(2,1)}, u32[]{:S(2)}, u32[]{:S(2)}) collective-permute-start(bf16[4,1024,128]{2,1,0:T(8,128)(2,1)} %shard_map.61.rest_4_), channel_id=1, source_target_pairs={{0,1},{1,2},{2,3},{4,5},{5,6},{6,7},{8,9},{9,10},{10,11},{12,13},{... | collective-permute-start | bytes 3145736 | tf_op jit(solution)/shard_map/ppermute | solution.py:350
  99.8 32.7 %collective-permute-start.20 = (bf16[512,2048]{1,0:T(8,128)(2,1)S(1)}, bf16[512,2048]{1,0:T(8,128)(2,1)S(1)}, u32[]{:S(2)}, u32[]{:S(2)}) collective-permute-start(bf16[512,2048]{1,0:T(8,128)(2,1)S(1)} %collective-permute-done.18.rest_15_), channel_id=1, source_target_pairs={{0,4},{4,0},{8,12},{12,8},{16,20},{20,16},{24,28},{28,24},{1,5},{5... | collective-permute-start | bytes 6291464 | tf_op jit(solution)/shard_map/ppermute | solution.py:332
  99.9 34.0 %collective-permute-start.21 = (bf16[512,2048]{1,0:T(8,128)(2,1)}, bf16[512,2048]{1,0:T(8,128)(2,1)}, u32[]{:S(2)}, u32[]{:S(2)}) collective-permute-start(bf16[512,2048]{1,0:T(8,128)(2,1)} %collective-permute-done.17.rest_13_), channel_id=1, source_target_pairs={{0,16},{4,12},{8,24},{12,4},{16,0},{20,28},{24,8},{28,20},{1,17},{... | collective-permute-start | bytes 6291464 | tf_op jit(solution)/shard_map/ppermute | solution.py:336
  100.8 33.1 %collective-permute-start.19 = (bf16[512,2048]{1,0:T(8,128)(2,1)}, bf16[512,2048]{1,0:T(8,128)(2,1)}, u32[]{:S(2)}, u32[]{:S(2)}) collective-permute-start(bf16[512,2048]{1,0:T(8,128)(2,1)} %collective-permute-done.17.rest_13_), channel_id=1, source_target_pairs={{0,4},{4,0},{8,12},{12,8},{16,20},{20,16},{24,28},{28,24},{1,5},{5... | collective-permute-start | bytes 6291464 | tf_op jit(solution)/shard_map/ppermute | solution.py:332
  100.8 17.3 %collective-permute-start.22 = (bf16[4,1024,128]{2,1,0:T(8,128)(2,1)}, bf16[4,1024,128]{2,1,0:T(8,128)(2,1)S(1)}, u32[]{:S(2)}, u32[]{:S(2)}) collective-permute-start(bf16[4,1024,128]{2,1,0:T(8,128)(2,1)} %collective-permute-done.14.rest_5_), channel_id=1, source_target_pairs={{1,2},{2,3},{5,6},{6,7},{9,10},{10,11},{13,14},{14,15},{17,18},{18... | collective-permute-start | bytes 3145736 | tf_op jit(solution)/shard_map/ppermute | solution.py:350
  101.5 31.0 %collective-permute-start.23 = (bf16[4,1024,128]{2,1,0:T(8,128)(2,1)}, bf16[4,1024,128]{2,1,0:T(8,128)(2,1)S(1)}, u32[]{:S(2)}, u32[]{:S(2)}) collective-permute-start(bf16[4,1024,128]{2,1,0:T(8,128)(2,1)} %collective-permute-done.15.rest_6_), channel_id=1, source_target_pairs={{1,0},{2,1},{5,4},{6,5},{9,8},{10,9},{13,12},{14,13},{17,16},{18,1... | collective-permute-start | bytes 3145736 | tf_op jit(solution)/shard_map/ppermute | solution.py:351
  134.2 25.8 %collective-permute-start.26 = (bf16[1024,512]{1,0:T(8,128)(2,1)}, bf16[1024,512]{1,0:T(8,128)(2,1)S(1)}, u32[]{:S(2)}, u32[]{:S(2)}) collective-permute-start(bf16[1024,512]{1,0:T(8,128)(2,1)} %get-tuple-element.104), channel_id=1, source_target_pairs={{0,8},{4,12},{8,0},{12,4},{16,24},{20,28},{24,16},{28,20},{1,9},{5... | collective-permute-start | bytes 3145736 | tf_op jit(solution)/shard_map/ppermute | solution.py:332
  134.8 25.3 %collective-permute-start.27 = (bf16[1024,512]{1,0:T(8,128)(2,1)S(1)}, bf16[1024,512]{1,0:T(8,128)(2,1)S(1)}, u32[]{:S(2)}, u32[]{:S(2)}) collective-permute-start(bf16[1024,512]{1,0:T(8,128)(2,1)S(1)} %get-tuple-element.105), channel_id=1, source_target_pairs={{0,16},{4,20},{8,24},{12,28},{16,0},{20,4},{24,8},{28,12},{1,17},{... | collective-permute-start | bytes 3145736 | tf_op jit(solution)/shard_map/ppermute | solution.py:332
  136.0 24.1 %collective-permute-start.28 = (bf16[4,1024,128]{2,1,0:T(8,128)(2,1)}, bf16[4,1024,128]{2,1,0:T(8,128)(2,1)S(1)}, u32[]{:S(2)}, u32[]{:S(2)}) collective-permute-start(bf16[4,1024,128]{2,1,0:T(8,128)(2,1)} %copy-done.7), channel_id=1, source_target_pairs={{2,3},{6,7},{10,11},{14,15},{18,19},{22,23},{26,27},{30,31}} | collective-permute-start | bytes 3145736 | tf_op jit(solution)/shard_map/ppermute | solution.py:350
  136.7 27.1 %collective-permute-start.29 = (bf16[4,1024,128]{2,1,0:T(8,128)(2,1)}, bf16[4,1024,128]{2,1,0:T(8,128)(2,1)S(1)}, u32[]{:S(2)}, u32[]{:S(2)}) collective-permute-start(bf16[4,1024,128]{2,1,0:T(8,128)(2,1)} %copy-done.8), channel_id=1, source_target_pairs={{1,0},{5,4},{9,8},{13,12},{17,16},{21,20},{25,24},{29,28}} | collective-permute-start | bytes 3145736 | tf_op jit(solution)/shard_map/ppermute | solution.py:351
  140.9 22.9 %collective-permute-start.25 = (bf16[1024,512]{1,0:T(8,128)(2,1)S(1)}, bf16[1024,512]{1,0:T(8,128)(2,1)S(1)}, u32[]{:S(2)}, u32[]{:S(2)}) collective-permute-start(bf16[1024,512]{1,0:T(8,128)(2,1)S(1)} %get-tuple-element.103), channel_id=1, source_target_pairs={{0,4},{4,0},{8,12},{12,8},{16,20},{20,16},{24,28},{28,24},{1,5},{5... | collective-permute-start | bytes 3145736 | tf_op jit(solution)/shard_map/ppermute | solution.py:332
  (25 other events, 211.9 us)

commit v13 on v12

--- a/solution.py
+++ b/solution.py
@@ -12,6 +12,7 @@
 VMEM_LIMIT = 56 * 1024 * 1024
 NEAR = (0, 1, 2, 4)
 FAR = (3, 5, 6, 7)
+TABLE_ROWS = 16
 
 
 def contact_values(coords, frame_scale, pairs):
@@ -167,7 +168,7 @@
             pltpu.make_async_copy(table, table_out, left).wait()
 
 
-def contacts(form, pairs, sources, scale, mean=None, block=512, group=32):
+def contacts(form, pairs, sources, scale, mean=None, block=512, group=128):
     feats = pairs.shape[1]
     chunks = scale.shape[0]
     stride = -(-3 * chunks // 8) * 8
@@ -176,7 +177,7 @@
     any_spec = pl.BlockSpec(memory_space=pl.ANY)
     in_specs = [pl.BlockSpec(memory_space=pltpu.SMEM), pl.BlockSpec((chunks, CHUNK), lambda n: (0, 0))]
     in_specs += [any_spec] * len(sources)
-    args = [pairs * stride, scale, *sources]
+    args = [pairs, scale, *sources]
     scratch = [
         pltpu.VMEM((rows, CHUNK), jnp.int32),
         pltpu.VMEM((group * chunks, CHUNK), jnp.float32),
@@ -374,7 +375,7 @@
     quarter = lax.dynamic_slice_in_dim(coords_t, z * CHUNK, CHUNK, axis=2).astype(jnp.int16)
     quarters = {3: swap(quarter, 3), 5: swap(quarter, 5)}
 
-    raw, sums, table = contacts("first", pairs, [coords_t], scale_own)
+    raw, sums, table = contacts("first", pairs * TABLE_ROWS, [coords_t], scale_own)
     quarters, _ = together(quarters, sums)
     quarters[7] = corner(quarters[3], quarters[5])
     note = jnp.concatenate([sums, frame_scale.reshape(1, frames_dev)], axis=1)
@@ -402,12 +403,13 @@
         axis=1,
     )
     row_facts, out_facts, scales = together(row_facts, out_facts, scales)
-    row_mean, row_pairs = row_facts[0:1], row_facts[1:3].astype(jnp.int32)
-    out_mean, out_pairs = out_facts[0:1], out_facts[1:3].astype(jnp.int32)
-
-    row_pairs, mine, quarters = together(row_pairs, mine, quarters)
+    row_mean, row_pairs = row_facts[0:1], row_facts[1:3].astype(jnp.int32) * TABLE_ROWS
+    out_mean, out_pairs = out_facts[0:1], out_facts[1:3].astype(jnp.int32) * TABLE_ROWS
+    mixed_scale = scale_of(*FAR)
+
+    row_pairs, row_mean, mixed_scale, mine, quarters = together(row_pairs, row_mean, mixed_scale, mine, quarters)
     cols[1] = swap(mine, 1)
-    mixed = contacts("sent", row_pairs, [quarters[d] for d in FAR], scale_of(*FAR), row_mean)
+    mixed = contacts("sent", row_pairs, [quarters[d] for d in FAR], mixed_scale, row_mean)
 
     out_pairs, mixed, walker_lengths = together(out_pairs, mixed, walker_lengths)
     up, down = line_hop(mixed, mixed, 1, feat_count)

time: 212 us -> 211 us (level)
  Pallas kernels: 110 us -> 107 us
  waiting for transfers between devices: 44.9 us -> 47.4 us
    pallas_call x4, Pallas kernels: 59.5 us -> 55.8 us  [contacts(): pl.pallas_call(functools.partial(gather_kernel, form, chunks, len(sources...]
    ppermute x4, waiting for transfers between devices: 2.41 us -> 5.26 us  [swap_by_parity(): lax.ppermute(x, 'tm', [(i, i ^ (odd if i % 2 else even)) for i in range(8)])]
  transfers between devices with their start and end apart: 30 -> 30, of which waited for: 9 -> 10; matrix products, arithmetic and copies ran while one was open for 7% -> 7% of each run, Pallas kernels for 30% -> 29%
where the time goes in v13:
time: 211 us; the launch traced here: 210 us
  Pallas kernels  107 us (51%)
  waiting for transfers between devices  47.4 us (22%)
  starting transfers between devices  34.4 us (16%)
  local copies, waits for them, and re-layouts  11.7 us (6%)
  other arithmetic  8.47 us (4%)
    pallas_call x4, Pallas kernels, contacts(): pl.pallas_call(functools.partial(gather_kernel, form, chunks, len(sources...  55.8 us
    pallas_call x1, Pallas kernels, products(): pl.pallas_call(product_kernel, out_shape=[out, out], grid_spec=pltpu.Pref...  45.9 us
    ppermute x17, waiting for transfers between devices, swap(): return lax.ppermute(x, 'tm', [(i, i ^ bits) for i in range(8)])  23.6 us
    ppermute x3, waiting for transfers between devices, line_hop(): down = lax.ppermute(down, 'feat', [(i + 1, i) for i in range(count - hop)])  18.6 us
    ppermute x17, starting transfers between devices, swap(): return lax.ppermute(x, 'tm', [(i, i ^ bits) for i in range(8)])  13.8 us
    ppermute x3, starting transfers between devices, line_hop(): lax.ppermute(up, 'feat', [(i, i + 1) for i in range(hop - 1, count - 1)])  6.99 us
    ppermute x3, starting transfers between devices, line_gather(): lax.ppermute(x, 'feat', shift(s))  6.48 us
    ppermute x4, waiting for transfers between devices, swap_by_parity(): lax.ppermute(x, 'tm', [(i, i ^ (odd if i % 2 else even)) for i in range(8)])  5.26 us
  transfers between devices with their start and end apart: 30, of which 10 were waited for; matrix products, arithmetic and copies ran while one was open for 7% of the time, Pallas kernels for 29%

profile of v13, /device:TPU:0, one launch (start us, length us, event | category | flops | bytes accessed | tf_op | source)
XLA Modules:
  0.0 210.3 jit_solution(17150330962689117341)
XLA Ops:
  0.6 1.8 fusion
  2.5 2.5 %collective-permute-start.11 = (s16[3,1500,128]{2,1,0:T(8,128)(2,1)S(1)}, s16[3,1500,128]{2,1,0:T(8,128)(2,1)S(1)}, u32[]{:S(2)}, u32[]{:S(2)}) collective-permute-start(s16[3,1500,128]{2,1,0:T(8,128)(2,1)S(1)} %fusion), channel_id=1, source_target_pairs={{0,20},{4,16},{8,28},{12,24},{16,4},{20,0},{24,12},{28,8},{1,21},{... | collective-permute-start | bytes 3456008 | tf_op jit(solution)/shard_map/ppermute | solution.py:333
  4.9 1.8 collective-permute-start.10
  7.3 17.5 %shard_map.59 = (f32[2048,512]{1,0:T(8,128)}, f32[1,2048]{1,0:T(1,128)}, s32[24000,128]{1,0:T(8,128)}) custom-call(s32[2,2048]{1,0:T(2,128)} %get-tuple-element.136.pairs_ref, f32[4,128]{1,0:T(4,128)} %bitcast.25, s32[3,1500,512]{2,1,0:T(8,128)} %bitcast.24), custom_call_target="tpu_custom_call" | custom-call | flops 10000000 | bytes 36900 | tf_op jit(solution)/shard_map/pallas_call | solution.py:209
  25.7 2.3 %collective-permute-start.5 = (f32[1,2560]{1,0:T(1,128)S(1)}, f32[1,2560]{1,0:T(1,128)S(1)}, u32[]{:S(2)}, u32[]{:S(2)}) collective-permute-start(f32[1,2560]{1,0:T(1,128)S(1)} %pad_maximum_fusion.3), channel_id=1, source_target_pairs={{0,24},{4,28},{8,16},{12,20},{16,8},{20,12},{24,0},{28,4},{1,25},{... | collective-permute-start | bytes 30728 | tf_op jit(solution)/shard_map/ppermute | solution.py:333
  28.6 2.2 %collective-permute-done.11.rest_1_ = s16[3,1500,128]{2,1,0:T(8,128)(2,1)S(1)} collective-permute-done((s16[3,1500,128]{2,1,0:T(8,128)(2,1)S(1)}, s16[3,1500,128]{2,1,0:T(8,128)(2,1)S(1)}, u32[]{:S(2)}, u32[]{:S(2)}) %collective-permute-start.11) | collective-permute-done | bytes 1152032 | tf_op jit(solution)/shard_map/ppermute | solution.py:333
  30.8 2.5 %collective-permute-start.3 = (f32[1,2560]{1,0:T(1,128)S(1)}, f32[1,2560]{1,0:T(1,128)S(1)}, u32[]{:S(2)}, u32[]{:S(2)}) collective-permute-start(f32[1,2560]{1,0:T(1,128)S(1)} %pad_maximum_fusion.3), channel_id=1, source_target_pairs={{0,16},{4,20},{8,24},{12,28},{16,0},{20,4},{24,8},{28,12},{1,17},{... | collective-permute-start | bytes 30728 | tf_op jit(solution)/shard_map/ppermute | solution.py:333
  36.3 1.6 collective-permute-done.1
  38.7 2.7 %collective-permute-start.8 = (f32[3,2048]{1,0:T(4,128)S(1)}, f32[3,2048]{1,0:T(4,128)S(1)}, u32[]{:S(2)}, u32[]{:S(2)}) collective-permute-start(f32[3,2048]{1,0:T(4,128)S(1)} %get-tuple-element.134), channel_id=1, source_target_pairs={{0,2},{1,3},{2,0},{3,1},{4,6},{5,7},{6,4},{7,5},{8,10},{9,11},{10,... | collective-permute-start | bytes 73736 | tf_op jit(solution)/shard_map/ppermute | solution.py:347
  41.4 1.6 collective-permute-start.7
  43.0 2.2 %collective-permute-start.9 = (f32[3,2048]{1,0:T(4,128)S(1)}, f32[3,2048]{1,0:T(4,128)S(1)}, u32[]{:S(2)}, u32[]{:S(2)}) collective-permute-start(f32[3,2048]{1,0:T(4,128)S(1)} %get-tuple-element.134), channel_id=1, source_target_pairs={{0,3},{1,0},{2,1},{3,2},{4,7},{5,4},{6,5},{7,6},{8,11},{9,8},{10,9... | collective-permute-start | bytes 73736 | tf_op jit(solution)/shard_map/ppermute | solution.py:347
  45.8 4.9 %shard_map.60.rest_11_ = bf16[512,2048]{1,0:T(8,128)(2,1)} custom-call(f32[2048,512]{1,0:T(8,128)} %get-tuple-element.61.raw_ref, f32[1,2048]{1,0:T(1,128)} %copy-done.14), custom_call_target="tpu_custom_call" | custom-call | flops 10000000 | bytes 36900 | tf_op jit(solution)/shard_map/pallas_call | solution.py:229
  51.9 1.5 collective-permute-start.17
  57.2 11.6 %shard_map.61.rest_4_ = bf16[4,1024,128]{2,1,0:T(8,128)(2,1)} custom-call(s32[2,1024]{1,0:T(2,128)} %convert_multiply_fusion.1.pairs_ref, f32[4,128]{1,0:T(4,128)} %pad_maximum_fusion.4.scale_ref, s16[3,1500,128]{2,1,0:T(8,128)(2,1)} %copy-done.1, s16[3,1500,128]{2,1,0:T(8,128)(2,1)} %copy-done, s16[3,1500,128]{2,1,0:T(8,128)(2,1)} %copy-done.6, ...), custom_call_target="tpu_custom_call" | custom-call | flops 10000000 | bytes 36900 | tf_op jit(solution)/shard_map/pallas_call | solution.py:209
  70.1 5.6 %collective-permute-start.14 = (bf16[4,1024,128]{2,1,0:T(8,128)(2,1)}, bf16[4,1024,128]{2,1,0:T(8,128)(2,1)}, u32[]{:S(2)}, u32[]{:S(2)}) collective-permute-start(bf16[4,1024,128]{2,1,0:T(8,128)(2,1)} %shard_map.61.rest_4_), channel_id=1, source_target_pairs={{0,1},{1,2},{2,3},{4,5},{5,6},{6,7},{8,9},{9,10},{10,11},{12,13},{... | collective-permute-start | bytes 3145736 | tf_op jit(solution)/shard_map/ppermute | solution.py:351
  78.0 13.4 %shard_map.62 = bf16[2048,512]{1,0:T(8,128)(2,1)} custom-call(s32[2,2048]{1,0:T(2,128)} %get-tuple-element.132.pairs_ref, f32[4,128]{1,0:T(4,128)} %bitcast.26, s32[24000,128]{1,0:T(8,128)} %get-tuple-element.84.rest_0_, f32[1,2048]{1,0:T(1,128)} %get-tuple-element.130.rest_1_), custom_call_target="tpu_custom_call" | custom-call | flops 10000000 | bytes 36900 | tf_op jit(solution)/shard_map/pallas_call | solution.py:209
  92.6 2.6 %fusion.4 = (bf16[1024,512]{1,0:T(8,128)(2,1)S(1)}, bf16[1024,512]{1,0:T(8,128)(2,1)}) fusion(bf16[2048,512]{1,0:T(8,128)(2,1)} %shard_map.62), kind=kLoop, calls=%fused_computation.39 | loop fusion | bytes 4194304 | tf_op jit(solution)/shard_map/slice | solution.py:421
  95.3 4.6 %collective-permute-done.18.rest_15_ = bf16[512,2048]{1,0:T(8,128)(2,1)S(1)} collective-permute-done((bf16[512,2048]{1,0:T(8,128)(2,1)}, bf16[512,2048]{1,0:T(8,128)(2,1)S(1)}, u32[]{:S(2)}, u32[]{:S(2)}) %collective-permute-start.18) | collective-permute-done | bytes 2097184 | tf_op jit(solution)/shard_map/ppermute | solution.py:337
  102.9 13.3 %shard_map.63 = bf16[2048,512]{1,0:T(8,128)(2,1)} custom-call(s32[2,2048]{1,0:T(2,128)} %get-tuple-element.91.pairs_ref, f32[4,128]{1,0:T(4,128)} %bitcast.27, s32[24000,128]{1,0:T(8,128)} %get-tuple-element.84.rest_0_, f32[1,2048]{1,0:T(1,128)} %get-tuple-element.129.rest_1_), custom_call_target="tpu_custom_call" | custom-call | flops 10000000 | bytes 36900 | tf_op jit(solution)/shard_map/pallas_call | solution.py:209
  116.2 15.1 %collective-permute-done.23.rest_8_ = bf16[4,1024,128]{2,1,0:T(8,128)(2,1)S(1)} collective-permute-done((bf16[4,1024,128]{2,1,0:T(8,128)(2,1)}, bf16[4,1024,128]{2,1,0:T(8,128)(2,1)S(1)}, u32[]{:S(2)}, u32[]{:S(2)}) %collective-permute-start.23) | collective-permute-done | bytes 1048608 | tf_op jit(solution)/shard_map/ppermute | solution.py:352
  137.1 2.7 %constant_dynamic-slice_fusion = (bf16[1024,512]{1,0:T(8,128)(2,1)S(1)}, bf16[1024,512]{1,0:T(8,128)(2,1)}) fusion(bf16[2048,512]{1,0:T(8,128)(2,1)} %shard_map.63, s32[]{:T(128)S(6)} %select_n.89, s32[]{:T(128)S(6)} %select_n.81), kind=kLoop, calls=%fused_computation.28 | loop fusion | bytes 4194312 | tf_op jit(solution)/shard_map/dynamic_slice | solution.py:435
  140.5 18.4 %collective-permute-done.26.rest_2_ = bf16[1024,512]{1,0:T(8,128)(2,1)S(1)} collective-permute-done((bf16[1024,512]{1,0:T(8,128)(2,1)}, bf16[1024,512]{1,0:T(8,128)(2,1)S(1)}, u32[]{:S(2)}, u32[]{:S(2)}) %collective-permute-start.26) | collective-permute-done | bytes 1048608 | tf_op jit(solution)/shard_map/ppermute | solution.py:333
  159.5 3.4 %collective-permute-done.29.rest_10_ = bf16[4,1024,128]{2,1,0:T(8,128)(2,1)S(1)} collective-permute-done((bf16[4,1024,128]{2,1,0:T(8,128)(2,1)}, bf16[4,1024,128]{2,1,0:T(8,128)(2,1)S(1)}, u32[]{:S(2)}, u32[]{:S(2)}) %collective-permute-start.29) | collective-permute-done | bytes 1048608 | tf_op jit(solution)/shard_map/ppermute | solution.py:352
  164.2 45.9 %shard_map.64 = (f32[1024,2048]{1,0:T(8,128)}, f32[1024,2048]{1,0:T(8,128)}) custom-call(s32[2]{0:T(128)} %pad_add_fusion.place_ref, f32[8,4,1,128]{3,2,1,0:T(1,128)} %fusion.1.mask_ref, f32[2]{0:T(128)} %pad_maximum_fusion.5.factors_ref, bf16[1024,512]{1,0:T(8,128)(2,1)} %get-tuple-element.123.rest_0_, bf16[1024,512]{1,0:T(8,128)(2,1)} %copy-done.13, ...), custom_call_target="tpu_custom_call" | custom-call | flops 10000000 | bytes 36900 | tf_op jit(solution)/shard_map/pallas_call | solution.py:307
  (110 shorter events, 26.9 us)
Async XLA Ops:
  2.5 28.3 %collective-permute-start.11 = (s16[3,1500,128]{2,1,0:T(8,128)(2,1)S(1)}, s16[3,1500,128]{2,1,0:T(8,128)(2,1)S(1)}, u32[]{:S(2)}, u32[]{:S(2)}) collective-permute-start(s16[3,1500,128]{2,1,0:T(8,128)(2,1)S(1)} %fusion), channel_id=1, source_target_pairs={{0,20},{4,16},{8,28},{12,24},{16,4},{20,0},{24,12},{28,8},{1,21},{... | collective-permute-start | bytes 3456008 | tf_op jit(solution)/shard_map/ppermute | solution.py:333
  4.9 28.3 %collective-permute-start.10 = (s16[3,1500,128]{2,1,0:T(8,128)(2,1)S(1)}, s16[3,1500,128]{2,1,0:T(8,128)(2,1)S(1)}, u32[]{:S(2)}, u32[]{:S(2)}) collective-permute-start(s16[3,1500,128]{2,1,0:T(8,128)(2,1)S(1)} %fusion), channel_id=1, source_target_pairs={{0,12},{4,8},{8,4},{12,0},{16,28},{20,24},{24,20},{28,16},{1,13},{... | collective-permute-start | bytes 3456008 | tf_op jit(solution)/shard_map/ppermute | solution.py:333
  25.6 8.7 %collective-permute-start.6 = (f32[1,2560]{1,0:T(1,128)S(1)}, f32[1,2560]{1,0:T(1,128)S(1)}, u32[]{:S(2)}, u32[]{:S(2)}) collective-permute-start(f32[1,2560]{1,0:T(1,128)S(1)} %pad_maximum_fusion.3), channel_id=1, source_target_pairs={{0,28},{4,24},{8,20},{12,16},{16,12},{20,8},{24,4},{28,0},{1,29},{... | collective-permute-start | bytes 30728 | tf_op jit(solution)/shard_map/ppermute | solution.py:333
  25.7 9.1 %collective-permute-start.5 = (f32[1,2560]{1,0:T(1,128)S(1)}, f32[1,2560]{1,0:T(1,128)S(1)}, u32[]{:S(2)}, u32[]{:S(2)}) collective-permute-start(f32[1,2560]{1,0:T(1,128)S(1)} %pad_maximum_fusion.3), channel_id=1, source_target_pairs={{0,24},{4,28},{8,16},{12,20},{16,8},{20,12},{24,0},{28,4},{1,25},{... | collective-permute-start | bytes 30728 | tf_op jit(solution)/shard_map/ppermute | solution.py:333
  28.0 7.4 %collective-permute-start.4 = (f32[1,2560]{1,0:T(1,128)S(1)}, f32[1,2560]{1,0:T(1,128)}, u32[]{:S(2)}, u32[]{:S(2)}) collective-permute-start(f32[1,2560]{1,0:T(1,128)S(1)} %pad_maximum_fusion.3), channel_id=1, source_target_pairs={{0,20},{4,16},{8,28},{12,24},{16,4},{20,0},{24,12},{28,8},{1,21},{... | collective-permute-start | bytes 30728 | tf_op jit(solution)/shard_map/ppermute | solution.py:333
  35.5 16.0 %collective-permute-start.12 = (s16[3,1500,128]{2,1,0:T(8,128)(2,1)S(1)}, s16[3,1500,128]{2,1,0:T(8,128)(2,1)S(1)}, u32[]{:S(2)}, u32[]{:S(2)}) collective-permute-start(s16[3,1500,128]{2,1,0:T(8,128)(2,1)S(1)} %broadcast_select_fusion), channel_id=1, source_target_pairs={{0,16},{4,12},{8,24},{12,4},{16,0},{20,28},{24,8},{28,20},{1,17},{... | collective-permute-start | bytes 3456008 | tf_op jit(solution)/shard_map/ppermute | solution.py:337
  38.7 12.0 %collective-permute-start.8 = (f32[3,2048]{1,0:T(4,128)S(1)}, f32[3,2048]{1,0:T(4,128)S(1)}, u32[]{:S(2)}, u32[]{:S(2)}) collective-permute-start(f32[3,2048]{1,0:T(4,128)S(1)} %get-tuple-element.134), channel_id=1, source_target_pairs={{0,2},{1,3},{2,0},{3,1},{4,6},{5,7},{6,4},{7,5},{8,10},{9,11},{10,... | collective-permute-start | bytes 73736 | tf_op jit(solution)/shard_map/ppermute | solution.py:347
  41.4 9.3 %collective-permute-start.7 = (f32[3,2048]{1,0:T(4,128)S(1)}, f32[3,2048]{1,0:T(4,128)S(1)}, u32[]{:S(2)}, u32[]{:S(2)}) collective-permute-start(f32[3,2048]{1,0:T(4,128)S(1)} %get-tuple-element.134), channel_id=1, source_target_pairs={{0,1},{1,2},{2,3},{3,0},{4,5},{5,6},{6,7},{7,4},{8,9},{9,10},{10,1... | collective-permute-start | bytes 73736 | tf_op jit(solution)/shard_map/ppermute | solution.py:347
  43.0 7.7 %collective-permute-start.9 = (f32[3,2048]{1,0:T(4,128)S(1)}, f32[3,2048]{1,0:T(4,128)S(1)}, u32[]{:S(2)}, u32[]{:S(2)}) collective-permute-start(f32[3,2048]{1,0:T(4,128)S(1)} %get-tuple-element.134), channel_id=1, source_target_pairs={{0,3},{1,0},{2,1},{3,2},{4,7},{5,4},{6,5},{7,6},{8,11},{9,8},{10,9... | collective-permute-start | bytes 73736 | tf_op jit(solution)/shard_map/ppermute | solution.py:347
  51.5 48.3 %collective-permute-start.18 = (bf16[512,2048]{1,0:T(8,128)(2,1)}, bf16[512,2048]{1,0:T(8,128)(2,1)S(1)}, u32[]{:S(2)}, u32[]{:S(2)}) collective-permute-start(bf16[512,2048]{1,0:T(8,128)(2,1)} %shard_map.60.rest_11_), channel_id=1, source_target_pairs={{0,16},{4,12},{8,24},{12,4},{16,0},{20,28},{24,8},{28,20},{1,17},{... | collective-permute-start | bytes 6291464 | tf_op jit(solution)/shard_map/ppermute | solution.py:337
  51.9 47.9 %collective-permute-start.17 = (bf16[512,2048]{1,0:T(8,128)(2,1)}, bf16[512,2048]{1,0:T(8,128)(2,1)}, u32[]{:S(2)}, u32[]{:S(2)}) collective-permute-start(bf16[512,2048]{1,0:T(8,128)(2,1)} %shard_map.60.rest_11_), channel_id=1, source_target_pairs={{0,8},{4,20},{8,0},{12,28},{16,24},{20,4},{24,16},{28,12},{1,9},{5... | collective-permute-start | bytes 6291464 | tf_op jit(solution)/shard_map/ppermute | solution.py:337
  56.2 43.6 %collective-permute-start.16 = (bf16[512,2048]{1,0:T(8,128)(2,1)}, bf16[512,2048]{1,0:T(8,128)(2,1)}, u32[]{:S(2)}, u32[]{:S(2)}) collective-permute-start(bf16[512,2048]{1,0:T(8,128)(2,1)} %shard_map.60.rest_11_), channel_id=1, source_target_pairs={{0,4},{4,0},{8,12},{12,8},{16,20},{20,16},{24,28},{28,24},{1,5},{5... | collective-permute-start | bytes 6291464 | tf_op jit(solution)/shard_map/ppermute | solution.py:333
  68.8 31.0 %collective-permute-start.15 = (bf16[4,1024,128]{2,1,0:T(8,128)(2,1)}, bf16[4,1024,128]{2,1,0:T(8,128)(2,1)}, u32[]{:S(2)}, u32[]{:S(2)}) collective-permute-start(bf16[4,1024,128]{2,1,0:T(8,128)(2,1)} %shard_map.61.rest_4_), channel_id=1, source_target_pairs={{1,0},{2,1},{3,2},{5,4},{6,5},{7,6},{9,8},{10,9},{11,10},{13,12},{... | collective-permute-start | bytes 3145736 | tf_op jit(solution)/shard_map/ppermute | solution.py:352
  70.1 29.7 %collective-permute-start.14 = (bf16[4,1024,128]{2,1,0:T(8,128)(2,1)}, bf16[4,1024,128]{2,1,0:T(8,128)(2,1)}, u32[]{:S(2)}, u32[]{:S(2)}) collective-permute-start(bf16[4,1024,128]{2,1,0:T(8,128)(2,1)} %shard_map.61.rest_4_), channel_id=1, source_target_pairs={{0,1},{1,2},{2,3},{4,5},{5,6},{6,7},{8,9},{9,10},{10,11},{12,13},{... | collective-permute-start | bytes 3145736 | tf_op jit(solution)/shard_map/ppermute | solution.py:351
  99.8 31.5 %collective-permute-start.20 = (bf16[512,2048]{1,0:T(8,128)(2,1)S(1)}, bf16[512,2048]{1,0:T(8,128)(2,1)S(1)}, u32[]{:S(2)}, u32[]{:S(2)}) collective-permute-start(bf16[512,2048]{1,0:T(8,128)(2,1)S(1)} %collective-permute-done.18.rest_15_), channel_id=1, source_target_pairs={{0,4},{4,0},{8,12},{12,8},{16,20},{20,16},{24,28},{28,24},{1,5},{5... | collective-permute-start | bytes 6291464 | tf_op jit(solution)/shard_map/ppermute | solution.py:333
  99.9 32.8 %collective-permute-start.21 = (bf16[512,2048]{1,0:T(8,128)(2,1)}, bf16[512,2048]{1,0:T(8,128)(2,1)}, u32[]{:S(2)}, u32[]{:S(2)}) collective-permute-start(bf16[512,2048]{1,0:T(8,128)(2,1)} %collective-permute-done.17.rest_13_), channel_id=1, source_target_pairs={{0,16},{4,12},{8,24},{12,4},{16,0},{20,28},{24,8},{28,20},{1,17},{... | collective-permute-start | bytes 6291464 | tf_op jit(solution)/shard_map/ppermute | solution.py:337
  100.6 32.2 %collective-permute-start.19 = (bf16[512,2048]{1,0:T(8,128)(2,1)}, bf16[512,2048]{1,0:T(8,128)(2,1)}, u32[]{:S(2)}, u32[]{:S(2)}) collective-permute-start(bf16[512,2048]{1,0:T(8,128)(2,1)} %collective-permute-done.17.rest_13_), channel_id=1, source_target_pairs={{0,4},{4,0},{8,12},{12,8},{16,20},{20,16},{24,28},{28,24},{1,5},{5... | collective-permute-start | bytes 6291464 | tf_op jit(solution)/shard_map/ppermute | solution.py:333
  100.7 15.5 %collective-permute-start.22 = (bf16[4,1024,128]{2,1,0:T(8,128)(2,1)}, bf16[4,1024,128]{2,1,0:T(8,128)(2,1)S(1)}, u32[]{:S(2)}, u32[]{:S(2)}) collective-permute-start(bf16[4,1024,128]{2,1,0:T(8,128)(2,1)} %collective-permute-done.14.rest_5_), channel_id=1, source_target_pairs={{1,2},{2,3},{5,6},{6,7},{9,10},{10,11},{13,14},{14,15},{17,18},{18... | collective-permute-start | bytes 3145736 | tf_op jit(solution)/shard_map/ppermute | solution.py:351
  101.4 29.9 %collective-permute-start.23 = (bf16[4,1024,128]{2,1,0:T(8,128)(2,1)}, bf16[4,1024,128]{2,1,0:T(8,128)(2,1)S(1)}, u32[]{:S(2)}, u32[]{:S(2)}) collective-permute-start(bf16[4,1024,128]{2,1,0:T(8,128)(2,1)} %collective-permute-done.15.rest_6_), channel_id=1, source_target_pairs={{1,0},{2,1},{5,4},{6,5},{9,8},{10,9},{13,12},{14,13},{17,16},{18,1... | collective-permute-start | bytes 3145736 | tf_op jit(solution)/shard_map/ppermute | solution.py:352
  133.1 25.8 %collective-permute-start.26 = (bf16[1024,512]{1,0:T(8,128)(2,1)}, bf16[1024,512]{1,0:T(8,128)(2,1)S(1)}, u32[]{:S(2)}, u32[]{:S(2)}) collective-permute-start(bf16[1024,512]{1,0:T(8,128)(2,1)} %get-tuple-element.108), channel_id=1, source_target_pairs={{0,8},{4,12},{8,0},{12,4},{16,24},{20,28},{24,16},{28,20},{1,9},{5... | collective-permute-start | bytes 3145736 | tf_op jit(solution)/shard_map/ppermute | solution.py:333
  134.2 25.3 %collective-permute-start.27 = (bf16[1024,512]{1,0:T(8,128)(2,1)S(1)}, bf16[1024,512]{1,0:T(8,128)(2,1)S(1)}, u32[]{:S(2)}, u32[]{:S(2)}) collective-permute-start(bf16[1024,512]{1,0:T(8,128)(2,1)S(1)} %get-tuple-element.109), channel_id=1, source_target_pairs={{0,16},{4,20},{8,24},{12,28},{16,0},{20,4},{24,8},{28,12},{1,17},{... | collective-permute-start | bytes 3145736 | tf_op jit(solution)/shard_map/ppermute | solution.py:333
  135.1 24.4 %collective-permute-start.28 = (bf16[4,1024,128]{2,1,0:T(8,128)(2,1)}, bf16[4,1024,128]{2,1,0:T(8,128)(2,1)S(1)}, u32[]{:S(2)}, u32[]{:S(2)}) collective-permute-start(bf16[4,1024,128]{2,1,0:T(8,128)(2,1)} %copy-done.7), channel_id=1, source_target_pairs={{2,3},{6,7},{10,11},{14,15},{18,19},{22,23},{26,27},{30,31}} | collective-permute-start | bytes 3145736 | tf_op jit(solution)/shard_map/ppermute | solution.py:351
  135.8 27.1 %collective-permute-start.29 = (bf16[4,1024,128]{2,1,0:T(8,128)(2,1)}, bf16[4,1024,128]{2,1,0:T(8,128)(2,1)S(1)}, u32[]{:S(2)}, u32[]{:S(2)}) collective-permute-start(bf16[4,1024,128]{2,1,0:T(8,128)(2,1)} %copy-done.8), channel_id=1, source_target_pairs={{1,0},{5,4},{9,8},{13,12},{17,16},{21,20},{25,24},{29,28}} | collective-permute-start | bytes 3145736 | tf_op jit(solution)/shard_map/ppermute | solution.py:352
  139.8 23.1 %collective-permute-start.25 = (bf16[1024,512]{1,0:T(8,128)(2,1)S(1)}, bf16[1024,512]{1,0:T(8,128)(2,1)S(1)}, u32[]{:S(2)}, u32[]{:S(2)}) collective-permute-start(bf16[1024,512]{1,0:T(8,128)(2,1)S(1)} %get-tuple-element.107), channel_id=1, source_target_pairs={{0,4},{4,0},{8,12},{12,8},{16,20},{20,16},{24,28},{28,24},{1,5},{5... | collective-permute-start | bytes 3145736 | tf_op jit(solution)/shard_map/ppermute | solution.py:333
  (25 other events, 207.1 us)

commit v14 on v13

--- a/solution.py
+++ b/solution.py
@@ -9,7 +9,7 @@
 
 LAG = 384
 CHUNK = 128
-VMEM_LIMIT = 56 * 1024 * 1024
+VMEM_LIMIT = 63 * 1024 * 1024
 NEAR = (0, 1, 2, 4)
 FAR = (3, 5, 6, 7)
 TABLE_ROWS = 16

time: 211 us -> 215 us (1.019)
  waiting for transfers between devices: 47.4 us -> 49.9 us
  other arithmetic: 8.47 us -> 10.9 us
    ppermute x4, waiting for transfers between devices: 5.26 us -> 9.01 us  [swap_by_parity(): lax.ppermute(x, 'tm', [(i, i ^ (odd if i % 2 else even)) for i in range(8)])]
    select_n x1, other arithmetic: 0.35 us -> 2.57 us  [corner(): return swap_by_parity(jnp.where(even, along_x, along_y), 4, 2)]
  transfers between devices with their start and end apart: 30 -> 30, of which waited for: 10 -> 8; matrix products, arithmetic and copies ran while one was open for 7% -> 7% of each run, Pallas kernels for 29% -> 28%
where the time goes in v14:
time: 215 us; the launch traced here: 214 us
  Pallas kernels  106 us (49%)
  waiting for transfers between devices  49.9 us (23%)
  starting transfers between devices  35.5 us (17%)
  other arithmetic  10.9 us (5%)
  local copies, waits for them, and re-layouts  9.63 us (4%)
    pallas_call x4, Pallas kernels, contacts(): pl.pallas_call(functools.partial(gather_kernel, form, chunks, len(sources...  55.7 us
    pallas_call x1, Pallas kernels, products(): pl.pallas_call(product_kernel, out_shape=[out, out], grid_spec=pltpu.Pref...  46 us
    ppermute x17, waiting for transfers between devices, swap(): return lax.ppermute(x, 'tm', [(i, i ^ bits) for i in range(8)])  22.4 us
    ppermute x3, waiting for transfers between devices, line_hop(): down = lax.ppermute(down, 'feat', [(i + 1, i) for i in range(count - hop)])  18.5 us
    ppermute x17, starting transfers between devices, swap(): return lax.ppermute(x, 'tm', [(i, i ^ bits) for i in range(8)])  14.1 us
    ppermute x4, waiting for transfers between devices, swap_by_parity(): lax.ppermute(x, 'tm', [(i, i ^ (odd if i % 2 else even)) for i in range(8)])  9.01 us
    ppermute x3, starting transfers between devices, line_hop(): lax.ppermute(up, 'feat', [(i, i + 1) for i in range(hop - 1, count - 1)])  7.92 us
    ppermute x3, starting transfers between devices, line_gather(): lax.ppermute(x, 'feat', shift(s))  6.61 us
  transfers between devices with their start and end apart: 30, of which 8 were waited for; matrix products, arithmetic and copies ran while one was open for 7% of the time, Pallas kernels for 28%

profile of v14, /device:TPU:0, one launch (start us, length us, event | category | flops | bytes accessed | tf_op | source)
XLA Modules:
  0.0 214.3 jit_solution(1874543606327274752)
XLA Ops:
  0.6 2.8 %fusion = s16[3,1500,128]{2,1,0:T(8,128)(2,1)} fusion(s32[512,3,1500]{0,2,1:T(8,128)} %param.4, s32[]{:T(128)S(6)} %select_n.74), kind=kLoop, calls=%fused_computation.1 | loop fusion | flops 576000 | bytes 3456004 | tf_op jit(solution)/shard_map/convert_element_type | solution.py:375
  3.5 2.4 %collective-permute-start.11 = (s16[3,1500,128]{2,1,0:T(8,128)(2,1)}, s16[3,1500,128]{2,1,0:T(8,128)(2,1)}, u32[]{:S(2)}, u32[]{:S(2)}) collective-permute-start(s16[3,1500,128]{2,1,0:T(8,128)(2,1)} %fusion), channel_id=1, source_target_pairs={{0,20},{4,16},{8,28},{12,24},{16,4},{20,0},{24,12},{28,8},{1,21},{... | collective-permute-start | bytes 3456008 | tf_op jit(solution)/shard_map/ppermute | solution.py:333
  5.9 1.8 collective-permute-start.10
  8.2 17.5 %shard_map.59 = (f32[2048,512]{1,0:T(8,128)}, f32[1,2048]{1,0:T(1,128)}, s32[24000,128]{1,0:T(8,128)}) custom-call(s32[2,2048]{1,0:T(2,128)} %get-tuple-element.136.pairs_ref, f32[4,128]{1,0:T(4,128)} %bitcast.25, s32[3,1500,512]{2,1,0:T(8,128)} %bitcast.24), custom_call_target="tpu_custom_call" | custom-call | flops 10000000 | bytes 36900 | tf_op jit(solution)/shard_map/pallas_call | solution.py:209
  26.6 2.4 %collective-permute-start.5 = (f32[1,2560]{1,0:T(1,128)S(1)}, f32[1,2560]{1,0:T(1,128)S(1)}, u32[]{:S(2)}, u32[]{:S(2)}) collective-permute-start(f32[1,2560]{1,0:T(1,128)S(1)} %pad_maximum_fusion.3), channel_id=1, source_target_pairs={{0,24},{4,28},{8,16},{12,20},{16,8},{20,12},{24,0},{28,4},{1,25},{... | collective-permute-start | bytes 30728 | tf_op jit(solution)/shard_map/ppermute | solution.py:333
  29.5 2.5 %collective-permute-done.11.rest_1_ = s16[3,1500,128]{2,1,0:T(8,128)(2,1)} collective-permute-done((s16[3,1500,128]{2,1,0:T(8,128)(2,1)}, s16[3,1500,128]{2,1,0:T(8,128)(2,1)}, u32[]{:S(2)}, u32[]{:S(2)}) %collective-permute-start.11) | collective-permute-done | bytes 1152032 | tf_op jit(solution)/shard_map/ppermute | solution.py:333
  32.0 2.5 %collective-permute-start.3 = (f32[1,2560]{1,0:T(1,128)S(1)}, f32[1,2560]{1,0:T(1,128)S(1)}, u32[]{:S(2)}, u32[]{:S(2)}) collective-permute-start(f32[1,2560]{1,0:T(1,128)S(1)} %pad_maximum_fusion.3), channel_id=1, source_target_pairs={{0,16},{4,20},{8,24},{12,28},{16,0},{20,4},{24,8},{28,12},{1,17},{... | collective-permute-start | bytes 30728 | tf_op jit(solution)/shard_map/ppermute | solution.py:333
  36.3 2.6 %broadcast_select_fusion = s16[3,1500,128]{2,1,0:T(8,128)(2,1)} fusion(s16[3,1500,128]{2,1,0:T(8,128)(2,1)} %collective-permute-done.10.rest_0_, s16[3,1500,128]{2,1,0:T(8,128)(2,1)} %collective-permute-done.11.rest_1_, pred[]{:T(512)S(6)} %eq.23), kind=kLoop, calls=%fused_computation.2 | loop fusion | flops 576000 | bytes 3456001 | tf_op jit(solution)/shard_map/jit(_where)/select_n | solution.py:342
  39.3 2.8 %collective-permute-start.8 = (f32[3,2048]{1,0:T(4,128)S(1)}, f32[3,2048]{1,0:T(4,128)S(1)}, u32[]{:S(2)}, u32[]{:S(2)}) collective-permute-start(f32[3,2048]{1,0:T(4,128)S(1)} %get-tuple-element.134), channel_id=1, source_target_pairs={{0,2},{1,3},{2,0},{3,1},{4,6},{5,7},{6,4},{7,5},{8,10},{9,11},{10,... | collective-permute-start | bytes 73736 | tf_op jit(solution)/shard_map/ppermute | solution.py:347
  43.7 2.2 %collective-permute-start.9 = (f32[3,2048]{1,0:T(4,128)S(1)}, f32[3,2048]{1,0:T(4,128)S(1)}, u32[]{:S(2)}, u32[]{:S(2)}) collective-permute-start(f32[3,2048]{1,0:T(4,128)S(1)} %get-tuple-element.134), channel_id=1, source_target_pairs={{0,3},{1,0},{2,1},{3,2},{4,7},{5,4},{6,5},{7,6},{8,11},{9,8},{10,9... | collective-permute-start | bytes 73736 | tf_op jit(solution)/shard_map/ppermute | solution.py:347
  46.0 4.9 %shard_map.60.rest_11_ = bf16[512,2048]{1,0:T(8,128)(2,1)} custom-call(f32[2048,512]{1,0:T(8,128)} %get-tuple-element.61.raw_ref, f32[1,2048]{1,0:T(1,128)} %copy-done.5), custom_call_target="tpu_custom_call" | custom-call | flops 10000000 | bytes 36900 | tf_op jit(solution)/shard_map/pallas_call | solution.py:229
  50.9 4.3 %collective-permute-done.12.rest_3_ = s16[3,1500,128]{2,1,0:T(8,128)(2,1)} collective-permute-done((s16[3,1500,128]{2,1,0:T(8,128)(2,1)}, s16[3,1500,128]{2,1,0:T(8,128)(2,1)}, u32[]{:S(2)}, u32[]{:S(2)}) %collective-permute-start.12) | collective-permute-done | bytes 1152032 | tf_op jit(solution)/shard_map/ppermute | solution.py:337
  55.5 1.6 collective-permute-start.17
  60.4 11.5 %shard_map.61.rest_4_ = bf16[4,1024,128]{2,1,0:T(8,128)(2,1)} custom-call(s32[2,1024]{1,0:T(2,128)} %convert_multiply_fusion.1.pairs_ref, f32[4,128]{1,0:T(4,128)} %pad_maximum_fusion.4.scale_ref, s16[3,1500,128]{2,1,0:T(8,128)(2,1)} %collective-permute-done.10.rest_0_, s16[3,1500,128]{2,1,0:T(8,128)(2,1)} %collective-permute-done.11.rest_1_, ...), custom_call_target="tpu_custom_call" | custom-call | flops 10000000 | bytes 36900 | tf_op jit(solution)/shard_map/pallas_call | solution.py:209
  73.2 5.6 %collective-permute-start.14 = (bf16[4,1024,128]{2,1,0:T(8,128)(2,1)}, bf16[4,1024,128]{2,1,0:T(8,128)(2,1)}, u32[]{:S(2)}, u32[]{:S(2)}) collective-permute-start(bf16[4,1024,128]{2,1,0:T(8,128)(2,1)} %shard_map.61.rest_4_), channel_id=1, source_target_pairs={{0,1},{1,2},{2,3},{4,5},{5,6},{6,7},{8,9},{9,10},{10,11},{12,13},{... | collective-permute-start | bytes 3145736 | tf_op jit(solution)/shard_map/ppermute | solution.py:351
  81.0 13.4 %shard_map.62 = bf16[2048,512]{1,0:T(8,128)(2,1)} custom-call(s32[2,2048]{1,0:T(2,128)} %get-tuple-element.132.pairs_ref, f32[4,128]{1,0:T(4,128)} %bitcast.26, s32[24000,128]{1,0:T(8,128)} %get-tuple-element.84.rest_0_, f32[1,2048]{1,0:T(1,128)} %get-tuple-element.130.rest_1_), custom_call_target="tpu_custom_call" | custom-call | flops 10000000 | bytes 36900 | tf_op jit(solution)/shard_map/pallas_call | solution.py:209
  95.7 3.0 %fusion.4 = (bf16[1024,512]{1,0:T(8,128)(2,1)}, bf16[1024,512]{1,0:T(8,128)(2,1)}) fusion(bf16[2048,512]{1,0:T(8,128)(2,1)} %shard_map.62), kind=kLoop, calls=%fused_computation.39 | loop fusion | bytes 4194304 | tf_op jit(solution)/shard_map/slice | solution.py:421
  98.7 4.7 %collective-permute-done.18.rest_15_ = bf16[512,2048]{1,0:T(8,128)(2,1)} collective-permute-done((bf16[512,2048]{1,0:T(8,128)(2,1)}, bf16[512,2048]{1,0:T(8,128)(2,1)}, u32[]{:S(2)}, u32[]{:S(2)}) %collective-permute-start.18) | collective-permute-done | bytes 2097184 | tf_op jit(solution)/shard_map/ppermute | solution.py:337
  107.5 13.3 %shard_map.63 = bf16[2048,512]{1,0:T(8,128)(2,1)} custom-call(s32[2,2048]{1,0:T(2,128)} %get-tuple-element.91.pairs_ref, f32[4,128]{1,0:T(4,128)} %bitcast.27, s32[24000,128]{1,0:T(8,128)} %get-tuple-element.84.rest_0_, f32[1,2048]{1,0:T(1,128)} %get-tuple-element.129.rest_1_), custom_call_target="tpu_custom_call" | custom-call | flops 10000000 | bytes 36900 | tf_op jit(solution)/shard_map/pallas_call | solution.py:209
  120.8 15.2 %collective-permute-done.23.rest_8_ = bf16[4,1024,128]{2,1,0:T(8,128)(2,1)} collective-permute-done((bf16[4,1024,128]{2,1,0:T(8,128)(2,1)}, bf16[4,1024,128]{2,1,0:T(8,128)(2,1)}, u32[]{:S(2)}, u32[]{:S(2)}) %collective-permute-start.23) | collective-permute-done | bytes 1048608 | tf_op jit(solution)/shard_map/ppermute | solution.py:352
  140.3 2.7 %constant_dynamic-slice_fusion = (bf16[1024,512]{1,0:T(8,128)(2,1)S(1)}, bf16[1024,512]{1,0:T(8,128)(2,1)}) fusion(bf16[2048,512]{1,0:T(8,128)(2,1)} %shard_map.63, s32[]{:T(128)S(6)} %select_n.89, s32[]{:T(128)S(6)} %select_n.81), kind=kLoop, calls=%fused_computation.28 | loop fusion | bytes 4194312 | tf_op jit(solution)/shard_map/dynamic_slice | solution.py:435
  143.6 18.3 %collective-permute-done.26.rest_2_ = bf16[1024,512]{1,0:T(8,128)(2,1)S(1)} collective-permute-done((bf16[1024,512]{1,0:T(8,128)(2,1)}, bf16[1024,512]{1,0:T(8,128)(2,1)S(1)}, u32[]{:S(2)}, u32[]{:S(2)}) %collective-permute-start.26) | collective-permute-done | bytes 1048608 | tf_op jit(solution)/shard_map/ppermute | solution.py:333
  162.7 3.3 %collective-permute-done.29.rest_10_ = bf16[4,1024,128]{2,1,0:T(8,128)(2,1)S(1)} collective-permute-done((bf16[4,1024,128]{2,1,0:T(8,128)(2,1)}, bf16[4,1024,128]{2,1,0:T(8,128)(2,1)S(1)}, u32[]{:S(2)}, u32[]{:S(2)}) %collective-permute-start.29) | collective-permute-done | bytes 1048608 | tf_op jit(solution)/shard_map/ppermute | solution.py:352
  168.1 46.0 %shard_map.64 = (f32[1024,2048]{1,0:T(8,128)}, f32[1024,2048]{1,0:T(8,128)}) custom-call(s32[2]{0:T(128)} %pad_add_fusion.place_ref, f32[8,4,1,128]{3,2,1,0:T(1,128)} %fusion.1.mask_ref, f32[2]{0:T(128)} %pad_maximum_fusion.5.factors_ref, bf16[1024,512]{1,0:T(8,128)(2,1)} %get-tuple-element.123.rest_0_, bf16[1024,512]{1,0:T(8,128)(2,1)} %copy-done.4, ...), custom_call_target="tpu_custom_call" | custom-call | flops 10000000 | bytes 36900 | tf_op jit(solution)/shard_map/pallas_call | solution.py:307
  (92 shorter events, 25.3 us)
Async XLA Ops:
  3.5 28.6 %collective-permute-start.11 = (s16[3,1500,128]{2,1,0:T(8,128)(2,1)}, s16[3,1500,128]{2,1,0:T(8,128)(2,1)}, u32[]{:S(2)}, u32[]{:S(2)}) collective-permute-start(s16[3,1500,128]{2,1,0:T(8,128)(2,1)} %fusion), channel_id=1, source_target_pairs={{0,20},{4,16},{8,28},{12,24},{16,4},{20,0},{24,12},{28,8},{1,21},{... | collective-permute-start | bytes 3456008 | tf_op jit(solution)/shard_map/ppermute | solution.py:333
  5.9 28.6 %collective-permute-start.10 = (s16[3,1500,128]{2,1,0:T(8,128)(2,1)}, s16[3,1500,128]{2,1,0:T(8,128)(2,1)}, u32[]{:S(2)}, u32[]{:S(2)}) collective-permute-start(s16[3,1500,128]{2,1,0:T(8,128)(2,1)} %fusion), channel_id=1, source_target_pairs={{0,12},{4,8},{8,4},{12,0},{16,28},{20,24},{24,20},{28,16},{1,13},{... | collective-permute-start | bytes 3456008 | tf_op jit(solution)/shard_map/ppermute | solution.py:333
  26.5 8.9 %collective-permute-start.6 = (f32[1,2560]{1,0:T(1,128)S(1)}, f32[1,2560]{1,0:T(1,128)S(1)}, u32[]{:S(2)}, u32[]{:S(2)}) collective-permute-start(f32[1,2560]{1,0:T(1,128)S(1)} %pad_maximum_fusion.3), channel_id=1, source_target_pairs={{0,28},{4,24},{8,20},{12,16},{16,12},{20,8},{24,4},{28,0},{1,29},{... | collective-permute-start | bytes 30728 | tf_op jit(solution)/shard_map/ppermute | solution.py:333
  26.6 9.4 %collective-permute-start.5 = (f32[1,2560]{1,0:T(1,128)S(1)}, f32[1,2560]{1,0:T(1,128)S(1)}, u32[]{:S(2)}, u32[]{:S(2)}) collective-permute-start(f32[1,2560]{1,0:T(1,128)S(1)} %pad_maximum_fusion.3), channel_id=1, source_target_pairs={{0,24},{4,28},{8,16},{12,20},{16,8},{20,12},{24,0},{28,4},{1,25},{... | collective-permute-start | bytes 30728 | tf_op jit(solution)/shard_map/ppermute | solution.py:333
  29.0 9.9 %collective-permute-start.4 = (f32[1,2560]{1,0:T(1,128)S(1)}, f32[1,2560]{1,0:T(1,128)S(1)}, u32[]{:S(2)}, u32[]{:S(2)}) collective-permute-start(f32[1,2560]{1,0:T(1,128)S(1)} %pad_maximum_fusion.3), channel_id=1, source_target_pairs={{0,20},{4,16},{8,28},{12,24},{16,4},{20,0},{24,12},{28,8},{1,21},{... | collective-permute-start | bytes 30728 | tf_op jit(solution)/shard_map/ppermute | solution.py:333
  32.0 7.2 %collective-permute-start.3 = (f32[1,2560]{1,0:T(1,128)S(1)}, f32[1,2560]{1,0:T(1,128)S(1)}, u32[]{:S(2)}, u32[]{:S(2)}) collective-permute-start(f32[1,2560]{1,0:T(1,128)S(1)} %pad_maximum_fusion.3), channel_id=1, source_target_pairs={{0,16},{4,20},{8,24},{12,28},{16,0},{20,4},{24,8},{28,12},{1,17},{... | collective-permute-start | bytes 30728 | tf_op jit(solution)/shard_map/ppermute | solution.py:333
  38.9 16.3 %collective-permute-start.12 = (s16[3,1500,128]{2,1,0:T(8,128)(2,1)}, s16[3,1500,128]{2,1,0:T(8,128)(2,1)}, u32[]{:S(2)}, u32[]{:S(2)}) collective-permute-start(s16[3,1500,128]{2,1,0:T(8,128)(2,1)} %broadcast_select_fusion), channel_id=1, source_target_pairs={{0,16},{4,12},{8,24},{12,4},{16,0},{20,28},{24,8},{28,20},{1,17},{... | collective-permute-start | bytes 3456008 | tf_op jit(solution)/shard_map/ppermute | solution.py:337
  39.3 11.5 %collective-permute-start.8 = (f32[3,2048]{1,0:T(4,128)S(1)}, f32[3,2048]{1,0:T(4,128)S(1)}, u32[]{:S(2)}, u32[]{:S(2)}) collective-permute-start(f32[3,2048]{1,0:T(4,128)S(1)} %get-tuple-element.134), channel_id=1, source_target_pairs={{0,2},{1,3},{2,0},{3,1},{4,6},{5,7},{6,4},{7,5},{8,10},{9,11},{10,... | collective-permute-start | bytes 73736 | tf_op jit(solution)/shard_map/ppermute | solution.py:347
  42.1 8.7 %collective-permute-start.7 = (f32[3,2048]{1,0:T(4,128)S(1)}, f32[3,2048]{1,0:T(4,128)S(1)}, u32[]{:S(2)}, u32[]{:S(2)}) collective-permute-start(f32[3,2048]{1,0:T(4,128)S(1)} %get-tuple-element.134), channel_id=1, source_target_pairs={{0,1},{1,2},{2,3},{3,0},{4,5},{5,6},{6,7},{7,4},{8,9},{9,10},{10,1... | collective-permute-start | bytes 73736 | tf_op jit(solution)/shard_map/ppermute | solution.py:347
  55.2 48.3 %collective-permute-start.18 = (bf16[512,2048]{1,0:T(8,128)(2,1)}, bf16[512,2048]{1,0:T(8,128)(2,1)}, u32[]{:S(2)}, u32[]{:S(2)}) collective-permute-start(bf16[512,2048]{1,0:T(8,128)(2,1)} %shard_map.60.rest_11_), channel_id=1, source_target_pairs={{0,16},{4,12},{8,24},{12,4},{16,0},{20,28},{24,8},{28,20},{1,17},{... | collective-permute-start | bytes 6291464 | tf_op jit(solution)/shard_map/ppermute | solution.py:337
  55.5 48.0 %collective-permute-start.17 = (bf16[512,2048]{1,0:T(8,128)(2,1)}, bf16[512,2048]{1,0:T(8,128)(2,1)}, u32[]{:S(2)}, u32[]{:S(2)}) collective-permute-start(bf16[512,2048]{1,0:T(8,128)(2,1)} %shard_map.60.rest_11_), channel_id=1, source_target_pairs={{0,8},{4,20},{8,0},{12,28},{16,24},{20,4},{24,16},{28,12},{1,9},{5... | collective-permute-start | bytes 6291464 | tf_op jit(solution)/shard_map/ppermute | solution.py:337
  60.3 43.2 %collective-permute-start.16 = (bf16[512,2048]{1,0:T(8,128)(2,1)}, bf16[512,2048]{1,0:T(8,128)(2,1)}, u32[]{:S(2)}, u32[]{:S(2)}) collective-permute-start(bf16[512,2048]{1,0:T(8,128)(2,1)} %shard_map.60.rest_11_), channel_id=1, source_target_pairs={{0,4},{4,0},{8,12},{12,8},{16,20},{20,16},{24,28},{28,24},{1,5},{5... | collective-permute-start | bytes 6291464 | tf_op jit(solution)/shard_map/ppermute | solution.py:333
  71.9 31.6 %collective-permute-start.15 = (bf16[4,1024,128]{2,1,0:T(8,128)(2,1)}, bf16[4,1024,128]{2,1,0:T(8,128)(2,1)}, u32[]{:S(2)}, u32[]{:S(2)}) collective-permute-start(bf16[4,1024,128]{2,1,0:T(8,128)(2,1)} %shard_map.61.rest_4_), channel_id=1, source_target_pairs={{1,0},{2,1},{3,2},{5,4},{6,5},{7,6},{9,8},{10,9},{11,10},{13,12},{... | collective-permute-start | bytes 3145736 | tf_op jit(solution)/shard_map/ppermute | solution.py:352
  73.2 30.3 %collective-permute-start.14 = (bf16[4,1024,128]{2,1,0:T(8,128)(2,1)}, bf16[4,1024,128]{2,1,0:T(8,128)(2,1)}, u32[]{:S(2)}, u32[]{:S(2)}) collective-permute-start(bf16[4,1024,128]{2,1,0:T(8,128)(2,1)} %shard_map.61.rest_4_), channel_id=1, source_target_pairs={{0,1},{1,2},{2,3},{4,5},{5,6},{6,7},{8,9},{9,10},{10,11},{12,13},{... | collective-permute-start | bytes 3145736 | tf_op jit(solution)/shard_map/ppermute | solution.py:351
  103.5 32.5 %collective-permute-start.20 = (bf16[512,2048]{1,0:T(8,128)(2,1)}, bf16[512,2048]{1,0:T(8,128)(2,1)}, u32[]{:S(2)}, u32[]{:S(2)}) collective-permute-start(bf16[512,2048]{1,0:T(8,128)(2,1)} %collective-permute-done.18.rest_15_), channel_id=1, source_target_pairs={{0,4},{4,0},{8,12},{12,8},{16,20},{20,16},{24,28},{28,24},{1,5},{5... | collective-permute-start | bytes 6291464 | tf_op jit(solution)/shard_map/ppermute | solution.py:333
  103.6 32.4 %collective-permute-start.21 = (bf16[512,2048]{1,0:T(8,128)(2,1)}, bf16[512,2048]{1,0:T(8,128)(2,1)}, u32[]{:S(2)}, u32[]{:S(2)}) collective-permute-start(bf16[512,2048]{1,0:T(8,128)(2,1)} %collective-permute-done.17.rest_13_), channel_id=1, source_target_pairs={{0,16},{4,12},{8,24},{12,4},{16,0},{20,28},{24,8},{28,20},{1,17},{... | collective-permute-start | bytes 6291464 | tf_op jit(solution)/shard_map/ppermute | solution.py:337
  104.2 31.8 %collective-permute-start.19 = (bf16[512,2048]{1,0:T(8,128)(2,1)}, bf16[512,2048]{1,0:T(8,128)(2,1)}, u32[]{:S(2)}, u32[]{:S(2)}) collective-permute-start(bf16[512,2048]{1,0:T(8,128)(2,1)} %collective-permute-done.17.rest_13_), channel_id=1, source_target_pairs={{0,4},{4,0},{8,12},{12,8},{16,20},{20,16},{24,28},{28,24},{1,5},{5... | collective-permute-start | bytes 6291464 | tf_op jit(solution)/shard_map/ppermute | solution.py:333
  104.4 16.4 %collective-permute-start.22 = (bf16[4,1024,128]{2,1,0:T(8,128)(2,1)}, bf16[4,1024,128]{2,1,0:T(8,128)(2,1)}, u32[]{:S(2)}, u32[]{:S(2)}) collective-permute-start(bf16[4,1024,128]{2,1,0:T(8,128)(2,1)} %collective-permute-done.14.rest_5_), channel_id=1, source_target_pairs={{1,2},{2,3},{5,6},{6,7},{9,10},{10,11},{13,14},{14,15},{17,18},{18... | collective-permute-start | bytes 3145736 | tf_op jit(solution)/shard_map/ppermute | solution.py:351
  106.1 30.0 %collective-permute-start.23 = (bf16[4,1024,128]{2,1,0:T(8,128)(2,1)}, bf16[4,1024,128]{2,1,0:T(8,128)(2,1)}, u32[]{:S(2)}, u32[]{:S(2)}) collective-permute-start(bf16[4,1024,128]{2,1,0:T(8,128)(2,1)} %collective-permute-done.15.rest_6_), channel_id=1, source_target_pairs={{1,0},{2,1},{5,4},{6,5},{9,8},{10,9},{13,12},{14,13},{17,16},{18,1... | collective-permute-start | bytes 3145736 | tf_op jit(solution)/shard_map/ppermute | solution.py:352
  136.1 25.8 %collective-permute-start.26 = (bf16[1024,512]{1,0:T(8,128)(2,1)}, bf16[1024,512]{1,0:T(8,128)(2,1)S(1)}, u32[]{:S(2)}, u32[]{:S(2)}) collective-permute-start(bf16[1024,512]{1,0:T(8,128)(2,1)} %get-tuple-element.108), channel_id=1, source_target_pairs={{0,8},{4,12},{8,0},{12,4},{16,24},{20,28},{24,16},{28,20},{1,9},{5... | collective-permute-start | bytes 3145736 | tf_op jit(solution)/shard_map/ppermute | solution.py:333
  137.3 25.4 %collective-permute-start.27 = (bf16[1024,512]{1,0:T(8,128)(2,1)}, bf16[1024,512]{1,0:T(8,128)(2,1)S(1)}, u32[]{:S(2)}, u32[]{:S(2)}) collective-permute-start(bf16[1024,512]{1,0:T(8,128)(2,1)} %get-tuple-element.109), channel_id=1, source_target_pairs={{0,16},{4,20},{8,24},{12,28},{16,0},{20,4},{24,8},{28,12},{1,17},{... | collective-permute-start | bytes 3145736 | tf_op jit(solution)/shard_map/ppermute | solution.py:333
  138.3 24.4 %collective-permute-start.28 = (bf16[4,1024,128]{2,1,0:T(8,128)(2,1)}, bf16[4,1024,128]{2,1,0:T(8,128)(2,1)S(1)}, u32[]{:S(2)}, u32[]{:S(2)}) collective-permute-start(bf16[4,1024,128]{2,1,0:T(8,128)(2,1)} %collective-permute-done.22.rest_7_), channel_id=1, source_target_pairs={{2,3},{6,7},{10,11},{14,15},{18,19},{22,23},{26,27},{30,31}} | collective-permute-start | bytes 3145736 | tf_op jit(solution)/shard_map/ppermute | solution.py:351
  139.0 27.0 %collective-permute-start.29 = (bf16[4,1024,128]{2,1,0:T(8,128)(2,1)}, bf16[4,1024,128]{2,1,0:T(8,128)(2,1)S(1)}, u32[]{:S(2)}, u32[]{:S(2)}) collective-permute-start(bf16[4,1024,128]{2,1,0:T(8,128)(2,1)} %collective-permute-done.23.rest_8_), channel_id=1, source_target_pairs={{1,0},{5,4},{9,8},{13,12},{17,16},{21,20},{25,24},{29,28}} | collective-permute-start | bytes 3145736 | tf_op jit(solution)/shard_map/ppermute | solution.py:352
  143.0 23.1 %collective-permute-start.25 = (bf16[1024,512]{1,0:T(8,128)(2,1)S(1)}, bf16[1024,512]{1,0:T(8,128)(2,1)S(1)}, u32[]{:S(2)}, u32[]{:S(2)}) collective-permute-start(bf16[1024,512]{1,0:T(8,128)(2,1)S(1)} %get-tuple-element.107), channel_id=1, source_target_pairs={{0,4},{4,0},{8,12},{12,8},{16,20},{20,16},{24,28},{28,24},{1,5},{5... | collective-permute-start | bytes 3145736 | tf_op jit(solution)/shard_map/ppermute | solution.py:333
  (16 other events, 105.1 us)

commit v15 on v14

--- a/solution.py
+++ b/solution.py
@@ -9,7 +9,7 @@
 
 LAG = 384
 CHUNK = 128
-VMEM_LIMIT = 63 * 1024 * 1024
+VMEM_LIMIT = 48 * 1024 * 1024
 NEAR = (0, 1, 2, 4)
 FAR = (3, 5, 6, 7)
 TABLE_ROWS = 16

time: 215 us -> 209 us (0.972)
  waiting for transfers between devices: 49.9 us -> 62.5 us
  other arithmetic: 10.9 us -> 4.44 us
  Pallas kernels: 106 us -> 100 us
  local copies, waits for them, and re-layouts: 9.63 us -> 4.31 us
    ppermute x17, waiting for transfers between devices: 22.4 us -> 31 us  [swap(): return lax.ppermute(x, 'tm', [(i, i ^ bits) for i in range(8)])]
    pallas_call x4, Pallas kernels: 55.7 us -> 52 us  [contacts(): pl.pallas_call(functools.partial(gather_kernel, form, chunks, len(sources...]
    ppermute x4, waiting for transfers between devices: 9.01 us -> 11.7 us  [swap_by_parity(): lax.ppermute(x, 'tm', [(i, i ^ (odd if i % 2 else even)) for i in range(8)])]
    dynamic_slice x1, local copies, waits for them, and re-layouts: 2.68 us -> 0.14 us  [shards(): cut = lambda x, start: lax.dynamic_slice_in_dim(x, start, row_feats, axis=0)]
    select_n x1, other arithmetic: 2.57 us -> 0.3 us  [corner(): return swap_by_parity(jnp.where(even, along_x, along_y), 4, 2)]
  transfers between devices with their start and end apart: 30 -> 30, of which waited for: 8 -> 11; matrix products, arithmetic and copies ran while one was open for 7% -> 1% of each run, Pallas kernels for 28% -> 27%
where the time goes in v15:
time: 209 us
  Pallas kernels  100 us (48%)
  waiting for transfers between devices  62.5 us (30%)
  starting transfers between devices  35.5 us (17%)
  other arithmetic  4.44 us (2%)
  local copies, waits for them, and re-layouts  4.31 us (2%)
    pallas_call x4, Pallas kernels, contacts(): pl.pallas_call(functools.partial(gather_kernel, form, chunks, len(sources...  52 us
    pallas_call x1, Pallas kernels, products(): pl.pallas_call(product_kernel, out_shape=[out, out], grid_spec=pltpu.Pref...  44.6 us
    ppermute x17, waiting for transfers between devices, swap(): return lax.ppermute(x, 'tm', [(i, i ^ bits) for i in range(8)])  31 us
    ppermute x3, waiting for transfers between devices, line_hop(): down = lax.ppermute(down, 'feat', [(i + 1, i) for i in range(count - hop)])  19.7 us
    ppermute x17, starting transfers between devices, swap(): return lax.ppermute(x, 'tm', [(i, i ^ bits) for i in range(8)])  14 us
    ppermute x4, waiting for transfers between devices, swap_by_parity(): lax.ppermute(x, 'tm', [(i, i ^ (odd if i % 2 else even)) for i in range(8)])  11.7 us
    ppermute x3, starting transfers between devices, line_hop(): lax.ppermute(up, 'feat', [(i, i + 1) for i in range(hop - 1, count - 1)])  7.9 us
    ppermute x3, starting transfers between devices, line_gather(): lax.ppermute(x, 'feat', shift(s))  6.48 us
  transfers between devices with their start and end apart: 30, of which 11 were waited for; matrix products, arithmetic and copies ran while one was open for 1% of the time, Pallas kernels for 27%

profile of v15, /device:TPU:0, one launch (start us, length us, event | category | flops | bytes accessed | tf_op | source)
XLA Modules:
  0.0 209.0 jit_solution(7668813631286133256)
XLA Ops:
  0.7 2.8 %fusion = s16[3,1500,128]{2,1,0:T(8,128)(2,1)} fusion(s32[512,3,1500]{0,2,1:T(8,128)} %param.4, s32[]{:T(128)S(6)} %select_n.74), kind=kLoop, calls=%fused_computation.1 | loop fusion | flops 576000 | bytes 3456004 | tf_op jit(solution)/shard_map/convert_element_type | solution.py:375
  3.5 2.4 %collective-permute-start.11 = (s16[3,1500,128]{2,1,0:T(8,128)(2,1)}, s16[3,1500,128]{2,1,0:T(8,128)(2,1)S(1)}, u32[]{:S(2)}, u32[]{:S(2)}) collective-permute-start(s16[3,1500,128]{2,1,0:T(8,128)(2,1)} %fusion), channel_id=1, source_target_pairs={{0,20},{4,16},{8,28},{12,24},{16,4},{20,0},{24,12},{28,8},{1,21},{... | collective-permute-start | bytes 3456008 | tf_op jit(solution)/shard_map/ppermute | solution.py:333
  5.9 1.8 collective-permute-start.10
  7.7 14.9 %shard_map.59 = (f32[2048,512]{1,0:T(8,128)S(1)}, f32[1,2048]{1,0:T(1,128)S(1)}, s32[24000,128]{1,0:T(8,128)}) custom-call(s32[2,2048]{1,0:T(2,128)S(1)} %get-tuple-element.136.pairs_ref, f32[4,128]{1,0:T(4,128)S(1)} %bitcast.24, s32[3,1500,512]{2,1,0:T(8,128)} %bitcast.28), custom_call_target="tpu_custom_call" | custom-call | flops 10000000 | bytes 36900 | tf_op jit(solution)/shard_map/pallas_call | solution.py:209
  22.6 2.0 copy-done.3
  24.7 2.4 %collective-permute-start.5 = (f32[1,2560]{1,0:T(1,128)S(1)}, f32[1,2560]{1,0:T(1,128)S(1)}, u32[]{:S(2)}, u32[]{:S(2)}) collective-permute-start(f32[1,2560]{1,0:T(1,128)S(1)} %pad_maximum_fusion.3), channel_id=1, source_target_pairs={{0,24},{4,28},{8,16},{12,20},{16,8},{20,12},{24,0},{28,4},{1,25},{... | collective-permute-start | bytes 30728 | tf_op jit(solution)/shard_map/ppermute | solution.py:333
  27.5 4.5 %collective-permute-done.11.rest_1_ = s16[3,1500,128]{2,1,0:T(8,128)(2,1)S(1)} collective-permute-done((s16[3,1500,128]{2,1,0:T(8,128)(2,1)}, s16[3,1500,128]{2,1,0:T(8,128)(2,1)S(1)}, u32[]{:S(2)}, u32[]{:S(2)}) %collective-permute-start.11) | collective-permute-done | bytes 1152032 | tf_op jit(solution)/shard_map/ppermute | solution.py:333
  32.0 2.3 %collective-permute-start.3 = (f32[1,2560]{1,0:T(1,128)S(1)}, f32[1,2560]{1,0:T(1,128)S(1)}, u32[]{:S(2)}, u32[]{:S(2)}) collective-permute-start(f32[1,2560]{1,0:T(1,128)S(1)} %pad_maximum_fusion.3), channel_id=1, source_target_pairs={{0,16},{4,20},{8,24},{12,28},{16,0},{20,4},{24,8},{28,12},{1,17},{... | collective-permute-start | bytes 30728 | tf_op jit(solution)/shard_map/ppermute | solution.py:333
  39.1 2.7 %collective-permute-start.8 = (f32[3,2048]{1,0:T(4,128)S(1)}, f32[3,2048]{1,0:T(4,128)S(1)}, u32[]{:S(2)}, u32[]{:S(2)}) collective-permute-start(f32[3,2048]{1,0:T(4,128)S(1)} %get-tuple-element.134), channel_id=1, source_target_pairs={{0,2},{1,3},{2,0},{3,1},{4,6},{5,7},{6,4},{7,5},{8,10},{9,11},{10,... | collective-permute-start | bytes 73736 | tf_op jit(solution)/shard_map/ppermute | solution.py:347
  41.7 1.6 collective-permute-start.7
  43.3 2.2 %collective-permute-start.9 = (f32[3,2048]{1,0:T(4,128)S(1)}, f32[3,2048]{1,0:T(4,128)S(1)}, u32[]{:S(2)}, u32[]{:S(2)}) collective-permute-start(f32[3,2048]{1,0:T(4,128)S(1)} %get-tuple-element.134), channel_id=1, source_target_pairs={{0,3},{1,0},{2,1},{3,2},{4,7},{5,4},{6,5},{7,6},{8,11},{9,8},{10,9... | collective-permute-start | bytes 73736 | tf_op jit(solution)/shard_map/ppermute | solution.py:347
  45.6 3.7 %shard_map.60.rest_11_ = bf16[512,2048]{1,0:T(8,128)(2,1)S(1)} custom-call(f32[2048,512]{1,0:T(8,128)} %copy-done.3, f32[1,2048]{1,0:T(1,128)S(1)} %fusion.2.mean_ref), custom_call_target="tpu_custom_call" | custom-call | flops 10000000 | bytes 36900 | tf_op jit(solution)/shard_map/pallas_call | solution.py:229
  49.4 3.1 %collective-permute-done.12.rest_3_ = s16[3,1500,128]{2,1,0:T(8,128)(2,1)S(1)} collective-permute-done((s16[3,1500,128]{2,1,0:T(8,128)(2,1)S(1)}, s16[3,1500,128]{2,1,0:T(8,128)(2,1)S(1)}, u32[]{:S(2)}, u32[]{:S(2)}) %collective-permute-start.12) | collective-permute-done | bytes 1152032 | tf_op jit(solution)/shard_map/ppermute | solution.py:337
  54.6 2.7 %collective-permute-done.13.rest_2_ = s16[3,1500,128]{2,1,0:T(8,128)(2,1)S(1)} collective-permute-done((s16[3,1500,128]{2,1,0:T(8,128)(2,1)S(1)}, s16[3,1500,128]{2,1,0:T(8,128)(2,1)S(1)}, u32[]{:S(2)}, u32[]{:S(2)}) %collective-permute-start.13) | collective-permute-done | bytes 1152032 | tf_op jit(solution)/shard_map/ppermute | solution.py:333
  57.5 12.5 %shard_map.61.rest_4_ = bf16[4,1024,128]{2,1,0:T(8,128)(2,1)} custom-call(s32[2,1024]{1,0:T(2,128)S(1)} %convert_multiply_fusion.1.pairs_ref, f32[4,128]{1,0:T(4,128)S(1)} %pad_maximum_fusion.4.scale_ref, s16[3,1500,128]{2,1,0:T(8,128)(2,1)S(1)} %copy-done.2, s16[3,1500,128]{2,1,0:T(8,128)(2,1)S(1)} %collective-permute-done.11.rest_1_, ...), custom_call_target="tpu_custom_call" | custom-call | flops 10000000 | bytes 36900 | tf_op jit(solution)/shard_map/pallas_call | solution.py:209
  71.3 5.6 %collective-permute-start.14 = (bf16[4,1024,128]{2,1,0:T(8,128)(2,1)}, bf16[4,1024,128]{2,1,0:T(8,128)(2,1)}, u32[]{:S(2)}, u32[]{:S(2)}) collective-permute-start(bf16[4,1024,128]{2,1,0:T(8,128)(2,1)} %shard_map.61.rest_4_), channel_id=1, source_target_pairs={{0,1},{1,2},{2,3},{4,5},{5,6},{6,7},{8,9},{9,10},{10,11},{12,13},{... | collective-permute-start | bytes 3145736 | tf_op jit(solution)/shard_map/ppermute | solution.py:351
  78.6 12.3 %shard_map.62 = bf16[2048,512]{1,0:T(8,128)(2,1)S(1)} custom-call(s32[2,2048]{1,0:T(2,128)S(1)} %get-tuple-element.132.pairs_ref, f32[4,128]{1,0:T(4,128)S(1)} %bitcast.26, s32[24000,128]{1,0:T(8,128)} %get-tuple-element.84.rest_0_, f32[1,2048]{1,0:T(1,128)S(1)} %get-tuple-element.130.rest_1_), custom_call_target="tpu_custom_call" | custom-call | flops 10000000 | bytes 36900 | tf_op jit(solution)/shard_map/pallas_call | solution.py:209
  92.1 8.6 %collective-permute-done.18.rest_15_ = bf16[512,2048]{1,0:T(8,128)(2,1)} collective-permute-done((bf16[512,2048]{1,0:T(8,128)(2,1)S(1)}, bf16[512,2048]{1,0:T(8,128)(2,1)}, u32[]{:S(2)}, u32[]{:S(2)}) %collective-permute-start.18) | collective-permute-done | bytes 2097184 | tf_op jit(solution)/shard_map/ppermute | solution.py:337
  101.6 1.6 collective-permute-start.22
  104.7 12.3 %shard_map.63 = bf16[2048,512]{1,0:T(8,128)(2,1)S(1)} custom-call(s32[2,2048]{1,0:T(2,128)S(1)} %get-tuple-element.91.pairs_ref, f32[4,128]{1,0:T(4,128)S(1)} %bitcast.27, s32[24000,128]{1,0:T(8,128)} %get-tuple-element.84.rest_0_, f32[1,2048]{1,0:T(1,128)S(1)} %get-tuple-element.129.rest_1_), custom_call_target="tpu_custom_call" | custom-call | flops 10000000 | bytes 36900 | tf_op jit(solution)/shard_map/pallas_call | solution.py:209
  117.1 16.2 %collective-permute-done.23.rest_8_ = bf16[4,1024,128]{2,1,0:T(8,128)(2,1)} collective-permute-done((bf16[4,1024,128]{2,1,0:T(8,128)(2,1)}, bf16[4,1024,128]{2,1,0:T(8,128)(2,1)}, u32[]{:S(2)}, u32[]{:S(2)}) %collective-permute-start.23) | collective-permute-done | bytes 1048608 | tf_op jit(solution)/shard_map/ppermute | solution.py:352
  138.1 21.1 %collective-permute-done.26.rest_2_ = bf16[1024,512]{1,0:T(8,128)(2,1)S(1)} collective-permute-done((bf16[1024,512]{1,0:T(8,128)(2,1)}, bf16[1024,512]{1,0:T(8,128)(2,1)S(1)}, u32[]{:S(2)}, u32[]{:S(2)}) %collective-permute-start.26) | collective-permute-done | bytes 1048608 | tf_op jit(solution)/shard_map/ppermute | solution.py:333
  159.7 3.5 %collective-permute-done.29.rest_10_ = bf16[4,1024,128]{2,1,0:T(8,128)(2,1)S(1)} collective-permute-done((bf16[4,1024,128]{2,1,0:T(8,128)(2,1)}, bf16[4,1024,128]{2,1,0:T(8,128)(2,1)S(1)}, u32[]{:S(2)}, u32[]{:S(2)}) %collective-permute-start.29) | collective-permute-done | bytes 1048608 | tf_op jit(solution)/shard_map/ppermute | solution.py:352
  164.2 44.6 %shard_map.64 = (f32[1024,2048]{1,0:T(8,128)}, f32[1024,2048]{1,0:T(8,128)}) custom-call(s32[2]{0:T(128)S(1)} %pad_add_fusion.place_ref, f32[8,4,1,128]{3,2,1,0:T(1,128)S(1)} %fusion.1.mask_ref, f32[2]{0:T(128)S(1)} %pad_maximum_fusion.5.factors_ref, bf16[1024,512]{1,0:T(8,128)(2,1)S(1)} %get-tuple-element.123.rest_0_, ...), custom_call_target="tpu_custom_call" | custom-call | flops 10000000 | bytes 36900 | tf_op jit(solution)/shard_map/pallas_call | solution.py:307
  (90 shorter events, 19.7 us)
Async XLA Ops:
  3.5 28.6 %collective-permute-start.11 = (s16[3,1500,128]{2,1,0:T(8,128)(2,1)}, s16[3,1500,128]{2,1,0:T(8,128)(2,1)S(1)}, u32[]{:S(2)}, u32[]{:S(2)}) collective-permute-start(s16[3,1500,128]{2,1,0:T(8,128)(2,1)} %fusion), channel_id=1, source_target_pairs={{0,20},{4,16},{8,28},{12,24},{16,4},{20,0},{24,12},{28,8},{1,21},{... | collective-permute-start | bytes 3456008 | tf_op jit(solution)/shard_map/ppermute | solution.py:333
  5.9 28.5 %collective-permute-start.10 = (s16[3,1500,128]{2,1,0:T(8,128)(2,1)}, s16[3,1500,128]{2,1,0:T(8,128)(2,1)S(1)}, u32[]{:S(2)}, u32[]{:S(2)}) collective-permute-start(s16[3,1500,128]{2,1,0:T(8,128)(2,1)} %fusion), channel_id=1, source_target_pairs={{0,12},{4,8},{8,4},{12,0},{16,28},{20,24},{24,20},{28,16},{1,13},{... | collective-permute-start | bytes 3456008 | tf_op jit(solution)/shard_map/ppermute | solution.py:333
  24.6 10.7 %collective-permute-start.6 = (f32[1,2560]{1,0:T(1,128)S(1)}, f32[1,2560]{1,0:T(1,128)S(1)}, u32[]{:S(2)}, u32[]{:S(2)}) collective-permute-start(f32[1,2560]{1,0:T(1,128)S(1)} %pad_maximum_fusion.3), channel_id=1, source_target_pairs={{0,28},{4,24},{8,20},{12,16},{16,12},{20,8},{24,4},{28,0},{1,29},{... | collective-permute-start | bytes 30728 | tf_op jit(solution)/shard_map/ppermute | solution.py:333
  24.7 11.3 %collective-permute-start.5 = (f32[1,2560]{1,0:T(1,128)S(1)}, f32[1,2560]{1,0:T(1,128)S(1)}, u32[]{:S(2)}, u32[]{:S(2)}) collective-permute-start(f32[1,2560]{1,0:T(1,128)S(1)} %pad_maximum_fusion.3), channel_id=1, source_target_pairs={{0,24},{4,28},{8,16},{12,20},{16,8},{20,12},{24,0},{28,4},{1,25},{... | collective-permute-start | bytes 30728 | tf_op jit(solution)/shard_map/ppermute | solution.py:333
  27.0 9.5 %collective-permute-start.4 = (f32[1,2560]{1,0:T(1,128)S(1)}, f32[1,2560]{1,0:T(1,128)S(1)}, u32[]{:S(2)}, u32[]{:S(2)}) collective-permute-start(f32[1,2560]{1,0:T(1,128)S(1)} %pad_maximum_fusion.3), channel_id=1, source_target_pairs={{0,20},{4,16},{8,28},{12,24},{16,4},{20,0},{24,12},{28,8},{1,21},{... | collective-permute-start | bytes 30728 | tf_op jit(solution)/shard_map/ppermute | solution.py:333
  36.6 16.0 %collective-permute-start.12 = (s16[3,1500,128]{2,1,0:T(8,128)(2,1)S(1)}, s16[3,1500,128]{2,1,0:T(8,128)(2,1)S(1)}, u32[]{:S(2)}, u32[]{:S(2)}) collective-permute-start(s16[3,1500,128]{2,1,0:T(8,128)(2,1)S(1)} %broadcast_select_fusion), channel_id=1, source_target_pairs={{0,16},{4,12},{8,24},{12,4},{16,0},{20,28},{24,8},{28,20},{1,17},{... | collective-permute-start | bytes 3456008 | tf_op jit(solution)/shard_map/ppermute | solution.py:337
  39.1 10.3 %collective-permute-start.8 = (f32[3,2048]{1,0:T(4,128)S(1)}, f32[3,2048]{1,0:T(4,128)S(1)}, u32[]{:S(2)}, u32[]{:S(2)}) collective-permute-start(f32[3,2048]{1,0:T(4,128)S(1)} %get-tuple-element.134), channel_id=1, source_target_pairs={{0,2},{1,3},{2,0},{3,1},{4,6},{5,7},{6,4},{7,5},{8,10},{9,11},{10,... | collective-permute-start | bytes 73736 | tf_op jit(solution)/shard_map/ppermute | solution.py:347
  41.7 7.6 %collective-permute-start.7 = (f32[3,2048]{1,0:T(4,128)S(1)}, f32[3,2048]{1,0:T(4,128)S(1)}, u32[]{:S(2)}, u32[]{:S(2)}) collective-permute-start(f32[3,2048]{1,0:T(4,128)S(1)} %get-tuple-element.134), channel_id=1, source_target_pairs={{0,1},{1,2},{2,3},{3,0},{4,5},{5,6},{6,7},{7,4},{8,9},{9,10},{10,1... | collective-permute-start | bytes 73736 | tf_op jit(solution)/shard_map/ppermute | solution.py:347
  43.3 6.1 %collective-permute-start.9 = (f32[3,2048]{1,0:T(4,128)S(1)}, f32[3,2048]{1,0:T(4,128)S(1)}, u32[]{:S(2)}, u32[]{:S(2)}) collective-permute-start(f32[3,2048]{1,0:T(4,128)S(1)} %get-tuple-element.134), channel_id=1, source_target_pairs={{0,3},{1,0},{2,1},{3,2},{4,7},{5,4},{6,5},{7,6},{8,11},{9,8},{10,9... | collective-permute-start | bytes 73736 | tf_op jit(solution)/shard_map/ppermute | solution.py:347
  52.6 48.1 %collective-permute-start.18 = (bf16[512,2048]{1,0:T(8,128)(2,1)S(1)}, bf16[512,2048]{1,0:T(8,128)(2,1)}, u32[]{:S(2)}, u32[]{:S(2)}) collective-permute-start(bf16[512,2048]{1,0:T(8,128)(2,1)S(1)} %shard_map.60.rest_11_), channel_id=1, source_target_pairs={{0,16},{4,12},{8,24},{12,4},{16,0},{20,28},{24,8},{28,20},{1,17},{... | collective-permute-start | bytes 6291464 | tf_op jit(solution)/shard_map/ppermute | solution.py:337
  53.0 47.7 %collective-permute-start.17 = (bf16[512,2048]{1,0:T(8,128)(2,1)S(1)}, bf16[512,2048]{1,0:T(8,128)(2,1)}, u32[]{:S(2)}, u32[]{:S(2)}) collective-permute-start(bf16[512,2048]{1,0:T(8,128)(2,1)S(1)} %shard_map.60.rest_11_), channel_id=1, source_target_pairs={{0,8},{4,20},{8,0},{12,28},{16,24},{20,4},{24,16},{28,12},{1,9},{5... | collective-permute-start | bytes 6291464 | tf_op jit(solution)/shard_map/ppermute | solution.py:337
  57.3 43.4 %collective-permute-start.16 = (bf16[512,2048]{1,0:T(8,128)(2,1)S(1)}, bf16[512,2048]{1,0:T(8,128)(2,1)}, u32[]{:S(2)}, u32[]{:S(2)}) collective-permute-start(bf16[512,2048]{1,0:T(8,128)(2,1)S(1)} %shard_map.60.rest_11_), channel_id=1, source_target_pairs={{0,4},{4,0},{8,12},{12,8},{16,20},{20,16},{24,28},{28,24},{1,5},{5... | collective-permute-start | bytes 6291464 | tf_op jit(solution)/shard_map/ppermute | solution.py:333
  70.0 30.7 %collective-permute-start.15 = (bf16[4,1024,128]{2,1,0:T(8,128)(2,1)}, bf16[4,1024,128]{2,1,0:T(8,128)(2,1)}, u32[]{:S(2)}, u32[]{:S(2)}) collective-permute-start(bf16[4,1024,128]{2,1,0:T(8,128)(2,1)} %shard_map.61.rest_4_), channel_id=1, source_target_pairs={{1,0},{2,1},{3,2},{5,4},{6,5},{7,6},{9,8},{10,9},{11,10},{13,12},{... | collective-permute-start | bytes 3145736 | tf_op jit(solution)/shard_map/ppermute | solution.py:352
  71.3 29.4 %collective-permute-start.14 = (bf16[4,1024,128]{2,1,0:T(8,128)(2,1)}, bf16[4,1024,128]{2,1,0:T(8,128)(2,1)}, u32[]{:S(2)}, u32[]{:S(2)}) collective-permute-start(bf16[4,1024,128]{2,1,0:T(8,128)(2,1)} %shard_map.61.rest_4_), channel_id=1, source_target_pairs={{0,1},{1,2},{2,3},{4,5},{5,6},{6,7},{8,9},{9,10},{10,11},{12,13},{... | collective-permute-start | bytes 3145736 | tf_op jit(solution)/shard_map/ppermute | solution.py:351
  100.7 32.5 %collective-permute-start.20 = (bf16[512,2048]{1,0:T(8,128)(2,1)}, bf16[512,2048]{1,0:T(8,128)(2,1)}, u32[]{:S(2)}, u32[]{:S(2)}) collective-permute-start(bf16[512,2048]{1,0:T(8,128)(2,1)} %collective-permute-done.18.rest_15_), channel_id=1, source_target_pairs={{0,4},{4,0},{8,12},{12,8},{16,20},{20,16},{24,28},{28,24},{1,5},{5... | collective-permute-start | bytes 6291464 | tf_op jit(solution)/shard_map/ppermute | solution.py:333
  100.8 32.5 %collective-permute-start.21 = (bf16[512,2048]{1,0:T(8,128)(2,1)}, bf16[512,2048]{1,0:T(8,128)(2,1)}, u32[]{:S(2)}, u32[]{:S(2)}) collective-permute-start(bf16[512,2048]{1,0:T(8,128)(2,1)} %collective-permute-done.17.rest_13_), channel_id=1, source_target_pairs={{0,16},{4,12},{8,24},{12,4},{16,0},{20,28},{24,8},{28,20},{1,17},{... | collective-permute-start | bytes 6291464 | tf_op jit(solution)/shard_map/ppermute | solution.py:337
  101.4 31.8 %collective-permute-start.19 = (bf16[512,2048]{1,0:T(8,128)(2,1)}, bf16[512,2048]{1,0:T(8,128)(2,1)}, u32[]{:S(2)}, u32[]{:S(2)}) collective-permute-start(bf16[512,2048]{1,0:T(8,128)(2,1)} %collective-permute-done.17.rest_13_), channel_id=1, source_target_pairs={{0,4},{4,0},{8,12},{12,8},{16,20},{20,16},{24,28},{28,24},{1,5},{5... | collective-permute-start | bytes 6291464 | tf_op jit(solution)/shard_map/ppermute | solution.py:333
  101.6 15.4 %collective-permute-start.22 = (bf16[4,1024,128]{2,1,0:T(8,128)(2,1)}, bf16[4,1024,128]{2,1,0:T(8,128)(2,1)}, u32[]{:S(2)}, u32[]{:S(2)}) collective-permute-start(bf16[4,1024,128]{2,1,0:T(8,128)(2,1)} %collective-permute-done.14.rest_5_), channel_id=1, source_target_pairs={{1,2},{2,3},{5,6},{6,7},{9,10},{10,11},{13,14},{14,15},{17,18},{18... | collective-permute-start | bytes 3145736 | tf_op jit(solution)/shard_map/ppermute | solution.py:351
  103.3 30.0 %collective-permute-start.23 = (bf16[4,1024,128]{2,1,0:T(8,128)(2,1)}, bf16[4,1024,128]{2,1,0:T(8,128)(2,1)}, u32[]{:S(2)}, u32[]{:S(2)}) collective-permute-start(bf16[4,1024,128]{2,1,0:T(8,128)(2,1)} %collective-permute-done.15.rest_6_), channel_id=1, source_target_pairs={{1,0},{2,1},{5,4},{6,5},{9,8},{10,9},{13,12},{14,13},{17,16},{18,1... | collective-permute-start | bytes 3145736 | tf_op jit(solution)/shard_map/ppermute | solution.py:352
  133.4 25.8 %collective-permute-start.26 = (bf16[1024,512]{1,0:T(8,128)(2,1)}, bf16[1024,512]{1,0:T(8,128)(2,1)S(1)}, u32[]{:S(2)}, u32[]{:S(2)}) collective-permute-start(bf16[1024,512]{1,0:T(8,128)(2,1)} %get-tuple-element.108), channel_id=1, source_target_pairs={{0,8},{4,12},{8,0},{12,4},{16,24},{20,28},{24,16},{28,20},{1,9},{5... | collective-permute-start | bytes 3145736 | tf_op jit(solution)/shard_map/ppermute | solution.py:333
  134.5 25.2 %collective-permute-start.27 = (bf16[1024,512]{1,0:T(8,128)(2,1)S(1)}, bf16[1024,512]{1,0:T(8,128)(2,1)S(1)}, u32[]{:S(2)}, u32[]{:S(2)}) collective-permute-start(bf16[1024,512]{1,0:T(8,128)(2,1)S(1)} %get-tuple-element.109), channel_id=1, source_target_pairs={{0,16},{4,20},{8,24},{12,28},{16,0},{20,4},{24,8},{28,12},{1,17},{... | collective-permute-start | bytes 3145736 | tf_op jit(solution)/shard_map/ppermute | solution.py:333
  135.5 24.3 %collective-permute-start.28 = (bf16[4,1024,128]{2,1,0:T(8,128)(2,1)}, bf16[4,1024,128]{2,1,0:T(8,128)(2,1)S(1)}, u32[]{:S(2)}, u32[]{:S(2)}) collective-permute-start(bf16[4,1024,128]{2,1,0:T(8,128)(2,1)} %collective-permute-done.22.rest_7_), channel_id=1, source_target_pairs={{2,3},{6,7},{10,11},{14,15},{18,19},{22,23},{26,27},{30,31}} | collective-permute-start | bytes 3145736 | tf_op jit(solution)/shard_map/ppermute | solution.py:351
  136.2 27.0 %collective-permute-start.29 = (bf16[4,1024,128]{2,1,0:T(8,128)(2,1)}, bf16[4,1024,128]{2,1,0:T(8,128)(2,1)S(1)}, u32[]{:S(2)}, u32[]{:S(2)}) collective-permute-start(bf16[4,1024,128]{2,1,0:T(8,128)(2,1)} %collective-permute-done.23.rest_8_), channel_id=1, source_target_pairs={{1,0},{5,4},{9,8},{13,12},{17,16},{21,20},{25,24},{29,28}} | collective-permute-start | bytes 3145736 | tf_op jit(solution)/shard_map/ppermute | solution.py:352
  137.8 25.4 %collective-permute-start.25 = (bf16[1024,512]{1,0:T(8,128)(2,1)S(1)}, bf16[1024,512]{1,0:T(8,128)(2,1)S(1)}, u32[]{:S(2)}, u32[]{:S(2)}) collective-permute-start(bf16[1024,512]{1,0:T(8,128)(2,1)S(1)} %get-tuple-element.107), channel_id=1, source_target_pairs={{0,4},{4,0},{8,12},{12,8},{16,20},{20,16},{24,28},{28,24},{1,5},{5... | collective-permute-start | bytes 3145736 | tf_op jit(solution)/shard_map/ppermute | solution.py:333
  (15 other events, 106.1 us)
